TPU v7x, 32 devices: a whole 2x2x4 slice. The times are simulated.
32 devices in a mesh: dp: 8 (over y, x, core), tensor: 4 (over z).
Axes of the slice: x: 2, y: 2, z: 4, core: 2. Of those that a mesh axis runs over, the one named last changes fastest.
Arguments:
- inputs: bfloat16 [256, 4096], P(('dp', 'tensor')), may hold values from -6 to 6
- block_values: bfloat16 [4, 40, 64, 64], P('tensor', 'dp'), may hold values from -0.1875 to 0.1875
- block_slot: int32 [4, 40], P('tensor', 'dp'), may hold values from -1 to 895, as said below
- grad_out: bfloat16 [256, 3584], P('dp', 'tensor'), may hold values from -6 to 6
Outputs:
- outputs: bfloat16 [256, 3584], P('dp', 'tensor')
- grad_in: bfloat16 [256, 4096], P(('dp', 'tensor'))
Inputs may be any that keep to these rules, and one draw needn't show every extreme that they name: `block_slot`: A tensor shard's slots hold distinct block positions row * 14 + col, or -1 for an empty slot; empty slots come after all filled ones; a shard fills at least 13 of its 40 slots, in every draw some shard fills all of them and some shard leaves a slot empty.
All inputs are finite; a program needn't handle non-finite values.
Results may differ from a plain program's by a relative error of at most 0.022.
Values may be sent and summed in bfloat16 or wider, within the bound.
No kernel may reach another device: no remote copies, remote signals or barrier semaphores. Data moves between devices by JAX's collectives and lax.ppermute only.
A program may use at most 128 MiB of HBM per device.

v0:
```python
import jax
import jax.numpy as jnp
from jax import lax
from jax.sharding import PartitionSpec as P


def assemble(values, slot_ids, row_count, col_count):
    positions = row_count * col_count
    target = jnp.where(slot_ids >= 0, slot_ids, positions).astype(jnp.int32)
    side = values.shape[1]
    dense_blocks = jnp.zeros((positions + 1, side, side), jnp.bfloat16).at[target].set(values)
    return dense_blocks[:positions].reshape(row_count, col_count, side, side)


def on_device(inputs, block_values, block_slot, grad_out):
    width = inputs.shape[1]
    hidden = grad_out.shape[1]
    side = block_values.shape[2]
    row_count = width // side
    col_count = hidden // side
    token_rows = lax.all_gather(inputs, "tensor", axis=0, tiled=True)
    gathered_values, gathered_slots = (
        lax.all_gather(block_values, "dp", axis=1, tiled=True),
        lax.all_gather(block_slot, "dp", axis=1, tiled=True),
    )
    dense_blocks = assemble(gathered_values[0], gathered_slots[0], row_count, col_count)
    row_blocks = token_rows.reshape(-1, row_count, side)
    outputs = jnp.einsum(
        "trj,rfjk->tfk", row_blocks, dense_blocks, preferred_element_type=jnp.float32
    )
    outputs = outputs.reshape(-1, hidden).astype(jnp.bfloat16)
    second_values, second_slots = (
        lax.all_gather(block_values, "dp", axis=1, tiled=True),
        lax.all_gather(block_slot, "dp", axis=1, tiled=True),
    )
    backward_blocks = assemble(second_values[0], second_slots[0], row_count, col_count)
    grad_blocks = grad_out.reshape(-1, col_count, side)
    partial_value = jnp.einsum(
        "tfk,rfjk->trj", grad_blocks, backward_blocks, preferred_element_type=jnp.float32
    )
    grad_in = lax.psum_scatter(
        partial_value.reshape(-1, width).astype(jnp.bfloat16),
        "tensor",
        scatter_dimension=0,
        tiled=True,
    )
    return (outputs, grad_in)


def solution(mesh):
    placed = (
        P(("dp", "tensor"), None),
        P("tensor", "dp", None, None),
        P("tensor", "dp"),
        P("dp", "tensor"),
    )
    return jax.shard_map(
        on_device,
        mesh=mesh,
        in_specs=placed,
        out_specs=(P("dp", "tensor"), P(("dp", "tensor"), None)),
        check_vma=False,
    )
```

profile of v0, /device:TPU:0, one launch (start us, length us, event | category | flops | bytes accessed | tf_op | source)
XLA Modules:
  0.0 100.1 jit_solution(3511003500396484860)
XLA Ops:
  7.2 0.0 reduce-scatter.2.cloned.1.call-start
  7.2 11.9 %all_gather.12 = bf16[1,40,64,64]{3,2,0,1:T(8,128)(2,1)S(1)} all-gather(bf16[1,5,64,64]{3,2,0,1:T(8,128)(2,1)} %bitcast.37), channel_id=1, replica_groups=mesh['dp'=8,'tensor'=4] {'dp'}, dimensions={1}, use_global_device_ids=true | all-gather | bytes 368640 | tf_op jit(solution)/shard_map/all_gather | solution.py:23
  19.1 1.2 %dynamic-slice = u32[1]{0:T(128)} dynamic-slice(u32[32]{0:T(128)} %constant.13, u32[]{:T(128)S(6)} %add.14), dynamic_slice_sizes={1} | dynamic-slice | bytes 12
  21.0 0.8 bitcast_dynamic-update-slice_fusion
  21.8 7.0 %all-reduce = s32[40]{0:T(128)S(1)} all-reduce(s32[40]{0:T(128)S(1)} %bitcast_dynamic-update-slice_fusion), channel_id=1, replica_groups=mesh['dp'=8,'tensor'=4] {'dp'}, use_global_device_ids=true, to_apply=%add | all-reduce | flops 40 | bytes 320
  28.8 9.0 %broadcast.37 = bf16[897,64,64]{2,1,0:T(8,128)(2,1)} broadcast(bf16[]{:T(256)} %constant.0.clone.1), dimensions={} | broadcast | bytes 7348226 | tf_op jit(solution)/shard_map/broadcast.4
  37.8 6.4 %scatter_fusion = bf16[897,64,64]{2,1,0:T(8,128)(2,1)} fusion(bf16[897,64,64]{2,1,0:T(8,128)(2,1)} %broadcast.37, s32[40]{0:T(128)S(1)} %fusion.7, bf16[40,64,64]{2,1,0:T(8,128)(2,1)S(1)} %bitcast.35), kind=kCustom, calls=%fused_computation | custom fusion | bytes 983200 | tf_op jit(solution)/shard_map/scatter | solution.py:11
  44.2 0.0 copy-start.1
  44.3 13.2 %slice.5 = bf16[896,64,64]{2,1,0:T(8,128)(2,1)} slice(bf16[897,64,64]{2,1,0:T(8,128)(2,1)} %scatter_fusion), slice={[0:896], [0:64], [0:64]} | slice | bytes 14680064 | tf_op jit(solution)/shard_map/slice | solution.py:12
  57.5 0.0 copy-done.1
  57.5 0.0 copy-start
  57.5 0.1 reshape.48
  57.6 10.9 %fusion.1 = bf16[32,64,64]{2,0,1:T(8,128)(2,1)S(1)} fusion(bf16[64,14,64,64]{3,2,1,0:T(8,128)(2,1)} %bitcast.33, bf16[32,14,64]{2,1,0:T(8,128)(2,1)S(1)} %reshape.48), kind=kOutput, calls=%fused_computation.3 | convolution fusion | flops 235012096 | bytes 7659520 | tf_op jit(solution)/shard_map/tfk,rfjk->trj/dot_general | solution.py:38
  68.5 0.2 copy.17
  68.8 1.2 %convert_element_type.23 = bf16[32,4096]{1,0:T(8,128)(2,1)} reshape(bf16[32,64,64]{2,1,0:T(8,128)(2,1)S(1)} %copy.17) | data formatting | bytes 524288 | tf_op jit(solution)/shard_map/convert_element_type | solution.py:42
  69.9 0.0 reduce-scatter.2.cloned.1.call-update
  69.9 0.0 copy-done
  70.0 14.9 %all_gather.13 = bf16[32,4096]{1,0:T(8,128)(2,1)S(1)} all-gather(bf16[8,4096]{1,0:T(8,128)(2,1)S(1)} %copy-done), channel_id=1, replica_groups=mesh['dp'=8,'tensor'=4] {'tensor'}, dimensions={0}, use_global_device_ids=true | all-gather | bytes 327680 | tf_op jit(solution)/shard_map/all_gather | solution.py:21
  84.9 0.5 reshape.47
  85.4 7.0 %fusion.3 = bf16[32,14,64]{2,0,1:T(8,128)(2,1)S(1)} fusion(bf16[64,14,64,64]{3,2,1,0:T(8,128)(2,1)} %bitcast.34, bf16[32,64,64,1]{2,1,0,3:T(8,128)(2,1)S(1)} %bitcast.36), kind=kOutput, calls=%fused_computation.6 | convolution fusion | flops 234909696 | bytes 7659520 | tf_op jit(solution)/shard_map/trj,rfjk->tfk/dot_general | solution.py:28
  92.5 0.8 convert_element_type.20
  93.3 0.0 reduce-scatter.2.cloned.1.call-done
  (3 shorter events, 0.1 us)
Async XLA Ops:
  7.2 86.1 %reduce-scatter.2.cloned.1.call-start = ((), (), s32[]{:S(2)}) async-start(), calls=%async_computation.1 | async-start | bytes 327680 | tf_op jit(solution)/shard_map/reduce_scatter | solution.py:41
  44.2 13.2 %copy-start.1 = (bf16[32,896]{1,0:T(8,128)(2,1)S(1)}, bf16[32,896]{1,0:T(8,128)(2,1)}, u32[]{:S(2)}) copy-start(bf16[32,896]{1,0:T(8,128)(2,1)} %param.7) | copy-start | bytes 172036
  57.5 12.5 %copy-start = (bf16[8,4096]{1,0:T(8,128)(2,1)S(1)}, bf16[8,4096]{1,0:T(8,128)(2,1)}, u32[]{:S(2)}) copy-start(bf16[8,4096]{1,0:T(8,128)(2,1)} %param.4) | copy-start | bytes 196612
Sparse Core Ops, SparseCore 0:
  70.1 20.2 reduce-scatter.1
where the time goes:
time: 101 us; the launch traced here: 100 us
  blocking collectives  33.9 us (34%)
  local copies, waits for them, and re-layouts  33.5 us (33%)
  matrix products  17.9 us (18%)
  between operations  14.8 us (15%)
    all_gather x1, blocking collectives, on_device(): token_rows = lax.all_gather(inputs, 'tensor', axis=0, tiled=True)  14.9 us
    slice x1, local copies, waits for them, and re-layouts, assemble(): return dense_blocks[:positions].reshape(row_count, col_count, side, side)  13.2 us
    all_gather x1, blocking collectives, on_device(): lax.all_gather(block_values, 'dp', axis=1, tiled=True)  11.9 us
    dot_general x1, matrix products, on_device(): jnp.einsum('tfk,rfjk->trj', grad_blocks, backward_blocks, preferred_eleme...  10.9 us
    another operation x1, local copies, waits for them, and re-layouts  8.98 us
    unnamed x1, blocking collectives  7.03 us
    dot_general x1, matrix products, on_device(): jnp.einsum('trj,rfjk->tfk', row_blocks, dense_blocks, preferred_element_t...  7.02 us
    scatter x1, local copies, waits for them, and re-layouts, assemble(): jnp.zeros((positions + 1, side, side), jnp.bfloat16).at[target].set(values)  6.44 us
  transfers between devices with their start and end apart: 1, of which 0 were waited for; matrix products, arithmetic and copies ran while one was open for 8% of the time, Pallas kernels for 0%

commit v1 on v0

v1 whole, which is shorter than its diff:
```python
import functools

import jax
import jax.numpy as jnp
from jax import lax
from jax.experimental import pallas as pl
from jax.experimental.pallas import tpu as pltpu
from jax.sharding import PartitionSpec as P

VMEM = pl.BlockSpec(memory_space=pltpu.VMEM)
SMEM = pl.BlockSpec(memory_space=pltpu.SMEM)
LIMIT = 48 * 1024 * 1024


def pack_kernel(count, row_count, col_count, slots, values, packed):
    side = values.shape[2]
    pairs = packed.shape[0]
    lane = lax.broadcasted_iota(jnp.int32, (side, side), 1)
    line = lax.broadcasted_iota(jnp.int32, (side, side), 0)
    head = jnp.zeros((side, side), jnp.float32)
    for j in range(count):
        p = slots[0, j]
        row = jnp.where(p >= 0, p // col_count, row_count)
        col = jnp.where(p >= 0, p % col_count, col_count)
        here = jnp.where(line == 0, row, col).astype(jnp.float32)
        head = jnp.where(lane == j, here, head)
    head = head.astype(jnp.bfloat16)
    for k in range(pairs):
        left = values[0, k]
        right = values[0, k + pairs] if k + pairs < count else head
        packed[k] = jnp.concatenate([left, right], axis=1)


def load_ids(gathered, ids_vmem, ids, sem):
    side = gathered.shape[2]
    head = gathered[:, gathered.shape[1] - 1, 0:16, :].astype(jnp.float32).astype(jnp.int32)
    ids_vmem[...] = head[:, 0:8, :]
    copy = pltpu.make_async_copy(ids_vmem, ids, sem)
    copy.start()
    return copy


def over(n, body):
    if n <= 8:
        for d in range(n):
            body(d)
    else:
        def step(d, carry):
            body(d)
            return carry
        lax.fori_loop(0, n, step, 0)


def backward_kernel(count, n_tensor, gathered, cot, *rest):
    outs = rest[:n_tensor]
    ids_vmem, ids, cot_left, cot_right, prod, acc, sem = rest[n_tensor:]
    n_dp, pairs, side, _ = gathered.shape
    col_count = cot_left.shape[0] - 1
    row_count = acc.shape[0] - 1
    copy = load_ids(gathered, ids_vmem, ids, sem)
    acc[...] = jnp.zeros_like(acc)
    zero = jnp.zeros((cot.shape[0], side), jnp.bfloat16)
    for c in range(col_count):
        part = cot[:, c * side:(c + 1) * side]
        cot_left[c] = jnp.concatenate([part, zero], axis=1)
        cot_right[c] = jnp.concatenate([zero, part], axis=1)
    both = jnp.concatenate([zero, zero], axis=1)
    cot_left[col_count] = both
    cot_right[col_count] = both
    copy.wait()
    rows = cot.shape[0]

    def multiply(d):
        for k in range(pairs):
            left = cot_left[ids[d, 1, side + k]]
            if k + pairs < count:
                right = cot_right[ids[d, 1, side + k + pairs]]
            else:
                right = both
            lhs = jnp.concatenate([left, right], axis=0)
            prod[d * pairs + k] = lax.dot_general(
                lhs, gathered[d, k], (((1,), (1,)), ((), ())), preferred_element_type=jnp.float32
            )

    def add(d):
        for k in range(pairs):
            acc[ids[d, 0, side + k]] += prod[d * pairs + k, 0:rows, :]
            if k + pairs < count:
                acc[ids[d, 0, side + k + pairs]] += prod[d * pairs + k, rows:2 * rows, :]

    over(n_dp, multiply)
    over(n_dp, add)
    me = lax.axis_index("tensor")
    share = rows // n_tensor
    for k in range(n_tensor):
        start = pl.multiple_of(lax.rem(me + k, n_tensor) * share, share)
        for r in range(0, row_count, 2):
            pair = jnp.concatenate(
                [acc[r, pl.ds(start, share), :], acc[r + 1, pl.ds(start, share), :]], axis=1
            )
            outs[k][:, r * side:(r + 2) * side] = pair.astype(jnp.bfloat16)


def forward_kernel(count, n_tensor, gathered, *rest):
    tokens = rest[:n_tensor]
    out = rest[n_tensor]
    ids_vmem, ids, blocks, prod, acc, stage, sem = rest[n_tensor + 1:]
    n_dp, pairs, side, _ = gathered.shape
    row_count = blocks.shape[0] - 1
    col_count = acc.shape[0] - 1
    rows = blocks.shape[1]
    share = rows // n_tensor
    copy = load_ids(gathered, ids_vmem, ids, sem)
    acc[...] = jnp.zeros_like(acc)
    for r in range(row_count):
        parts = [tokens[k][:, r * side:(r + 1) * side].astype(jnp.float32) for k in range(n_tensor)]
        blocks[r] = jnp.concatenate(parts, axis=0).astype(jnp.bfloat16)
    blocks[row_count] = jnp.zeros((rows, side), jnp.bfloat16)
    copy.wait()

    def multiply(d):
        for k in range(pairs):
            left = blocks[ids[d, 0, side + k]]
            right = blocks[ids[d, 0, side + k + pairs]] if k + pairs < count else jnp.zeros_like(left)
            lhs = jnp.concatenate([left, right], axis=0)
            prod[d * pairs + k] = jnp.dot(lhs, gathered[d, k], preferred_element_type=jnp.float32)

    lane = lax.broadcasted_iota(jnp.int32, (rows, 2 * side), 1)

    def add(d):
        for k in range(pairs):
            acc[ids[d, 1, side + k]] += jnp.where(lane < side, prod[d * pairs + k, 0:rows, :], 0.0)
            if k + pairs < count:
                acc[ids[d, 1, side + k + pairs]] += jnp.where(
                    lane >= side, prod[d * pairs + k, rows:2 * rows, :], 0.0
                )

    over(n_dp, multiply)
    over(n_dp, add)
    me = lax.axis_index("tensor")
    for k in range(n_tensor):
        start = pl.multiple_of(lax.rem(me - k + n_tensor, n_tensor) * share, share)
        for c in range(0, col_count, 2):
            sums = []
            for i in (c, c + 1):
                value = acc[i, k * share:(k + 1) * share, :]
                sums.append(value[:, :side] + value[:, side:])
            stage[pl.ds(start, share), c * side:(c + 2) * side] = jnp.concatenate(sums, axis=1)
    out[...] = stage[...].astype(jnp.bfloat16)


def on_device(n_dp, n_tensor, inputs, block_values, block_slot, grad_out):
    share, width = inputs.shape
    rows, hidden = grad_out.shape
    _, count, side, _ = block_values.shape
    row_count, col_count = width // side, hidden // side
    pairs = count // 2 + 1
    bf16, f32, i32 = jnp.bfloat16, jnp.float32, jnp.int32

    def shift(value, k):
        return lax.ppermute(value, "tensor", [(i, (i + k) % n_tensor) for i in range(n_tensor)])

    tokens = [inputs] + [shift(inputs, k) for k in range(1, n_tensor)]
    packed = pl.pallas_call(
        functools.partial(pack_kernel, count, row_count, col_count),
        out_shape=jax.ShapeDtypeStruct((pairs, side, 2 * side), bf16),
        in_specs=[SMEM, VMEM],
        out_specs=VMEM,
    )(block_slot, block_values)
    gathered = lax.all_gather(packed, "dp", axis=0, tiled=False)
    total = n_dp * pairs
    ids = [
        pltpu.VMEM((n_dp, 8, 2 * side), i32),
        pltpu.SMEM((n_dp, 8, 2 * side), i32),
    ]
    partial_sums = pl.pallas_call(
        functools.partial(backward_kernel, count, n_tensor),
        out_shape=[jax.ShapeDtypeStruct((share, width), bf16)] * n_tensor,
        in_specs=[VMEM] * 2,
        out_specs=[VMEM] * n_tensor,
        scratch_shapes=ids + [
            pltpu.VMEM((col_count + 1, rows, 2 * side), bf16),
            pltpu.VMEM((col_count + 1, rows, 2 * side), bf16),
            pltpu.VMEM((total, 2 * rows, side), f32),
            pltpu.VMEM((row_count + 1, rows, side), f32),
            pltpu.SemaphoreType.DMA,
        ],
        compiler_params=pltpu.CompilerParams(vmem_limit_bytes=LIMIT),
    )(gathered, grad_out)
    arrived = [partial_sums[0]] + [shift(partial_sums[k], k) for k in range(1, n_tensor)]
    outputs = pl.pallas_call(
        functools.partial(forward_kernel, count, n_tensor),
        out_shape=jax.ShapeDtypeStruct((rows, hidden), bf16),
        in_specs=[VMEM] * (1 + n_tensor),
        out_specs=VMEM,
        scratch_shapes=ids + [
            pltpu.VMEM((row_count + 1, rows, side), bf16),
            pltpu.VMEM((total, 2 * rows, 2 * side), f32),
            pltpu.VMEM((col_count + 1, rows, 2 * side), f32),
            pltpu.VMEM((rows, hidden), f32),
            pltpu.SemaphoreType.DMA,
        ],
        compiler_params=pltpu.CompilerParams(vmem_limit_bytes=LIMIT),
    )(gathered, *tokens)
    total_grad = arrived[0].astype(f32)
    for value in arrived[1:]:
        total_grad = total_grad + value.astype(f32)
    return (outputs, total_grad.astype(bf16))


def solution(mesh):
    placed = (
        P(("dp", "tensor"), None),
        P("tensor", "dp", None, None),
        P("tensor", "dp"),
        P("dp", "tensor"),
    )
    return jax.shard_map(
        functools.partial(on_device, mesh.shape["dp"], mesh.shape["tensor"]),
        mesh=mesh,
        in_specs=placed,
        out_specs=(P("dp", "tensor"), P(("dp", "tensor"), None)),
        check_vma=False,
    )
```

time: 101 us -> 31.4 us (0.31)
  local copies, waits for them, and re-layouts: 33.5 us -> 0.01 us
  blocking collectives: 33.9 us -> 9.96 us
  matrix products: 17.9 us -> 0 us
  between operations: 14.8 us -> 0.67 us
  starting transfers between devices: 0.04 us -> 11.8 us
  Pallas kernels: 0 us -> 5.71 us
  waiting for transfers between devices: 0.02 us -> 2.36 us
    dot_general x2 -> x0, matrix products: 17.9 us -> none  [the longest x1 10.9 us: on_device(): jnp.einsum('tfk,rfjk->trj', grad_blocks, backward_blocks, preferred_eleme...]
    all_gather x2 -> x1, blocking collectives: 26.8 us -> 9.96 us  [on_device(): gathered = lax.all_gather(packed, 'dp', axis=0, tiled=False)]
    slice x1 -> x0, local copies, waits for them, and re-layouts: 13.2 us -> none  [assemble(): return dense_blocks[:positions].reshape(row_count, col_count, side, side)]
    ppermute x0 -> x6, starting transfers between devices: none -> 11.8 us  [shift(): lax.ppermute(value, 'tensor', [(i, (i + k) % n_tensor) for i in range(n_t...]
    another operation x1 -> x0, local copies, waits for them, and re-layouts: 8.98 us -> none
    unnamed x1 -> x0, blocking collectives: 7.03 us -> none
    scatter x1 -> x0, local copies, waits for them, and re-layouts: 6.44 us -> none  [assemble(): jnp.zeros((positions + 1, side, side), jnp.bfloat16).at[target].set(values)]
    pallas_call x0 -> x3, Pallas kernels: none -> 5.71 us  [the longest x1 2.41 us: on_device(): pl.pallas_call(functools.partial(forward_kernel, count, n_tensor), out_sh...]
  transfers between devices with their start and end apart: 1 -> 6, of which waited for: 0 -> 2; matrix products, arithmetic and copies ran while one was open for 8% -> 0% of each run, Pallas kernels for 0% -> 18%
where the time goes in v1:
time: 31.4 us; the launch traced here: 31.2 us
  starting transfers between devices  11.8 us (38%)
  blocking collectives  9.96 us (32%)
  Pallas kernels  5.71 us (18%)
  waiting for transfers between devices  2.36 us (8%)
  other arithmetic  0.67 us (2%)
  between operations  0.67 us (2%)
    ppermute x6, starting transfers between devices, shift(): lax.ppermute(value, 'tensor', [(i, (i + k) % n_tensor) for i in range(n_t...  11.8 us
    all_gather x1, blocking collectives, on_device(): gathered = lax.all_gather(packed, 'dp', axis=0, tiled=False)  9.96 us
    pallas_call x1, Pallas kernels, on_device(): pl.pallas_call(functools.partial(forward_kernel, count, n_tensor), out_sh...  2.41 us
    ppermute x6, waiting for transfers between devices, shift(): lax.ppermute(value, 'tensor', [(i, (i + k) % n_tensor) for i in range(n_t...  2.36 us
    pallas_call x1, Pallas kernels, on_device(): pl.pallas_call(functools.partial(backward_kernel, count, n_tensor), out_s...  1.68 us
    pallas_call x1, Pallas kernels, on_device(): pl.pallas_call(functools.partial(pack_kernel, count, row_count, col_count...  1.62 us
    convert_element_type x1, other arithmetic, on_device(): return (outputs, total_grad.astype(bf16))  0.67 us
  transfers between devices with their start and end apart: 6, of which 2 were waited for; matrix products, arithmetic and copies ran while one was open for 0% of the time, Pallas kernels for 18%

profile of v1, /device:TPU:0, one launch (start us, length us, event | category | flops | bytes accessed | tf_op | source)
XLA Modules:
  0.0 31.2 jit_solution(4297445249258269111)
XLA Ops:
  0.6 4.1 %collective-permute-start.1 = (bf16[8,4096]{1,0:T(8,128)(2,1)}, bf16[8,4096]{1,0:T(8,128)(2,1)S(1)}, u32[]{:S(2)}, u32[]{:S(2)}) collective-permute-start(bf16[8,4096]{1,0:T(8,128)(2,1)} %rest_0_.1), channel_id=1, source_target_pairs={{0,2},{1,3},{2,0},{3,1},{4,6},{5,7},{6,4},{7,5},{8,10},{9,11},{10,... | collective-permute-start | bytes 196616 | tf_op jit(solution)/shard_map/ppermute | solution.py:161
  4.7 1.6 %collective-permute-start = (bf16[8,4096]{1,0:T(8,128)(2,1)}, bf16[8,4096]{1,0:T(8,128)(2,1)S(1)}, u32[]{:S(2)}, u32[]{:S(2)}) collective-permute-start(bf16[8,4096]{1,0:T(8,128)(2,1)} %rest_0_.1), channel_id=1, source_target_pairs={{0,1},{1,2},{2,3},{3,0},{4,5},{5,6},{6,7},{7,4},{8,9},{9,10},{10,1... | collective-permute-start | bytes 196616 | tf_op jit(solution)/shard_map/ppermute | solution.py:161
  6.3 2.2 %collective-permute-start.2 = (bf16[8,4096]{1,0:T(8,128)(2,1)}, bf16[8,4096]{1,0:T(8,128)(2,1)S(1)}, u32[]{:S(2)}, u32[]{:S(2)}) collective-permute-start(bf16[8,4096]{1,0:T(8,128)(2,1)} %rest_0_.1), channel_id=1, source_target_pairs={{0,3},{1,0},{2,1},{3,2},{4,7},{5,4},{6,5},{7,6},{8,11},{9,8},{10,9... | collective-permute-start | bytes 196616 | tf_op jit(solution)/shard_map/ppermute | solution.py:161
  8.6 1.6 %shard_map.59 = bf16[3,64,128]{2,1,0:T(8,128)(2,1)} custom-call(s32[1,5]{1,0:T(1,128)} %slots.1, bf16[1,5,64,64]{3,2,1,0:T(8,128)(2,1)} %values.1), custom_call_target="tpu_custom_call" | custom-call | tf_op jit(solution)/shard_map/pallas_call | solution.py:164
  10.2 0.0 copy-start.1
  10.2 10.0 %all-gather = bf16[24,64,128]{2,1,0:T(8,128)(2,1)S(1)} all-gather(bf16[3,64,128]{2,1,0:T(8,128)(2,1)} %shard_map.59), channel_id=2, replica_groups=mesh['dp'=8,'tensor'=4] {'dp'}, dimensions={0}, use_global_device_ids=true | all-gather | bytes 442368 | tf_op jit(solution)/shard_map/all_gather | solution.py:170
  20.1 0.0 copy-done.1
  20.1 0.0 copy-start
  20.1 1.7 %shard_map.61 = (bf16[8,4096]{1,0:T(8,128)(2,1)S(1)}, bf16[8,4096]{1,0:T(8,128)(2,1)S(1)}, bf16[8,4096]{1,0:T(8,128)(2,1)S(1)}, bf16[8,4096]{1,0:T(8,128)(2,1)S(1)}) custom-call(bf16[8,3,64,128]{3,2,1,0:T(8,128)(2,1)S(1)} %bitcast.1, bf16[32,896]{1,0:T(8,128)(2,1)S(1)} %copy-done.1), custom_call_target="tpu_custom_call" | custom-call | tf_op jit(solution)/shard_map/pallas_call | solution.py:176
  21.8 0.1 collective-permute-start.3
  21.9 0.5 %collective-permute-start.4 = (bf16[8,4096]{1,0:T(8,128)(2,1)S(1)}, bf16[8,4096]{1,0:T(8,128)(2,1)S(1)}, u32[]{:S(2)}, u32[]{:S(2)}) collective-permute-start(bf16[8,4096]{1,0:T(8,128)(2,1)S(1)} %get-tuple-element.8), channel_id=1, source_target_pairs={{0,2},{1,3},{2,0},{3,1},{4,6},{5,7},{6,4},{7,5},{8,10},{9,11},{10,... | collective-permute-start | bytes 196616 | tf_op jit(solution)/shard_map/ppermute | solution.py:161
  22.4 0.0 collective-permute-done.1.rest_2_
  22.4 3.3 %collective-permute-start.5 = (bf16[8,4096]{1,0:T(8,128)(2,1)S(1)}, bf16[8,4096]{1,0:T(8,128)(2,1)S(1)}, u32[]{:S(2)}, u32[]{:S(2)}) collective-permute-start(bf16[8,4096]{1,0:T(8,128)(2,1)S(1)} %get-tuple-element.9), channel_id=1, source_target_pairs={{0,3},{1,0},{2,1},{3,2},{4,7},{5,4},{6,5},{7,6},{8,11},{9,8},{10,9... | collective-permute-start | bytes 196616 | tf_op jit(solution)/shard_map/ppermute | solution.py:161
  25.7 0.0 collective-permute-done.rest_1_
  25.7 0.0 collective-permute-done.2.rest_3_
  25.7 0.0 copy-done
  25.7 2.4 %shard_map.60 = bf16[32,896]{1,0:T(8,128)(2,1)} custom-call(bf16[8,3,64,128]{3,2,1,0:T(8,128)(2,1)S(1)} %bitcast.2, bf16[8,4096]{1,0:T(8,128)(2,1)S(1)} %copy-done, bf16[8,4096]{1,0:T(8,128)(2,1)S(1)} %collective-permute-done.rest_1_, bf16[8,4096]{1,0:T(8,128)(2,1)S(1)} %collective-permute-done.1.rest_2_, bf16[8,4096]{1,0:T(8,128)(2,1)S(1)} %collective-permute-done.2.rest_3_), custom_call_target="tpu_custom_call" | custom-call | tf_op jit(solution)/shard_map/pallas_call | solution.py:191
  28.1 0.5 %collective-permute-done.3 = bf16[8,4096]{1,0:T(8,128)(2,1)S(1)} collective-permute-done((bf16[8,4096]{1,0:T(8,128)(2,1)S(1)}, bf16[8,4096]{1,0:T(8,128)(2,1)S(1)}, u32[]{:S(2)}, u32[]{:S(2)}) %collective-permute-start.3) | collective-permute-done | bytes 65568 | tf_op jit(solution)/shard_map/ppermute | solution.py:161
  28.7 1.8 %collective-permute-done.4 = bf16[8,4096]{1,0:T(8,128)(2,1)S(1)} collective-permute-done((bf16[8,4096]{1,0:T(8,128)(2,1)S(1)}, bf16[8,4096]{1,0:T(8,128)(2,1)S(1)}, u32[]{:S(2)}, u32[]{:S(2)}) %collective-permute-start.4) | collective-permute-done | bytes 65568 | tf_op jit(solution)/shard_map/ppermute | solution.py:161
  30.5 0.0 collective-permute-done.5
  30.5 0.7 %add_convert_fusion = bf16[8,4096]{1,0:T(8,128)(2,1)} fusion(bf16[8,4096]{1,0:T(8,128)(2,1)S(1)} %collective-permute-done.5, bf16[8,4096]{1,0:T(8,128)(2,1)S(1)} %collective-permute-done.4, bf16[8,4096]{1,0:T(8,128)(2,1)S(1)} %collective-permute-done.3, bf16[8,4096]{1,0:T(8,128)(2,1)S(1)} %get-tuple-element.6), kind=kLoop, calls=%fused_computation | loop fusion | flops 262144 | bytes 327680 | tf_op jit(solution)/shard_map/convert_element_type | solution.py:208
Async XLA Ops:
  0.6 21.8 %collective-permute-start.1 = (bf16[8,4096]{1,0:T(8,128)(2,1)}, bf16[8,4096]{1,0:T(8,128)(2,1)S(1)}, u32[]{:S(2)}, u32[]{:S(2)}) collective-permute-start(bf16[8,4096]{1,0:T(8,128)(2,1)} %rest_0_.1), channel_id=1, source_target_pairs={{0,2},{1,3},{2,0},{3,1},{4,6},{5,7},{6,4},{7,5},{8,10},{9,11},{10,... | collective-permute-start | bytes 196616 | tf_op jit(solution)/shard_map/ppermute | solution.py:161
  4.7 21.0 %collective-permute-start = (bf16[8,4096]{1,0:T(8,128)(2,1)}, bf16[8,4096]{1,0:T(8,128)(2,1)S(1)}, u32[]{:S(2)}, u32[]{:S(2)}) collective-permute-start(bf16[8,4096]{1,0:T(8,128)(2,1)} %rest_0_.1), channel_id=1, source_target_pairs={{0,1},{1,2},{2,3},{3,0},{4,5},{5,6},{6,7},{7,4},{8,9},{9,10},{10,1... | collective-permute-start | bytes 196616 | tf_op jit(solution)/shard_map/ppermute | solution.py:161
  6.3 19.4 %collective-permute-start.2 = (bf16[8,4096]{1,0:T(8,128)(2,1)}, bf16[8,4096]{1,0:T(8,128)(2,1)S(1)}, u32[]{:S(2)}, u32[]{:S(2)}) collective-permute-start(bf16[8,4096]{1,0:T(8,128)(2,1)} %rest_0_.1), channel_id=1, source_target_pairs={{0,3},{1,0},{2,1},{3,2},{4,7},{5,4},{6,5},{7,6},{8,11},{9,8},{10,9... | collective-permute-start | bytes 196616 | tf_op jit(solution)/shard_map/ppermute | solution.py:161
  10.2 10.0 %copy-start.1 = (bf16[32,896]{1,0:T(8,128)(2,1)S(1)}, bf16[32,896]{1,0:T(8,128)(2,1)}, u32[]{:S(2)}) copy-start(bf16[32,896]{1,0:T(8,128)(2,1)} %cot.1) | copy-start | bytes 172036
  20.1 5.6 %copy-start = (bf16[8,4096]{1,0:T(8,128)(2,1)S(1)}, bf16[8,4096]{1,0:T(8,128)(2,1)}, u32[]{:S(2)}) copy-start(bf16[8,4096]{1,0:T(8,128)(2,1)} %rest_0_.1) | copy-start | bytes 196612
  21.8 6.9 %collective-permute-start.3 = (bf16[8,4096]{1,0:T(8,128)(2,1)S(1)}, bf16[8,4096]{1,0:T(8,128)(2,1)S(1)}, u32[]{:S(2)}, u32[]{:S(2)}) collective-permute-start(bf16[8,4096]{1,0:T(8,128)(2,1)S(1)} %get-tuple-element.7), channel_id=1, source_target_pairs={{0,1},{1,2},{2,3},{3,0},{4,5},{5,6},{6,7},{7,4},{8,9},{9,10},{10,1... | collective-permute-start | bytes 196616 | tf_op jit(solution)/shard_map/ppermute | solution.py:161
  21.9 8.6 %collective-permute-start.4 = (bf16[8,4096]{1,0:T(8,128)(2,1)S(1)}, bf16[8,4096]{1,0:T(8,128)(2,1)S(1)}, u32[]{:S(2)}, u32[]{:S(2)}) collective-permute-start(bf16[8,4096]{1,0:T(8,128)(2,1)S(1)} %get-tuple-element.8), channel_id=1, source_target_pairs={{0,2},{1,3},{2,0},{3,1},{4,6},{5,7},{6,4},{7,5},{8,10},{9,11},{10,... | collective-permute-start | bytes 196616 | tf_op jit(solution)/shard_map/ppermute | solution.py:161
  22.4 8.1 %collective-permute-start.5 = (bf16[8,4096]{1,0:T(8,128)(2,1)S(1)}, bf16[8,4096]{1,0:T(8,128)(2,1)S(1)}, u32[]{:S(2)}, u32[]{:S(2)}) collective-permute-start(bf16[8,4096]{1,0:T(8,128)(2,1)S(1)} %get-tuple-element.9), channel_id=1, source_target_pairs={{0,3},{1,0},{2,1},{3,2},{4,7},{5,4},{6,5},{7,6},{8,11},{9,8},{10,9... | collective-permute-start | bytes 196616 | tf_op jit(solution)/shard_map/ppermute | solution.py:161

commit v2 on v1

--- a/solution.py
+++ b/solution.py
@@ -14,7 +14,7 @@
 
 def pack_kernel(count, row_count, col_count, slots, values, packed):
     side = values.shape[2]
-    pairs = packed.shape[0]
+    copies, pairs = packed.shape[:2]
     lane = lax.broadcasted_iota(jnp.int32, (side, side), 1)
     line = lax.broadcasted_iota(jnp.int32, (side, side), 0)
     head = jnp.zeros((side, side), jnp.float32)
@@ -28,7 +28,9 @@
     for k in range(pairs):
         left = values[0, k]
         right = values[0, k + pairs] if k + pairs < count else head
-        packed[k] = jnp.concatenate([left, right], axis=1)
+        tile = jnp.concatenate([left, right], axis=1)
+        for i in range(copies):
+            packed[i, k] = tile
 
 
 def load_ids(gathered, ids_vmem, ids, sem):
@@ -52,8 +54,7 @@
 
 
 def backward_kernel(count, n_tensor, gathered, cot, *rest):
-    outs = rest[:n_tensor]
-    ids_vmem, ids, cot_left, cot_right, prod, acc, sem = rest[n_tensor:]
+    out, ids_vmem, ids, cot_left, cot_right, prod, acc, sem = rest
     n_dp, pairs, side, _ = gathered.shape
     col_count = cot_left.shape[0] - 1
     row_count = acc.shape[0] - 1
@@ -90,15 +91,12 @@
 
     over(n_dp, multiply)
     over(n_dp, add)
-    me = lax.axis_index("tensor")
     share = rows // n_tensor
-    for k in range(n_tensor):
-        start = pl.multiple_of(lax.rem(me + k, n_tensor) * share, share)
-        for r in range(0, row_count, 2):
-            pair = jnp.concatenate(
-                [acc[r, pl.ds(start, share), :], acc[r + 1, pl.ds(start, share), :]], axis=1
-            )
-            outs[k][:, r * side:(r + 2) * side] = pair.astype(jnp.bfloat16)
+    for r in range(0, row_count, 2):
+        pair = jnp.concatenate([acc[r], acc[r + 1]], axis=1)
+        for k in range(n_tensor):
+            part = pair[k * share:(k + 1) * share].astype(jnp.bfloat16)
+            out[k, :, r * side:(r + 2) * side] = part
 
 
 def forward_kernel(count, n_tensor, gathered, *rest):
@@ -163,11 +161,11 @@
     tokens = [inputs] + [shift(inputs, k) for k in range(1, n_tensor)]
     packed = pl.pallas_call(
         functools.partial(pack_kernel, count, row_count, col_count),
-        out_shape=jax.ShapeDtypeStruct((pairs, side, 2 * side), bf16),
+        out_shape=jax.ShapeDtypeStruct((n_dp, pairs, side, 2 * side), bf16),
         in_specs=[SMEM, VMEM],
         out_specs=VMEM,
     )(block_slot, block_values)
-    gathered = lax.all_gather(packed, "dp", axis=0, tiled=False)
+    gathered = lax.all_to_all(packed, "dp", 0, 0, tiled=True)
     total = n_dp * pairs
     ids = [
         pltpu.VMEM((n_dp, 8, 2 * side), i32),
@@ -175,9 +173,9 @@
     ]
     partial_sums = pl.pallas_call(
         functools.partial(backward_kernel, count, n_tensor),
-        out_shape=[jax.ShapeDtypeStruct((share, width), bf16)] * n_tensor,
+        out_shape=jax.ShapeDtypeStruct((n_tensor, share, width), bf16),
         in_specs=[VMEM] * 2,
-        out_specs=[VMEM] * n_tensor,
+        out_specs=VMEM,
         scratch_shapes=ids + [
             pltpu.VMEM((col_count + 1, rows, 2 * side), bf16),
             pltpu.VMEM((col_count + 1, rows, 2 * side), bf16),
@@ -187,7 +185,7 @@
         ],
         compiler_params=pltpu.CompilerParams(vmem_limit_bytes=LIMIT),
     )(gathered, grad_out)
-    arrived = [partial_sums[0]] + [shift(partial_sums[k], k) for k in range(1, n_tensor)]
+    arrived = lax.all_to_all(partial_sums, "tensor", 0, 0, tiled=True)
     outputs = pl.pallas_call(
         functools.partial(forward_kernel, count, n_tensor),
         out_shape=jax.ShapeDtypeStruct((rows, hidden), bf16),
@@ -203,8 +201,8 @@
         compiler_params=pltpu.CompilerParams(vmem_limit_bytes=LIMIT),
     )(gathered, *tokens)
     total_grad = arrived[0].astype(f32)
-    for value in arrived[1:]:
-        total_grad = total_grad + value.astype(f32)
+    for k in range(1, n_tensor):
+        total_grad = total_grad + arrived[k].astype(f32)
     return (outputs, total_grad.astype(bf16))
 
 

time: 31.4 us -> 40.6 us (1.29)
  waiting for transfers between devices: 2.36 us -> 7.74 us
  blocking collectives: 9.96 us -> 13.6 us
  Pallas kernels: 5.71 us -> 6.61 us
  starting transfers between devices: 11.8 us -> 10.9 us
    all_to_all x0 -> x1, blocking collectives: none -> 13.6 us  [on_device(): gathered = lax.all_to_all(packed, 'dp', 0, 0, tiled=True)]
    all_gather x1 -> x0, blocking collectives: 9.96 us -> none  [on_device(): gathered = lax.all_gather(packed, 'dp', axis=0, tiled=False)]
    ppermute x6 -> x3, starting transfers between devices: 11.8 us -> 5.85 us  [shift(): lax.ppermute(value, 'tensor', [(i, (i + k) % n_tensor) for i in range(n_t...]
    ppermute x6 -> x3, waiting for transfers between devices: 2.36 us -> 7.74 us  [shift(): lax.ppermute(value, 'tensor', [(i, (i + k) % n_tensor) for i in range(n_t...]
    all_to_all x0 -> x1, starting transfers between devices: none -> 5.02 us  [on_device(): arrived = lax.all_to_all(partial_sums, 'tensor', 0, 0, tiled=True)]
    pallas_call x1, Pallas kernels: 1.68 us -> 2.43 us  [on_device(): pl.pallas_call(functools.partial(backward_kernel, count, n_tensor), out_s...]
    convert_element_type x1 -> x0, other arithmetic: 0.67 us -> none  [on_device(): return (outputs, total_grad.astype(bf16))]
    add x0 -> x1, other arithmetic: none -> 0.67 us  [on_device(): total_grad = total_grad + arrived[k].astype(f32)]
  transfers between devices with their start and end apart: 6 -> 4, of which waited for: 2 -> 2; matrix products, arithmetic and copies ran while one was open for 0% -> 0% of each run, Pallas kernels for 18% -> 6%
where the time goes in v2:
time: 40.6 us; the launch traced here: 40.2 us
  blocking collectives  13.6 us (33%)
  starting transfers between devices  10.9 us (27%)
  waiting for transfers between devices  7.74 us (19%)
  Pallas kernels  6.61 us (16%)
  other arithmetic  0.67 us (2%)
  between operations  0.67 us (2%)
    all_to_all x1, blocking collectives, on_device(): gathered = lax.all_to_all(packed, 'dp', 0, 0, tiled=True)  13.6 us
    ppermute x3, waiting for transfers between devices, shift(): lax.ppermute(value, 'tensor', [(i, (i + k) % n_tensor) for i in range(n_t...  7.74 us
    ppermute x3, starting transfers between devices, shift(): lax.ppermute(value, 'tensor', [(i, (i + k) % n_tensor) for i in range(n_t...  5.85 us
    all_to_all x1, starting transfers between devices, on_device(): arrived = lax.all_to_all(partial_sums, 'tensor', 0, 0, tiled=True)  5.02 us
    pallas_call x1, Pallas kernels, on_device(): pl.pallas_call(functools.partial(backward_kernel, count, n_tensor), out_s...  2.43 us
    pallas_call x1, Pallas kernels, on_device(): pl.pallas_call(functools.partial(forward_kernel, count, n_tensor), out_sh...  2.41 us
    pallas_call x1, Pallas kernels, on_device(): pl.pallas_call(functools.partial(pack_kernel, count, row_count, col_count...  1.77 us
  transfers between devices with their start and end apart: 4, of which 2 were waited for; matrix products, arithmetic and copies ran while one was open for 0% of the time, Pallas kernels for 6%

profile of v2, /device:TPU:0, one launch (start us, length us, event | category | flops | bytes accessed | tf_op | source)
XLA Modules:
  0.0 40.2 jit_solution(6631118816936644834)
XLA Ops:
  0.6 1.8 %shard_map.59 = bf16[8,3,64,128]{3,2,1,0:T(8,128)(2,1)} custom-call(s32[1,5]{1,0:T(1,128)} %slots.1, bf16[1,5,64,64]{3,2,1,0:T(8,128)(2,1)} %values.1), custom_call_target="tpu_custom_call" | custom-call | tf_op jit(solution)/shard_map/pallas_call | solution.py:162
  2.4 0.0 copy-start.1
  2.4 13.6 %all_to_all.10.gathered = bf16[8,3,64,128]{3,2,1,0:T(8,128)(2,1)S(1)} all-to-all(bf16[8,3,64,128]{3,2,1,0:T(8,128)(2,1)} %shard_map.59), channel_id=1, replica_groups=mesh['dp'=8,'tensor'=4] {'dp'}, dimensions={0} | all-to-all | bytes 786432 | tf_op jit(solution)/shard_map/all_to_all | solution.py:168
  16.0 0.0 copy-done.1
  16.0 2.4 %shard_map.61 = bf16[4,8,4096]{2,1,0:T(8,128)(2,1)} custom-call(bf16[8,3,64,128]{3,2,1,0:T(8,128)(2,1)S(1)} %all_to_all.10.gathered, bf16[32,896]{1,0:T(8,128)(2,1)S(1)} %copy-done.1), custom_call_target="tpu_custom_call" | custom-call | tf_op jit(solution)/shard_map/pallas_call | solution.py:174
  18.5 0.0 copy-start
  18.5 5.0 %all-to-all-start.1 = ((bf16[4,8,4096]{2,1,0:T(8,128)(2,1)}), bf16[4,8,4096]{2,1,0:T(8,128)(2,1)S(1)}, u32[]{:S(2)}, u32[]{:S(2)}) async-start(bf16[4,8,4096]{2,1,0:T(8,128)(2,1)} %shard_map.61), calls=%async_computation.1 | async-start | bytes 524288 | tf_op jit(solution)/shard_map/all_to_all | solution.py:188
  23.5 0.0 copy-done
  23.5 2.0 %collective-permute-start = (bf16[8,4096]{1,0:T(8,128)(2,1)S(1)}, bf16[8,4096]{1,0:T(8,128)(2,1)S(1)}, u32[]{:S(2)}, u32[]{:S(2)}) collective-permute-start(bf16[8,4096]{1,0:T(8,128)(2,1)S(1)} %copy-done), channel_id=1, source_target_pairs={{0,1},{1,2},{2,3},{3,0},{4,5},{5,6},{6,7},{7,4},{8,9},{9,10},{10,1... | collective-permute-start | bytes 196616 | tf_op jit(solution)/shard_map/ppermute | solution.py:159
  25.5 2.4 %collective-permute-start.1 = (bf16[8,4096]{1,0:T(8,128)(2,1)S(1)}, bf16[8,4096]{1,0:T(8,128)(2,1)S(1)}, u32[]{:S(2)}, u32[]{:S(2)}) collective-permute-start(bf16[8,4096]{1,0:T(8,128)(2,1)S(1)} %copy-done), channel_id=1, source_target_pairs={{0,2},{1,3},{2,0},{3,1},{4,6},{5,7},{6,4},{7,5},{8,10},{9,11},{10,... | collective-permute-start | bytes 196616 | tf_op jit(solution)/shard_map/ppermute | solution.py:159
  27.9 1.5 %collective-permute-start.2 = (bf16[8,4096]{1,0:T(8,128)(2,1)S(1)}, bf16[8,4096]{1,0:T(8,128)(2,1)S(1)}, u32[]{:S(2)}, u32[]{:S(2)}) collective-permute-start(bf16[8,4096]{1,0:T(8,128)(2,1)S(1)} %copy-done), channel_id=1, source_target_pairs={{0,3},{1,0},{2,1},{3,2},{4,7},{5,4},{6,5},{7,6},{8,11},{9,8},{10,9... | collective-permute-start | bytes 196616 | tf_op jit(solution)/shard_map/ppermute | solution.py:159
  29.4 5.2 %collective-permute-done.rest_1_ = bf16[8,4096]{1,0:T(8,128)(2,1)S(1)} collective-permute-done((bf16[8,4096]{1,0:T(8,128)(2,1)S(1)}, bf16[8,4096]{1,0:T(8,128)(2,1)S(1)}, u32[]{:S(2)}, u32[]{:S(2)}) %collective-permute-start) | collective-permute-done | bytes 65568 | tf_op jit(solution)/shard_map/ppermute | solution.py:159
  34.5 2.6 %collective-permute-done.1.rest_2_ = bf16[8,4096]{1,0:T(8,128)(2,1)S(1)} collective-permute-done((bf16[8,4096]{1,0:T(8,128)(2,1)S(1)}, bf16[8,4096]{1,0:T(8,128)(2,1)S(1)}, u32[]{:S(2)}, u32[]{:S(2)}) %collective-permute-start.1) | collective-permute-done | bytes 65568 | tf_op jit(solution)/shard_map/ppermute | solution.py:159
  37.1 0.0 collective-permute-done.2.rest_3_
  37.1 2.4 %shard_map.60 = bf16[32,896]{1,0:T(8,128)(2,1)} custom-call(bf16[8,3,64,128]{3,2,1,0:T(8,128)(2,1)S(1)} %all_to_all.10.gathered, bf16[8,4096]{1,0:T(8,128)(2,1)S(1)} %copy-done, bf16[8,4096]{1,0:T(8,128)(2,1)S(1)} %collective-permute-done.rest_1_, bf16[8,4096]{1,0:T(8,128)(2,1)S(1)} %collective-permute-done.1.rest_2_, ...), custom_call_target="tpu_custom_call" | custom-call | tf_op jit(solution)/shard_map/pallas_call | solution.py:189
  39.5 0.0 all-to-all-done.1
  39.5 0.7 %fusion = bf16[8,4096]{1,0:T(8,128)(2,1)} fusion(bf16[4,8,4096]{2,1,0:T(8,128)(2,1)S(1)} %all-to-all-done.1), kind=kLoop, calls=%fused_computation.1 | loop fusion | flops 262144 | bytes 327680 | tf_op jit(solution)/shard_map/add | solution.py:205
Async XLA Ops:
  2.4 13.6 %copy-start.1 = (bf16[32,896]{1,0:T(8,128)(2,1)S(1)}, bf16[32,896]{1,0:T(8,128)(2,1)}, u32[]{:S(2)}) copy-start(bf16[32,896]{1,0:T(8,128)(2,1)} %cot.1) | copy-start | bytes 172036
  18.5 5.0 %copy-start = (bf16[8,4096]{1,0:T(8,128)(2,1)S(1)}, bf16[8,4096]{1,0:T(8,128)(2,1)}, u32[]{:S(2)}) copy-start(bf16[8,4096]{1,0:T(8,128)(2,1)} %rest_0_.1) | copy-start | bytes 196612
  18.5 21.0 %all-to-all-start.1 = ((bf16[4,8,4096]{2,1,0:T(8,128)(2,1)}), bf16[4,8,4096]{2,1,0:T(8,128)(2,1)S(1)}, u32[]{:S(2)}, u32[]{:S(2)}) async-start(bf16[4,8,4096]{2,1,0:T(8,128)(2,1)} %shard_map.61), calls=%async_computation.1 | async-start | bytes 524288 | tf_op jit(solution)/shard_map/all_to_all | solution.py:188
  23.5 11.0 %collective-permute-start = (bf16[8,4096]{1,0:T(8,128)(2,1)S(1)}, bf16[8,4096]{1,0:T(8,128)(2,1)S(1)}, u32[]{:S(2)}, u32[]{:S(2)}) collective-permute-start(bf16[8,4096]{1,0:T(8,128)(2,1)S(1)} %copy-done), channel_id=1, source_target_pairs={{0,1},{1,2},{2,3},{3,0},{4,5},{5,6},{6,7},{7,4},{8,9},{9,10},{10,1... | collective-permute-start | bytes 196616 | tf_op jit(solution)/shard_map/ppermute | solution.py:159
  25.5 11.6 %collective-permute-start.1 = (bf16[8,4096]{1,0:T(8,128)(2,1)S(1)}, bf16[8,4096]{1,0:T(8,128)(2,1)S(1)}, u32[]{:S(2)}, u32[]{:S(2)}) collective-permute-start(bf16[8,4096]{1,0:T(8,128)(2,1)S(1)} %copy-done), channel_id=1, source_target_pairs={{0,2},{1,3},{2,0},{3,1},{4,6},{5,7},{6,4},{7,5},{8,10},{9,11},{10,... | collective-permute-start | bytes 196616 | tf_op jit(solution)/shard_map/ppermute | solution.py:159
  27.9 9.2 %collective-permute-start.2 = (bf16[8,4096]{1,0:T(8,128)(2,1)S(1)}, bf16[8,4096]{1,0:T(8,128)(2,1)S(1)}, u32[]{:S(2)}, u32[]{:S(2)}) collective-permute-start(bf16[8,4096]{1,0:T(8,128)(2,1)S(1)} %copy-done), channel_id=1, source_target_pairs={{0,3},{1,0},{2,1},{3,2},{4,7},{5,4},{6,5},{7,6},{8,11},{9,8},{10,9... | collective-permute-start | bytes 196616 | tf_op jit(solution)/shard_map/ppermute | solution.py:159

commit v3 on v1

v3 whole, which is shorter than its diff:
```python
import functools

import jax
import jax.numpy as jnp
from jax import lax
from jax.experimental import pallas as pl
from jax.experimental.pallas import tpu as pltpu
from jax.sharding import PartitionSpec as P

VMEM = pl.BlockSpec(memory_space=pltpu.VMEM)
SMEM = pl.BlockSpec(memory_space=pltpu.SMEM)
LIMIT = 48 * 1024 * 1024


def pack_kernel(count, row_count, col_count, slots, values, packed):
    side = values.shape[2]
    pairs = packed.shape[1]
    lane = lax.broadcasted_iota(jnp.int32, (side, side), 1)
    line = lax.broadcasted_iota(jnp.int32, (side, side), 0)
    head = jnp.zeros((side, side), jnp.float32)
    for j in range(count):
        p = slots[0, j]
        row = jnp.where(p >= 0, p // col_count, row_count)
        col = jnp.where(p >= 0, p % col_count, col_count)
        here = jnp.where(line == 0, row, col).astype(jnp.float32)
        head = jnp.where(lane == j, here, head)
    head = head.astype(jnp.bfloat16)
    for k in range(pairs):
        left = values[0, k]
        right = values[0, k + pairs] if k + pairs < count else head
        packed[0, k] = jnp.concatenate([left, right], axis=1)


def load_ids(gathered, ids_vmem, ids, sem):
    start = 0
    for part in gathered:
        n, pairs = part.shape[:2]
        head = part[:, pairs - 1, 0:16, :].astype(jnp.float32).astype(jnp.int32)
        ids_vmem[start:start + n] = head[:, 0:8, :]
        start += n
    copy = pltpu.make_async_copy(ids_vmem, ids, sem)
    copy.start()
    return copy


def over(gathered, body):
    start = 0
    for part in gathered:
        n = part.shape[0]
        if n <= 8:
            for d in range(n):
                body(part, d, start + d)
        else:
            def step(d, carry, part=part, start=start):
                body(part, d, start + d)
                return carry
            lax.fori_loop(0, n, step, 0)
        start += n


def backward_kernel(count, n_parts, n_tensor, *refs):
    gathered, cot, outs = refs[:n_parts], refs[n_parts], refs[n_parts + 1:n_parts + 1 + n_tensor]
    ids_vmem, ids, cot_left, cot_right, prod, acc, sem = refs[n_parts + 1 + n_tensor:]
    pairs, side = gathered[0].shape[1:3]
    col_count = cot_left.shape[0] - 1
    row_count = acc.shape[0] - 1
    rows = cot.shape[0]
    copy = load_ids(gathered, ids_vmem, ids, sem)
    acc[...] = jnp.zeros_like(acc)
    zero = jnp.zeros((rows, side), jnp.bfloat16)
    for c in range(col_count):
        part = cot[:, c * side:(c + 1) * side]
        cot_left[c] = jnp.concatenate([part, zero], axis=1)
        cot_right[c] = jnp.concatenate([zero, part], axis=1)
    both = jnp.concatenate([zero, zero], axis=1)
    cot_left[col_count] = both
    cot_right[col_count] = both
    copy.wait()

    def multiply(part, d, i):
        for k in range(pairs):
            left = cot_left[ids[i, 1, side + k]]
            right = cot_right[ids[i, 1, side + k + pairs]] if k + pairs < count else both
            lhs = jnp.concatenate([left, right], axis=0)
            prod[i * pairs + k] = lax.dot_general(
                lhs, part[d, k], (((1,), (1,)), ((), ())), preferred_element_type=jnp.float32
            )

    def add(part, d, i):
        for k in range(pairs):
            acc[ids[i, 0, side + k]] += prod[i * pairs + k, 0:rows, :]
            if k + pairs < count:
                acc[ids[i, 0, side + k + pairs]] += prod[i * pairs + k, rows:2 * rows, :]

    over(gathered, multiply)
    over(gathered, add)
    me = lax.axis_index("tensor")
    share = rows // n_tensor
    for k in range(n_tensor):
        start = pl.multiple_of(lax.bitwise_xor(me, k) * share, share)
        for r in range(0, row_count, 2):
            pair = jnp.concatenate(
                [acc[r, pl.ds(start, share), :], acc[r + 1, pl.ds(start, share), :]], axis=1
            )
            outs[k][:, r * side:(r + 2) * side] = pair.astype(jnp.bfloat16)


def forward_kernel(count, n_parts, n_tensor, *refs):
    gathered, tokens = refs[:n_parts], refs[n_parts:n_parts + n_tensor]
    out, ids_vmem, ids, blocks, prod, acc, stage, sem = refs[n_parts + n_tensor:]
    pairs, side = gathered[0].shape[1:3]
    row_count = blocks.shape[0] - 1
    col_count = acc.shape[0] - 1
    rows = blocks.shape[1]
    share = rows // n_tensor
    copy = load_ids(gathered, ids_vmem, ids, sem)
    acc[...] = jnp.zeros_like(acc)
    for r in range(row_count):
        parts = [tokens[k][:, r * side:(r + 1) * side].astype(jnp.float32) for k in range(n_tensor)]
        blocks[r] = jnp.concatenate(parts, axis=0).astype(jnp.bfloat16)
    blocks[row_count] = jnp.zeros((rows, side), jnp.bfloat16)
    copy.wait()

    def multiply(part, d, i):
        for k in range(pairs):
            left = blocks[ids[i, 0, side + k]]
            right = blocks[ids[i, 0, side + k + pairs]] if k + pairs < count else jnp.zeros_like(left)
            lhs = jnp.concatenate([left, right], axis=0)
            prod[i * pairs + k] = jnp.dot(lhs, part[d, k], preferred_element_type=jnp.float32)

    lane = lax.broadcasted_iota(jnp.int32, (rows, 2 * side), 1)

    def add(part, d, i):
        for k in range(pairs):
            acc[ids[i, 1, side + k]] += jnp.where(lane < side, prod[i * pairs + k, 0:rows, :], 0.0)
            if k + pairs < count:
                acc[ids[i, 1, side + k + pairs]] += jnp.where(
                    lane >= side, prod[i * pairs + k, rows:2 * rows, :], 0.0
                )

    over(gathered, multiply)
    over(gathered, add)
    me = lax.axis_index("tensor")
    for k in range(n_tensor):
        start = pl.multiple_of(lax.bitwise_xor(me, k) * share, share)
        for c in range(0, col_count, 2):
            sums = []
            for i in (c, c + 1):
                value = acc[i, k * share:(k + 1) * share, :]
                sums.append(value[:, :side] + value[:, side:])
            stage[pl.ds(start, share), c * side:(c + 2) * side] = jnp.concatenate(sums, axis=1)
    out[...] = stage[...].astype(jnp.bfloat16)


def swap(value, axis, n, k):
    return lax.ppermute(value, axis, [(i, i ^ k) for i in range(n)])


def gather_parts(packed, n_dp):
    if n_dp > 8 or n_dp & (n_dp - 1):
        return [lax.all_gather(packed, "dp", axis=0, tiled=True)]
    same_core = [packed] + [swap(packed, "dp", n_dp, k) for k in range(n_dp - 2, 0, -2)]
    return same_core + [swap(part, "dp", n_dp, 1) for part in same_core]


def on_device(n_dp, n_tensor, inputs, block_values, block_slot, grad_out):
    share, width = inputs.shape
    rows, hidden = grad_out.shape
    _, count, side, _ = block_values.shape
    row_count, col_count = width // side, hidden // side
    pairs = count // 2 + 1
    bf16, f32, i32 = jnp.bfloat16, jnp.float32, jnp.int32
    far_first = range(n_tensor - 1, 0, -1)

    packed = pl.pallas_call(
        functools.partial(pack_kernel, count, row_count, col_count),
        out_shape=jax.ShapeDtypeStruct((1, pairs, side, 2 * side), bf16),
        in_specs=[SMEM, VMEM],
        out_specs=VMEM,
    )(block_slot, block_values)
    gathered = gather_parts(packed, n_dp)
    moved = {k: swap(inputs, "tensor", n_tensor, k) for k in far_first}
    tokens = [inputs] + [moved[k] for k in range(1, n_tensor)]
    n_parts = len(gathered)
    total = n_dp * pairs
    ids = [
        pltpu.VMEM((n_dp, 8, 2 * side), i32),
        pltpu.SMEM((n_dp, 8, 2 * side), i32),
    ]
    partial_sums = pl.pallas_call(
        functools.partial(backward_kernel, count, n_parts, n_tensor),
        out_shape=[jax.ShapeDtypeStruct((share, width), bf16)] * n_tensor,
        in_specs=[VMEM] * (n_parts + 1),
        out_specs=[VMEM] * n_tensor,
        scratch_shapes=ids + [
            pltpu.VMEM((col_count + 1, rows, 2 * side), bf16),
            pltpu.VMEM((col_count + 1, rows, 2 * side), bf16),
            pltpu.VMEM((total, 2 * rows, side), f32),
            pltpu.VMEM((row_count + 1, rows, side), f32),
            pltpu.SemaphoreType.DMA,
        ],
        compiler_params=pltpu.CompilerParams(vmem_limit_bytes=LIMIT),
    )(*gathered, grad_out)
    arrived = [partial_sums[0]] + [swap(partial_sums[k], "tensor", n_tensor, k) for k in far_first]
    outputs = pl.pallas_call(
        functools.partial(forward_kernel, count, n_parts, n_tensor),
        out_shape=jax.ShapeDtypeStruct((rows, hidden), bf16),
        in_specs=[VMEM] * (n_parts + n_tensor),
        out_specs=VMEM,
        scratch_shapes=ids + [
            pltpu.VMEM((row_count + 1, rows, side), bf16),
            pltpu.VMEM((total, 2 * rows, 2 * side), f32),
            pltpu.VMEM((col_count + 1, rows, 2 * side), f32),
            pltpu.VMEM((rows, hidden), f32),
            pltpu.SemaphoreType.DMA,
        ],
        compiler_params=pltpu.CompilerParams(vmem_limit_bytes=LIMIT),
    )(*gathered, *tokens)
    total_grad = arrived[0].astype(f32)
    for value in arrived[1:]:
        total_grad = total_grad + value.astype(f32)
    return (outputs, total_grad.astype(bf16))


def solution(mesh):
    placed = (
        P(("dp", "tensor"), None),
        P("tensor", "dp", None, None),
        P("tensor", "dp"),
        P("dp", "tensor"),
    )
    return jax.shard_map(
        functools.partial(on_device, mesh.shape["dp"], mesh.shape["tensor"]),
        mesh=mesh,
        in_specs=placed,
        out_specs=(P("dp", "tensor"), P(("dp", "tensor"), None)),
        check_vma=False,
    )
```

time: 31.4 us -> 28 us (0.89)
  blocking collectives: 9.96 us -> 0 us
  starting transfers between devices: 11.8 us -> 16.6 us
  waiting for transfers between devices: 2.36 us -> 3.29 us
  local copies, waits for them, and re-layouts: 0.01 us -> 0.8 us
    all_gather x1 -> x0, blocking collectives: 9.96 us -> none  [on_device(): gathered = lax.all_gather(packed, 'dp', axis=0, tiled=False)]
    ppermute x6 -> x13, starting transfers between devices: 11.8 us -> 16.6 us  [swap(): return lax.ppermute(value, axis, [(i, i ^ k) for i in range(n)])]
    ppermute x6 -> x13, waiting for transfers between devices: 2.36 us -> 3.29 us  [swap(): return lax.ppermute(value, axis, [(i, i ^ k) for i in range(n)])]
    unnamed x4 -> x6, local copies, waits for them, and re-layouts: 0.01 us -> 0.8 us
  transfers between devices with their start and end apart: 6 -> 13, of which waited for: 2 -> 2; matrix products, arithmetic and copies ran while one was open for 0% -> 0% of each run, Pallas kernels for 18% -> 15%
where the time goes in v3:
time: 28 us; the launch traced here: 27.8 us
  starting transfers between devices  16.6 us (59%)
  Pallas kernels  5.74 us (20%)
  waiting for transfers between devices  3.29 us (12%)
  local copies, waits for them, and re-layouts  0.8 us (3%)
  between operations  0.69 us (2%)
  other arithmetic  0.67 us (2%)
    ppermute x13, starting transfers between devices, swap(): return lax.ppermute(value, axis, [(i, i ^ k) for i in range(n)])  16.6 us
    ppermute x13, waiting for transfers between devices, swap(): return lax.ppermute(value, axis, [(i, i ^ k) for i in range(n)])  3.29 us
    pallas_call x1, Pallas kernels, on_device(): pl.pallas_call(functools.partial(forward_kernel, count, n_parts, n_tensor...  2.42 us
    pallas_call x1, Pallas kernels, on_device(): pl.pallas_call(functools.partial(backward_kernel, count, n_parts, n_tenso...  1.66 us
    pallas_call x1, Pallas kernels, on_device(): pl.pallas_call(functools.partial(pack_kernel, count, row_count, col_count...  1.66 us
    unnamed x6, local copies, waits for them, and re-layouts  0.8 us
    convert_element_type x1, other arithmetic, on_device(): return (outputs, total_grad.astype(bf16))  0.67 us
  transfers between devices with their start and end apart: 13, of which 2 were waited for; matrix products, arithmetic and copies ran while one was open for 0% of the time, Pallas kernels for 15%

profile of v3, /device:TPU:0, one launch (start us, length us, event | category | flops | bytes accessed | tf_op | source)
XLA Modules:
  0.0 27.8 jit_solution(12564822522595492812)
XLA Ops:
  0.7 1.7 %shard_map.59.refs_0_ = bf16[1,3,64,128]{3,2,1,0:T(8,128)(2,1)} custom-call(s32[1,5]{1,0:T(1,128)} %slots.1, bf16[1,5,64,64]{3,2,1,0:T(8,128)(2,1)} %values.1), custom_call_target="tpu_custom_call" | custom-call | tf_op jit(solution)/shard_map/pallas_call | solution.py:175
  2.3 2.9 %collective-permute-start.2 = (bf16[1,3,64,128]{3,2,1,0:T(8,128)(2,1)}, bf16[1,3,64,128]{3,2,1,0:T(8,128)(2,1)S(1)}, u32[]{:S(2)}, u32[]{:S(2)}) collective-permute-start(bf16[1,3,64,128]{3,2,1,0:T(8,128)(2,1)} %shard_map.59.refs_0_), channel_id=1, source_target_pairs={{0,8},{4,12},{8,0},{12,4},{16,24},{20,28},{24,16},{28,20},{1,9},{5... | collective-permute-start | bytes 147464 | tf_op jit(solution)/shard_map/ppermute | solution.py:156
  5.2 1.5 %collective-permute-start.1 = (bf16[1,3,64,128]{3,2,1,0:T(8,128)(2,1)}, bf16[1,3,64,128]{3,2,1,0:T(8,128)(2,1)S(1)}, u32[]{:S(2)}, u32[]{:S(2)}) collective-permute-start(bf16[1,3,64,128]{3,2,1,0:T(8,128)(2,1)} %shard_map.59.refs_0_), channel_id=1, source_target_pairs={{0,16},{4,20},{8,24},{12,28},{16,0},{20,4},{24,8},{28,12},{1,17},{... | collective-permute-start | bytes 147464 | tf_op jit(solution)/shard_map/ppermute | solution.py:156
  6.8 0.0 collective-permute-start
  6.8 3.1 %collective-permute-start.8 = (bf16[8,4096]{1,0:T(8,128)(2,1)S(1)}, bf16[8,4096]{1,0:T(8,128)(2,1)S(1)}, u32[]{:S(2)}, u32[]{:S(2)}) collective-permute-start(bf16[8,4096]{1,0:T(8,128)(2,1)S(1)} %copy-done.1), channel_id=1, source_target_pairs={{0,2},{1,3},{2,0},{3,1},{4,6},{5,7},{6,4},{7,5},{8,10},{9,11},{10,... | collective-permute-start | bytes 196616 | tf_op jit(solution)/shard_map/ppermute | solution.py:156
  9.8 0.0 collective-permute-start.3
  9.8 0.0 collective-permute-done.2.refs_3_
  9.8 0.5 %collective-permute-start.6 = (bf16[1,3,64,128]{3,2,1,0:T(8,128)(2,1)S(1)}, bf16[1,3,64,128]{3,2,1,0:T(8,128)(2,1)S(1)}, u32[]{:S(2)}, u32[]{:S(2)}) collective-permute-start(bf16[1,3,64,128]{3,2,1,0:T(8,128)(2,1)S(1)} %collective-permute-done.2.refs_3_), channel_id=1, source_target_pairs={{0,4},{4,0},{8,12},{12,8},{16,20},{20,16},{24,28},{28,24},{1,5},{5... | collective-permute-start | bytes 147464 | tf_op jit(solution)/shard_map/ppermute | solution.py:156
  10.3 0.0 collective-permute-done.1.refs_2_
  10.4 0.1 collective-permute-start.5
  10.4 1.5 %collective-permute-done.refs_1_ = bf16[1,3,64,128]{3,2,1,0:T(8,128)(2,1)S(1)} collective-permute-done((bf16[1,3,64,128]{3,2,1,0:T(8,128)(2,1)}, bf16[1,3,64,128]{3,2,1,0:T(8,128)(2,1)S(1)}, u32[]{:S(2)}, u32[]{:S(2)}) %collective-permute-start) | collective-permute-done | bytes 49184 | tf_op jit(solution)/shard_map/ppermute | solution.py:156
  12.0 0.0 collective-permute-start.4
  12.0 0.0 collective-permute-done.3.refs_4_
  12.0 1.6 %collective-permute-start.7 = (bf16[8,4096]{1,0:T(8,128)(2,1)S(1)}, bf16[8,4096]{1,0:T(8,128)(2,1)S(1)}, u32[]{:S(2)}, u32[]{:S(2)}) collective-permute-start(bf16[8,4096]{1,0:T(8,128)(2,1)S(1)} %copy-done.1), channel_id=1, source_target_pairs={{0,1},{1,0},{2,3},{3,2},{4,5},{5,4},{6,7},{7,6},{8,9},{9,8},{10,11... | collective-permute-start | bytes 196616 | tf_op jit(solution)/shard_map/ppermute | solution.py:156
  13.5 0.0 collective-permute-done.6.refs_7_
  13.6 2.5 %collective-permute-start.9 = (bf16[8,4096]{1,0:T(8,128)(2,1)S(1)}, bf16[8,4096]{1,0:T(8,128)(2,1)S(1)}, u32[]{:S(2)}, u32[]{:S(2)}) collective-permute-start(bf16[8,4096]{1,0:T(8,128)(2,1)S(1)} %copy-done.1), channel_id=1, source_target_pairs={{0,3},{1,2},{2,1},{3,0},{4,7},{5,6},{6,5},{7,4},{8,11},{9,10},{10,... | collective-permute-start | bytes 196616 | tf_op jit(solution)/shard_map/ppermute | solution.py:156
  16.0 0.0 collective-permute-done.5.refs_6_
  16.0 0.0 collective-permute-done.4.refs_5_
  16.0 0.0 copy-start
  16.1 0.8 %copy-done = bf16[1,3,64,128]{3,2,1,0:T(8,128)(2,1)S(1)} copy-done((bf16[1,3,64,128]{3,2,1,0:T(8,128)(2,1)S(1)}, bf16[1,3,64,128]{3,2,1,0:T(8,128)(2,1)}, u32[]{:S(2)}) %copy-start) | copy-done | bytes 49176
  16.8 1.7 %shard_map.61 = (bf16[8,4096]{1,0:T(8,128)(2,1)S(1)}, bf16[8,4096]{1,0:T(8,128)(2,1)S(1)}, bf16[8,4096]{1,0:T(8,128)(2,1)S(1)}, bf16[8,4096]{1,0:T(8,128)(2,1)S(1)}) custom-call(bf16[1,3,64,128]{3,2,1,0:T(8,128)(2,1)S(1)} %copy-done, bf16[1,3,64,128]{3,2,1,0:T(8,128)(2,1)S(1)} %collective-permute-done.refs_1_, ...), custom_call_target="tpu_custom_call" | custom-call | tf_op jit(solution)/shard_map/pallas_call | solution.py:190
  18.5 1.4 %collective-permute-start.10 = (bf16[8,4096]{1,0:T(8,128)(2,1)S(1)}, bf16[8,4096]{1,0:T(8,128)(2,1)S(1)}, u32[]{:S(2)}, u32[]{:S(2)}) collective-permute-start(bf16[8,4096]{1,0:T(8,128)(2,1)S(1)} %get-tuple-element.7), channel_id=1, source_target_pairs={{0,3},{1,2},{2,1},{3,0},{4,7},{5,6},{6,5},{7,4},{8,11},{9,10},{10,... | collective-permute-start | bytes 196616 | tf_op jit(solution)/shard_map/ppermute | solution.py:156
  19.9 0.8 %collective-permute-start.11 = (bf16[8,4096]{1,0:T(8,128)(2,1)S(1)}, bf16[8,4096]{1,0:T(8,128)(2,1)S(1)}, u32[]{:S(2)}, u32[]{:S(2)}) collective-permute-start(bf16[8,4096]{1,0:T(8,128)(2,1)S(1)} %get-tuple-element.8), channel_id=1, source_target_pairs={{0,2},{1,3},{2,0},{3,1},{4,6},{5,7},{6,4},{7,5},{8,10},{9,11},{10,... | collective-permute-start | bytes 196616 | tf_op jit(solution)/shard_map/ppermute | solution.py:156
  20.7 0.0 collective-permute-done.8.refs_10_
  20.7 2.3 %collective-permute-start.12 = (bf16[8,4096]{1,0:T(8,128)(2,1)S(1)}, bf16[8,4096]{1,0:T(8,128)(2,1)S(1)}, u32[]{:S(2)}, u32[]{:S(2)}) collective-permute-start(bf16[8,4096]{1,0:T(8,128)(2,1)S(1)} %get-tuple-element.9), channel_id=1, source_target_pairs={{0,1},{1,0},{2,3},{3,2},{4,5},{5,4},{6,7},{7,6},{8,9},{9,8},{10,11... | collective-permute-start | bytes 196616 | tf_op jit(solution)/shard_map/ppermute | solution.py:156
  23.0 0.0 collective-permute-done.7.refs_9_
  23.0 0.0 collective-permute-done.9.refs_11_
  23.0 2.4 %shard_map.60 = bf16[32,896]{1,0:T(8,128)(2,1)} custom-call(bf16[1,3,64,128]{3,2,1,0:T(8,128)(2,1)S(1)} %copy-done, bf16[1,3,64,128]{3,2,1,0:T(8,128)(2,1)S(1)} %collective-permute-done.refs_1_, bf16[1,3,64,128]{3,2,1,0:T(8,128)(2,1)S(1)} %collective-permute-done.1.refs_2_, bf16[1,3,64,128]{3,2,1,0:T(8,128)(2,1)S(1)} %collective-permute-done.2.refs_3_, ...), custom_call_target="tpu_custom_call" | custom-call | tf_op jit(solution)/shard_map/pallas_call | solution.py:205
  25.4 0.0 collective-permute-done.10
  25.4 1.7 %collective-permute-done.11 = bf16[8,4096]{1,0:T(8,128)(2,1)S(1)} collective-permute-done((bf16[8,4096]{1,0:T(8,128)(2,1)S(1)}, bf16[8,4096]{1,0:T(8,128)(2,1)S(1)}, u32[]{:S(2)}, u32[]{:S(2)}) %collective-permute-start.11) | collective-permute-done | bytes 65568 | tf_op jit(solution)/shard_map/ppermute | solution.py:156
  27.1 0.0 collective-permute-done.12
  27.1 0.7 %add_convert_fusion = bf16[8,4096]{1,0:T(8,128)(2,1)} fusion(bf16[8,4096]{1,0:T(8,128)(2,1)S(1)} %collective-permute-done.12, bf16[8,4096]{1,0:T(8,128)(2,1)S(1)} %collective-permute-done.11, bf16[8,4096]{1,0:T(8,128)(2,1)S(1)} %collective-permute-done.10, bf16[8,4096]{1,0:T(8,128)(2,1)S(1)} %get-tuple-element.6), kind=kLoop, calls=%fused_computation | loop fusion | flops 262144 | bytes 327680 | tf_op jit(solution)/shard_map/convert_element_type | solution.py:222
  (4 shorter events, 0.0 us)
Async XLA Ops:
  0.6 6.1 %copy-start.1 = (bf16[8,4096]{1,0:T(8,128)(2,1)S(1)}, bf16[8,4096]{1,0:T(8,128)(2,1)}, u32[]{:S(2)}) copy-start(bf16[8,4096]{1,0:T(8,128)(2,1)} %refs_8_.2) | copy-start | bytes 196612
  0.6 15.4 %copy-start.2 = (bf16[32,896]{1,0:T(8,128)(2,1)S(1)}, bf16[32,896]{1,0:T(8,128)(2,1)}, u32[]{:S(2)}) copy-start(bf16[32,896]{1,0:T(8,128)(2,1)} %refs_8_.3) | copy-start | bytes 172036
  2.3 7.5 %collective-permute-start.2 = (bf16[1,3,64,128]{3,2,1,0:T(8,128)(2,1)}, bf16[1,3,64,128]{3,2,1,0:T(8,128)(2,1)S(1)}, u32[]{:S(2)}, u32[]{:S(2)}) collective-permute-start(bf16[1,3,64,128]{3,2,1,0:T(8,128)(2,1)} %shard_map.59.refs_0_), channel_id=1, source_target_pairs={{0,8},{4,12},{8,0},{12,4},{16,24},{20,28},{24,16},{28,20},{1,9},{5... | collective-permute-start | bytes 147464 | tf_op jit(solution)/shard_map/ppermute | solution.py:156
  5.2 5.1 %collective-permute-start.1 = (bf16[1,3,64,128]{3,2,1,0:T(8,128)(2,1)}, bf16[1,3,64,128]{3,2,1,0:T(8,128)(2,1)S(1)}, u32[]{:S(2)}, u32[]{:S(2)}) collective-permute-start(bf16[1,3,64,128]{3,2,1,0:T(8,128)(2,1)} %shard_map.59.refs_0_), channel_id=1, source_target_pairs={{0,16},{4,20},{8,24},{12,28},{16,0},{20,4},{24,8},{28,12},{1,17},{... | collective-permute-start | bytes 147464 | tf_op jit(solution)/shard_map/ppermute | solution.py:156
  6.8 5.2 %collective-permute-start = (bf16[1,3,64,128]{3,2,1,0:T(8,128)(2,1)}, bf16[1,3,64,128]{3,2,1,0:T(8,128)(2,1)S(1)}, u32[]{:S(2)}, u32[]{:S(2)}) collective-permute-start(bf16[1,3,64,128]{3,2,1,0:T(8,128)(2,1)} %shard_map.59.refs_0_), channel_id=1, source_target_pairs={{0,24},{4,28},{8,16},{12,20},{16,8},{20,12},{24,0},{28,4},{1,25},{... | collective-permute-start | bytes 147464 | tf_op jit(solution)/shard_map/ppermute | solution.py:156
  6.8 13.9 %collective-permute-start.8 = (bf16[8,4096]{1,0:T(8,128)(2,1)S(1)}, bf16[8,4096]{1,0:T(8,128)(2,1)S(1)}, u32[]{:S(2)}, u32[]{:S(2)}) collective-permute-start(bf16[8,4096]{1,0:T(8,128)(2,1)S(1)} %copy-done.1), channel_id=1, source_target_pairs={{0,2},{1,3},{2,0},{3,1},{4,6},{5,7},{6,4},{7,5},{8,10},{9,11},{10,... | collective-permute-start | bytes 196616 | tf_op jit(solution)/shard_map/ppermute | solution.py:156
  9.8 2.1 %collective-permute-start.3 = (bf16[1,3,64,128]{3,2,1,0:T(8,128)(2,1)}, bf16[1,3,64,128]{3,2,1,0:T(8,128)(2,1)S(1)}, u32[]{:S(2)}, u32[]{:S(2)}) collective-permute-start(bf16[1,3,64,128]{3,2,1,0:T(8,128)(2,1)} %shard_map.59.refs_0_), channel_id=1, source_target_pairs={{0,4},{4,0},{8,12},{12,8},{16,20},{20,16},{24,28},{28,24},{1,5},{5... | collective-permute-start | bytes 147464 | tf_op jit(solution)/shard_map/ppermute | solution.py:156
  9.8 3.7 %collective-permute-start.6 = (bf16[1,3,64,128]{3,2,1,0:T(8,128)(2,1)S(1)}, bf16[1,3,64,128]{3,2,1,0:T(8,128)(2,1)S(1)}, u32[]{:S(2)}, u32[]{:S(2)}) collective-permute-start(bf16[1,3,64,128]{3,2,1,0:T(8,128)(2,1)S(1)} %collective-permute-done.2.refs_3_), channel_id=1, source_target_pairs={{0,4},{4,0},{8,12},{12,8},{16,20},{20,16},{24,28},{28,24},{1,5},{5... | collective-permute-start | bytes 147464 | tf_op jit(solution)/shard_map/ppermute | solution.py:156
  10.4 5.7 %collective-permute-start.5 = (bf16[1,3,64,128]{3,2,1,0:T(8,128)(2,1)S(1)}, bf16[1,3,64,128]{3,2,1,0:T(8,128)(2,1)S(1)}, u32[]{:S(2)}, u32[]{:S(2)}) collective-permute-start(bf16[1,3,64,128]{3,2,1,0:T(8,128)(2,1)S(1)} %collective-permute-done.1.refs_2_), channel_id=1, source_target_pairs={{0,4},{4,0},{8,12},{12,8},{16,20},{20,16},{24,28},{28,24},{1,5},{5... | collective-permute-start | bytes 147464 | tf_op jit(solution)/shard_map/ppermute | solution.py:156
  12.0 4.1 %collective-permute-start.4 = (bf16[1,3,64,128]{3,2,1,0:T(8,128)(2,1)S(1)}, bf16[1,3,64,128]{3,2,1,0:T(8,128)(2,1)S(1)}, u32[]{:S(2)}, u32[]{:S(2)}) collective-permute-start(bf16[1,3,64,128]{3,2,1,0:T(8,128)(2,1)S(1)} %collective-permute-done.refs_1_), channel_id=1, source_target_pairs={{0,4},{4,0},{8,12},{12,8},{16,20},{20,16},{24,28},{28,24},{1,5},{5... | collective-permute-start | bytes 147464 | tf_op jit(solution)/shard_map/ppermute | solution.py:156
  12.0 11.0 %collective-permute-start.7 = (bf16[8,4096]{1,0:T(8,128)(2,1)S(1)}, bf16[8,4096]{1,0:T(8,128)(2,1)S(1)}, u32[]{:S(2)}, u32[]{:S(2)}) collective-permute-start(bf16[8,4096]{1,0:T(8,128)(2,1)S(1)} %copy-done.1), channel_id=1, source_target_pairs={{0,1},{1,0},{2,3},{3,2},{4,5},{5,4},{6,7},{7,6},{8,9},{9,8},{10,11... | collective-permute-start | bytes 196616 | tf_op jit(solution)/shard_map/ppermute | solution.py:156
  13.6 9.4 %collective-permute-start.9 = (bf16[8,4096]{1,0:T(8,128)(2,1)S(1)}, bf16[8,4096]{1,0:T(8,128)(2,1)S(1)}, u32[]{:S(2)}, u32[]{:S(2)}) collective-permute-start(bf16[8,4096]{1,0:T(8,128)(2,1)S(1)} %copy-done.1), channel_id=1, source_target_pairs={{0,3},{1,2},{2,1},{3,0},{4,7},{5,6},{6,5},{7,4},{8,11},{9,10},{10,... | collective-permute-start | bytes 196616 | tf_op jit(solution)/shard_map/ppermute | solution.py:156
  16.0 0.8 %copy-start = (bf16[1,3,64,128]{3,2,1,0:T(8,128)(2,1)S(1)}, bf16[1,3,64,128]{3,2,1,0:T(8,128)(2,1)}, u32[]{:S(2)}) copy-start(bf16[1,3,64,128]{3,2,1,0:T(8,128)(2,1)} %shard_map.59.refs_0_) | copy-start | bytes 147460
  18.5 6.9 %collective-permute-start.10 = (bf16[8,4096]{1,0:T(8,128)(2,1)S(1)}, bf16[8,4096]{1,0:T(8,128)(2,1)S(1)}, u32[]{:S(2)}, u32[]{:S(2)}) collective-permute-start(bf16[8,4096]{1,0:T(8,128)(2,1)S(1)} %get-tuple-element.7), channel_id=1, source_target_pairs={{0,3},{1,2},{2,1},{3,0},{4,7},{5,6},{6,5},{7,4},{8,11},{9,10},{10,... | collective-permute-start | bytes 196616 | tf_op jit(solution)/shard_map/ppermute | solution.py:156
  19.9 7.2 %collective-permute-start.11 = (bf16[8,4096]{1,0:T(8,128)(2,1)S(1)}, bf16[8,4096]{1,0:T(8,128)(2,1)S(1)}, u32[]{:S(2)}, u32[]{:S(2)}) collective-permute-start(bf16[8,4096]{1,0:T(8,128)(2,1)S(1)} %get-tuple-element.8), channel_id=1, source_target_pairs={{0,2},{1,3},{2,0},{3,1},{4,6},{5,7},{6,4},{7,5},{8,10},{9,11},{10,... | collective-permute-start | bytes 196616 | tf_op jit(solution)/shard_map/ppermute | solution.py:156
  20.7 6.5 %collective-permute-start.12 = (bf16[8,4096]{1,0:T(8,128)(2,1)S(1)}, bf16[8,4096]{1,0:T(8,128)(2,1)S(1)}, u32[]{:S(2)}, u32[]{:S(2)}) collective-permute-start(bf16[8,4096]{1,0:T(8,128)(2,1)S(1)} %get-tuple-element.9), channel_id=1, source_target_pairs={{0,1},{1,0},{2,3},{3,2},{4,5},{5,4},{6,7},{7,6},{8,9},{9,8},{10,11... | collective-permute-start | bytes 196616 | tf_op jit(solution)/shard_map/ppermute | solution.py:156

commit v4 on v3

--- a/solution.py
+++ b/solution.py
@@ -9,7 +9,7 @@
 
 VMEM = pl.BlockSpec(memory_space=pltpu.VMEM)
 SMEM = pl.BlockSpec(memory_space=pltpu.SMEM)
-LIMIT = 48 * 1024 * 1024
+MIB = 1024 * 1024
 
 
 def pack_kernel(count, row_count, col_count, slots, values, packed):
@@ -59,8 +59,8 @@
 
 
 def backward_kernel(count, n_parts, n_tensor, *refs):
-    gathered, cot, outs = refs[:n_parts], refs[n_parts], refs[n_parts + 1:n_parts + 1 + n_tensor]
-    ids_vmem, ids, cot_left, cot_right, prod, acc, sem = refs[n_parts + 1 + n_tensor:]
+    gathered, cot = refs[:n_parts], refs[n_parts]
+    out, ids_vmem, ids, cot_left, cot_right, prod, acc, sem = refs[n_parts + 1:]
     pairs, side = gathered[0].shape[1:3]
     col_count = cot_left.shape[0] - 1
     row_count = acc.shape[0] - 1
@@ -94,15 +94,11 @@
 
     over(gathered, multiply)
     over(gathered, add)
-    me = lax.axis_index("tensor")
     share = rows // n_tensor
-    for k in range(n_tensor):
-        start = pl.multiple_of(lax.bitwise_xor(me, k) * share, share)
-        for r in range(0, row_count, 2):
-            pair = jnp.concatenate(
-                [acc[r, pl.ds(start, share), :], acc[r + 1, pl.ds(start, share), :]], axis=1
-            )
-            outs[k][:, r * side:(r + 2) * side] = pair.astype(jnp.bfloat16)
+    for r in range(0, row_count, 2):
+        pair = jnp.concatenate([acc[r], acc[r + 1]], axis=1)
+        for k in range(n_tensor):
+            out[k, :, r * side:(r + 2) * side] = pair[k * share:(k + 1) * share].astype(jnp.bfloat16)
 
 
 def forward_kernel(count, n_parts, n_tensor, *refs):
@@ -170,6 +166,7 @@
     row_count, col_count = width // side, hidden // side
     pairs = count // 2 + 1
     bf16, f32, i32 = jnp.bfloat16, jnp.float32, jnp.int32
+    grant = (12 if n_dp <= 8 else 48) * MIB
     far_first = range(n_tensor - 1, 0, -1)
 
     packed = pl.pallas_call(
@@ -177,6 +174,7 @@
         out_shape=jax.ShapeDtypeStruct((1, pairs, side, 2 * side), bf16),
         in_specs=[SMEM, VMEM],
         out_specs=VMEM,
+        compiler_params=pltpu.CompilerParams(vmem_limit_bytes=4 * MIB),
     )(block_slot, block_values)
     gathered = gather_parts(packed, n_dp)
     moved = {k: swap(inputs, "tensor", n_tensor, k) for k in far_first}
@@ -189,9 +187,9 @@
     ]
     partial_sums = pl.pallas_call(
         functools.partial(backward_kernel, count, n_parts, n_tensor),
-        out_shape=[jax.ShapeDtypeStruct((share, width), bf16)] * n_tensor,
+        out_shape=jax.ShapeDtypeStruct((n_tensor, share, width), bf16),
         in_specs=[VMEM] * (n_parts + 1),
-        out_specs=[VMEM] * n_tensor,
+        out_specs=VMEM,
         scratch_shapes=ids + [
             pltpu.VMEM((col_count + 1, rows, 2 * side), bf16),
             pltpu.VMEM((col_count + 1, rows, 2 * side), bf16),
@@ -199,9 +197,9 @@
             pltpu.VMEM((row_count + 1, rows, side), f32),
             pltpu.SemaphoreType.DMA,
         ],
-        compiler_params=pltpu.CompilerParams(vmem_limit_bytes=LIMIT),
+        compiler_params=pltpu.CompilerParams(vmem_limit_bytes=grant),
     )(*gathered, grad_out)
-    arrived = [partial_sums[0]] + [swap(partial_sums[k], "tensor", n_tensor, k) for k in far_first]
+    arrived = lax.all_to_all(partial_sums, "tensor", 0, 0, tiled=True)
     outputs = pl.pallas_call(
         functools.partial(forward_kernel, count, n_parts, n_tensor),
         out_shape=jax.ShapeDtypeStruct((rows, hidden), bf16),
@@ -214,11 +212,11 @@
             pltpu.VMEM((rows, hidden), f32),
             pltpu.SemaphoreType.DMA,
         ],
-        compiler_params=pltpu.CompilerParams(vmem_limit_bytes=LIMIT),
+        compiler_params=pltpu.CompilerParams(vmem_limit_bytes=grant),
     )(*gathered, *tokens)
     total_grad = arrived[0].astype(f32)
-    for value in arrived[1:]:
-        total_grad = total_grad + value.astype(f32)
+    for k in range(1, n_tensor):
+        total_grad = total_grad + arrived[k].astype(f32)
     return (outputs, total_grad.astype(bf16))
 
 

time: 28 us -> 38.5 us (1.38)
  waiting for transfers between devices: 3.29 us -> 15.9 us
  starting transfers between devices: 16.6 us -> 14 us
  local copies, waits for them, and re-layouts: 0.8 us -> 1.54 us
    ppermute x13 -> x10, waiting for transfers between devices: 3.29 us -> 15.9 us  [swap(): return lax.ppermute(value, axis, [(i, i ^ k) for i in range(n)])]
    ppermute x13 -> x10, starting transfers between devices: 16.6 us -> 8.95 us  [swap(): return lax.ppermute(value, axis, [(i, i ^ k) for i in range(n)])]
    all_to_all x0 -> x1, starting transfers between devices: none -> 5.03 us  [on_device(): arrived = lax.all_to_all(partial_sums, 'tensor', 0, 0, tiled=True)]
    pallas_call x1, Pallas kernels: 1.66 us -> 0.65 us  [on_device(): pl.pallas_call(functools.partial(pack_kernel, count, row_count, col_count...]
    unnamed x6 -> x8, local copies, waits for them, and re-layouts: 0.8 us -> 1.54 us
    pallas_call x1, Pallas kernels: 1.66 us -> 2.38 us  [on_device(): pl.pallas_call(functools.partial(backward_kernel, count, n_parts, n_tenso...]
    convert_element_type x1 -> x0, other arithmetic: 0.67 us -> none  [on_device(): return (outputs, total_grad.astype(bf16))]
    add x0 -> x1, other arithmetic: none -> 0.67 us  [on_device(): total_grad = total_grad + arrived[k].astype(f32)]
  transfers between devices with their start and end apart: 13 -> 11, of which waited for: 2 -> 5; matrix products, arithmetic and copies ran while one was open for 0% -> 0% of each run, Pallas kernels for 15% -> 6%
where the time goes in v4:
time: 38.5 us; the launch traced here: 38.2 us
  waiting for transfers between devices  15.9 us (41%)
  starting transfers between devices  14 us (36%)
  Pallas kernels  5.4 us (14%)
  local copies, waits for them, and re-layouts  1.54 us (4%)
  between operations  0.7 us (2%)
  other arithmetic  0.67 us (2%)
    ppermute x10, waiting for transfers between devices, swap(): return lax.ppermute(value, axis, [(i, i ^ k) for i in range(n)])  15.9 us
    ppermute x10, starting transfers between devices, swap(): return lax.ppermute(value, axis, [(i, i ^ k) for i in range(n)])  8.95 us
    all_to_all x1, starting transfers between devices, on_device(): arrived = lax.all_to_all(partial_sums, 'tensor', 0, 0, tiled=True)  5.03 us
    pallas_call x1, Pallas kernels, on_device(): pl.pallas_call(functools.partial(backward_kernel, count, n_parts, n_tenso...  2.38 us
    pallas_call x1, Pallas kernels, on_device(): pl.pallas_call(functools.partial(forward_kernel, count, n_parts, n_tensor...  2.37 us
    unnamed x8, local copies, waits for them, and re-layouts  1.54 us
  transfers between devices with their start and end apart: 11, of which 5 were waited for; matrix products, arithmetic and copies ran while one was open for 0% of the time, Pallas kernels for 6%

profile of v4, /device:TPU:0, one launch (start us, length us, event | category | flops | bytes accessed | tf_op | source)
XLA Modules:
  0.0 38.2 jit_solution(5742305110855118985)
XLA Ops:
  0.6 0.0 copy-start
  0.6 0.9 %copy-done = bf16[1,5,64,64]{3,2,1,0:T(8,128)(2,1)S(1)} copy-done((bf16[1,5,64,64]{3,2,1,0:T(8,128)(2,1)S(1)}, bf16[1,5,64,64]{3,2,1,0:T(8,128)(2,1)}, u32[]{:S(2)}) %copy-start) | copy-done | bytes 40984
  1.5 0.7 %copy-done.3 = s32[1,5]{1,0:T(1,128)S(1)} copy-done((s32[1,5]{1,0:T(1,128)S(1)}, s32[1,5]{1,0:T(1,128)}, u32[]{:S(2)}) %copy-start.3) | copy-done | bytes 44
  2.2 0.6 %shard_map.59.refs_0_ = bf16[1,3,64,128]{3,2,1,0:T(8,128)(2,1)S(1)} custom-call(s32[1,5]{1,0:T(1,128)S(1)} %copy-done.3, bf16[1,5,64,64]{3,2,1,0:T(8,128)(2,1)S(1)} %copy-done), custom_call_target="tpu_custom_call" | custom-call | tf_op jit(solution)/shard_map/pallas_call | solution.py:172
  2.8 3.0 %collective-permute-start.2 = (bf16[1,3,64,128]{3,2,1,0:T(8,128)(2,1)S(1)}, bf16[1,3,64,128]{3,2,1,0:T(8,128)(2,1)S(1)}, u32[]{:S(2)}, u32[]{:S(2)}) collective-permute-start(bf16[1,3,64,128]{3,2,1,0:T(8,128)(2,1)S(1)} %shard_map.59.refs_0_), channel_id=1, source_target_pairs={{0,8},{4,12},{8,0},{12,4},{16,24},{20,28},{24,16},{28,20},{1,9},{5... | collective-permute-start | bytes 147464 | tf_op jit(solution)/shard_map/ppermute | solution.py:152
  5.8 1.5 %collective-permute-start.1 = (bf16[1,3,64,128]{3,2,1,0:T(8,128)(2,1)S(1)}, bf16[1,3,64,128]{3,2,1,0:T(8,128)(2,1)S(1)}, u32[]{:S(2)}, u32[]{:S(2)}) collective-permute-start(bf16[1,3,64,128]{3,2,1,0:T(8,128)(2,1)S(1)} %shard_map.59.refs_0_), channel_id=1, source_target_pairs={{0,16},{4,20},{8,24},{12,28},{16,0},{20,4},{24,8},{28,12},{1,17},{... | collective-permute-start | bytes 147464 | tf_op jit(solution)/shard_map/ppermute | solution.py:152
  7.3 0.0 collective-permute-start
  7.4 0.0 collective-permute-start.3
  7.4 0.5 %collective-permute-done.2.refs_3_ = bf16[1,3,64,128]{3,2,1,0:T(8,128)(2,1)S(1)} collective-permute-done((bf16[1,3,64,128]{3,2,1,0:T(8,128)(2,1)S(1)}, bf16[1,3,64,128]{3,2,1,0:T(8,128)(2,1)S(1)}, u32[]{:S(2)}, u32[]{:S(2)}) %collective-permute-start.2) | collective-permute-done | bytes 49184 | tf_op jit(solution)/shard_map/ppermute | solution.py:152
  7.9 0.0 collective-permute-start.6
  7.9 2.0 %collective-permute-done.1.refs_2_ = bf16[1,3,64,128]{3,2,1,0:T(8,128)(2,1)S(1)} collective-permute-done((bf16[1,3,64,128]{3,2,1,0:T(8,128)(2,1)S(1)}, bf16[1,3,64,128]{3,2,1,0:T(8,128)(2,1)S(1)}, u32[]{:S(2)}, u32[]{:S(2)}) %collective-permute-start.1) | collective-permute-done | bytes 49184 | tf_op jit(solution)/shard_map/ppermute | solution.py:152
  9.9 0.0 collective-permute-start.5
  9.9 2.4 %collective-permute-done.refs_1_ = bf16[1,3,64,128]{3,2,1,0:T(8,128)(2,1)S(1)} collective-permute-done((bf16[1,3,64,128]{3,2,1,0:T(8,128)(2,1)S(1)}, bf16[1,3,64,128]{3,2,1,0:T(8,128)(2,1)S(1)}, u32[]{:S(2)}, u32[]{:S(2)}) %collective-permute-start) | collective-permute-done | bytes 49184 | tf_op jit(solution)/shard_map/ppermute | solution.py:152
  12.3 0.0 collective-permute-start.4
  12.3 0.0 collective-permute-done.3.refs_4_
  12.3 0.0 collective-permute-done.6.refs_7_
  12.3 0.0 collective-permute-done.5.refs_6_
  12.3 1.2 %collective-permute-done.4.refs_5_ = bf16[1,3,64,128]{3,2,1,0:T(8,128)(2,1)S(1)} collective-permute-done((bf16[1,3,64,128]{3,2,1,0:T(8,128)(2,1)S(1)}, bf16[1,3,64,128]{3,2,1,0:T(8,128)(2,1)S(1)}, u32[]{:S(2)}, u32[]{:S(2)}) %collective-permute-start.4) | collective-permute-done | bytes 49184 | tf_op jit(solution)/shard_map/ppermute | solution.py:152
  13.6 0.0 copy-done.2
  13.6 2.4 %shard_map.61 = bf16[4,8,4096]{2,1,0:T(8,128)(2,1)} custom-call(bf16[1,3,64,128]{3,2,1,0:T(8,128)(2,1)S(1)} %shard_map.59.refs_0_, bf16[1,3,64,128]{3,2,1,0:T(8,128)(2,1)S(1)} %collective-permute-done.refs_1_, bf16[1,3,64,128]{3,2,1,0:T(8,128)(2,1)S(1)} %collective-permute-done.1.refs_2_, bf16[1,3,64,128]{3,2,1,0:T(8,128)(2,1)S(1)} %collective-permute-done.2.refs_3_, ...), custom_call_target="tpu_custom_call" | custom-call | tf_op jit(solution)/shard_map/pallas_call | solution.py:188
  15.9 0.0 copy-start.1
  16.0 5.0 %all-to-all-start = ((bf16[4,8,4096]{2,1,0:T(8,128)(2,1)}), bf16[4,8,4096]{2,1,0:T(8,128)(2,1)S(1)}, u32[]{:S(2)}, u32[]{:S(2)}) async-start(bf16[4,8,4096]{2,1,0:T(8,128)(2,1)} %shard_map.61), calls=%async_computation | async-start | bytes 524288 | tf_op jit(solution)/shard_map/all_to_all | solution.py:202
  21.0 0.0 copy-done.1
  21.0 2.9 %collective-permute-start.8 = (bf16[8,4096]{1,0:T(8,128)(2,1)S(1)}, bf16[8,4096]{1,0:T(8,128)(2,1)S(1)}, u32[]{:S(2)}, u32[]{:S(2)}) collective-permute-start(bf16[8,4096]{1,0:T(8,128)(2,1)S(1)} %copy-done.1), channel_id=1, source_target_pairs={{0,2},{1,3},{2,0},{3,1},{4,6},{5,7},{6,4},{7,5},{8,10},{9,11},{10,... | collective-permute-start | bytes 196616 | tf_op jit(solution)/shard_map/ppermute | solution.py:152
  23.9 1.5 %collective-permute-start.7 = (bf16[8,4096]{1,0:T(8,128)(2,1)S(1)}, bf16[8,4096]{1,0:T(8,128)(2,1)S(1)}, u32[]{:S(2)}, u32[]{:S(2)}) collective-permute-start(bf16[8,4096]{1,0:T(8,128)(2,1)S(1)} %copy-done.1), channel_id=1, source_target_pairs={{0,1},{1,0},{2,3},{3,2},{4,5},{5,4},{6,7},{7,6},{8,9},{9,8},{10,11... | collective-permute-start | bytes 196616 | tf_op jit(solution)/shard_map/ppermute | solution.py:152
  25.4 0.0 collective-permute-start.9
  25.4 9.7 %collective-permute-done.8.refs_10_ = bf16[8,4096]{1,0:T(8,128)(2,1)S(1)} collective-permute-done((bf16[8,4096]{1,0:T(8,128)(2,1)S(1)}, bf16[8,4096]{1,0:T(8,128)(2,1)S(1)}, u32[]{:S(2)}, u32[]{:S(2)}) %collective-permute-start.8) | collective-permute-done | bytes 65568 | tf_op jit(solution)/shard_map/ppermute | solution.py:152
  35.1 0.0 collective-permute-done.7.refs_9_
  35.1 0.0 collective-permute-done.9.refs_11_
  35.1 2.4 %shard_map.60 = bf16[32,896]{1,0:T(8,128)(2,1)} custom-call(bf16[1,3,64,128]{3,2,1,0:T(8,128)(2,1)S(1)} %shard_map.59.refs_0_, bf16[1,3,64,128]{3,2,1,0:T(8,128)(2,1)S(1)} %collective-permute-done.refs_1_, bf16[1,3,64,128]{3,2,1,0:T(8,128)(2,1)S(1)} %collective-permute-done.1.refs_2_, bf16[1,3,64,128]{3,2,1,0:T(8,128)(2,1)S(1)} %collective-permute-done.2.refs_3_, ...), custom_call_target="tpu_custom_call" | custom-call | tf_op jit(solution)/shard_map/pallas_call | solution.py:203
  37.5 0.0 all-to-all-done
  37.5 0.7 %fusion = bf16[8,4096]{1,0:T(8,128)(2,1)} fusion(bf16[4,8,4096]{2,1,0:T(8,128)(2,1)S(1)} %all-to-all-done), kind=kLoop, calls=%fused_computation.1 | loop fusion | flops 262144 | bytes 327680 | tf_op jit(solution)/shard_map/add | solution.py:219
  (2 shorter events, 0.0 us)
Async XLA Ops:
  0.6 0.9 %copy-start = (bf16[1,5,64,64]{3,2,1,0:T(8,128)(2,1)S(1)}, bf16[1,5,64,64]{3,2,1,0:T(8,128)(2,1)}, u32[]{:S(2)}) copy-start(bf16[1,5,64,64]{3,2,1,0:T(8,128)(2,1)} %values.1) | copy-start | bytes 122884
  1.5 0.7 %copy-start.3 = (s32[1,5]{1,0:T(1,128)S(1)}, s32[1,5]{1,0:T(1,128)}, u32[]{:S(2)}) copy-start(s32[1,5]{1,0:T(1,128)} %slots.1) | copy-start | bytes 64
  2.2 11.4 %copy-start.2 = (bf16[32,896]{1,0:T(8,128)(2,1)S(1)}, bf16[32,896]{1,0:T(8,128)(2,1)}, u32[]{:S(2)}) copy-start(bf16[32,896]{1,0:T(8,128)(2,1)} %refs_8_.3) | copy-start | bytes 172036
  2.8 5.1 %collective-permute-start.2 = (bf16[1,3,64,128]{3,2,1,0:T(8,128)(2,1)S(1)}, bf16[1,3,64,128]{3,2,1,0:T(8,128)(2,1)S(1)}, u32[]{:S(2)}, u32[]{:S(2)}) collective-permute-start(bf16[1,3,64,128]{3,2,1,0:T(8,128)(2,1)S(1)} %shard_map.59.refs_0_), channel_id=1, source_target_pairs={{0,8},{4,12},{8,0},{12,4},{16,24},{20,28},{24,16},{28,20},{1,9},{5... | collective-permute-start | bytes 147464 | tf_op jit(solution)/shard_map/ppermute | solution.py:152
  5.8 4.1 %collective-permute-start.1 = (bf16[1,3,64,128]{3,2,1,0:T(8,128)(2,1)S(1)}, bf16[1,3,64,128]{3,2,1,0:T(8,128)(2,1)S(1)}, u32[]{:S(2)}, u32[]{:S(2)}) collective-permute-start(bf16[1,3,64,128]{3,2,1,0:T(8,128)(2,1)S(1)} %shard_map.59.refs_0_), channel_id=1, source_target_pairs={{0,16},{4,20},{8,24},{12,28},{16,0},{20,4},{24,8},{28,12},{1,17},{... | collective-permute-start | bytes 147464 | tf_op jit(solution)/shard_map/ppermute | solution.py:152
  7.3 5.0 %collective-permute-start = (bf16[1,3,64,128]{3,2,1,0:T(8,128)(2,1)S(1)}, bf16[1,3,64,128]{3,2,1,0:T(8,128)(2,1)S(1)}, u32[]{:S(2)}, u32[]{:S(2)}) collective-permute-start(bf16[1,3,64,128]{3,2,1,0:T(8,128)(2,1)S(1)} %shard_map.59.refs_0_), channel_id=1, source_target_pairs={{0,24},{4,28},{8,16},{12,20},{16,8},{20,12},{24,0},{28,4},{1,25},{... | collective-permute-start | bytes 147464 | tf_op jit(solution)/shard_map/ppermute | solution.py:152
  7.4 5.0 %collective-permute-start.3 = (bf16[1,3,64,128]{3,2,1,0:T(8,128)(2,1)S(1)}, bf16[1,3,64,128]{3,2,1,0:T(8,128)(2,1)S(1)}, u32[]{:S(2)}, u32[]{:S(2)}) collective-permute-start(bf16[1,3,64,128]{3,2,1,0:T(8,128)(2,1)S(1)} %shard_map.59.refs_0_), channel_id=1, source_target_pairs={{0,4},{4,0},{8,12},{12,8},{16,20},{20,16},{24,28},{28,24},{1,5},{5... | collective-permute-start | bytes 147464 | tf_op jit(solution)/shard_map/ppermute | solution.py:152
  7.9 4.4 %collective-permute-start.6 = (bf16[1,3,64,128]{3,2,1,0:T(8,128)(2,1)S(1)}, bf16[1,3,64,128]{3,2,1,0:T(8,128)(2,1)S(1)}, u32[]{:S(2)}, u32[]{:S(2)}) collective-permute-start(bf16[1,3,64,128]{3,2,1,0:T(8,128)(2,1)S(1)} %collective-permute-done.2.refs_3_), channel_id=1, source_target_pairs={{0,4},{4,0},{8,12},{12,8},{16,20},{20,16},{24,28},{28,24},{1,5},{5... | collective-permute-start | bytes 147464 | tf_op jit(solution)/shard_map/ppermute | solution.py:152
  9.9 2.4 %collective-permute-start.5 = (bf16[1,3,64,128]{3,2,1,0:T(8,128)(2,1)S(1)}, bf16[1,3,64,128]{3,2,1,0:T(8,128)(2,1)S(1)}, u32[]{:S(2)}, u32[]{:S(2)}) collective-permute-start(bf16[1,3,64,128]{3,2,1,0:T(8,128)(2,1)S(1)} %collective-permute-done.1.refs_2_), channel_id=1, source_target_pairs={{0,4},{4,0},{8,12},{12,8},{16,20},{20,16},{24,28},{28,24},{1,5},{5... | collective-permute-start | bytes 147464 | tf_op jit(solution)/shard_map/ppermute | solution.py:152
  12.3 1.2 %collective-permute-start.4 = (bf16[1,3,64,128]{3,2,1,0:T(8,128)(2,1)S(1)}, bf16[1,3,64,128]{3,2,1,0:T(8,128)(2,1)S(1)}, u32[]{:S(2)}, u32[]{:S(2)}) collective-permute-start(bf16[1,3,64,128]{3,2,1,0:T(8,128)(2,1)S(1)} %collective-permute-done.refs_1_), channel_id=1, source_target_pairs={{0,4},{4,0},{8,12},{12,8},{16,20},{20,16},{24,28},{28,24},{1,5},{5... | collective-permute-start | bytes 147464 | tf_op jit(solution)/shard_map/ppermute | solution.py:152
  15.9 5.0 %copy-start.1 = (bf16[8,4096]{1,0:T(8,128)(2,1)S(1)}, bf16[8,4096]{1,0:T(8,128)(2,1)}, u32[]{:S(2)}) copy-start(bf16[8,4096]{1,0:T(8,128)(2,1)} %refs_8_.2) | copy-start | bytes 196612
  16.0 21.6 %all-to-all-start = ((bf16[4,8,4096]{2,1,0:T(8,128)(2,1)}), bf16[4,8,4096]{2,1,0:T(8,128)(2,1)S(1)}, u32[]{:S(2)}, u32[]{:S(2)}) async-start(bf16[4,8,4096]{2,1,0:T(8,128)(2,1)} %shard_map.61), calls=%async_computation | async-start | bytes 524288 | tf_op jit(solution)/shard_map/all_to_all | solution.py:202
  21.0 14.1 %collective-permute-start.8 = (bf16[8,4096]{1,0:T(8,128)(2,1)S(1)}, bf16[8,4096]{1,0:T(8,128)(2,1)S(1)}, u32[]{:S(2)}, u32[]{:S(2)}) collective-permute-start(bf16[8,4096]{1,0:T(8,128)(2,1)S(1)} %copy-done.1), channel_id=1, source_target_pairs={{0,2},{1,3},{2,0},{3,1},{4,6},{5,7},{6,4},{7,5},{8,10},{9,11},{10,... | collective-permute-start | bytes 196616 | tf_op jit(solution)/shard_map/ppermute | solution.py:152
  23.9 11.2 %collective-permute-start.7 = (bf16[8,4096]{1,0:T(8,128)(2,1)S(1)}, bf16[8,4096]{1,0:T(8,128)(2,1)S(1)}, u32[]{:S(2)}, u32[]{:S(2)}) collective-permute-start(bf16[8,4096]{1,0:T(8,128)(2,1)S(1)} %copy-done.1), channel_id=1, source_target_pairs={{0,1},{1,0},{2,3},{3,2},{4,5},{5,4},{6,7},{7,6},{8,9},{9,8},{10,11... | collective-permute-start | bytes 196616 | tf_op jit(solution)/shard_map/ppermute | solution.py:152
  25.4 9.8 %collective-permute-start.9 = (bf16[8,4096]{1,0:T(8,128)(2,1)S(1)}, bf16[8,4096]{1,0:T(8,128)(2,1)S(1)}, u32[]{:S(2)}, u32[]{:S(2)}) collective-permute-start(bf16[8,4096]{1,0:T(8,128)(2,1)S(1)} %copy-done.1), channel_id=1, source_target_pairs={{0,3},{1,2},{2,1},{3,0},{4,7},{5,6},{6,5},{7,4},{8,11},{9,10},{10,... | collective-permute-start | bytes 196616 | tf_op jit(solution)/shard_map/ppermute | solution.py:152

commit v5 on v3

--- a/solution.py
+++ b/solution.py
@@ -9,12 +9,20 @@
 
 VMEM = pl.BlockSpec(memory_space=pltpu.VMEM)
 SMEM = pl.BlockSpec(memory_space=pltpu.SMEM)
-LIMIT = 48 * 1024 * 1024
-
-
-def pack_kernel(count, row_count, col_count, slots, values, packed):
+HBM = pl.BlockSpec(memory_space=pltpu.HBM)
+MIB = 1024 * 1024
+
+
+def pack_kernel(count, row_count, col_count, slots_hbm, values_hbm, packed, slots, values, sems):
+    copies = [
+        pltpu.make_async_copy(slots_hbm, slots, sems.at[0]),
+        pltpu.make_async_copy(values_hbm, values, sems.at[1]),
+    ]
+    for copy in copies:
+        copy.start()
     side = values.shape[2]
     pairs = packed.shape[1]
+    copies[0].wait()
     lane = lax.broadcasted_iota(jnp.int32, (side, side), 1)
     line = lax.broadcasted_iota(jnp.int32, (side, side), 0)
     head = jnp.zeros((side, side), jnp.float32)
@@ -25,6 +33,7 @@
         here = jnp.where(line == 0, row, col).astype(jnp.float32)
         head = jnp.where(lane == j, here, head)
     head = head.astype(jnp.bfloat16)
+    copies[1].wait()
     for k in range(pairs):
         left = values[0, k]
         right = values[0, k + pairs] if k + pairs < count else head
@@ -59,8 +68,10 @@
 
 
 def backward_kernel(count, n_parts, n_tensor, *refs):
-    gathered, cot, outs = refs[:n_parts], refs[n_parts], refs[n_parts + 1:n_parts + 1 + n_tensor]
-    ids_vmem, ids, cot_left, cot_right, prod, acc, sem = refs[n_parts + 1 + n_tensor:]
+    gathered, cot, own_tokens = refs[:n_parts], refs[n_parts], refs[n_parts + 1]
+    outs, own_later = refs[n_parts + 2:n_parts + 2 + n_tensor], refs[n_parts + 2 + n_tensor]
+    ids_vmem, ids, cot_left, cot_right, prod, acc, sem = refs[n_parts + 3 + n_tensor:]
+    own_later[...] = own_tokens[...]
     pairs, side = gathered[0].shape[1:3]
     col_count = cot_left.shape[0] - 1
     row_count = acc.shape[0] - 1
@@ -159,8 +170,10 @@
 def gather_parts(packed, n_dp):
     if n_dp > 8 or n_dp & (n_dp - 1):
         return [lax.all_gather(packed, "dp", axis=0, tiled=True)]
-    same_core = [packed] + [swap(packed, "dp", n_dp, k) for k in range(n_dp - 2, 0, -2)]
-    return same_core + [swap(part, "dp", n_dp, 1) for part in same_core]
+    same_core = [swap(packed, "dp", n_dp, k) for k in range(n_dp - 2, 0, -2)]
+    later, first = lax.optimization_barrier((packed, same_core[-1]))
+    same_core = same_core[:-1] + [first]
+    return [packed] + same_core + [swap(part, "dp", n_dp, 1) for part in same_core + [later]]
 
 
 def on_device(n_dp, n_tensor, inputs, block_values, block_slot, grad_out):
@@ -170,28 +183,34 @@
     row_count, col_count = width // side, hidden // side
     pairs = count // 2 + 1
     bf16, f32, i32 = jnp.bfloat16, jnp.float32, jnp.int32
+    grant = (12 if n_dp <= 8 else 48) * MIB
     far_first = range(n_tensor - 1, 0, -1)
 
     packed = pl.pallas_call(
         functools.partial(pack_kernel, count, row_count, col_count),
-        out_shape=jax.ShapeDtypeStruct((1, pairs, side, 2 * side), bf16),
-        in_specs=[SMEM, VMEM],
+        out_shape=pltpu.VMEM((1, pairs, side, 2 * side), bf16),
+        in_specs=[HBM, HBM],
         out_specs=VMEM,
-    )(block_slot, block_values)
+        scratch_shapes=[
+            pltpu.SMEM(block_slot.shape, i32),
+            pltpu.VMEM(block_values.shape, bf16),
+            pltpu.SemaphoreType.DMA((2,)),
+        ],
+        compiler_params=pltpu.CompilerParams(vmem_limit_bytes=4 * MIB),
+    )(pltpu.with_memory_space_constraint(block_slot, pltpu.HBM), pltpu.with_memory_space_constraint(block_values, pltpu.HBM))
     gathered = gather_parts(packed, n_dp)
-    moved = {k: swap(inputs, "tensor", n_tensor, k) for k in far_first}
-    tokens = [inputs] + [moved[k] for k in range(1, n_tensor)]
+    moved = {k: swap(inputs, "tensor", n_tensor, k) for k in range(2, n_tensor)}
     n_parts = len(gathered)
     total = n_dp * pairs
     ids = [
         pltpu.VMEM((n_dp, 8, 2 * side), i32),
         pltpu.SMEM((n_dp, 8, 2 * side), i32),
     ]
-    partial_sums = pl.pallas_call(
+    *partial_sums, own_later = pl.pallas_call(
         functools.partial(backward_kernel, count, n_parts, n_tensor),
-        out_shape=[jax.ShapeDtypeStruct((share, width), bf16)] * n_tensor,
-        in_specs=[VMEM] * (n_parts + 1),
-        out_specs=[VMEM] * n_tensor,
+        out_shape=[jax.ShapeDtypeStruct((share, width), bf16)] * (n_tensor + 1),
+        in_specs=[VMEM] * (n_parts + 2),
+        out_specs=[VMEM] * (n_tensor + 1),
         scratch_shapes=ids + [
             pltpu.VMEM((col_count + 1, rows, 2 * side), bf16),
             pltpu.VMEM((col_count + 1, rows, 2 * side), bf16),
@@ -199,9 +218,11 @@
             pltpu.VMEM((row_count + 1, rows, side), f32),
             pltpu.SemaphoreType.DMA,
         ],
-        compiler_params=pltpu.CompilerParams(vmem_limit_bytes=LIMIT),
-    )(*gathered, grad_out)
+        compiler_params=pltpu.CompilerParams(vmem_limit_bytes=grant),
+    )(*gathered, grad_out, inputs)
     arrived = [partial_sums[0]] + [swap(partial_sums[k], "tensor", n_tensor, k) for k in far_first]
+    moved[1] = swap(own_later, "tensor", n_tensor, 1)
+    tokens = [inputs] + [moved[k] for k in range(1, n_tensor)]
     outputs = pl.pallas_call(
         functools.partial(forward_kernel, count, n_parts, n_tensor),
         out_shape=jax.ShapeDtypeStruct((rows, hidden), bf16),
@@ -214,7 +235,7 @@
             pltpu.VMEM((rows, hidden), f32),
             pltpu.SemaphoreType.DMA,
         ],
-        compiler_params=pltpu.CompilerParams(vmem_limit_bytes=LIMIT),
+        compiler_params=pltpu.CompilerParams(vmem_limit_bytes=grant),
     )(*gathered, *tokens)
     total_grad = arrived[0].astype(f32)
     for value in arrived[1:]:

time: 28 us -> 27.6 us (0.986)
  waiting for transfers between devices: 3.29 us -> 5.03 us
  local copies, waits for them, and re-layouts: 0.8 us -> 0.01 us
  Pallas kernels: 5.74 us -> 5.07 us
  starting transfers between devices: 16.6 us -> 16 us
    ppermute x13, waiting for transfers between devices: 3.29 us -> 5.03 us  [swap(): return lax.ppermute(value, axis, [(i, i ^ k) for i in range(n)])]
    unnamed x6 -> x4, local copies, waits for them, and re-layouts: 0.8 us -> 0.01 us
    ppermute x13, starting transfers between devices: 16.6 us -> 16 us  [swap(): return lax.ppermute(value, axis, [(i, i ^ k) for i in range(n)])]
    pallas_call x1, Pallas kernels: 1.66 us -> 1.02 us  [on_device(): pl.pallas_call(functools.partial(pack_kernel, count, row_count, col_count...]
  transfers between devices with their start and end apart: 13 -> 13, of which waited for: 2 -> 3; matrix products, arithmetic and copies ran while one was open for 0% -> 0% of each run, Pallas kernels for 15% -> 15%
where the time goes in v5:
time: 27.6 us; the launch traced here: 27.5 us
  starting transfers between devices  16 us (58%)
  Pallas kernels  5.07 us (18%)
  waiting for transfers between devices  5.03 us (18%)
  between operations  0.72 us (3%)
  other arithmetic  0.67 us (2%)
    ppermute x13, starting transfers between devices, swap(): return lax.ppermute(value, axis, [(i, i ^ k) for i in range(n)])  16 us
    ppermute x13, waiting for transfers between devices, swap(): return lax.ppermute(value, axis, [(i, i ^ k) for i in range(n)])  5.03 us
    pallas_call x1, Pallas kernels, on_device(): pl.pallas_call(functools.partial(forward_kernel, count, n_parts, n_tensor...  2.37 us
    pallas_call x1, Pallas kernels, on_device(): pl.pallas_call(functools.partial(backward_kernel, count, n_parts, n_tenso...  1.69 us
    pallas_call x1, Pallas kernels, on_device(): pl.pallas_call(functools.partial(pack_kernel, count, row_count, col_count...  1.02 us
    convert_element_type x1, other arithmetic, on_device(): return (outputs, total_grad.astype(bf16))  0.67 us
  transfers between devices with their start and end apart: 13, of which 3 were waited for; matrix products, arithmetic and copies ran while one was open for 0% of the time, Pallas kernels for 15%

profile of v5, /device:TPU:0, one launch (start us, length us, event | category | flops | bytes accessed | tf_op | source)
XLA Modules:
  0.0 27.5 jit_solution(7496074282753698219)
XLA Ops:
  0.6 0.0 copy-start
  0.6 0.0 copy-start.1
  0.7 1.0 %shard_map.59.refs_0_ = bf16[1,3,64,128]{3,2,1,0:T(8,128)(2,1)S(1)} custom-call(s32[1,5]{1,0:T(1,128)} %slots_hbm.1, bf16[1,5,64,64]{3,2,1,0:T(8,128)(2,1)} %values_hbm.1), custom_call_target="tpu_custom_call" | custom-call | tf_op jit(solution)/shard_map/pallas_call | solution.py:189
  1.7 3.0 %collective-permute-start.2 = (bf16[1,3,64,128]{3,2,1,0:T(8,128)(2,1)S(1)}, bf16[1,3,64,128]{3,2,1,0:T(8,128)(2,1)S(1)}, u32[]{:S(2)}, u32[]{:S(2)}) collective-permute-start(bf16[1,3,64,128]{3,2,1,0:T(8,128)(2,1)S(1)} %shard_map.59.refs_0_), channel_id=1, source_target_pairs={{0,8},{4,12},{8,0},{12,4},{16,24},{20,28},{24,16},{28,20},{1,9},{5... | collective-permute-start | bytes 147464 | tf_op jit(solution)/shard_map/ppermute | solution.py:167
  4.7 1.5 %collective-permute-start = (bf16[1,3,64,128]{3,2,1,0:T(8,128)(2,1)S(1)}, bf16[1,3,64,128]{3,2,1,0:T(8,128)(2,1)S(1)}, u32[]{:S(2)}, u32[]{:S(2)}) collective-permute-start(bf16[1,3,64,128]{3,2,1,0:T(8,128)(2,1)S(1)} %shard_map.59.refs_0_), channel_id=1, source_target_pairs={{0,24},{4,28},{8,16},{12,20},{16,8},{20,12},{24,0},{28,4},{1,25},{... | collective-permute-start | bytes 147464 | tf_op jit(solution)/shard_map/ppermute | solution.py:167
  6.2 0.1 collective-permute-start.1
  6.2 3.0 %collective-permute-start.8 = (bf16[8,4096]{1,0:T(8,128)(2,1)S(1)}, bf16[8,4096]{1,0:T(8,128)(2,1)S(1)}, u32[]{:S(2)}, u32[]{:S(2)}) collective-permute-start(bf16[8,4096]{1,0:T(8,128)(2,1)S(1)} %copy-done), channel_id=1, source_target_pairs={{0,2},{1,3},{2,0},{3,1},{4,6},{5,7},{6,4},{7,5},{8,10},{9,11},{10,... | collective-permute-start | bytes 196616 | tf_op jit(solution)/shard_map/ppermute | solution.py:167
  9.3 0.0 collective-permute-done.2.refs_3_
  9.3 0.0 collective-permute-start.5
  9.3 0.5 %collective-permute-start.6 = (bf16[1,3,64,128]{3,2,1,0:T(8,128)(2,1)S(1)}, bf16[1,3,64,128]{3,2,1,0:T(8,128)(2,1)S(1)}, u32[]{:S(2)}, u32[]{:S(2)}) collective-permute-start(bf16[1,3,64,128]{3,2,1,0:T(8,128)(2,1)S(1)} %shard_map.59.refs_0_), channel_id=1, source_target_pairs={{0,4},{4,0},{8,12},{12,8},{16,20},{20,16},{24,28},{28,24},{1,5},{5... | collective-permute-start | bytes 147464 | tf_op jit(solution)/shard_map/ppermute | solution.py:167
  9.8 0.0 collective-permute-done.refs_1_
  9.8 0.0 collective-permute-start.3
  9.8 0.5 %collective-permute-done.1.refs_2_ = bf16[1,3,64,128]{3,2,1,0:T(8,128)(2,1)S(1)} collective-permute-done((bf16[1,3,64,128]{3,2,1,0:T(8,128)(2,1)S(1)}, bf16[1,3,64,128]{3,2,1,0:T(8,128)(2,1)S(1)}, u32[]{:S(2)}, u32[]{:S(2)}) %collective-permute-start.1) | collective-permute-done | bytes 49184 | tf_op jit(solution)/shard_map/ppermute | solution.py:167
  10.3 0.0 collective-permute-start.4
  10.3 0.2 collective-permute-done.5.refs_6_
  10.5 3.4 %collective-permute-start.9 = (bf16[8,4096]{1,0:T(8,128)(2,1)S(1)}, bf16[8,4096]{1,0:T(8,128)(2,1)S(1)}, u32[]{:S(2)}, u32[]{:S(2)}) collective-permute-start(bf16[8,4096]{1,0:T(8,128)(2,1)S(1)} %copy-done), channel_id=1, source_target_pairs={{0,3},{1,2},{2,1},{3,0},{4,7},{5,6},{6,5},{7,4},{8,11},{9,10},{10,... | collective-permute-start | bytes 196616 | tf_op jit(solution)/shard_map/ppermute | solution.py:167
  13.9 0.0 collective-permute-done.6.refs_7_
  13.9 0.0 collective-permute-done.3.refs_4_
  13.9 0.0 collective-permute-done.4.refs_5_
  13.9 1.7 %shard_map.60 = (bf16[8,4096]{1,0:T(8,128)(2,1)S(1)}, bf16[8,4096]{1,0:T(8,128)(2,1)S(1)}, bf16[8,4096]{1,0:T(8,128)(2,1)S(1)}, bf16[8,4096]{1,0:T(8,128)(2,1)S(1)}, bf16[8,4096]{1,0:T(8,128)(2,1)S(1)}) custom-call(bf16[1,3,64,128]{3,2,1,0:T(8,128)(2,1)S(1)} %shard_map.59.refs_0_, bf16[1,3,64,128]{3,2,1,0:T(8,128)(2,1)S(1)} %collective-permute-done.refs_1_, ...), custom_call_target="tpu_custom_call" | custom-call | tf_op jit(solution)/shard_map/pallas_call | solution.py:209
  15.6 1.3 %collective-permute-start.10 = (bf16[8,4096]{1,0:T(8,128)(2,1)S(1)}, bf16[8,4096]{1,0:T(8,128)(2,1)S(1)}, u32[]{:S(2)}, u32[]{:S(2)}) collective-permute-start(bf16[8,4096]{1,0:T(8,128)(2,1)S(1)} %get-tuple-element.13), channel_id=1, source_target_pairs={{0,3},{1,2},{2,1},{3,0},{4,7},{5,6},{6,5},{7,4},{8,11},{9,10},{10,... | collective-permute-start | bytes 196616 | tf_op jit(solution)/shard_map/ppermute | solution.py:167
  16.9 0.0 collective-permute-start.7
  16.9 3.2 %collective-permute-start.11 = (bf16[8,4096]{1,0:T(8,128)(2,1)S(1)}, bf16[8,4096]{1,0:T(8,128)(2,1)S(1)}, u32[]{:S(2)}, u32[]{:S(2)}) collective-permute-start(bf16[8,4096]{1,0:T(8,128)(2,1)S(1)} %get-tuple-element.14), channel_id=1, source_target_pairs={{0,2},{1,3},{2,0},{3,1},{4,6},{5,7},{6,4},{7,5},{8,10},{9,11},{10,... | collective-permute-start | bytes 196616 | tf_op jit(solution)/shard_map/ppermute | solution.py:167
  20.0 0.0 collective-permute-done.8.refs_10_
  20.1 0.0 collective-permute-start.12
  20.1 0.0 collective-permute-done.9.refs_11_
  20.1 4.3 %collective-permute-done.7.refs_9_ = bf16[8,4096]{1,0:T(8,128)(2,1)S(1)} collective-permute-done((bf16[8,4096]{1,0:T(8,128)(2,1)S(1)}, bf16[8,4096]{1,0:T(8,128)(2,1)S(1)}, u32[]{:S(2)}, u32[]{:S(2)}) %collective-permute-start.7) | collective-permute-done | bytes 65568 | tf_op jit(solution)/shard_map/ppermute | solution.py:167
  24.4 2.4 %shard_map.61 = bf16[32,896]{1,0:T(8,128)(2,1)} custom-call(bf16[1,3,64,128]{3,2,1,0:T(8,128)(2,1)S(1)} %shard_map.59.refs_0_, bf16[1,3,64,128]{3,2,1,0:T(8,128)(2,1)S(1)} %collective-permute-done.refs_1_, bf16[1,3,64,128]{3,2,1,0:T(8,128)(2,1)S(1)} %collective-permute-done.1.refs_2_, bf16[1,3,64,128]{3,2,1,0:T(8,128)(2,1)S(1)} %collective-permute-done.2.refs_3_, ...), custom_call_target="tpu_custom_call" | custom-call | tf_op jit(solution)/shard_map/pallas_call | solution.py:226
  26.8 0.0 collective-permute-done.10
  26.8 0.0 collective-permute-done.11
  26.8 0.0 collective-permute-done.12
  26.8 0.7 %add_convert_fusion = bf16[8,4096]{1,0:T(8,128)(2,1)} fusion(bf16[8,4096]{1,0:T(8,128)(2,1)S(1)} %collective-permute-done.12, bf16[8,4096]{1,0:T(8,128)(2,1)S(1)} %collective-permute-done.11, bf16[8,4096]{1,0:T(8,128)(2,1)S(1)} %collective-permute-done.10, bf16[8,4096]{1,0:T(8,128)(2,1)S(1)} %get-tuple-element.12), kind=kLoop, calls=%fused_computation | loop fusion | flops 262144 | bytes 327680 | tf_op jit(solution)/shard_map/convert_element_type | solution.py:243
  (2 shorter events, 0.0 us)
Async XLA Ops:
  0.6 5.6 %copy-start = (bf16[8,4096]{1,0:T(8,128)(2,1)S(1)}, bf16[8,4096]{1,0:T(8,128)(2,1)}, u32[]{:S(2)}) copy-start(bf16[8,4096]{1,0:T(8,128)(2,1)} %refs_8_.3) | copy-start | bytes 196612
  0.6 13.2 %copy-start.1 = (bf16[32,896]{1,0:T(8,128)(2,1)S(1)}, bf16[32,896]{1,0:T(8,128)(2,1)}, u32[]{:S(2)}) copy-start(bf16[32,896]{1,0:T(8,128)(2,1)} %refs_8_.2) | copy-start | bytes 172036
  1.7 7.6 %collective-permute-start.2 = (bf16[1,3,64,128]{3,2,1,0:T(8,128)(2,1)S(1)}, bf16[1,3,64,128]{3,2,1,0:T(8,128)(2,1)S(1)}, u32[]{:S(2)}, u32[]{:S(2)}) collective-permute-start(bf16[1,3,64,128]{3,2,1,0:T(8,128)(2,1)S(1)} %shard_map.59.refs_0_), channel_id=1, source_target_pairs={{0,8},{4,12},{8,0},{12,4},{16,24},{20,28},{24,16},{28,20},{1,9},{5... | collective-permute-start | bytes 147464 | tf_op jit(solution)/shard_map/ppermute | solution.py:167
  4.7 5.1 %collective-permute-start = (bf16[1,3,64,128]{3,2,1,0:T(8,128)(2,1)S(1)}, bf16[1,3,64,128]{3,2,1,0:T(8,128)(2,1)S(1)}, u32[]{:S(2)}, u32[]{:S(2)}) collective-permute-start(bf16[1,3,64,128]{3,2,1,0:T(8,128)(2,1)S(1)} %shard_map.59.refs_0_), channel_id=1, source_target_pairs={{0,24},{4,28},{8,16},{12,20},{16,8},{20,12},{24,0},{28,4},{1,25},{... | collective-permute-start | bytes 147464 | tf_op jit(solution)/shard_map/ppermute | solution.py:167
  6.2 4.1 %collective-permute-start.1 = (bf16[1,3,64,128]{3,2,1,0:T(8,128)(2,1)S(1)}, bf16[1,3,64,128]{3,2,1,0:T(8,128)(2,1)S(1)}, u32[]{:S(2)}, u32[]{:S(2)}) collective-permute-start(bf16[1,3,64,128]{3,2,1,0:T(8,128)(2,1)S(1)} %shard_map.59.refs_0_), channel_id=1, source_target_pairs={{0,16},{4,20},{8,24},{12,28},{16,0},{20,4},{24,8},{28,12},{1,17},{... | collective-permute-start | bytes 147464 | tf_op jit(solution)/shard_map/ppermute | solution.py:167
  6.2 13.8 %collective-permute-start.8 = (bf16[8,4096]{1,0:T(8,128)(2,1)S(1)}, bf16[8,4096]{1,0:T(8,128)(2,1)S(1)}, u32[]{:S(2)}, u32[]{:S(2)}) collective-permute-start(bf16[8,4096]{1,0:T(8,128)(2,1)S(1)} %copy-done), channel_id=1, source_target_pairs={{0,2},{1,3},{2,0},{3,1},{4,6},{5,7},{6,4},{7,5},{8,10},{9,11},{10,... | collective-permute-start | bytes 196616 | tf_op jit(solution)/shard_map/ppermute | solution.py:167
  9.3 1.2 %collective-permute-start.5 = (bf16[1,3,64,128]{3,2,1,0:T(8,128)(2,1)S(1)}, bf16[1,3,64,128]{3,2,1,0:T(8,128)(2,1)S(1)}, u32[]{:S(2)}, u32[]{:S(2)}) collective-permute-start(bf16[1,3,64,128]{3,2,1,0:T(8,128)(2,1)S(1)} %collective-permute-done.2.refs_3_), channel_id=1, source_target_pairs={{0,4},{4,0},{8,12},{12,8},{16,20},{20,16},{24,28},{28,24},{1,5},{5... | collective-permute-start | bytes 147464 | tf_op jit(solution)/shard_map/ppermute | solution.py:167
  9.3 4.6 %collective-permute-start.6 = (bf16[1,3,64,128]{3,2,1,0:T(8,128)(2,1)S(1)}, bf16[1,3,64,128]{3,2,1,0:T(8,128)(2,1)S(1)}, u32[]{:S(2)}, u32[]{:S(2)}) collective-permute-start(bf16[1,3,64,128]{3,2,1,0:T(8,128)(2,1)S(1)} %shard_map.59.refs_0_), channel_id=1, source_target_pairs={{0,4},{4,0},{8,12},{12,8},{16,20},{20,16},{24,28},{28,24},{1,5},{5... | collective-permute-start | bytes 147464 | tf_op jit(solution)/shard_map/ppermute | solution.py:167
  9.8 4.1 %collective-permute-start.3 = (bf16[1,3,64,128]{3,2,1,0:T(8,128)(2,1)S(1)}, bf16[1,3,64,128]{3,2,1,0:T(8,128)(2,1)S(1)}, u32[]{:S(2)}, u32[]{:S(2)}) collective-permute-start(bf16[1,3,64,128]{3,2,1,0:T(8,128)(2,1)S(1)} %collective-permute-done.refs_1_), channel_id=1, source_target_pairs={{0,4},{4,0},{8,12},{12,8},{16,20},{20,16},{24,28},{28,24},{1,5},{5... | collective-permute-start | bytes 147464 | tf_op jit(solution)/shard_map/ppermute | solution.py:167
  10.3 3.6 %collective-permute-start.4 = (bf16[1,3,64,128]{3,2,1,0:T(8,128)(2,1)S(1)}, bf16[1,3,64,128]{3,2,1,0:T(8,128)(2,1)S(1)}, u32[]{:S(2)}, u32[]{:S(2)}) collective-permute-start(bf16[1,3,64,128]{3,2,1,0:T(8,128)(2,1)S(1)} %collective-permute-done.1.refs_2_), channel_id=1, source_target_pairs={{0,4},{4,0},{8,12},{12,8},{16,20},{20,16},{24,28},{28,24},{1,5},{5... | collective-permute-start | bytes 147464 | tf_op jit(solution)/shard_map/ppermute | solution.py:167
  10.5 9.6 %collective-permute-start.9 = (bf16[8,4096]{1,0:T(8,128)(2,1)S(1)}, bf16[8,4096]{1,0:T(8,128)(2,1)S(1)}, u32[]{:S(2)}, u32[]{:S(2)}) collective-permute-start(bf16[8,4096]{1,0:T(8,128)(2,1)S(1)} %copy-done), channel_id=1, source_target_pairs={{0,3},{1,2},{2,1},{3,0},{4,7},{5,6},{6,5},{7,4},{8,11},{9,10},{10,... | collective-permute-start | bytes 196616 | tf_op jit(solution)/shard_map/ppermute | solution.py:167
  15.6 11.2 %collective-permute-start.10 = (bf16[8,4096]{1,0:T(8,128)(2,1)S(1)}, bf16[8,4096]{1,0:T(8,128)(2,1)S(1)}, u32[]{:S(2)}, u32[]{:S(2)}) collective-permute-start(bf16[8,4096]{1,0:T(8,128)(2,1)S(1)} %get-tuple-element.13), channel_id=1, source_target_pairs={{0,3},{1,2},{2,1},{3,0},{4,7},{5,6},{6,5},{7,4},{8,11},{9,10},{10,... | collective-permute-start | bytes 196616 | tf_op jit(solution)/shard_map/ppermute | solution.py:167
  16.9 7.5 %collective-permute-start.7 = (bf16[8,4096]{1,0:T(8,128)(2,1)S(1)}, bf16[8,4096]{1,0:T(8,128)(2,1)S(1)}, u32[]{:S(2)}, u32[]{:S(2)}) collective-permute-start(bf16[8,4096]{1,0:T(8,128)(2,1)S(1)} %get-tuple-element.11), channel_id=1, source_target_pairs={{0,1},{1,0},{2,3},{3,2},{4,5},{5,4},{6,7},{7,6},{8,9},{9,8},{10,11... | collective-permute-start | bytes 196616 | tf_op jit(solution)/shard_map/ppermute | solution.py:167
  16.9 9.9 %collective-permute-start.11 = (bf16[8,4096]{1,0:T(8,128)(2,1)S(1)}, bf16[8,4096]{1,0:T(8,128)(2,1)S(1)}, u32[]{:S(2)}, u32[]{:S(2)}) collective-permute-start(bf16[8,4096]{1,0:T(8,128)(2,1)S(1)} %get-tuple-element.14), channel_id=1, source_target_pairs={{0,2},{1,3},{2,0},{3,1},{4,6},{5,7},{6,4},{7,5},{8,10},{9,11},{10,... | collective-permute-start | bytes 196616 | tf_op jit(solution)/shard_map/ppermute | solution.py:167
  20.1 6.7 %collective-permute-start.12 = (bf16[8,4096]{1,0:T(8,128)(2,1)S(1)}, bf16[8,4096]{1,0:T(8,128)(2,1)S(1)}, u32[]{:S(2)}, u32[]{:S(2)}) collective-permute-start(bf16[8,4096]{1,0:T(8,128)(2,1)S(1)} %get-tuple-element.15), channel_id=1, source_target_pairs={{0,1},{1,0},{2,3},{3,2},{4,5},{5,4},{6,7},{7,6},{8,9},{9,8},{10,11... | collective-permute-start | bytes 196616 | tf_op jit(solution)/shard_map/ppermute | solution.py:167

commit v6 on v5

--- a/solution.py
+++ b/solution.py
@@ -40,6 +40,11 @@
         packed[0, k] = jnp.concatenate([left, right], axis=1)
 
 
+def join_kernel(*refs):
+    for i, part in enumerate(refs[:-1]):
+        refs[-1][i] = part[0]
+
+
 def load_ids(gathered, ids_vmem, ids, sem):
     start = 0
     for part in gathered:
@@ -68,10 +73,8 @@
 
 
 def backward_kernel(count, n_parts, n_tensor, *refs):
-    gathered, cot, own_tokens = refs[:n_parts], refs[n_parts], refs[n_parts + 1]
-    outs, own_later = refs[n_parts + 2:n_parts + 2 + n_tensor], refs[n_parts + 2 + n_tensor]
-    ids_vmem, ids, cot_left, cot_right, prod, acc, sem = refs[n_parts + 3 + n_tensor:]
-    own_later[...] = own_tokens[...]
+    gathered, cot, outs = refs[:n_parts], refs[n_parts], refs[n_parts + 1:n_parts + 1 + n_tensor]
+    ids_vmem, ids, cot_left, cot_right, prod, acc, sem = refs[n_parts + 1 + n_tensor:]
     pairs, side = gathered[0].shape[1:3]
     col_count = cot_left.shape[0] - 1
     row_count = acc.shape[0] - 1
@@ -170,10 +173,16 @@
 def gather_parts(packed, n_dp):
     if n_dp > 8 or n_dp & (n_dp - 1):
         return [lax.all_gather(packed, "dp", axis=0, tiled=True)]
-    same_core = [swap(packed, "dp", n_dp, k) for k in range(n_dp - 2, 0, -2)]
-    later, first = lax.optimization_barrier((packed, same_core[-1]))
-    same_core = same_core[:-1] + [first]
-    return [packed] + same_core + [swap(part, "dp", n_dp, 1) for part in same_core + [later]]
+    *near, second, last = [packed] + [swap(packed, "dp", n_dp, k) for k in range(2, n_dp, 2)]
+    joined = pl.pallas_call(
+        join_kernel,
+        out_shape=pltpu.VMEM((len(near), *packed.shape[1:]), packed.dtype),
+        in_specs=[VMEM] * len(near),
+        out_specs=VMEM,
+        compiler_params=pltpu.CompilerParams(vmem_limit_bytes=4 * MIB),
+    )(*near)
+    same_core = [joined, second, last]
+    return same_core + [swap(part, "dp", n_dp, 1) for part in same_core]
 
 
 def on_device(n_dp, n_tensor, inputs, block_values, block_slot, grad_out):
@@ -199,18 +208,19 @@
         compiler_params=pltpu.CompilerParams(vmem_limit_bytes=4 * MIB),
     )(pltpu.with_memory_space_constraint(block_slot, pltpu.HBM), pltpu.with_memory_space_constraint(block_values, pltpu.HBM))
     gathered = gather_parts(packed, n_dp)
-    moved = {k: swap(inputs, "tensor", n_tensor, k) for k in range(2, n_tensor)}
+    moved = {k: swap(inputs, "tensor", n_tensor, k) for k in far_first}
+    tokens = [inputs] + [moved[k] for k in range(1, n_tensor)]
     n_parts = len(gathered)
     total = n_dp * pairs
     ids = [
         pltpu.VMEM((n_dp, 8, 2 * side), i32),
         pltpu.SMEM((n_dp, 8, 2 * side), i32),
     ]
-    *partial_sums, own_later = pl.pallas_call(
+    partial_sums = pl.pallas_call(
         functools.partial(backward_kernel, count, n_parts, n_tensor),
-        out_shape=[jax.ShapeDtypeStruct((share, width), bf16)] * (n_tensor + 1),
-        in_specs=[VMEM] * (n_parts + 2),
-        out_specs=[VMEM] * (n_tensor + 1),
+        out_shape=[jax.ShapeDtypeStruct((share, width), bf16)] * n_tensor,
+        in_specs=[VMEM] * (n_parts + 1),
+        out_specs=[VMEM] * n_tensor,
         scratch_shapes=ids + [
             pltpu.VMEM((col_count + 1, rows, 2 * side), bf16),
             pltpu.VMEM((col_count + 1, rows, 2 * side), bf16),
@@ -219,10 +229,8 @@
             pltpu.SemaphoreType.DMA,
         ],
         compiler_params=pltpu.CompilerParams(vmem_limit_bytes=grant),
-    )(*gathered, grad_out, inputs)
+    )(*gathered, grad_out)
     arrived = [partial_sums[0]] + [swap(partial_sums[k], "tensor", n_tensor, k) for k in far_first]
-    moved[1] = swap(own_later, "tensor", n_tensor, 1)
-    tokens = [inputs] + [moved[k] for k in range(1, n_tensor)]
     outputs = pl.pallas_call(
         functools.partial(forward_kernel, count, n_parts, n_tensor),
         out_shape=jax.ShapeDtypeStruct((rows, hidden), bf16),

time: 27.6 us -> 25.5 us (0.924)
  waiting for transfers between devices: 5.03 us -> 2.27 us
  starting transfers between devices: 16 us -> 16.6 us
    ppermute x13 -> x12, waiting for transfers between devices: 5.03 us -> 2.27 us  [swap(): return lax.ppermute(value, axis, [(i, i ^ k) for i in range(n)])]
    ppermute x13 -> x12, starting transfers between devices: 16 us -> 16.6 us  [swap(): return lax.ppermute(value, axis, [(i, i ^ k) for i in range(n)])]
  transfers between devices with their start and end apart: 13 -> 12, of which waited for: 3 -> 3; matrix products, arithmetic and copies ran while one was open for 0% -> 0% of each run, Pallas kernels for 15% -> 16%
where the time goes in v6:
time: 25.5 us; the launch traced here: 25.4 us
  starting transfers between devices  16.6 us (65%)
  Pallas kernels  5.07 us (20%)
  waiting for transfers between devices  2.27 us (9%)
  between operations  0.7 us (3%)
  other arithmetic  0.67 us (3%)
    ppermute x12, starting transfers between devices, swap(): return lax.ppermute(value, axis, [(i, i ^ k) for i in range(n)])  16.6 us
    pallas_call x1, Pallas kernels, on_device(): pl.pallas_call(functools.partial(forward_kernel, count, n_parts, n_tensor...  2.42 us
    ppermute x12, waiting for transfers between devices, swap(): return lax.ppermute(value, axis, [(i, i ^ k) for i in range(n)])  2.27 us
    pallas_call x1, Pallas kernels, on_device(): pl.pallas_call(functools.partial(backward_kernel, count, n_parts, n_tenso...  1.66 us
    pallas_call x1, Pallas kernels, on_device(): pl.pallas_call(functools.partial(pack_kernel, count, row_count, col_count...  0.99 us
    convert_element_type x1, other arithmetic, on_device(): return (outputs, total_grad.astype(bf16))  0.67 us
  transfers between devices with their start and end apart: 12, of which 3 were waited for; matrix products, arithmetic and copies ran while one was open for 0% of the time, Pallas kernels for 16%

profile of v6, /device:TPU:0, one launch (start us, length us, event | category | flops | bytes accessed | tf_op | source)
XLA Modules:
  0.0 25.4 jit_solution(1086683807365831961)
XLA Ops:
  0.6 1.0 %shard_map.59.refs_0_ = bf16[1,3,64,128]{3,2,1,0:T(8,128)(2,1)S(1)} custom-call(s32[1,5]{1,0:T(1,128)} %slots_hbm.1, bf16[1,5,64,64]{3,2,1,0:T(8,128)(2,1)} %values_hbm.1), custom_call_target="tpu_custom_call" | custom-call | tf_op jit(solution)/shard_map/pallas_call | solution.py:198
  1.6 0.0 copy-start
  1.6 0.0 copy-start.1
  1.6 3.0 %collective-permute-start = (bf16[1,3,64,128]{3,2,1,0:T(8,128)(2,1)S(1)}, bf16[1,3,64,128]{3,2,1,0:T(8,128)(2,1)S(1)}, u32[]{:S(2)}, u32[]{:S(2)}) collective-permute-start(bf16[1,3,64,128]{3,2,1,0:T(8,128)(2,1)S(1)} %shard_map.59.refs_0_), channel_id=1, source_target_pairs={{0,8},{4,12},{8,0},{12,4},{16,24},{20,28},{24,16},{28,20},{1,9},{5... | collective-permute-start | bytes 147464 | tf_op jit(solution)/shard_map/ppermute | solution.py:170
  4.7 1.5 %collective-permute-start.2 = (bf16[1,3,64,128]{3,2,1,0:T(8,128)(2,1)S(1)}, bf16[1,3,64,128]{3,2,1,0:T(8,128)(2,1)S(1)}, u32[]{:S(2)}, u32[]{:S(2)}) collective-permute-start(bf16[1,3,64,128]{3,2,1,0:T(8,128)(2,1)S(1)} %shard_map.59.refs_0_), channel_id=1, source_target_pairs={{0,24},{4,28},{8,16},{12,20},{16,8},{20,12},{24,0},{28,4},{1,25},{... | collective-permute-start | bytes 147464 | tf_op jit(solution)/shard_map/ppermute | solution.py:170
  6.1 0.1 collective-permute-start.1
  6.2 0.5 %collective-permute-done.refs_1_ = bf16[1,3,64,128]{3,2,1,0:T(8,128)(2,1)S(1)} collective-permute-done((bf16[1,3,64,128]{3,2,1,0:T(8,128)(2,1)S(1)}, bf16[1,3,64,128]{3,2,1,0:T(8,128)(2,1)S(1)}, u32[]{:S(2)}, u32[]{:S(2)}) %collective-permute-start) | collective-permute-done | bytes 49184 | tf_op jit(solution)/shard_map/ppermute | solution.py:170
  6.7 0.1 collective-permute-start.3
  6.8 0.0 copy-done
  6.8 3.2 %collective-permute-start.7 = (bf16[8,4096]{1,0:T(8,128)(2,1)S(1)}, bf16[8,4096]{1,0:T(8,128)(2,1)S(1)}, u32[]{:S(2)}, u32[]{:S(2)}) collective-permute-start(bf16[8,4096]{1,0:T(8,128)(2,1)S(1)} %copy-done), channel_id=1, source_target_pairs={{0,2},{1,3},{2,0},{3,1},{4,6},{5,7},{6,4},{7,5},{8,10},{9,11},{10,... | collective-permute-start | bytes 196616 | tf_op jit(solution)/shard_map/ppermute | solution.py:170
  10.0 0.0 collective-permute-done.2.refs_2_
  10.0 0.2 collective-permute-start.5
  10.2 0.1 collective-permute-done.1.refs_1_
  10.2 0.3 %collective-permute-start.4 = (bf16[1,3,64,128]{3,2,1,0:T(8,128)(2,1)S(1)}, bf16[1,3,64,128]{3,2,1,0:T(8,128)(2,1)S(1)}, u32[]{:S(2)}, u32[]{:S(2)}) collective-permute-start(bf16[1,3,64,128]{3,2,1,0:T(8,128)(2,1)S(1)} %collective-permute-done.1.refs_1_), channel_id=1, source_target_pairs={{0,4},{4,0},{8,12},{12,8},{16,20},{20,16},{24,28},{28,24},{1,5},{5... | collective-permute-start | bytes 147464 | tf_op jit(solution)/shard_map/ppermute | solution.py:170
  10.5 1.6 %collective-permute-start.6 = (bf16[8,4096]{1,0:T(8,128)(2,1)S(1)}, bf16[8,4096]{1,0:T(8,128)(2,1)S(1)}, u32[]{:S(2)}, u32[]{:S(2)}) collective-permute-start(bf16[8,4096]{1,0:T(8,128)(2,1)S(1)} %copy-done), channel_id=1, source_target_pairs={{0,1},{1,0},{2,3},{3,2},{4,5},{5,4},{6,7},{7,6},{8,9},{9,8},{10,11... | collective-permute-start | bytes 196616 | tf_op jit(solution)/shard_map/ppermute | solution.py:170
  12.1 0.0 collective-permute-done.5.refs_5_
  12.1 2.4 %collective-permute-start.8 = (bf16[8,4096]{1,0:T(8,128)(2,1)S(1)}, bf16[8,4096]{1,0:T(8,128)(2,1)S(1)}, u32[]{:S(2)}, u32[]{:S(2)}) collective-permute-start(bf16[8,4096]{1,0:T(8,128)(2,1)S(1)} %copy-done), channel_id=1, source_target_pairs={{0,3},{1,2},{2,1},{3,0},{4,7},{5,6},{6,5},{7,4},{8,11},{9,10},{10,... | collective-permute-start | bytes 196616 | tf_op jit(solution)/shard_map/ppermute | solution.py:170
  14.5 0.0 collective-permute-done.4.refs_4_
  14.5 0.0 collective-permute-done.3.refs_3_
  14.5 0.0 copy-done.1
  14.5 1.7 %shard_map.62 = (bf16[8,4096]{1,0:T(8,128)(2,1)S(1)}, bf16[8,4096]{1,0:T(8,128)(2,1)S(1)}, bf16[8,4096]{1,0:T(8,128)(2,1)S(1)}, bf16[8,4096]{1,0:T(8,128)(2,1)S(1)}) custom-call(bf16[2,3,64,128]{3,2,1,0:T(8,128)(2,1)S(1)} %shard_map.60.refs_0_, bf16[1,3,64,128]{3,2,1,0:T(8,128)(2,1)S(1)} %collective-permute-done.1.refs_1_, ...), custom_call_target="tpu_custom_call" | custom-call | tf_op jit(solution)/shard_map/pallas_call | solution.py:219
  16.2 1.5 %collective-permute-start.9 = (bf16[8,4096]{1,0:T(8,128)(2,1)S(1)}, bf16[8,4096]{1,0:T(8,128)(2,1)S(1)}, u32[]{:S(2)}, u32[]{:S(2)}) collective-permute-start(bf16[8,4096]{1,0:T(8,128)(2,1)S(1)} %get-tuple-element.7), channel_id=1, source_target_pairs={{0,3},{1,2},{2,1},{3,0},{4,7},{5,6},{6,5},{7,4},{8,11},{9,10},{10,... | collective-permute-start | bytes 196616 | tf_op jit(solution)/shard_map/ppermute | solution.py:170
  17.7 0.5 %collective-permute-start.10 = (bf16[8,4096]{1,0:T(8,128)(2,1)S(1)}, bf16[8,4096]{1,0:T(8,128)(2,1)S(1)}, u32[]{:S(2)}, u32[]{:S(2)}) collective-permute-start(bf16[8,4096]{1,0:T(8,128)(2,1)S(1)} %get-tuple-element.8), channel_id=1, source_target_pairs={{0,2},{1,3},{2,0},{3,1},{4,6},{5,7},{6,4},{7,5},{8,10},{9,11},{10,... | collective-permute-start | bytes 196616 | tf_op jit(solution)/shard_map/ppermute | solution.py:170
  18.1 0.0 collective-permute-done.7.refs_8_
  18.1 2.5 %collective-permute-start.11 = (bf16[8,4096]{1,0:T(8,128)(2,1)S(1)}, bf16[8,4096]{1,0:T(8,128)(2,1)S(1)}, u32[]{:S(2)}, u32[]{:S(2)}) collective-permute-start(bf16[8,4096]{1,0:T(8,128)(2,1)S(1)} %get-tuple-element.9), channel_id=1, source_target_pairs={{0,1},{1,0},{2,3},{3,2},{4,5},{5,4},{6,7},{7,6},{8,9},{9,8},{10,11... | collective-permute-start | bytes 196616 | tf_op jit(solution)/shard_map/ppermute | solution.py:170
  20.6 0.0 collective-permute-done.6.refs_7_
  20.6 0.0 collective-permute-done.8.refs_9_
  20.6 2.4 %shard_map.61 = bf16[32,896]{1,0:T(8,128)(2,1)} custom-call(bf16[2,3,64,128]{3,2,1,0:T(8,128)(2,1)S(1)} %shard_map.60.refs_0_, bf16[1,3,64,128]{3,2,1,0:T(8,128)(2,1)S(1)} %collective-permute-done.1.refs_1_, bf16[1,3,64,128]{3,2,1,0:T(8,128)(2,1)S(1)} %collective-permute-done.2.refs_2_, bf16[2,3,64,128]{3,2,1,0:T(8,128)(2,1)S(1)} %collective-permute-done.3.refs_3_, ...), custom_call_target="tpu_custom_call" | custom-call | tf_op jit(solution)/shard_map/pallas_call | solution.py:234
  23.0 0.0 collective-permute-done.9
  23.1 1.6 %collective-permute-done.10 = bf16[8,4096]{1,0:T(8,128)(2,1)S(1)} collective-permute-done((bf16[8,4096]{1,0:T(8,128)(2,1)S(1)}, bf16[8,4096]{1,0:T(8,128)(2,1)S(1)}, u32[]{:S(2)}, u32[]{:S(2)}) %collective-permute-start.10) | collective-permute-done | bytes 65568 | tf_op jit(solution)/shard_map/ppermute | solution.py:170
  24.7 0.0 collective-permute-done.11
  24.7 0.7 %add_convert_fusion = bf16[8,4096]{1,0:T(8,128)(2,1)} fusion(bf16[8,4096]{1,0:T(8,128)(2,1)S(1)} %collective-permute-done.11, bf16[8,4096]{1,0:T(8,128)(2,1)S(1)} %collective-permute-done.10, bf16[8,4096]{1,0:T(8,128)(2,1)S(1)} %collective-permute-done.9, bf16[8,4096]{1,0:T(8,128)(2,1)S(1)} %get-tuple-element.6), kind=kLoop, calls=%fused_computation | loop fusion | flops 262144 | bytes 327680 | tf_op jit(solution)/shard_map/convert_element_type | solution.py:251
  (1 shorter events, 0.0 us)
Async XLA Ops:
  1.6 5.2 %copy-start = (bf16[8,4096]{1,0:T(8,128)(2,1)S(1)}, bf16[8,4096]{1,0:T(8,128)(2,1)}, u32[]{:S(2)}) copy-start(bf16[8,4096]{1,0:T(8,128)(2,1)} %refs_6_.2) | copy-start | bytes 196612
  1.6 12.8 %copy-start.1 = (bf16[32,896]{1,0:T(8,128)(2,1)S(1)}, bf16[32,896]{1,0:T(8,128)(2,1)}, u32[]{:S(2)}) copy-start(bf16[32,896]{1,0:T(8,128)(2,1)} %refs_6_.3) | copy-start | bytes 172036
  1.6 5.1 %collective-permute-start = (bf16[1,3,64,128]{3,2,1,0:T(8,128)(2,1)S(1)}, bf16[1,3,64,128]{3,2,1,0:T(8,128)(2,1)S(1)}, u32[]{:S(2)}, u32[]{:S(2)}) collective-permute-start(bf16[1,3,64,128]{3,2,1,0:T(8,128)(2,1)S(1)} %shard_map.59.refs_0_), channel_id=1, source_target_pairs={{0,8},{4,12},{8,0},{12,4},{16,24},{20,28},{24,16},{28,20},{1,9},{5... | collective-permute-start | bytes 147464 | tf_op jit(solution)/shard_map/ppermute | solution.py:170
  4.7 5.4 %collective-permute-start.2 = (bf16[1,3,64,128]{3,2,1,0:T(8,128)(2,1)S(1)}, bf16[1,3,64,128]{3,2,1,0:T(8,128)(2,1)S(1)}, u32[]{:S(2)}, u32[]{:S(2)}) collective-permute-start(bf16[1,3,64,128]{3,2,1,0:T(8,128)(2,1)S(1)} %shard_map.59.refs_0_), channel_id=1, source_target_pairs={{0,24},{4,28},{8,16},{12,20},{16,8},{20,12},{24,0},{28,4},{1,25},{... | collective-permute-start | bytes 147464 | tf_op jit(solution)/shard_map/ppermute | solution.py:170
  6.1 4.1 %collective-permute-start.1 = (bf16[1,3,64,128]{3,2,1,0:T(8,128)(2,1)S(1)}, bf16[1,3,64,128]{3,2,1,0:T(8,128)(2,1)S(1)}, u32[]{:S(2)}, u32[]{:S(2)}) collective-permute-start(bf16[1,3,64,128]{3,2,1,0:T(8,128)(2,1)S(1)} %shard_map.59.refs_0_), channel_id=1, source_target_pairs={{0,16},{4,20},{8,24},{12,28},{16,0},{20,4},{24,8},{28,12},{1,17},{... | collective-permute-start | bytes 147464 | tf_op jit(solution)/shard_map/ppermute | solution.py:170
  6.7 7.7 %collective-permute-start.3 = (bf16[2,3,64,128]{3,2,1,0:T(8,128)(2,1)S(1)}, bf16[2,3,64,128]{3,2,1,0:T(8,128)(2,1)S(1)}, u32[]{:S(2)}, u32[]{:S(2)}) collective-permute-start(bf16[2,3,64,128]{3,2,1,0:T(8,128)(2,1)S(1)} %shard_map.60.refs_0_), channel_id=1, source_target_pairs={{0,4},{4,0},{8,12},{12,8},{16,20},{20,16},{24,28},{28,24},{1,5},{5... | collective-permute-start | bytes 294920 | tf_op jit(solution)/shard_map/ppermute | solution.py:170
  6.8 11.3 %collective-permute-start.7 = (bf16[8,4096]{1,0:T(8,128)(2,1)S(1)}, bf16[8,4096]{1,0:T(8,128)(2,1)S(1)}, u32[]{:S(2)}, u32[]{:S(2)}) collective-permute-start(bf16[8,4096]{1,0:T(8,128)(2,1)S(1)} %copy-done), channel_id=1, source_target_pairs={{0,2},{1,3},{2,0},{3,1},{4,6},{5,7},{6,4},{7,5},{8,10},{9,11},{10,... | collective-permute-start | bytes 196616 | tf_op jit(solution)/shard_map/ppermute | solution.py:170
  10.0 2.1 %collective-permute-start.5 = (bf16[1,3,64,128]{3,2,1,0:T(8,128)(2,1)S(1)}, bf16[1,3,64,128]{3,2,1,0:T(8,128)(2,1)S(1)}, u32[]{:S(2)}, u32[]{:S(2)}) collective-permute-start(bf16[1,3,64,128]{3,2,1,0:T(8,128)(2,1)S(1)} %collective-permute-done.2.refs_2_), channel_id=1, source_target_pairs={{0,4},{4,0},{8,12},{12,8},{16,20},{20,16},{24,28},{28,24},{1,5},{5... | collective-permute-start | bytes 147464 | tf_op jit(solution)/shard_map/ppermute | solution.py:170
  10.2 4.2 %collective-permute-start.4 = (bf16[1,3,64,128]{3,2,1,0:T(8,128)(2,1)S(1)}, bf16[1,3,64,128]{3,2,1,0:T(8,128)(2,1)S(1)}, u32[]{:S(2)}, u32[]{:S(2)}) collective-permute-start(bf16[1,3,64,128]{3,2,1,0:T(8,128)(2,1)S(1)} %collective-permute-done.1.refs_1_), channel_id=1, source_target_pairs={{0,4},{4,0},{8,12},{12,8},{16,20},{20,16},{24,28},{28,24},{1,5},{5... | collective-permute-start | bytes 147464 | tf_op jit(solution)/shard_map/ppermute | solution.py:170
  10.5 10.1 %collective-permute-start.6 = (bf16[8,4096]{1,0:T(8,128)(2,1)S(1)}, bf16[8,4096]{1,0:T(8,128)(2,1)S(1)}, u32[]{:S(2)}, u32[]{:S(2)}) collective-permute-start(bf16[8,4096]{1,0:T(8,128)(2,1)S(1)} %copy-done), channel_id=1, source_target_pairs={{0,1},{1,0},{2,3},{3,2},{4,5},{5,4},{6,7},{7,6},{8,9},{9,8},{10,11... | collective-permute-start | bytes 196616 | tf_op jit(solution)/shard_map/ppermute | solution.py:170
  12.1 8.5 %collective-permute-start.8 = (bf16[8,4096]{1,0:T(8,128)(2,1)S(1)}, bf16[8,4096]{1,0:T(8,128)(2,1)S(1)}, u32[]{:S(2)}, u32[]{:S(2)}) collective-permute-start(bf16[8,4096]{1,0:T(8,128)(2,1)S(1)} %copy-done), channel_id=1, source_target_pairs={{0,3},{1,2},{2,1},{3,0},{4,7},{5,6},{6,5},{7,4},{8,11},{9,10},{10,... | collective-permute-start | bytes 196616 | tf_op jit(solution)/shard_map/ppermute | solution.py:170
  16.2 6.9 %collective-permute-start.9 = (bf16[8,4096]{1,0:T(8,128)(2,1)S(1)}, bf16[8,4096]{1,0:T(8,128)(2,1)S(1)}, u32[]{:S(2)}, u32[]{:S(2)}) collective-permute-start(bf16[8,4096]{1,0:T(8,128)(2,1)S(1)} %get-tuple-element.7), channel_id=1, source_target_pairs={{0,3},{1,2},{2,1},{3,0},{4,7},{5,6},{6,5},{7,4},{8,11},{9,10},{10,... | collective-permute-start | bytes 196616 | tf_op jit(solution)/shard_map/ppermute | solution.py:170
  17.7 7.0 %collective-permute-start.10 = (bf16[8,4096]{1,0:T(8,128)(2,1)S(1)}, bf16[8,4096]{1,0:T(8,128)(2,1)S(1)}, u32[]{:S(2)}, u32[]{:S(2)}) collective-permute-start(bf16[8,4096]{1,0:T(8,128)(2,1)S(1)} %get-tuple-element.8), channel_id=1, source_target_pairs={{0,2},{1,3},{2,0},{3,1},{4,6},{5,7},{6,4},{7,5},{8,10},{9,11},{10,... | collective-permute-start | bytes 196616 | tf_op jit(solution)/shard_map/ppermute | solution.py:170
  18.1 6.6 %collective-permute-start.11 = (bf16[8,4096]{1,0:T(8,128)(2,1)S(1)}, bf16[8,4096]{1,0:T(8,128)(2,1)S(1)}, u32[]{:S(2)}, u32[]{:S(2)}) collective-permute-start(bf16[8,4096]{1,0:T(8,128)(2,1)S(1)} %get-tuple-element.9), channel_id=1, source_target_pairs={{0,1},{1,0},{2,3},{3,2},{4,5},{5,4},{6,7},{7,6},{8,9},{9,8},{10,11... | collective-permute-start | bytes 196616 | tf_op jit(solution)/shard_map/ppermute | solution.py:170

commit v7 on v6

v7 whole, which is shorter than its diff:
```python
import functools

import jax
import jax.numpy as jnp
from jax import lax
from jax.experimental import pallas as pl
from jax.experimental.pallas import tpu as pltpu
from jax.sharding import PartitionSpec as P

VMEM = pl.BlockSpec(memory_space=pltpu.VMEM)
HBM = pl.BlockSpec(memory_space=pltpu.HBM)
MIB = 1024 * 1024
BF16, F32, I32 = jnp.bfloat16, jnp.float32, jnp.int32


def pack_kernel(count, row_count, col_count, slots_hbm, values_hbm, packed, slots, values, sems):
    copies = [
        pltpu.make_async_copy(slots_hbm, slots, sems.at[0]),
        pltpu.make_async_copy(values_hbm, values, sems.at[1]),
    ]
    for copy in copies:
        copy.start()
    side = values.shape[2]
    pairs = packed.shape[1]
    copies[0].wait()
    lane = lax.broadcasted_iota(I32, (side, side), 1)
    line = lax.broadcasted_iota(I32, (side, side), 0)
    head = jnp.zeros((side, side), F32)
    for j in range(count):
        p = slots[0, j]
        row = jnp.where(p >= 0, p // col_count, row_count)
        col = jnp.where(p >= 0, p % col_count, col_count)
        here = jnp.where(line == 0, row, col).astype(F32)
        head = jnp.where(lane == j, here, head)
    head = head.astype(BF16)
    copies[1].wait()
    for k in range(pairs):
        left = values[0, k]
        right = values[0, k + pairs] if k + pairs < count else head
        packed[0, k] = jnp.concatenate([left, right], axis=1)


def join_kernel(*refs):
    for i, part in enumerate(refs[:-1]):
        refs[-1][i] = part[0]


def load_ids(gathered, ids_vmem, ids, sem):
    i = 0
    for part in gathered:
        n, pairs = part.shape[:2]
        for d in range(n):
            head = part[d, pairs - 1, 0:16, :].astype(F32).astype(I32)
            ids_vmem[0, i:i + 1, :] = head[0:1]
            ids_vmem[1, i:i + 1, :] = head[1:2]
            i += 1
    copy = pltpu.make_async_copy(ids_vmem, ids, sem)
    copy.start()
    return copy


def over(gathered, body):
    start = 0
    for part in gathered:
        n = part.shape[0]
        if n <= 8:
            for d in range(n):
                body(part, d, start + d)
        else:
            def step(d, carry, part=part, start=start):
                body(part, d, start + d)
                return carry
            lax.fori_loop(0, n, step, 0)
        start += n


def low_half(shape):
    return lax.broadcasted_iota(I32, shape, 1) < shape[1] // 2


def swap_halves(x):
    half = x.shape[1] // 2
    return jnp.concatenate([x[:, half:], x[:, :half]], axis=1)


def twice(x):
    low, y = low_half(x.shape), swap_halves(x)
    return jnp.where(low, x, y), jnp.where(low, y, x)


def diagonal(tile, other=None):
    low = low_half(tile.shape)
    zero = jnp.zeros_like(tile)
    top = jnp.where(low, tile, zero)
    bottom = jnp.where(low, zero, tile if other is None else swap_halves(other))
    return jnp.concatenate([top, bottom], axis=0)


def fold(x):
    return x + pltpu.roll(x, x.shape[1] // 2, 1)


def across(lhs, rhs):
    return lax.dot_general(lhs, rhs, (((1,), (1,)), ((), ())), preferred_element_type=F32)


def load_cotangent(cot, cots):
    col_count = cots.shape[0] - 1
    for c in range(0, col_count, 2):
        width = cots.shape[2]
        cots[c], cots[c + 1] = twice(cot[:, c * width // 2:(c + 2) * width // 2])
    cots[col_count] = jnp.zeros_like(cots[col_count])


def slots_kernel(count, n_parts, n_tensor, *refs):
    gathered, cot, outs = refs[:n_parts], refs[n_parts], refs[n_parts + 1:n_parts + 1 + n_tensor]
    ids_vmem, ids, cots, prod, sem = refs[n_parts + 1 + n_tensor:]
    pairs, side = gathered[0].shape[1:3]
    rows = cot.shape[0]
    share = rows // n_tensor
    copy = load_ids(gathered, ids_vmem, ids, sem)
    load_cotangent(cot, cots)
    low = low_half((rows, 2 * side))
    heads = jnp.concatenate([ids_vmem[0].astype(F32)] * 2, axis=0).astype(BF16)
    where = [(part, d) for part in gathered for d in range(part.shape[0])]
    copy.wait()
    tiles = slot_tiles(len(where), pairs)
    for t, ((i, j), (m, l)) in enumerate(tiles):
        part, d = where[i]
        other, e = where[m]
        blocks = diagonal(part[d, j]) if i == m else diagonal(part[d, j], other[e, l])
        lhs = jnp.where(low, cots[ids[1, i, side + j]], cots[ids[1, m, side + l]])
        prod[t] = across(lhs, blocks)
    me = lax.axis_index("tensor")
    for k in range(n_tensor):
        start = pl.multiple_of(lax.bitwise_xor(me, k) * share, share)
        for t in range(0, len(tiles), 2):
            two = [prod[t, pl.ds(start, share), :], prod[t + 1, pl.ds(start, share), :]]
            outs[k][t * share:(t + 2) * share, :] = jnp.concatenate(two, axis=0).astype(BF16)
        outs[k][len(tiles) * share:, :] = heads


def slot_tiles(n, pairs):
    full = [((i, j), (i, j + pairs)) for i in range(n) for j in range(pairs - 1)]
    return full + [((i, pairs - 1), (i + 1, pairs - 1)) for i in range(0, n, 2)]


def sum_kernel(n_tensor, pairs, n_dp, *refs):
    messages, out = refs[:n_tensor], refs[n_tensor]
    ids_vmem, ids, sem = refs[n_tensor + 1:n_tensor + 4]
    accs = refs[n_tensor + 4:]
    share, width = out.shape
    side = messages[0].shape[1] // 2
    tiles = slot_tiles(n_dp, pairs)
    for m, message in enumerate(messages):
        ids_vmem[m] = message[len(tiles) * share:, :].astype(F32)[:n_dp].astype(I32)
    copy = pltpu.make_async_copy(ids_vmem, ids, sem)
    copy.start()
    for acc in accs:
        acc[...] = jnp.zeros_like(acc)
    low = low_half((share, 2 * side))
    copy.wait()
    for t in range(0, len(tiles), 2):
        for m, (message, acc) in enumerate(zip(messages, accs)):
            two = message[t * share:(t + 2) * share, :].astype(F32)
            for u in range(2):
                value = two[u * share:(u + 1) * share]
                (i, j), (p, l) = tiles[t + u]
                acc[ids[m, i, side + j]] += jnp.where(low, value, 0.0)
                acc[ids[m, p, side + l]] += jnp.where(low, 0.0, value)

    def total(r):
        value = accs[0][r]
        for acc in accs[1:]:
            value = value + acc[r]
        return fold(value)

    for r in range(0, width // side, 2):
        out[:, r * side:(r + 2) * side] = jnp.where(low, total(r), total(r + 1)).astype(BF16)


def rows_kernel(count, n_parts, n_tensor, *refs):
    gathered, cot, outs = refs[:n_parts], refs[n_parts], refs[n_parts + 1:n_parts + 1 + n_tensor]
    ids_vmem, ids, cots, acc, sem = refs[n_parts + 1 + n_tensor:]
    pairs, side = gathered[0].shape[1:3]
    row_count = acc.shape[0] - 1
    rows = cot.shape[0]
    copy = load_ids(gathered, ids_vmem, ids, sem)
    acc[...] = jnp.zeros_like(acc)
    load_cotangent(cot, cots)
    low = low_half((rows, 2 * side))
    copy.wait()

    def add(part, d, i):
        for k in range(pairs):
            left, right = ids[1, i, side + k], ids[1, i, side + k + pairs]
            lhs = cots[left]
            if k + pairs >= count:
                prod = across(lhs[:, :side], part[d, k][:, :side])
                acc[ids[0, i, side + k], :, :side] += prod
            else:
                prod = across(jnp.where(low, lhs, cots[right]), diagonal(part[d, k]))
                acc[ids[0, i, side + k]] += jnp.where(low, prod, 0.0)
                acc[ids[0, i, side + k + pairs]] += jnp.where(low, 0.0, prod)

    over(gathered, add)
    me = lax.axis_index("tensor")
    share = rows // n_tensor
    for k in range(n_tensor):
        start = pl.multiple_of(lax.bitwise_xor(me, k) * share, share)
        half = low_half((share, 2 * side))
        for r in range(0, row_count, 2):
            pair = [fold(acc[r + u, pl.ds(start, share), :]) for u in range(2)]
            outs[k][:, r * side:(r + 2) * side] = jnp.where(half, *pair).astype(BF16)


def forward_kernel(count, n_parts, n_tensor, *refs):
    gathered, tokens = refs[:n_parts], refs[n_parts:n_parts + n_tensor]
    out, ids_vmem, ids, blocks, prod, left_acc, right_acc, stage, sem = refs[n_parts + n_tensor:]
    pairs, side = gathered[0].shape[1:3]
    row_count = blocks.shape[0] - 1
    col_count = left_acc.shape[0] - 1
    rows = blocks.shape[1]
    share = rows // n_tensor
    copy = load_ids(gathered, ids_vmem, ids, sem)
    left_acc[...] = jnp.zeros_like(left_acc)
    right_acc[...] = jnp.zeros_like(right_acc)
    for r in range(0, row_count, 2):
        parts = [tokens[k][:, r * side:(r + 2) * side].astype(F32) for k in range(n_tensor)]
        blocks[r], blocks[r + 1] = twice(jnp.concatenate(parts, axis=0).astype(BF16))
    blocks[row_count] = jnp.zeros_like(blocks[row_count])
    low = low_half((rows, 2 * side))
    copy.wait()

    def multiply(part, d, i):
        for k in range(pairs):
            lhs = blocks[ids[0, i, side + k]]
            if k + pairs < count:
                lhs = jnp.where(low, lhs, blocks[ids[0, i, side + k + pairs]])
                tile = diagonal(part[d, k])
            else:
                lhs, tile = lhs[:, :side], part[d, k]
            prod[i * pairs + k] = jnp.dot(lhs, tile, preferred_element_type=F32)

    def add(part, d, i):
        for k in range(pairs):
            left_acc[ids[1, i, side + k]] += prod[i * pairs + k]
            if k + pairs < count:
                right_acc[ids[1, i, side + k + pairs]] += prod[i * pairs + k]

    over(gathered, multiply)
    over(gathered, add)
    me = lax.axis_index("tensor")
    half = low_half((share, 2 * side))
    for k in range(n_tensor):
        start = pl.multiple_of(lax.bitwise_xor(me, k) * share, share)
        mine = slice(k * share, (k + 1) * share)
        for c in range(0, col_count, 2):
            sums = [fold(jnp.where(half, left_acc[c + u, mine, :], right_acc[c + u, mine, :])) for u in range(2)]
            stage[pl.ds(start, share), c * side:(c + 2) * side] = jnp.where(half, *sums)
    out[...] = stage[...].astype(BF16)


def swap(value, axis, n, k):
    return lax.ppermute(value, axis, [(i, i ^ k) for i in range(n)])


def gather_parts(packed, n_dp):
    if n_dp != 8:
        return [lax.all_gather(packed, "dp", axis=0, tiled=True)]
    near, second, last = [packed, swap(packed, "dp", n_dp, 2)], swap(packed, "dp", n_dp, 4), swap(packed, "dp", n_dp, 6)
    joined = pl.pallas_call(
        join_kernel,
        out_shape=pltpu.VMEM((len(near), *packed.shape[1:]), packed.dtype),
        in_specs=[VMEM] * len(near),
        out_specs=VMEM,
        compiler_params=pltpu.CompilerParams(vmem_limit_bytes=4 * MIB),
    )(*near)
    same_core = [joined, second, last]
    return same_core + [swap(part, "dp", n_dp, 1) for part in same_core]


def on_device(n_dp, n_tensor, inputs, block_values, block_slot, grad_out):
    share, width = inputs.shape
    rows, hidden = grad_out.shape
    _, count, side, _ = block_values.shape
    row_count, col_count = width // side, hidden // side
    pairs = count // 2 + 1
    small = n_dp == 8
    per_slot = small and n_dp * count < row_count and count == 2 * pairs - 1
    params = pltpu.CompilerParams(vmem_limit_bytes=(12 if small else 48) * MIB)

    packed = pl.pallas_call(
        functools.partial(pack_kernel, count, row_count, col_count),
        out_shape=pltpu.VMEM((1, pairs, side, 2 * side), BF16),
        in_specs=[HBM, HBM],
        out_specs=VMEM,
        scratch_shapes=[
            pltpu.SMEM(block_slot.shape, I32),
            pltpu.VMEM(block_values.shape, BF16),
            pltpu.SemaphoreType.DMA((2,)),
        ],
        compiler_params=pltpu.CompilerParams(vmem_limit_bytes=4 * MIB),
    )(
        pltpu.with_memory_space_constraint(block_slot, pltpu.HBM),
        pltpu.with_memory_space_constraint(block_values, pltpu.HBM),
    )
    gathered = gather_parts(packed, n_dp)
    moved = {k: swap(inputs, "tensor", n_tensor, k) for k in range(n_tensor - 1, 0, -1)}
    tokens = [inputs] + [moved[k] for k in range(1, n_tensor)]
    n_parts = len(gathered)
    ids = [pltpu.VMEM((2, n_dp, 2 * side), I32), pltpu.SMEM((2, n_dp, 2 * side), I32)]
    cots = pltpu.VMEM((col_count + 1, rows, 2 * side), BF16)
    tiles = len(slot_tiles(n_dp, pairs))
    if per_slot:
        kernel, shape = slots_kernel, (tiles * share + 2 * n_dp, 2 * side)
        scratch = pltpu.VMEM((tiles, rows, 2 * side), F32)
    else:
        kernel, shape = rows_kernel, (share, width)
        scratch = pltpu.VMEM((row_count + 1, rows, 2 * side), F32)
    partial_sums = pl.pallas_call(
        functools.partial(kernel, count, n_parts, n_tensor),
        out_shape=[jax.ShapeDtypeStruct(shape, BF16)] * n_tensor,
        in_specs=[VMEM] * (n_parts + 1),
        out_specs=[VMEM] * n_tensor,
        scratch_shapes=ids + [cots, scratch, pltpu.SemaphoreType.DMA],
        compiler_params=params,
    )(*gathered, grad_out)
    order = sorted(range(1, n_tensor), key=lambda k: (k != 2, -k))
    received = {k: swap(partial_sums[k], "tensor", n_tensor, k) for k in order}
    arrived = [partial_sums[0]] + [received[k] for k in order]
    outputs = pl.pallas_call(
        functools.partial(forward_kernel, count, n_parts, n_tensor),
        out_shape=jax.ShapeDtypeStruct((rows, hidden), BF16),
        in_specs=[VMEM] * (n_parts + n_tensor),
        out_specs=VMEM,
        scratch_shapes=ids + [
            pltpu.VMEM((row_count + 1, rows, 2 * side), BF16),
            pltpu.VMEM((n_dp * pairs, rows, 2 * side), F32),
            pltpu.VMEM((col_count + 1, rows, 2 * side), F32),
            pltpu.VMEM((col_count + 1, rows, 2 * side), F32),
            pltpu.VMEM((rows, hidden), F32),
            pltpu.SemaphoreType.DMA,
        ],
        compiler_params=params,
    )(*gathered, *tokens)
    if per_slot:
        grad_in = pl.pallas_call(
            functools.partial(sum_kernel, n_tensor, pairs, n_dp),
            out_shape=jax.ShapeDtypeStruct((share, width), BF16),
            in_specs=[VMEM] * n_tensor,
            out_specs=VMEM,
            scratch_shapes=[
                pltpu.VMEM((n_tensor, n_dp, 2 * side), I32),
                pltpu.SMEM((n_tensor, n_dp, 2 * side), I32),
                pltpu.SemaphoreType.DMA,
            ] + [pltpu.VMEM((row_count + 1, share, 2 * side), F32)] * n_tensor,
            compiler_params=params,
        )(*arrived)
    else:
        total = arrived[0].astype(F32)
        for value in arrived[1:]:
            total = total + value.astype(F32)
        grad_in = total.astype(BF16)
    return (outputs, grad_in)


def solution(mesh):
    placed = (
        P(("dp", "tensor"), None),
        P("tensor", "dp", None, None),
        P("tensor", "dp"),
        P("dp", "tensor"),
    )
    return jax.shard_map(
        functools.partial(on_device, mesh.shape["dp"], mesh.shape["tensor"]),
        mesh=mesh,
        in_specs=placed,
        out_specs=(P("dp", "tensor"), P(("dp", "tensor"), None)),
        check_vma=False,
    )
```

time: 25.5 us -> 25.7 us (level)
  waiting for transfers between devices: 2.27 us -> 5.46 us
  starting transfers between devices: 16.6 us -> 13.5 us
  Pallas kernels: 5.07 us -> 5.91 us
  other arithmetic: 0.67 us -> 0 us
    ppermute x12, waiting for transfers between devices: 2.27 us -> 5.46 us  [swap(): return lax.ppermute(value, axis, [(i, i ^ k) for i in range(n)])]
    ppermute x12, starting transfers between devices: 16.6 us -> 13.5 us  [swap(): return lax.ppermute(value, axis, [(i, i ^ k) for i in range(n)])]
    pallas_call x1 -> x2, Pallas kernels: 1.66 us -> 3.08 us  [the longest x1 1.9 us: on_device(): pl.pallas_call(functools.partial(sum_kernel, n_tensor, pairs, n_dp), out_...]
    convert_element_type x1 -> x0, other arithmetic: 0.67 us -> none  [on_device(): return (outputs, total_grad.astype(bf16))]
    pallas_call x1, Pallas kernels: 2.42 us -> 1.84 us  [on_device(): pl.pallas_call(functools.partial(forward_kernel, count, n_parts, n_tensor...]
  transfers between devices with their start and end apart: 12 -> 12, of which waited for: 3 -> 6; matrix products, arithmetic and copies ran while one was open for 0% -> 0% of each run, Pallas kernels for 16% -> 12%
where the time goes in v7:
time: 25.7 us; the launch traced here: 25.6 us
  starting transfers between devices  13.5 us (53%)
  Pallas kernels  5.91 us (23%)
  waiting for transfers between devices  5.46 us (21%)
  between operations  0.7 us (3%)
    ppermute x12, starting transfers between devices, swap(): return lax.ppermute(value, axis, [(i, i ^ k) for i in range(n)])  13.5 us
    ppermute x12, waiting for transfers between devices, swap(): return lax.ppermute(value, axis, [(i, i ^ k) for i in range(n)])  5.46 us
    pallas_call x1, Pallas kernels, on_device(): pl.pallas_call(functools.partial(sum_kernel, n_tensor, pairs, n_dp), out_...  1.9 us
    pallas_call x1, Pallas kernels, on_device(): pl.pallas_call(functools.partial(forward_kernel, count, n_parts, n_tensor...  1.84 us
    pallas_call x1, Pallas kernels, on_device(): pl.pallas_call(functools.partial(kernel, count, n_parts, n_tensor), out_s...  1.19 us
    pallas_call x1, Pallas kernels, on_device(): pl.pallas_call(functools.partial(pack_kernel, count, row_count, col_count...  0.99 us
  transfers between devices with their start and end apart: 12, of which 6 were waited for; matrix products, arithmetic and copies ran while one was open for 0% of the time, Pallas kernels for 12%

profile of v7, /device:TPU:0, one launch (start us, length us, event | category | flops | bytes accessed | tf_op | source)
XLA Modules:
  0.0 25.6 jit_solution(5252750446821918658)
XLA Ops:
  0.6 1.0 %shard_map.59.refs_0_ = bf16[1,3,64,128]{3,2,1,0:T(8,128)(2,1)S(1)} custom-call(s32[1,5]{1,0:T(1,128)} %slots_hbm.1, bf16[1,5,64,64]{3,2,1,0:T(8,128)(2,1)} %values_hbm.1), custom_call_target="tpu_custom_call" | custom-call | tf_op jit(solution)/shard_map/pallas_call | solution.py:293
  1.6 0.0 copy-start
  1.6 0.0 copy-start.1
  1.6 3.0 %collective-permute-start = (bf16[1,3,64,128]{3,2,1,0:T(8,128)(2,1)S(1)}, bf16[1,3,64,128]{3,2,1,0:T(8,128)(2,1)S(1)}, u32[]{:S(2)}, u32[]{:S(2)}) collective-permute-start(bf16[1,3,64,128]{3,2,1,0:T(8,128)(2,1)S(1)} %shard_map.59.refs_0_), channel_id=1, source_target_pairs={{0,8},{4,12},{8,0},{12,4},{16,24},{20,28},{24,16},{28,20},{1,9},{5... | collective-permute-start | bytes 147464 | tf_op jit(solution)/shard_map/ppermute | solution.py:265
  4.7 1.5 %collective-permute-start.2 = (bf16[1,3,64,128]{3,2,1,0:T(8,128)(2,1)S(1)}, bf16[1,3,64,128]{3,2,1,0:T(8,128)(2,1)S(1)}, u32[]{:S(2)}, u32[]{:S(2)}) collective-permute-start(bf16[1,3,64,128]{3,2,1,0:T(8,128)(2,1)S(1)} %shard_map.59.refs_0_), channel_id=1, source_target_pairs={{0,24},{4,28},{8,16},{12,20},{16,8},{20,12},{24,0},{28,4},{1,25},{... | collective-permute-start | bytes 147464 | tf_op jit(solution)/shard_map/ppermute | solution.py:265
  6.1 0.1 collective-permute-start.1
  6.2 0.5 %collective-permute-done.refs_1_ = bf16[1,3,64,128]{3,2,1,0:T(8,128)(2,1)S(1)} collective-permute-done((bf16[1,3,64,128]{3,2,1,0:T(8,128)(2,1)S(1)}, bf16[1,3,64,128]{3,2,1,0:T(8,128)(2,1)S(1)}, u32[]{:S(2)}, u32[]{:S(2)}) %collective-permute-start) | collective-permute-done | bytes 49184 | tf_op jit(solution)/shard_map/ppermute | solution.py:265
  6.7 0.1 collective-permute-start.3
  6.8 2.8 %collective-permute-done.2.refs_2_ = bf16[1,3,64,128]{3,2,1,0:T(8,128)(2,1)S(1)} collective-permute-done((bf16[1,3,64,128]{3,2,1,0:T(8,128)(2,1)S(1)}, bf16[1,3,64,128]{3,2,1,0:T(8,128)(2,1)S(1)}, u32[]{:S(2)}, u32[]{:S(2)}) %collective-permute-start.2) | collective-permute-done | bytes 49184 | tf_op jit(solution)/shard_map/ppermute | solution.py:265
  9.6 0.0 collective-permute-start.5
  9.6 0.0 copy-done
  9.6 2.6 %collective-permute-start.7 = (bf16[8,4096]{1,0:T(8,128)(2,1)S(1)}, bf16[8,4096]{1,0:T(8,128)(2,1)S(1)}, u32[]{:S(2)}, u32[]{:S(2)}) collective-permute-start(bf16[8,4096]{1,0:T(8,128)(2,1)S(1)} %copy-done), channel_id=1, source_target_pairs={{0,2},{1,3},{2,0},{3,1},{4,6},{5,7},{6,4},{7,5},{8,10},{9,11},{10,... | collective-permute-start | bytes 196616 | tf_op jit(solution)/shard_map/ppermute | solution.py:265
  12.2 0.0 collective-permute-done.1.refs_1_
  12.2 0.2 collective-permute-start.4
  12.5 1.6 %collective-permute-start.6 = (bf16[8,4096]{1,0:T(8,128)(2,1)S(1)}, bf16[8,4096]{1,0:T(8,128)(2,1)S(1)}, u32[]{:S(2)}, u32[]{:S(2)}) collective-permute-start(bf16[8,4096]{1,0:T(8,128)(2,1)S(1)} %copy-done), channel_id=1, source_target_pairs={{0,1},{1,0},{2,3},{3,2},{4,5},{5,4},{6,7},{7,6},{8,9},{9,8},{10,11... | collective-permute-start | bytes 196616 | tf_op jit(solution)/shard_map/ppermute | solution.py:265
  14.0 0.0 collective-permute-done.5.refs_5_
  14.0 0.4 %collective-permute-start.8 = (bf16[8,4096]{1,0:T(8,128)(2,1)S(1)}, bf16[8,4096]{1,0:T(8,128)(2,1)S(1)}, u32[]{:S(2)}, u32[]{:S(2)}) collective-permute-start(bf16[8,4096]{1,0:T(8,128)(2,1)S(1)} %copy-done), channel_id=1, source_target_pairs={{0,3},{1,2},{2,1},{3,0},{4,7},{5,6},{6,5},{7,4},{8,11},{9,10},{10,... | collective-permute-start | bytes 196616 | tf_op jit(solution)/shard_map/ppermute | solution.py:265
  14.5 0.0 collective-permute-done.4.refs_4_
  14.5 0.0 collective-permute-done.3.refs_3_
  14.5 0.0 copy-done.1
  14.5 1.2 %shard_map.62 = (bf16[176,128]{1,0:T(8,128)(2,1)S(1)}, bf16[176,128]{1,0:T(8,128)(2,1)S(1)}, bf16[176,128]{1,0:T(8,128)(2,1)S(1)}, bf16[176,128]{1,0:T(8,128)(2,1)S(1)}) custom-call(bf16[2,3,64,128]{3,2,1,0:T(8,128)(2,1)S(1)} %shard_map.60.refs_0_, bf16[1,3,64,128]{3,2,1,0:T(8,128)(2,1)S(1)} %collective-permute-done.1.refs_1_, ...), custom_call_target="tpu_custom_call" | custom-call | tf_op jit(solution)/shard_map/pallas_call | solution.py:321
  15.7 1.6 %collective-permute-start.9 = (bf16[176,128]{1,0:T(8,128)(2,1)S(1)}, bf16[176,128]{1,0:T(8,128)(2,1)S(1)}, u32[]{:S(2)}, u32[]{:S(2)}) collective-permute-start(bf16[176,128]{1,0:T(8,128)(2,1)S(1)} %get-tuple-element.7), channel_id=1, source_target_pairs={{0,2},{1,3},{2,0},{3,1},{4,6},{5,7},{6,4},{7,5},{8,10},{9,11},{10,... | collective-permute-start | bytes 135176 | tf_op jit(solution)/shard_map/ppermute | solution.py:265
  17.2 2.0 %collective-permute-start.10 = (bf16[176,128]{1,0:T(8,128)(2,1)S(1)}, bf16[176,128]{1,0:T(8,128)(2,1)S(1)}, u32[]{:S(2)}, u32[]{:S(2)}) collective-permute-start(bf16[176,128]{1,0:T(8,128)(2,1)S(1)} %get-tuple-element.8), channel_id=1, source_target_pairs={{0,3},{1,2},{2,1},{3,0},{4,7},{5,6},{6,5},{7,4},{8,11},{9,10},{10,... | collective-permute-start | bytes 135176 | tf_op jit(solution)/shard_map/ppermute | solution.py:265
  19.2 0.0 collective-permute-done.7.refs_8_
  19.2 0.5 %collective-permute-start.11 = (bf16[176,128]{1,0:T(8,128)(2,1)S(1)}, bf16[176,128]{1,0:T(8,128)(2,1)S(1)}, u32[]{:S(2)}, u32[]{:S(2)}) collective-permute-start(bf16[176,128]{1,0:T(8,128)(2,1)S(1)} %get-tuple-element.9), channel_id=1, source_target_pairs={{0,1},{1,0},{2,3},{3,2},{4,5},{5,4},{6,7},{7,6},{8,9},{9,8},{10,11... | collective-permute-start | bytes 135176 | tf_op jit(solution)/shard_map/ppermute | solution.py:265
  19.7 0.0 collective-permute-done.6.refs_7_
  19.7 0.8 %collective-permute-done.8.refs_9_ = bf16[8,4096]{1,0:T(8,128)(2,1)S(1)} collective-permute-done((bf16[8,4096]{1,0:T(8,128)(2,1)S(1)}, bf16[8,4096]{1,0:T(8,128)(2,1)S(1)}, u32[]{:S(2)}, u32[]{:S(2)}) %collective-permute-start.8) | collective-permute-done | bytes 65568 | tf_op jit(solution)/shard_map/ppermute | solution.py:265
  20.5 1.8 %shard_map.61 = bf16[32,896]{1,0:T(8,128)(2,1)} custom-call(bf16[2,3,64,128]{3,2,1,0:T(8,128)(2,1)S(1)} %shard_map.60.refs_0_, bf16[1,3,64,128]{3,2,1,0:T(8,128)(2,1)S(1)} %collective-permute-done.1.refs_1_, bf16[1,3,64,128]{3,2,1,0:T(8,128)(2,1)S(1)} %collective-permute-done.2.refs_2_, bf16[2,3,64,128]{3,2,1,0:T(8,128)(2,1)S(1)} %collective-permute-done.3.refs_3_, ...), custom_call_target="tpu_custom_call" | custom-call | tf_op jit(solution)/shard_map/pallas_call | solution.py:332
  22.3 0.2 collective-permute-done.9.refs_1_
  22.5 0.9 %collective-permute-done.10.refs_2_ = bf16[176,128]{1,0:T(8,128)(2,1)S(1)} collective-permute-done((bf16[176,128]{1,0:T(8,128)(2,1)S(1)}, bf16[176,128]{1,0:T(8,128)(2,1)S(1)}, u32[]{:S(2)}, u32[]{:S(2)}) %collective-permute-start.10) | collective-permute-done | bytes 45088 | tf_op jit(solution)/shard_map/ppermute | solution.py:265
  23.5 0.2 collective-permute-done.11.refs_3_
  23.7 1.9 %shard_map.63 = bf16[8,4096]{1,0:T(8,128)(2,1)} custom-call(bf16[176,128]{1,0:T(8,128)(2,1)S(1)} %get-tuple-element.6.refs_0_, bf16[176,128]{1,0:T(8,128)(2,1)S(1)} %collective-permute-done.9.refs_1_, bf16[176,128]{1,0:T(8,128)(2,1)S(1)} %collective-permute-done.10.refs_2_, bf16[176,128]{1,0:T(8,128)(2,1)S(1)} %collective-permute-done.11.refs_3_), custom_call_target="tpu_custom_call" | custom-call | tf_op jit(solution)/shard_map/pallas_call | solution.py:348
  (1 shorter events, 0.0 us)
Async XLA Ops:
  1.6 8.0 %copy-start = (bf16[8,4096]{1,0:T(8,128)(2,1)S(1)}, bf16[8,4096]{1,0:T(8,128)(2,1)}, u32[]{:S(2)}) copy-start(bf16[8,4096]{1,0:T(8,128)(2,1)} %refs_6_.2) | copy-start | bytes 196612
  1.6 12.8 %copy-start.1 = (bf16[32,896]{1,0:T(8,128)(2,1)S(1)}, bf16[32,896]{1,0:T(8,128)(2,1)}, u32[]{:S(2)}) copy-start(bf16[32,896]{1,0:T(8,128)(2,1)} %refs_6_.3) | copy-start | bytes 172036
  1.6 5.1 %collective-permute-start = (bf16[1,3,64,128]{3,2,1,0:T(8,128)(2,1)S(1)}, bf16[1,3,64,128]{3,2,1,0:T(8,128)(2,1)S(1)}, u32[]{:S(2)}, u32[]{:S(2)}) collective-permute-start(bf16[1,3,64,128]{3,2,1,0:T(8,128)(2,1)S(1)} %shard_map.59.refs_0_), channel_id=1, source_target_pairs={{0,8},{4,12},{8,0},{12,4},{16,24},{20,28},{24,16},{28,20},{1,9},{5... | collective-permute-start | bytes 147464 | tf_op jit(solution)/shard_map/ppermute | solution.py:265
  4.7 5.0 %collective-permute-start.2 = (bf16[1,3,64,128]{3,2,1,0:T(8,128)(2,1)S(1)}, bf16[1,3,64,128]{3,2,1,0:T(8,128)(2,1)S(1)}, u32[]{:S(2)}, u32[]{:S(2)}) collective-permute-start(bf16[1,3,64,128]{3,2,1,0:T(8,128)(2,1)S(1)} %shard_map.59.refs_0_), channel_id=1, source_target_pairs={{0,24},{4,28},{8,16},{12,20},{16,8},{20,12},{24,0},{28,4},{1,25},{... | collective-permute-start | bytes 147464 | tf_op jit(solution)/shard_map/ppermute | solution.py:265
  6.1 6.1 %collective-permute-start.1 = (bf16[1,3,64,128]{3,2,1,0:T(8,128)(2,1)S(1)}, bf16[1,3,64,128]{3,2,1,0:T(8,128)(2,1)S(1)}, u32[]{:S(2)}, u32[]{:S(2)}) collective-permute-start(bf16[1,3,64,128]{3,2,1,0:T(8,128)(2,1)S(1)} %shard_map.59.refs_0_), channel_id=1, source_target_pairs={{0,16},{4,20},{8,24},{12,28},{16,0},{20,4},{24,8},{28,12},{1,17},{... | collective-permute-start | bytes 147464 | tf_op jit(solution)/shard_map/ppermute | solution.py:265
  6.7 7.7 %collective-permute-start.3 = (bf16[2,3,64,128]{3,2,1,0:T(8,128)(2,1)S(1)}, bf16[2,3,64,128]{3,2,1,0:T(8,128)(2,1)S(1)}, u32[]{:S(2)}, u32[]{:S(2)}) collective-permute-start(bf16[2,3,64,128]{3,2,1,0:T(8,128)(2,1)S(1)} %shard_map.60.refs_0_), channel_id=1, source_target_pairs={{0,4},{4,0},{8,12},{12,8},{16,20},{20,16},{24,28},{28,24},{1,5},{5... | collective-permute-start | bytes 294920 | tf_op jit(solution)/shard_map/ppermute | solution.py:265
  9.6 4.4 %collective-permute-start.5 = (bf16[1,3,64,128]{3,2,1,0:T(8,128)(2,1)S(1)}, bf16[1,3,64,128]{3,2,1,0:T(8,128)(2,1)S(1)}, u32[]{:S(2)}, u32[]{:S(2)}) collective-permute-start(bf16[1,3,64,128]{3,2,1,0:T(8,128)(2,1)S(1)} %collective-permute-done.2.refs_2_), channel_id=1, source_target_pairs={{0,4},{4,0},{8,12},{12,8},{16,20},{20,16},{24,28},{28,24},{1,5},{5... | collective-permute-start | bytes 147464 | tf_op jit(solution)/shard_map/ppermute | solution.py:265
  9.6 9.6 %collective-permute-start.7 = (bf16[8,4096]{1,0:T(8,128)(2,1)S(1)}, bf16[8,4096]{1,0:T(8,128)(2,1)S(1)}, u32[]{:S(2)}, u32[]{:S(2)}) collective-permute-start(bf16[8,4096]{1,0:T(8,128)(2,1)S(1)} %copy-done), channel_id=1, source_target_pairs={{0,2},{1,3},{2,0},{3,1},{4,6},{5,7},{6,4},{7,5},{8,10},{9,11},{10,... | collective-permute-start | bytes 196616 | tf_op jit(solution)/shard_map/ppermute | solution.py:265
  12.2 2.2 %collective-permute-start.4 = (bf16[1,3,64,128]{3,2,1,0:T(8,128)(2,1)S(1)}, bf16[1,3,64,128]{3,2,1,0:T(8,128)(2,1)S(1)}, u32[]{:S(2)}, u32[]{:S(2)}) collective-permute-start(bf16[1,3,64,128]{3,2,1,0:T(8,128)(2,1)S(1)} %collective-permute-done.1.refs_1_), channel_id=1, source_target_pairs={{0,4},{4,0},{8,12},{12,8},{16,20},{20,16},{24,28},{28,24},{1,5},{5... | collective-permute-start | bytes 147464 | tf_op jit(solution)/shard_map/ppermute | solution.py:265
  12.5 7.3 %collective-permute-start.6 = (bf16[8,4096]{1,0:T(8,128)(2,1)S(1)}, bf16[8,4096]{1,0:T(8,128)(2,1)S(1)}, u32[]{:S(2)}, u32[]{:S(2)}) collective-permute-start(bf16[8,4096]{1,0:T(8,128)(2,1)S(1)} %copy-done), channel_id=1, source_target_pairs={{0,1},{1,0},{2,3},{3,2},{4,5},{5,4},{6,7},{7,6},{8,9},{9,8},{10,11... | collective-permute-start | bytes 196616 | tf_op jit(solution)/shard_map/ppermute | solution.py:265
  14.0 6.5 %collective-permute-start.8 = (bf16[8,4096]{1,0:T(8,128)(2,1)S(1)}, bf16[8,4096]{1,0:T(8,128)(2,1)S(1)}, u32[]{:S(2)}, u32[]{:S(2)}) collective-permute-start(bf16[8,4096]{1,0:T(8,128)(2,1)S(1)} %copy-done), channel_id=1, source_target_pairs={{0,3},{1,2},{2,1},{3,0},{4,7},{5,6},{6,5},{7,4},{8,11},{9,10},{10,... | collective-permute-start | bytes 196616 | tf_op jit(solution)/shard_map/ppermute | solution.py:265
  15.7 6.8 %collective-permute-start.9 = (bf16[176,128]{1,0:T(8,128)(2,1)S(1)}, bf16[176,128]{1,0:T(8,128)(2,1)S(1)}, u32[]{:S(2)}, u32[]{:S(2)}) collective-permute-start(bf16[176,128]{1,0:T(8,128)(2,1)S(1)} %get-tuple-element.7), channel_id=1, source_target_pairs={{0,2},{1,3},{2,0},{3,1},{4,6},{5,7},{6,4},{7,5},{8,10},{9,11},{10,... | collective-permute-start | bytes 135176 | tf_op jit(solution)/shard_map/ppermute | solution.py:265
  17.2 6.2 %collective-permute-start.10 = (bf16[176,128]{1,0:T(8,128)(2,1)S(1)}, bf16[176,128]{1,0:T(8,128)(2,1)S(1)}, u32[]{:S(2)}, u32[]{:S(2)}) collective-permute-start(bf16[176,128]{1,0:T(8,128)(2,1)S(1)} %get-tuple-element.8), channel_id=1, source_target_pairs={{0,3},{1,2},{2,1},{3,0},{4,7},{5,6},{6,5},{7,4},{8,11},{9,10},{10,... | collective-permute-start | bytes 135176 | tf_op jit(solution)/shard_map/ppermute | solution.py:265
  19.2 4.4 %collective-permute-start.11 = (bf16[176,128]{1,0:T(8,128)(2,1)S(1)}, bf16[176,128]{1,0:T(8,128)(2,1)S(1)}, u32[]{:S(2)}, u32[]{:S(2)}) collective-permute-start(bf16[176,128]{1,0:T(8,128)(2,1)S(1)} %get-tuple-element.9), channel_id=1, source_target_pairs={{0,1},{1,0},{2,3},{3,2},{4,5},{5,4},{6,7},{7,6},{8,9},{9,8},{10,11... | collective-permute-start | bytes 135176 | tf_op jit(solution)/shard_map/ppermute | solution.py:265

commit v8 on v7

--- a/solution.py
+++ b/solution.py
@@ -161,13 +161,15 @@
     low = low_half((share, 2 * side))
     copy.wait()
     for t in range(0, len(tiles), 2):
-        for m, (message, acc) in enumerate(zip(messages, accs)):
-            two = message[t * share:(t + 2) * share, :].astype(F32)
-            for u in range(2):
-                value = two[u * share:(u + 1) * share]
-                (i, j), (p, l) = tiles[t + u]
-                acc[ids[m, i, side + j]] += jnp.where(low, value, 0.0)
-                acc[ids[m, p, side + l]] += jnp.where(low, 0.0, value)
+        both = [message[t * share:(t + 2) * share, :].astype(F32) for message in messages]
+        for u in range(2):
+            values = [two[u * share:(u + 1) * share] for two in both]
+            for h, (i, j) in enumerate(tiles[t + u]):
+                rows = [ids[m, i, side + j] for m in range(n_tensor)]
+                halves = [jnp.where(low, 0.0, value) if h else jnp.where(low, value, 0.0) for value in values]
+                sums = [acc[row] + half for acc, row, half in zip(accs, rows, halves)]
+                for acc, row, value in zip(accs, rows, sums):
+                    acc[row] = value
 
     def total(r):
         value = accs[0][r]
@@ -244,9 +246,13 @@
 
     def add(part, d, i):
         for k in range(pairs):
-            left_acc[ids[1, i, side + k]] += prod[i * pairs + k]
+            value, left = prod[i * pairs + k], ids[1, i, side + k]
+            left_sum = left_acc[left] + value
             if k + pairs < count:
-                right_acc[ids[1, i, side + k + pairs]] += prod[i * pairs + k]
+                right = ids[1, i, side + k + pairs]
+                right_sum = right_acc[right] + value
+                right_acc[right] = right_sum
+            left_acc[left] = left_sum
 
     over(gathered, multiply)
     over(gathered, add)
@@ -306,8 +312,9 @@
         pltpu.with_memory_space_constraint(block_values, pltpu.HBM),
     )
     gathered = gather_parts(packed, n_dp)
-    moved = {k: swap(inputs, "tensor", n_tensor, k) for k in range(n_tensor - 1, 0, -1)}
-    tokens = [inputs] + [moved[k] for k in range(1, n_tensor)]
+    tokens = [inputs]
+    while len(tokens) < n_tensor:
+        tokens = tokens + [swap(value, "tensor", n_tensor, len(tokens)) for value in tokens]
     n_parts = len(gathered)
     ids = [pltpu.VMEM((2, n_dp, 2 * side), I32), pltpu.SMEM((2, n_dp, 2 * side), I32)]
     cots = pltpu.VMEM((col_count + 1, rows, 2 * side), BF16)

time: 25.7 us -> 25.8 us (level)
  starting transfers between devices: 13.5 us -> 15 us
  waiting for transfers between devices: 5.46 us -> 3.97 us
    ppermute x12, starting transfers between devices: 13.5 us -> 15 us  [swap(): return lax.ppermute(value, axis, [(i, i ^ k) for i in range(n)])]
    ppermute x12, waiting for transfers between devices: 5.46 us -> 3.97 us  [swap(): return lax.ppermute(value, axis, [(i, i ^ k) for i in range(n)])]
  transfers between devices with their start and end apart: 12 -> 12, of which waited for: 6 -> 7; matrix products, arithmetic and copies ran while one was open for 0% -> 0% of each run, Pallas kernels for 12% -> 12%
where the time goes in v8:
time: 25.8 us; the launch traced here: 25.6 us
  starting transfers between devices  15 us (58%)
  Pallas kernels  5.9 us (23%)
  waiting for transfers between devices  3.97 us (15%)
  between operations  0.71 us (3%)
    ppermute x12, starting transfers between devices, swap(): return lax.ppermute(value, axis, [(i, i ^ k) for i in range(n)])  15 us
    ppermute x12, waiting for transfers between devices, swap(): return lax.ppermute(value, axis, [(i, i ^ k) for i in range(n)])  3.97 us
    pallas_call x1, Pallas kernels, on_device(): pl.pallas_call(functools.partial(sum_kernel, n_tensor, pairs, n_dp), out_...  1.89 us
    pallas_call x1, Pallas kernels, on_device(): pl.pallas_call(functools.partial(forward_kernel, count, n_parts, n_tensor...  1.84 us
    pallas_call x1, Pallas kernels, on_device(): pl.pallas_call(functools.partial(kernel, count, n_parts, n_tensor), out_s...  1.19 us
    pallas_call x1, Pallas kernels, on_device(): pl.pallas_call(functools.partial(pack_kernel, count, row_count, col_count...  0.99 us
  transfers between devices with their start and end apart: 12, of which 7 were waited for; matrix products, arithmetic and copies ran while one was open for 0% of the time, Pallas kernels for 12%

profile of v8, /device:TPU:0, one launch (start us, length us, event | category | flops | bytes accessed | tf_op | source)
XLA Modules:
  0.0 25.6 jit_solution(14653630858138442827)
XLA Ops:
  0.6 1.0 %shard_map.59.refs_0_ = bf16[1,3,64,128]{3,2,1,0:T(8,128)(2,1)S(1)} custom-call(s32[1,5]{1,0:T(1,128)} %slots_hbm.1, bf16[1,5,64,64]{3,2,1,0:T(8,128)(2,1)} %values_hbm.1), custom_call_target="tpu_custom_call" | custom-call | tf_op jit(solution)/shard_map/pallas_call | solution.py:299
  1.6 0.0 copy-start
  1.6 0.0 copy-start.1
  1.6 3.0 %collective-permute-start = (bf16[1,3,64,128]{3,2,1,0:T(8,128)(2,1)S(1)}, bf16[1,3,64,128]{3,2,1,0:T(8,128)(2,1)S(1)}, u32[]{:S(2)}, u32[]{:S(2)}) collective-permute-start(bf16[1,3,64,128]{3,2,1,0:T(8,128)(2,1)S(1)} %shard_map.59.refs_0_), channel_id=1, source_target_pairs={{0,8},{4,12},{8,0},{12,4},{16,24},{20,28},{24,16},{28,20},{1,9},{5... | collective-permute-start | bytes 147464 | tf_op jit(solution)/shard_map/ppermute | solution.py:271
  4.7 1.5 %collective-permute-start.2 = (bf16[1,3,64,128]{3,2,1,0:T(8,128)(2,1)S(1)}, bf16[1,3,64,128]{3,2,1,0:T(8,128)(2,1)S(1)}, u32[]{:S(2)}, u32[]{:S(2)}) collective-permute-start(bf16[1,3,64,128]{3,2,1,0:T(8,128)(2,1)S(1)} %shard_map.59.refs_0_), channel_id=1, source_target_pairs={{0,24},{4,28},{8,16},{12,20},{16,8},{20,12},{24,0},{28,4},{1,25},{... | collective-permute-start | bytes 147464 | tf_op jit(solution)/shard_map/ppermute | solution.py:271
  6.1 0.1 collective-permute-start.1
  6.2 0.5 %collective-permute-done.refs_1_ = bf16[1,3,64,128]{3,2,1,0:T(8,128)(2,1)S(1)} collective-permute-done((bf16[1,3,64,128]{3,2,1,0:T(8,128)(2,1)S(1)}, bf16[1,3,64,128]{3,2,1,0:T(8,128)(2,1)S(1)}, u32[]{:S(2)}, u32[]{:S(2)}) %collective-permute-start) | collective-permute-done | bytes 49184 | tf_op jit(solution)/shard_map/ppermute | solution.py:271
  6.7 0.1 collective-permute-start.3
  6.8 0.0 copy-done
  6.8 2.2 %collective-permute-start.6 = (bf16[8,4096]{1,0:T(8,128)(2,1)S(1)}, bf16[8,4096]{1,0:T(8,128)(2,1)S(1)}, u32[]{:S(2)}, u32[]{:S(2)}) collective-permute-start(bf16[8,4096]{1,0:T(8,128)(2,1)S(1)} %copy-done), channel_id=1, source_target_pairs={{0,1},{1,0},{2,3},{3,2},{4,5},{5,4},{6,7},{7,6},{8,9},{9,8},{10,11... | collective-permute-start | bytes 196616 | tf_op jit(solution)/shard_map/ppermute | solution.py:271
  9.0 0.6 %collective-permute-done.2.refs_2_ = bf16[1,3,64,128]{3,2,1,0:T(8,128)(2,1)S(1)} collective-permute-done((bf16[1,3,64,128]{3,2,1,0:T(8,128)(2,1)S(1)}, bf16[1,3,64,128]{3,2,1,0:T(8,128)(2,1)S(1)}, u32[]{:S(2)}, u32[]{:S(2)}) %collective-permute-start.2) | collective-permute-done | bytes 49184 | tf_op jit(solution)/shard_map/ppermute | solution.py:271
  9.6 0.0 collective-permute-start.5
  9.6 0.6 %collective-permute-done.1.refs_1_ = bf16[1,3,64,128]{3,2,1,0:T(8,128)(2,1)S(1)} collective-permute-done((bf16[1,3,64,128]{3,2,1,0:T(8,128)(2,1)S(1)}, bf16[1,3,64,128]{3,2,1,0:T(8,128)(2,1)S(1)}, u32[]{:S(2)}, u32[]{:S(2)}) %collective-permute-start.1) | collective-permute-done | bytes 49184 | tf_op jit(solution)/shard_map/ppermute | solution.py:271
  10.2 0.0 collective-permute-start.4
  10.2 2.6 %collective-permute-start.7 = (bf16[8,4096]{1,0:T(8,128)(2,1)S(1)}, bf16[8,4096]{1,0:T(8,128)(2,1)S(1)}, u32[]{:S(2)}, u32[]{:S(2)}) collective-permute-start(bf16[8,4096]{1,0:T(8,128)(2,1)S(1)} %copy-done), channel_id=1, source_target_pairs={{0,2},{1,3},{2,0},{3,1},{4,6},{5,7},{6,4},{7,5},{8,10},{9,11},{10,... | collective-permute-start | bytes 196616 | tf_op jit(solution)/shard_map/ppermute | solution.py:271
  12.8 0.0 collective-permute-done.6.refs_7_
  12.8 1.6 %collective-permute-start.8 = (bf16[8,4096]{1,0:T(8,128)(2,1)S(1)}, bf16[8,4096]{1,0:T(8,128)(2,1)S(1)}, u32[]{:S(2)}, u32[]{:S(2)}) collective-permute-start(bf16[8,4096]{1,0:T(8,128)(2,1)S(1)} %collective-permute-done.6.refs_7_), channel_id=1, source_target_pairs={{0,2},{1,3},{2,0},{3,1},{4,6},{5,7},{6,4},{7,5},{8,10},{9,11},{10,... | collective-permute-start | bytes 196616 | tf_op jit(solution)/shard_map/ppermute | solution.py:271
  14.4 0.0 collective-permute-done.5.refs_5_
  14.4 0.0 collective-permute-done.4.refs_4_
  14.4 0.0 collective-permute-done.3.refs_3_
  14.5 0.0 copy-done.1
  14.5 1.2 %shard_map.62 = (bf16[176,128]{1,0:T(8,128)(2,1)S(1)}, bf16[176,128]{1,0:T(8,128)(2,1)S(1)}, bf16[176,128]{1,0:T(8,128)(2,1)S(1)}, bf16[176,128]{1,0:T(8,128)(2,1)S(1)}) custom-call(bf16[2,3,64,128]{3,2,1,0:T(8,128)(2,1)S(1)} %shard_map.60.refs_0_, bf16[1,3,64,128]{3,2,1,0:T(8,128)(2,1)S(1)} %collective-permute-done.1.refs_1_, ...), custom_call_target="tpu_custom_call" | custom-call | tf_op jit(solution)/shard_map/pallas_call | solution.py:328
  15.7 1.4 %collective-permute-start.9 = (bf16[176,128]{1,0:T(8,128)(2,1)S(1)}, bf16[176,128]{1,0:T(8,128)(2,1)S(1)}, u32[]{:S(2)}, u32[]{:S(2)}) collective-permute-start(bf16[176,128]{1,0:T(8,128)(2,1)S(1)} %get-tuple-element.7), channel_id=1, source_target_pairs={{0,2},{1,3},{2,0},{3,1},{4,6},{5,7},{6,4},{7,5},{8,10},{9,11},{10,... | collective-permute-start | bytes 135176 | tf_op jit(solution)/shard_map/ppermute | solution.py:271
  17.0 2.6 %collective-permute-start.10 = (bf16[176,128]{1,0:T(8,128)(2,1)S(1)}, bf16[176,128]{1,0:T(8,128)(2,1)S(1)}, u32[]{:S(2)}, u32[]{:S(2)}) collective-permute-start(bf16[176,128]{1,0:T(8,128)(2,1)S(1)} %get-tuple-element.8), channel_id=1, source_target_pairs={{0,3},{1,2},{2,1},{3,0},{4,7},{5,6},{6,5},{7,4},{8,11},{9,10},{10,... | collective-permute-start | bytes 135176 | tf_op jit(solution)/shard_map/ppermute | solution.py:271
  19.7 0.0 collective-permute-start.11
  19.7 0.0 collective-permute-done.7.refs_8_
  19.7 0.9 %collective-permute-done.8.refs_9_ = bf16[8,4096]{1,0:T(8,128)(2,1)S(1)} collective-permute-done((bf16[8,4096]{1,0:T(8,128)(2,1)S(1)}, bf16[8,4096]{1,0:T(8,128)(2,1)S(1)}, u32[]{:S(2)}, u32[]{:S(2)}) %collective-permute-start.8) | collective-permute-done | bytes 65568 | tf_op jit(solution)/shard_map/ppermute | solution.py:271
  20.6 1.8 %shard_map.61 = bf16[32,896]{1,0:T(8,128)(2,1)} custom-call(bf16[2,3,64,128]{3,2,1,0:T(8,128)(2,1)S(1)} %shard_map.60.refs_0_, bf16[1,3,64,128]{3,2,1,0:T(8,128)(2,1)S(1)} %collective-permute-done.1.refs_1_, bf16[1,3,64,128]{3,2,1,0:T(8,128)(2,1)S(1)} %collective-permute-done.2.refs_2_, bf16[2,3,64,128]{3,2,1,0:T(8,128)(2,1)S(1)} %collective-permute-done.3.refs_3_, ...), custom_call_target="tpu_custom_call" | custom-call | tf_op jit(solution)/shard_map/pallas_call | solution.py:339
  22.4 0.2 collective-permute-done.9.refs_1_
  22.6 0.5 %collective-permute-done.10.refs_2_ = bf16[176,128]{1,0:T(8,128)(2,1)S(1)} collective-permute-done((bf16[176,128]{1,0:T(8,128)(2,1)S(1)}, bf16[176,128]{1,0:T(8,128)(2,1)S(1)}, u32[]{:S(2)}, u32[]{:S(2)}) %collective-permute-start.10) | collective-permute-done | bytes 45088 | tf_op jit(solution)/shard_map/ppermute | solution.py:271
  23.1 0.6 %collective-permute-done.11.refs_3_ = bf16[176,128]{1,0:T(8,128)(2,1)S(1)} collective-permute-done((bf16[176,128]{1,0:T(8,128)(2,1)S(1)}, bf16[176,128]{1,0:T(8,128)(2,1)S(1)}, u32[]{:S(2)}, u32[]{:S(2)}) %collective-permute-start.11) | collective-permute-done | bytes 45088 | tf_op jit(solution)/shard_map/ppermute | solution.py:271
  23.7 1.9 %shard_map.63 = bf16[8,4096]{1,0:T(8,128)(2,1)} custom-call(bf16[176,128]{1,0:T(8,128)(2,1)S(1)} %get-tuple-element.6.refs_0_, bf16[176,128]{1,0:T(8,128)(2,1)S(1)} %collective-permute-done.9.refs_1_, bf16[176,128]{1,0:T(8,128)(2,1)S(1)} %collective-permute-done.10.refs_2_, bf16[176,128]{1,0:T(8,128)(2,1)S(1)} %collective-permute-done.11.refs_3_), custom_call_target="tpu_custom_call" | custom-call | tf_op jit(solution)/shard_map/pallas_call | solution.py:355
  (1 shorter events, 0.0 us)
Async XLA Ops:
  1.6 5.2 %copy-start = (bf16[8,4096]{1,0:T(8,128)(2,1)S(1)}, bf16[8,4096]{1,0:T(8,128)(2,1)}, u32[]{:S(2)}) copy-start(bf16[8,4096]{1,0:T(8,128)(2,1)} %refs_6_.2) | copy-start | bytes 196612
  1.6 12.8 %copy-start.1 = (bf16[32,896]{1,0:T(8,128)(2,1)S(1)}, bf16[32,896]{1,0:T(8,128)(2,1)}, u32[]{:S(2)}) copy-start(bf16[32,896]{1,0:T(8,128)(2,1)} %refs_6_.3) | copy-start | bytes 172036
  1.6 5.1 %collective-permute-start = (bf16[1,3,64,128]{3,2,1,0:T(8,128)(2,1)S(1)}, bf16[1,3,64,128]{3,2,1,0:T(8,128)(2,1)S(1)}, u32[]{:S(2)}, u32[]{:S(2)}) collective-permute-start(bf16[1,3,64,128]{3,2,1,0:T(8,128)(2,1)S(1)} %shard_map.59.refs_0_), channel_id=1, source_target_pairs={{0,8},{4,12},{8,0},{12,4},{16,24},{20,28},{24,16},{28,20},{1,9},{5... | collective-permute-start | bytes 147464 | tf_op jit(solution)/shard_map/ppermute | solution.py:271
  4.7 5.0 %collective-permute-start.2 = (bf16[1,3,64,128]{3,2,1,0:T(8,128)(2,1)S(1)}, bf16[1,3,64,128]{3,2,1,0:T(8,128)(2,1)S(1)}, u32[]{:S(2)}, u32[]{:S(2)}) collective-permute-start(bf16[1,3,64,128]{3,2,1,0:T(8,128)(2,1)S(1)} %shard_map.59.refs_0_), channel_id=1, source_target_pairs={{0,24},{4,28},{8,16},{12,20},{16,8},{20,12},{24,0},{28,4},{1,25},{... | collective-permute-start | bytes 147464 | tf_op jit(solution)/shard_map/ppermute | solution.py:271
  6.1 4.1 %collective-permute-start.1 = (bf16[1,3,64,128]{3,2,1,0:T(8,128)(2,1)S(1)}, bf16[1,3,64,128]{3,2,1,0:T(8,128)(2,1)S(1)}, u32[]{:S(2)}, u32[]{:S(2)}) collective-permute-start(bf16[1,3,64,128]{3,2,1,0:T(8,128)(2,1)S(1)} %shard_map.59.refs_0_), channel_id=1, source_target_pairs={{0,16},{4,20},{8,24},{12,28},{16,0},{20,4},{24,8},{28,12},{1,17},{... | collective-permute-start | bytes 147464 | tf_op jit(solution)/shard_map/ppermute | solution.py:271
  6.7 7.7 %collective-permute-start.3 = (bf16[2,3,64,128]{3,2,1,0:T(8,128)(2,1)S(1)}, bf16[2,3,64,128]{3,2,1,0:T(8,128)(2,1)S(1)}, u32[]{:S(2)}, u32[]{:S(2)}) collective-permute-start(bf16[2,3,64,128]{3,2,1,0:T(8,128)(2,1)S(1)} %shard_map.60.refs_0_), channel_id=1, source_target_pairs={{0,4},{4,0},{8,12},{12,8},{16,20},{20,16},{24,28},{28,24},{1,5},{5... | collective-permute-start | bytes 294920 | tf_op jit(solution)/shard_map/ppermute | solution.py:271
  6.8 6.0 %collective-permute-start.6 = (bf16[8,4096]{1,0:T(8,128)(2,1)S(1)}, bf16[8,4096]{1,0:T(8,128)(2,1)S(1)}, u32[]{:S(2)}, u32[]{:S(2)}) collective-permute-start(bf16[8,4096]{1,0:T(8,128)(2,1)S(1)} %copy-done), channel_id=1, source_target_pairs={{0,1},{1,0},{2,3},{3,2},{4,5},{5,4},{6,7},{7,6},{8,9},{9,8},{10,11... | collective-permute-start | bytes 196616 | tf_op jit(solution)/shard_map/ppermute | solution.py:271
  9.6 4.8 %collective-permute-start.5 = (bf16[1,3,64,128]{3,2,1,0:T(8,128)(2,1)S(1)}, bf16[1,3,64,128]{3,2,1,0:T(8,128)(2,1)S(1)}, u32[]{:S(2)}, u32[]{:S(2)}) collective-permute-start(bf16[1,3,64,128]{3,2,1,0:T(8,128)(2,1)S(1)} %collective-permute-done.2.refs_2_), channel_id=1, source_target_pairs={{0,4},{4,0},{8,12},{12,8},{16,20},{20,16},{24,28},{28,24},{1,5},{5... | collective-permute-start | bytes 147464 | tf_op jit(solution)/shard_map/ppermute | solution.py:271
  10.2 4.2 %collective-permute-start.4 = (bf16[1,3,64,128]{3,2,1,0:T(8,128)(2,1)S(1)}, bf16[1,3,64,128]{3,2,1,0:T(8,128)(2,1)S(1)}, u32[]{:S(2)}, u32[]{:S(2)}) collective-permute-start(bf16[1,3,64,128]{3,2,1,0:T(8,128)(2,1)S(1)} %collective-permute-done.1.refs_1_), channel_id=1, source_target_pairs={{0,4},{4,0},{8,12},{12,8},{16,20},{20,16},{24,28},{28,24},{1,5},{5... | collective-permute-start | bytes 147464 | tf_op jit(solution)/shard_map/ppermute | solution.py:271
  10.2 9.4 %collective-permute-start.7 = (bf16[8,4096]{1,0:T(8,128)(2,1)S(1)}, bf16[8,4096]{1,0:T(8,128)(2,1)S(1)}, u32[]{:S(2)}, u32[]{:S(2)}) collective-permute-start(bf16[8,4096]{1,0:T(8,128)(2,1)S(1)} %copy-done), channel_id=1, source_target_pairs={{0,2},{1,3},{2,0},{3,1},{4,6},{5,7},{6,4},{7,5},{8,10},{9,11},{10,... | collective-permute-start | bytes 196616 | tf_op jit(solution)/shard_map/ppermute | solution.py:271
  12.8 7.8 %collective-permute-start.8 = (bf16[8,4096]{1,0:T(8,128)(2,1)S(1)}, bf16[8,4096]{1,0:T(8,128)(2,1)S(1)}, u32[]{:S(2)}, u32[]{:S(2)}) collective-permute-start(bf16[8,4096]{1,0:T(8,128)(2,1)S(1)} %collective-permute-done.6.refs_7_), channel_id=1, source_target_pairs={{0,2},{1,3},{2,0},{3,1},{4,6},{5,7},{6,4},{7,5},{8,10},{9,11},{10,... | collective-permute-start | bytes 196616 | tf_op jit(solution)/shard_map/ppermute | solution.py:271
  15.7 6.9 %collective-permute-start.9 = (bf16[176,128]{1,0:T(8,128)(2,1)S(1)}, bf16[176,128]{1,0:T(8,128)(2,1)S(1)}, u32[]{:S(2)}, u32[]{:S(2)}) collective-permute-start(bf16[176,128]{1,0:T(8,128)(2,1)S(1)} %get-tuple-element.7), channel_id=1, source_target_pairs={{0,2},{1,3},{2,0},{3,1},{4,6},{5,7},{6,4},{7,5},{8,10},{9,11},{10,... | collective-permute-start | bytes 135176 | tf_op jit(solution)/shard_map/ppermute | solution.py:271
  17.0 6.0 %collective-permute-start.10 = (bf16[176,128]{1,0:T(8,128)(2,1)S(1)}, bf16[176,128]{1,0:T(8,128)(2,1)S(1)}, u32[]{:S(2)}, u32[]{:S(2)}) collective-permute-start(bf16[176,128]{1,0:T(8,128)(2,1)S(1)} %get-tuple-element.8), channel_id=1, source_target_pairs={{0,3},{1,2},{2,1},{3,0},{4,7},{5,6},{6,5},{7,4},{8,11},{9,10},{10,... | collective-permute-start | bytes 135176 | tf_op jit(solution)/shard_map/ppermute | solution.py:271
  19.7 4.0 %collective-permute-start.11 = (bf16[176,128]{1,0:T(8,128)(2,1)S(1)}, bf16[176,128]{1,0:T(8,128)(2,1)S(1)}, u32[]{:S(2)}, u32[]{:S(2)}) collective-permute-start(bf16[176,128]{1,0:T(8,128)(2,1)S(1)} %get-tuple-element.9), channel_id=1, source_target_pairs={{0,1},{1,0},{2,3},{3,2},{4,5},{5,4},{6,7},{7,6},{8,9},{9,8},{10,11... | collective-permute-start | bytes 135176 | tf_op jit(solution)/shard_map/ppermute | solution.py:271

commit v9 on v8

--- a/solution.py
+++ b/solution.py
@@ -40,8 +40,8 @@
         packed[0, k] = jnp.concatenate([left, right], axis=1)
 
 
-def join_kernel(*refs):
-    for i, part in enumerate(refs[:-1]):
+def join_kernel(n, *refs):
+    for i, part in enumerate(refs[:n]):
         refs[-1][i] = part[0]
 
 
@@ -271,17 +271,17 @@
     return lax.ppermute(value, axis, [(i, i ^ k) for i in range(n)])
 
 
-def gather_parts(packed, n_dp):
+def gather_parts(packed, n_dp, early):
     if n_dp != 8:
         return [lax.all_gather(packed, "dp", axis=0, tiled=True)]
     near, second, last = [packed, swap(packed, "dp", n_dp, 2)], swap(packed, "dp", n_dp, 4), swap(packed, "dp", n_dp, 6)
     joined = pl.pallas_call(
-        join_kernel,
+        functools.partial(join_kernel, len(near)),
         out_shape=pltpu.VMEM((len(near), *packed.shape[1:]), packed.dtype),
-        in_specs=[VMEM] * len(near),
+        in_specs=[VMEM] * len(near) + [pl.BlockSpec(memory_space=pl.ANY)] * len(early),
         out_specs=VMEM,
         compiler_params=pltpu.CompilerParams(vmem_limit_bytes=4 * MIB),
-    )(*near)
+    )(*near, *early)
     same_core = [joined, second, last]
     return same_core + [swap(part, "dp", n_dp, 1) for part in same_core]
 
@@ -311,10 +311,10 @@
         pltpu.with_memory_space_constraint(block_slot, pltpu.HBM),
         pltpu.with_memory_space_constraint(block_values, pltpu.HBM),
     )
-    gathered = gather_parts(packed, n_dp)
     tokens = [inputs]
     while len(tokens) < n_tensor:
         tokens = tokens + [swap(value, "tensor", n_tensor, len(tokens)) for value in tokens]
+    gathered = gather_parts(packed, n_dp, tokens[1:3])
     n_parts = len(gathered)
     ids = [pltpu.VMEM((2, n_dp, 2 * side), I32), pltpu.SMEM((2, n_dp, 2 * side), I32)]
     cots = pltpu.VMEM((col_count + 1, rows, 2 * side), BF16)

time: 25.8 us -> 27.1 us (1.050)
  waiting for transfers between devices: 3.97 us -> 7.09 us
  starting transfers between devices: 15 us -> 13.2 us
    ppermute x12, waiting for transfers between devices: 3.97 us -> 7.09 us  [swap(): return lax.ppermute(value, axis, [(i, i ^ k) for i in range(n)])]
    ppermute x12, starting transfers between devices: 15 us -> 13.2 us  [swap(): return lax.ppermute(value, axis, [(i, i ^ k) for i in range(n)])]
  transfers between devices with their start and end apart: 12 -> 12, of which waited for: 7 -> 8; matrix products, arithmetic and copies ran while one was open for 0% -> 0% of each run, Pallas kernels for 12% -> 15%
where the time goes in v9:
time: 27.1 us; the launch traced here: 26.9 us
  starting transfers between devices  13.2 us (49%)
  waiting for transfers between devices  7.09 us (26%)
  Pallas kernels  5.9 us (22%)
  between operations  0.7 us (3%)
    ppermute x12, starting transfers between devices, swap(): return lax.ppermute(value, axis, [(i, i ^ k) for i in range(n)])  13.2 us
    ppermute x12, waiting for transfers between devices, swap(): return lax.ppermute(value, axis, [(i, i ^ k) for i in range(n)])  7.09 us
    pallas_call x1, Pallas kernels, on_device(): pl.pallas_call(functools.partial(sum_kernel, n_tensor, pairs, n_dp), out_...  1.89 us
    pallas_call x1, Pallas kernels, on_device(): pl.pallas_call(functools.partial(forward_kernel, count, n_parts, n_tensor...  1.83 us
    pallas_call x1, Pallas kernels, on_device(): pl.pallas_call(functools.partial(kernel, count, n_parts, n_tensor), out_s...  1.19 us
    pallas_call x1, Pallas kernels, on_device(): pl.pallas_call(functools.partial(pack_kernel, count, row_count, col_count...  0.98 us
  transfers between devices with their start and end apart: 12, of which 8 were waited for; matrix products, arithmetic and copies ran while one was open for 0% of the time, Pallas kernels for 15%

profile of v9, /device:TPU:0, one launch (start us, length us, event | category | flops | bytes accessed | tf_op | source)
XLA Modules:
  0.0 26.9 jit_solution(11707410343347593443)
XLA Ops:
  0.6 3.1 %collective-permute-start.1 = (bf16[8,4096]{1,0:T(8,128)(2,1)}, bf16[8,4096]{1,0:T(8,128)(2,1)S(1)}, u32[]{:S(2)}, u32[]{:S(2)}) collective-permute-start(bf16[8,4096]{1,0:T(8,128)(2,1)} %refs_6_.2), channel_id=1, source_target_pairs={{0,1},{1,0},{2,3},{3,2},{4,5},{5,4},{6,7},{7,6},{8,9},{9,8},{10,11... | collective-permute-start | bytes 196616 | tf_op jit(solution)/shard_map/ppermute | solution.py:271
  3.7 2.6 %collective-permute-start.2 = (bf16[8,4096]{1,0:T(8,128)(2,1)}, bf16[8,4096]{1,0:T(8,128)(2,1)S(1)}, u32[]{:S(2)}, u32[]{:S(2)}) collective-permute-start(bf16[8,4096]{1,0:T(8,128)(2,1)} %refs_6_.2), channel_id=1, source_target_pairs={{0,2},{1,3},{2,0},{3,1},{4,6},{5,7},{6,4},{7,5},{8,10},{9,11},{10,... | collective-permute-start | bytes 196616 | tf_op jit(solution)/shard_map/ppermute | solution.py:271
  6.3 1.0 %shard_map.59.refs_0_ = bf16[1,3,64,128]{3,2,1,0:T(8,128)(2,1)S(1)} custom-call(s32[1,5]{1,0:T(1,128)} %slots_hbm.1, bf16[1,5,64,64]{3,2,1,0:T(8,128)(2,1)} %values_hbm.1), custom_call_target="tpu_custom_call" | custom-call | tf_op jit(solution)/shard_map/pallas_call | solution.py:299
  7.3 0.0 copy-start.1
  7.3 1.6 %collective-permute-start = (bf16[1,3,64,128]{3,2,1,0:T(8,128)(2,1)S(1)}, bf16[1,3,64,128]{3,2,1,0:T(8,128)(2,1)S(1)}, u32[]{:S(2)}, u32[]{:S(2)}) collective-permute-start(bf16[1,3,64,128]{3,2,1,0:T(8,128)(2,1)S(1)} %shard_map.59.refs_0_), channel_id=1, source_target_pairs={{0,8},{4,12},{8,0},{12,4},{16,24},{20,28},{24,16},{28,20},{1,9},{5... | collective-permute-start | bytes 147464 | tf_op jit(solution)/shard_map/ppermute | solution.py:271
  8.9 1.5 %collective-permute-start.4 = (bf16[1,3,64,128]{3,2,1,0:T(8,128)(2,1)S(1)}, bf16[1,3,64,128]{3,2,1,0:T(8,128)(2,1)S(1)}, u32[]{:S(2)}, u32[]{:S(2)}) collective-permute-start(bf16[1,3,64,128]{3,2,1,0:T(8,128)(2,1)S(1)} %shard_map.59.refs_0_), channel_id=1, source_target_pairs={{0,24},{4,28},{8,16},{12,20},{16,8},{20,12},{24,0},{28,4},{1,25},{... | collective-permute-start | bytes 147464 | tf_op jit(solution)/shard_map/ppermute | solution.py:271
  10.4 0.5 %collective-permute-start.3 = (bf16[1,3,64,128]{3,2,1,0:T(8,128)(2,1)S(1)}, bf16[1,3,64,128]{3,2,1,0:T(8,128)(2,1)S(1)}, u32[]{:S(2)}, u32[]{:S(2)}) collective-permute-start(bf16[1,3,64,128]{3,2,1,0:T(8,128)(2,1)S(1)} %shard_map.59.refs_0_), channel_id=1, source_target_pairs={{0,16},{4,20},{8,24},{12,28},{16,0},{20,4},{24,8},{28,12},{1,17},{... | collective-permute-start | bytes 147464 | tf_op jit(solution)/shard_map/ppermute | solution.py:271
  10.9 0.7 %collective-permute-done.refs_1_ = bf16[1,3,64,128]{3,2,1,0:T(8,128)(2,1)S(1)} collective-permute-done((bf16[1,3,64,128]{3,2,1,0:T(8,128)(2,1)S(1)}, bf16[1,3,64,128]{3,2,1,0:T(8,128)(2,1)S(1)}, u32[]{:S(2)}, u32[]{:S(2)}) %collective-permute-start) | collective-permute-done | bytes 49184 | tf_op jit(solution)/shard_map/ppermute | solution.py:271
  11.6 0.0 collective-permute-done.1.refs_2_.refs_7_
  11.6 0.0 collective-permute-done.2.refs_3_.refs_8_
  11.6 0.0 copy-start
  11.6 0.1 collective-permute-start.5
  11.7 2.2 %collective-permute-done.4.refs_2_ = bf16[1,3,64,128]{3,2,1,0:T(8,128)(2,1)S(1)} collective-permute-done((bf16[1,3,64,128]{3,2,1,0:T(8,128)(2,1)S(1)}, bf16[1,3,64,128]{3,2,1,0:T(8,128)(2,1)S(1)}, u32[]{:S(2)}, u32[]{:S(2)}) %collective-permute-start.4) | collective-permute-done | bytes 49184 | tf_op jit(solution)/shard_map/ppermute | solution.py:271
  13.9 0.0 collective-permute-start.7
  13.9 0.6 %collective-permute-done.3.refs_1_ = bf16[1,3,64,128]{3,2,1,0:T(8,128)(2,1)S(1)} collective-permute-done((bf16[1,3,64,128]{3,2,1,0:T(8,128)(2,1)S(1)}, bf16[1,3,64,128]{3,2,1,0:T(8,128)(2,1)S(1)}, u32[]{:S(2)}, u32[]{:S(2)}) %collective-permute-start.3) | collective-permute-done | bytes 49184 | tf_op jit(solution)/shard_map/ppermute | solution.py:271
  14.5 0.0 collective-permute-start.6
  14.5 0.3 %collective-permute-start.8 = (bf16[8,4096]{1,0:T(8,128)(2,1)S(1)}, bf16[8,4096]{1,0:T(8,128)(2,1)S(1)}, u32[]{:S(2)}, u32[]{:S(2)}) collective-permute-start(bf16[8,4096]{1,0:T(8,128)(2,1)S(1)} %collective-permute-done.1.refs_2_.refs_7_), channel_id=1, source_target_pairs={{0,2},{1,3},{2,0},{3,1},{4,6},{5,7},{6,4},{7,5},{8,10},{9,11},{10,... | collective-permute-start | bytes 196616 | tf_op jit(solution)/shard_map/ppermute | solution.py:271
  14.8 0.3 %collective-permute-done.7.refs_5_ = bf16[1,3,64,128]{3,2,1,0:T(8,128)(2,1)S(1)} collective-permute-done((bf16[1,3,64,128]{3,2,1,0:T(8,128)(2,1)S(1)}, bf16[1,3,64,128]{3,2,1,0:T(8,128)(2,1)S(1)}, u32[]{:S(2)}, u32[]{:S(2)}) %collective-permute-start.7) | collective-permute-done | bytes 49184 | tf_op jit(solution)/shard_map/ppermute | solution.py:271
  15.1 0.6 %collective-permute-done.6.refs_4_ = bf16[1,3,64,128]{3,2,1,0:T(8,128)(2,1)S(1)} collective-permute-done((bf16[1,3,64,128]{3,2,1,0:T(8,128)(2,1)S(1)}, bf16[1,3,64,128]{3,2,1,0:T(8,128)(2,1)S(1)}, u32[]{:S(2)}, u32[]{:S(2)}) %collective-permute-start.6) | collective-permute-done | bytes 49184 | tf_op jit(solution)/shard_map/ppermute | solution.py:271
  15.7 0.0 collective-permute-done.5.refs_3_
  15.7 0.0 copy-done.1
  15.7 1.2 %shard_map.62 = (bf16[176,128]{1,0:T(8,128)(2,1)S(1)}, bf16[176,128]{1,0:T(8,128)(2,1)S(1)}, bf16[176,128]{1,0:T(8,128)(2,1)S(1)}, bf16[176,128]{1,0:T(8,128)(2,1)S(1)}) custom-call(bf16[2,3,64,128]{3,2,1,0:T(8,128)(2,1)S(1)} %shard_map.60.refs_0_, bf16[1,3,64,128]{3,2,1,0:T(8,128)(2,1)S(1)} %collective-permute-done.3.refs_1_, ...), custom_call_target="tpu_custom_call" | custom-call | tf_op jit(solution)/shard_map/pallas_call | solution.py:328
  16.9 1.8 %collective-permute-start.9 = (bf16[176,128]{1,0:T(8,128)(2,1)S(1)}, bf16[176,128]{1,0:T(8,128)(2,1)S(1)}, u32[]{:S(2)}, u32[]{:S(2)}) collective-permute-start(bf16[176,128]{1,0:T(8,128)(2,1)S(1)} %get-tuple-element.7), channel_id=1, source_target_pairs={{0,2},{1,3},{2,0},{3,1},{4,6},{5,7},{6,4},{7,5},{8,10},{9,11},{10,... | collective-permute-start | bytes 135176 | tf_op jit(solution)/shard_map/ppermute | solution.py:271
  18.7 1.1 %collective-permute-start.10 = (bf16[176,128]{1,0:T(8,128)(2,1)S(1)}, bf16[176,128]{1,0:T(8,128)(2,1)S(1)}, u32[]{:S(2)}, u32[]{:S(2)}) collective-permute-start(bf16[176,128]{1,0:T(8,128)(2,1)S(1)} %get-tuple-element.8), channel_id=1, source_target_pairs={{0,3},{1,2},{2,1},{3,0},{4,7},{5,6},{6,5},{7,4},{8,11},{9,10},{10,... | collective-permute-start | bytes 135176 | tf_op jit(solution)/shard_map/ppermute | solution.py:271
  19.8 0.7 %collective-permute-start.11 = (bf16[176,128]{1,0:T(8,128)(2,1)S(1)}, bf16[176,128]{1,0:T(8,128)(2,1)S(1)}, u32[]{:S(2)}, u32[]{:S(2)}) collective-permute-start(bf16[176,128]{1,0:T(8,128)(2,1)S(1)} %get-tuple-element.9), channel_id=1, source_target_pairs={{0,1},{1,0},{2,3},{3,2},{4,5},{5,4},{6,7},{7,6},{8,9},{9,8},{10,11... | collective-permute-start | bytes 135176 | tf_op jit(solution)/shard_map/ppermute | solution.py:271
  20.4 1.7 %collective-permute-done.8.refs_9_ = bf16[8,4096]{1,0:T(8,128)(2,1)S(1)} collective-permute-done((bf16[8,4096]{1,0:T(8,128)(2,1)S(1)}, bf16[8,4096]{1,0:T(8,128)(2,1)S(1)}, u32[]{:S(2)}, u32[]{:S(2)}) %collective-permute-start.8) | collective-permute-done | bytes 65568 | tf_op jit(solution)/shard_map/ppermute | solution.py:271
  22.2 0.0 copy-done
  22.2 1.8 %shard_map.61 = bf16[32,896]{1,0:T(8,128)(2,1)} custom-call(bf16[2,3,64,128]{3,2,1,0:T(8,128)(2,1)S(1)} %shard_map.60.refs_0_, bf16[1,3,64,128]{3,2,1,0:T(8,128)(2,1)S(1)} %collective-permute-done.3.refs_1_, bf16[1,3,64,128]{3,2,1,0:T(8,128)(2,1)S(1)} %collective-permute-done.4.refs_2_, bf16[2,3,64,128]{3,2,1,0:T(8,128)(2,1)S(1)} %collective-permute-done.5.refs_3_, ...), custom_call_target="tpu_custom_call" | custom-call | tf_op jit(solution)/shard_map/pallas_call | solution.py:339
  24.0 0.0 collective-permute-done.9.refs_1_
  24.0 0.5 %collective-permute-done.10.refs_2_ = bf16[176,128]{1,0:T(8,128)(2,1)S(1)} collective-permute-done((bf16[176,128]{1,0:T(8,128)(2,1)S(1)}, bf16[176,128]{1,0:T(8,128)(2,1)S(1)}, u32[]{:S(2)}, u32[]{:S(2)}) %collective-permute-start.10) | collective-permute-done | bytes 45088 | tf_op jit(solution)/shard_map/ppermute | solution.py:271
  24.6 0.5 %collective-permute-done.11.refs_3_ = bf16[176,128]{1,0:T(8,128)(2,1)S(1)} collective-permute-done((bf16[176,128]{1,0:T(8,128)(2,1)S(1)}, bf16[176,128]{1,0:T(8,128)(2,1)S(1)}, u32[]{:S(2)}, u32[]{:S(2)}) %collective-permute-start.11) | collective-permute-done | bytes 45088 | tf_op jit(solution)/shard_map/ppermute | solution.py:271
  25.0 1.9 %shard_map.63 = bf16[8,4096]{1,0:T(8,128)(2,1)} custom-call(bf16[176,128]{1,0:T(8,128)(2,1)S(1)} %get-tuple-element.6.refs_0_, bf16[176,128]{1,0:T(8,128)(2,1)S(1)} %collective-permute-done.9.refs_1_, bf16[176,128]{1,0:T(8,128)(2,1)S(1)} %collective-permute-done.10.refs_2_, bf16[176,128]{1,0:T(8,128)(2,1)S(1)} %collective-permute-done.11.refs_3_), custom_call_target="tpu_custom_call" | custom-call | tf_op jit(solution)/shard_map/pallas_call | solution.py:355
  (1 shorter events, 0.0 us)
Async XLA Ops:
  0.6 11.0 %collective-permute-start.1 = (bf16[8,4096]{1,0:T(8,128)(2,1)}, bf16[8,4096]{1,0:T(8,128)(2,1)S(1)}, u32[]{:S(2)}, u32[]{:S(2)}) collective-permute-start(bf16[8,4096]{1,0:T(8,128)(2,1)} %refs_6_.2), channel_id=1, source_target_pairs={{0,1},{1,0},{2,3},{3,2},{4,5},{5,4},{6,7},{7,6},{8,9},{9,8},{10,11... | collective-permute-start | bytes 196616 | tf_op jit(solution)/shard_map/ppermute | solution.py:271
  3.7 7.9 %collective-permute-start.2 = (bf16[8,4096]{1,0:T(8,128)(2,1)}, bf16[8,4096]{1,0:T(8,128)(2,1)S(1)}, u32[]{:S(2)}, u32[]{:S(2)}) collective-permute-start(bf16[8,4096]{1,0:T(8,128)(2,1)} %refs_6_.2), channel_id=1, source_target_pairs={{0,2},{1,3},{2,0},{3,1},{4,6},{5,7},{6,4},{7,5},{8,10},{9,11},{10,... | collective-permute-start | bytes 196616 | tf_op jit(solution)/shard_map/ppermute | solution.py:271
  7.3 8.4 %copy-start.1 = (bf16[32,896]{1,0:T(8,128)(2,1)S(1)}, bf16[32,896]{1,0:T(8,128)(2,1)}, u32[]{:S(2)}) copy-start(bf16[32,896]{1,0:T(8,128)(2,1)} %refs_6_.3) | copy-start | bytes 172036
  7.3 4.3 %collective-permute-start = (bf16[1,3,64,128]{3,2,1,0:T(8,128)(2,1)S(1)}, bf16[1,3,64,128]{3,2,1,0:T(8,128)(2,1)S(1)}, u32[]{:S(2)}, u32[]{:S(2)}) collective-permute-start(bf16[1,3,64,128]{3,2,1,0:T(8,128)(2,1)S(1)} %shard_map.59.refs_0_), channel_id=1, source_target_pairs={{0,8},{4,12},{8,0},{12,4},{16,24},{20,28},{24,16},{28,20},{1,9},{5... | collective-permute-start | bytes 147464 | tf_op jit(solution)/shard_map/ppermute | solution.py:271
  8.9 5.0 %collective-permute-start.4 = (bf16[1,3,64,128]{3,2,1,0:T(8,128)(2,1)S(1)}, bf16[1,3,64,128]{3,2,1,0:T(8,128)(2,1)S(1)}, u32[]{:S(2)}, u32[]{:S(2)}) collective-permute-start(bf16[1,3,64,128]{3,2,1,0:T(8,128)(2,1)S(1)} %shard_map.59.refs_0_), channel_id=1, source_target_pairs={{0,24},{4,28},{8,16},{12,20},{16,8},{20,12},{24,0},{28,4},{1,25},{... | collective-permute-start | bytes 147464 | tf_op jit(solution)/shard_map/ppermute | solution.py:271
  10.4 4.1 %collective-permute-start.3 = (bf16[1,3,64,128]{3,2,1,0:T(8,128)(2,1)S(1)}, bf16[1,3,64,128]{3,2,1,0:T(8,128)(2,1)S(1)}, u32[]{:S(2)}, u32[]{:S(2)}) collective-permute-start(bf16[1,3,64,128]{3,2,1,0:T(8,128)(2,1)S(1)} %shard_map.59.refs_0_), channel_id=1, source_target_pairs={{0,16},{4,20},{8,24},{12,28},{16,0},{20,4},{24,8},{28,12},{1,17},{... | collective-permute-start | bytes 147464 | tf_op jit(solution)/shard_map/ppermute | solution.py:271
  11.6 10.6 %copy-start = (bf16[8,4096]{1,0:T(8,128)(2,1)S(1)}, bf16[8,4096]{1,0:T(8,128)(2,1)}, u32[]{:S(2)}) copy-start(bf16[8,4096]{1,0:T(8,128)(2,1)} %refs_6_.2) | copy-start | bytes 196612
  11.6 4.1 %collective-permute-start.5 = (bf16[2,3,64,128]{3,2,1,0:T(8,128)(2,1)S(1)}, bf16[2,3,64,128]{3,2,1,0:T(8,128)(2,1)S(1)}, u32[]{:S(2)}, u32[]{:S(2)}) collective-permute-start(bf16[2,3,64,128]{3,2,1,0:T(8,128)(2,1)S(1)} %shard_map.60.refs_0_), channel_id=1, source_target_pairs={{0,4},{4,0},{8,12},{12,8},{16,20},{20,16},{24,28},{28,24},{1,5},{5... | collective-permute-start | bytes 294920 | tf_op jit(solution)/shard_map/ppermute | solution.py:271
  13.9 1.2 %collective-permute-start.7 = (bf16[1,3,64,128]{3,2,1,0:T(8,128)(2,1)S(1)}, bf16[1,3,64,128]{3,2,1,0:T(8,128)(2,1)S(1)}, u32[]{:S(2)}, u32[]{:S(2)}) collective-permute-start(bf16[1,3,64,128]{3,2,1,0:T(8,128)(2,1)S(1)} %collective-permute-done.4.refs_2_), channel_id=1, source_target_pairs={{0,4},{4,0},{8,12},{12,8},{16,20},{20,16},{24,28},{28,24},{1,5},{5... | collective-permute-start | bytes 147464 | tf_op jit(solution)/shard_map/ppermute | solution.py:271
  14.5 1.2 %collective-permute-start.6 = (bf16[1,3,64,128]{3,2,1,0:T(8,128)(2,1)S(1)}, bf16[1,3,64,128]{3,2,1,0:T(8,128)(2,1)S(1)}, u32[]{:S(2)}, u32[]{:S(2)}) collective-permute-start(bf16[1,3,64,128]{3,2,1,0:T(8,128)(2,1)S(1)} %collective-permute-done.3.refs_1_), channel_id=1, source_target_pairs={{0,4},{4,0},{8,12},{12,8},{16,20},{20,16},{24,28},{28,24},{1,5},{5... | collective-permute-start | bytes 147464 | tf_op jit(solution)/shard_map/ppermute | solution.py:271
  14.5 7.7 %collective-permute-start.8 = (bf16[8,4096]{1,0:T(8,128)(2,1)S(1)}, bf16[8,4096]{1,0:T(8,128)(2,1)S(1)}, u32[]{:S(2)}, u32[]{:S(2)}) collective-permute-start(bf16[8,4096]{1,0:T(8,128)(2,1)S(1)} %collective-permute-done.1.refs_2_.refs_7_), channel_id=1, source_target_pairs={{0,2},{1,3},{2,0},{3,1},{4,6},{5,7},{6,4},{7,5},{8,10},{9,11},{10,... | collective-permute-start | bytes 196616 | tf_op jit(solution)/shard_map/ppermute | solution.py:271
  16.9 7.1 %collective-permute-start.9 = (bf16[176,128]{1,0:T(8,128)(2,1)S(1)}, bf16[176,128]{1,0:T(8,128)(2,1)S(1)}, u32[]{:S(2)}, u32[]{:S(2)}) collective-permute-start(bf16[176,128]{1,0:T(8,128)(2,1)S(1)} %get-tuple-element.7), channel_id=1, source_target_pairs={{0,2},{1,3},{2,0},{3,1},{4,6},{5,7},{6,4},{7,5},{8,10},{9,11},{10,... | collective-permute-start | bytes 135176 | tf_op jit(solution)/shard_map/ppermute | solution.py:271
  18.7 5.9 %collective-permute-start.10 = (bf16[176,128]{1,0:T(8,128)(2,1)S(1)}, bf16[176,128]{1,0:T(8,128)(2,1)S(1)}, u32[]{:S(2)}, u32[]{:S(2)}) collective-permute-start(bf16[176,128]{1,0:T(8,128)(2,1)S(1)} %get-tuple-element.8), channel_id=1, source_target_pairs={{0,3},{1,2},{2,1},{3,0},{4,7},{5,6},{6,5},{7,4},{8,11},{9,10},{10,... | collective-permute-start | bytes 135176 | tf_op jit(solution)/shard_map/ppermute | solution.py:271
  19.8 5.2 %collective-permute-start.11 = (bf16[176,128]{1,0:T(8,128)(2,1)S(1)}, bf16[176,128]{1,0:T(8,128)(2,1)S(1)}, u32[]{:S(2)}, u32[]{:S(2)}) collective-permute-start(bf16[176,128]{1,0:T(8,128)(2,1)S(1)} %get-tuple-element.9), channel_id=1, source_target_pairs={{0,1},{1,0},{2,3},{3,2},{4,5},{5,4},{6,7},{7,6},{8,9},{9,8},{10,11... | collective-permute-start | bytes 135176 | tf_op jit(solution)/shard_map/ppermute | solution.py:271

commit v10 on v8

--- a/solution.py
+++ b/solution.py
@@ -40,9 +40,9 @@
         packed[0, k] = jnp.concatenate([left, right], axis=1)
 
 
-def join_kernel(*refs):
-    for i, part in enumerate(refs[:-1]):
-        refs[-1][i] = part[0]
+def join_kernel(own, near, tokens, near_tokens, joined, joined_tokens):
+    joined[0], joined[1] = own[0], near[0]
+    joined_tokens[0], joined_tokens[1] = tokens[...], near_tokens[...]
 
 
 def load_ids(gathered, ids_vmem, ids, sem):
@@ -114,7 +114,7 @@
 
 def slots_kernel(count, n_parts, n_tensor, *refs):
     gathered, cot, outs = refs[:n_parts], refs[n_parts], refs[n_parts + 1:n_parts + 1 + n_tensor]
-    ids_vmem, ids, cots, prod, sem = refs[n_parts + 1 + n_tensor:]
+    ids_vmem, ids, cots, prod, blocks, sem = refs[n_parts + 1 + n_tensor:]
     pairs, side = gathered[0].shape[1:3]
     rows = cot.shape[0]
     share = rows // n_tensor
@@ -123,14 +123,15 @@
     low = low_half((rows, 2 * side))
     heads = jnp.concatenate([ids_vmem[0].astype(F32)] * 2, axis=0).astype(BF16)
     where = [(part, d) for part in gathered for d in range(part.shape[0])]
-    copy.wait()
     tiles = slot_tiles(len(where), pairs)
     for t, ((i, j), (m, l)) in enumerate(tiles):
         part, d = where[i]
         other, e = where[m]
-        blocks = diagonal(part[d, j]) if i == m else diagonal(part[d, j], other[e, l])
+        blocks[t] = diagonal(part[d, j]) if i == m else diagonal(part[d, j], other[e, l])
+    copy.wait()
+    for t, ((i, j), (m, l)) in enumerate(tiles):
         lhs = jnp.where(low, cots[ids[1, i, side + j]], cots[ids[1, m, side + l]])
-        prod[t] = across(lhs, blocks)
+        prod[t] = across(lhs, blocks[t])
     me = lax.axis_index("tensor")
     for k in range(n_tensor):
         start = pl.multiple_of(lax.bitwise_xor(me, k) * share, share)
@@ -145,10 +146,10 @@
     return full + [((i, pairs - 1), (i + 1, pairs - 1)) for i in range(0, n, 2)]
 
 
-def sum_kernel(n_tensor, pairs, n_dp, *refs):
-    messages, out = refs[:n_tensor], refs[n_tensor]
-    ids_vmem, ids, sem = refs[n_tensor + 1:n_tensor + 4]
-    accs = refs[n_tensor + 4:]
+def sum_kernel(n, pairs, n_dp, *refs):
+    messages, before, out = refs[:n], refs[n:-4 - n], refs[-4 - n]
+    ids_vmem, ids, sem = refs[-3 - n:-n]
+    accs = refs[-n:]
     share, width = out.shape
     side = messages[0].shape[1] // 2
     tiles = slot_tiles(n_dp, pairs)
@@ -165,7 +166,7 @@
         for u in range(2):
             values = [two[u * share:(u + 1) * share] for two in both]
             for h, (i, j) in enumerate(tiles[t + u]):
-                rows = [ids[m, i, side + j] for m in range(n_tensor)]
+                rows = [ids[m, i, side + j] for m in range(n)]
                 halves = [jnp.where(low, 0.0, value) if h else jnp.where(low, value, 0.0) for value in values]
                 sums = [acc[row] + half for acc, row, half in zip(accs, rows, halves)]
                 for acc, row, value in zip(accs, rows, sums):
@@ -178,7 +179,27 @@
         return fold(value)
 
     for r in range(0, width // side, 2):
-        out[:, r * side:(r + 2) * side] = jnp.where(low, total(r), total(r + 1)).astype(BF16)
+        here = slice(r * side, (r + 2) * side)
+        value = jnp.where(low, total(r), total(r + 1))
+        for earlier in before:
+            value = value + earlier[:, here]
+        out[:, here] = value.astype(out.dtype)
+
+
+def add_slots(messages, before, shape, dtype, n_dp, pairs, side, params):
+    n, (share, width) = len(messages), shape
+    return pl.pallas_call(
+        functools.partial(sum_kernel, n, pairs, n_dp),
+        out_shape=jax.ShapeDtypeStruct(shape, dtype),
+        in_specs=[VMEM] * (n + len(before)),
+        out_specs=VMEM,
+        scratch_shapes=[
+            pltpu.VMEM((n, n_dp, 2 * side), I32),
+            pltpu.SMEM((n, n_dp, 2 * side), I32),
+            pltpu.SemaphoreType.DMA,
+        ] + [pltpu.VMEM((width // side + 1, share, 2 * side), F32)] * n,
+        compiler_params=params,
+    )(*messages, *before)
 
 
 def rows_kernel(count, n_parts, n_tensor, *refs):
@@ -216,9 +237,10 @@
             outs[k][:, r * side:(r + 2) * side] = jnp.where(half, *pair).astype(BF16)
 
 
-def forward_kernel(count, n_parts, n_tensor, *refs):
-    gathered, tokens = refs[:n_parts], refs[n_parts:n_parts + n_tensor]
-    out, ids_vmem, ids, blocks, prod, left_acc, right_acc, stage, sem = refs[n_parts + n_tensor:]
+def forward_kernel(count, n_parts, n_token_parts, n_tensor, *refs):
+    gathered, token_parts = refs[:n_parts], refs[n_parts:n_parts + n_token_parts]
+    out, ids_vmem, ids, blocks, prod, left_acc, right_acc, stage, sem = refs[n_parts + n_token_parts:]
+    tokens = [part.at[i] for part in token_parts for i in range(part.shape[0])]
     pairs, side = gathered[0].shape[1:3]
     row_count = blocks.shape[0] - 1
     col_count = left_acc.shape[0] - 1
@@ -271,19 +293,27 @@
     return lax.ppermute(value, axis, [(i, i ^ k) for i in range(n)])
 
 
-def gather_parts(packed, n_dp):
-    if n_dp != 8:
-        return [lax.all_gather(packed, "dp", axis=0, tiled=True)]
-    near, second, last = [packed, swap(packed, "dp", n_dp, 2)], swap(packed, "dp", n_dp, 4), swap(packed, "dp", n_dp, 6)
-    joined = pl.pallas_call(
+def gather_all(packed, inputs, n_dp, n_tensor):
+    if (n_dp, n_tensor) != (8, 4):
+        tokens = [inputs[None]]
+        while len(tokens) < n_tensor:
+            tokens = tokens + [swap(value, "tensor", n_tensor, len(tokens)) for value in tokens]
+        return [lax.all_gather(packed, "dp", axis=0, tiled=True)], tokens
+    near_tokens = swap(inputs, "tensor", n_tensor, 1)
+    near, second, last = [swap(packed, "dp", n_dp, k) for k in (2, 4, 6)]
+    joined, tokens = pl.pallas_call(
         join_kernel,
-        out_shape=pltpu.VMEM((len(near), *packed.shape[1:]), packed.dtype),
-        in_specs=[VMEM] * len(near),
-        out_specs=VMEM,
+        out_shape=[
+            pltpu.VMEM((2, *packed.shape[1:]), packed.dtype),
+            pltpu.VMEM((2, *inputs.shape), inputs.dtype),
+        ],
+        in_specs=[VMEM] * 4,
+        out_specs=[VMEM] * 2,
         compiler_params=pltpu.CompilerParams(vmem_limit_bytes=4 * MIB),
-    )(*near)
+    )(packed, near, inputs, near_tokens)
     same_core = [joined, second, last]
-    return same_core + [swap(part, "dp", n_dp, 1) for part in same_core]
+    parts = same_core + [swap(part, "dp", n_dp, 1) for part in same_core]
+    return parts, [tokens, swap(tokens, "tensor", n_tensor, 2)]
 
 
 def on_device(n_dp, n_tensor, inputs, block_values, block_slot, grad_out):
@@ -292,7 +322,7 @@
     _, count, side, _ = block_values.shape
     row_count, col_count = width // side, hidden // side
     pairs = count // 2 + 1
-    small = n_dp == 8
+    small = (n_dp, n_tensor) == (8, 4)
     per_slot = small and n_dp * count < row_count and count == 2 * pairs - 1
     params = pltpu.CompilerParams(vmem_limit_bytes=(12 if small else 48) * MIB)
 
@@ -311,35 +341,32 @@
         pltpu.with_memory_space_constraint(block_slot, pltpu.HBM),
         pltpu.with_memory_space_constraint(block_values, pltpu.HBM),
     )
-    gathered = gather_parts(packed, n_dp)
-    tokens = [inputs]
-    while len(tokens) < n_tensor:
-        tokens = tokens + [swap(value, "tensor", n_tensor, len(tokens)) for value in tokens]
+    gathered, tokens = gather_all(packed, inputs, n_dp, n_tensor)
     n_parts = len(gathered)
     ids = [pltpu.VMEM((2, n_dp, 2 * side), I32), pltpu.SMEM((2, n_dp, 2 * side), I32)]
     cots = pltpu.VMEM((col_count + 1, rows, 2 * side), BF16)
     tiles = len(slot_tiles(n_dp, pairs))
     if per_slot:
         kernel, shape = slots_kernel, (tiles * share + 2 * n_dp, 2 * side)
-        scratch = pltpu.VMEM((tiles, rows, 2 * side), F32)
+        scratch = [pltpu.VMEM((tiles, rows, 2 * side), F32), pltpu.VMEM((tiles, 2 * side, 2 * side), BF16)]
     else:
         kernel, shape = rows_kernel, (share, width)
-        scratch = pltpu.VMEM((row_count + 1, rows, 2 * side), F32)
+        scratch = [pltpu.VMEM((row_count + 1, rows, 2 * side), F32)]
     partial_sums = pl.pallas_call(
         functools.partial(kernel, count, n_parts, n_tensor),
         out_shape=[jax.ShapeDtypeStruct(shape, BF16)] * n_tensor,
         in_specs=[VMEM] * (n_parts + 1),
         out_specs=[VMEM] * n_tensor,
-        scratch_shapes=ids + [cots, scratch, pltpu.SemaphoreType.DMA],
+        scratch_shapes=ids + [cots] + scratch + [pltpu.SemaphoreType.DMA],
         compiler_params=params,
     )(*gathered, grad_out)
     order = sorted(range(1, n_tensor), key=lambda k: (k != 2, -k))
     received = {k: swap(partial_sums[k], "tensor", n_tensor, k) for k in order}
     arrived = [partial_sums[0]] + [received[k] for k in order]
     outputs = pl.pallas_call(
-        functools.partial(forward_kernel, count, n_parts, n_tensor),
+        functools.partial(forward_kernel, count, n_parts, len(tokens), n_tensor),
         out_shape=jax.ShapeDtypeStruct((rows, hidden), BF16),
-        in_specs=[VMEM] * (n_parts + n_tensor),
+        in_specs=[VMEM] * (n_parts + len(tokens)),
         out_specs=VMEM,
         scratch_shapes=ids + [
             pltpu.VMEM((row_count + 1, rows, 2 * side), BF16),
@@ -352,18 +379,8 @@
         compiler_params=params,
     )(*gathered, *tokens)
     if per_slot:
-        grad_in = pl.pallas_call(
-            functools.partial(sum_kernel, n_tensor, pairs, n_dp),
-            out_shape=jax.ShapeDtypeStruct((share, width), BF16),
-            in_specs=[VMEM] * n_tensor,
-            out_specs=VMEM,
-            scratch_shapes=[
-                pltpu.VMEM((n_tensor, n_dp, 2 * side), I32),
-                pltpu.SMEM((n_tensor, n_dp, 2 * side), I32),
-                pltpu.SemaphoreType.DMA,
-            ] + [pltpu.VMEM((row_count + 1, share, 2 * side), F32)] * n_tensor,
-            compiler_params=params,
-        )(*arrived)
+        first_sum = add_slots(arrived[:2], [], (share, width), F32, n_dp, pairs, side, params)
+        grad_in = add_slots(arrived[2:], [first_sum], (share, width), BF16, n_dp, pairs, side, params)
     else:
         total = arrived[0].astype(F32)
         for value in arrived[1:]:

time: 25.8 us -> 24.7 us (0.957)
  starting transfers between devices: 15 us -> 13.4 us
  Pallas kernels: 5.9 us -> 6.84 us
  waiting for transfers between devices: 3.97 us -> 3.61 us
    ppermute x12 -> x11, starting transfers between devices: 15 us -> 13.4 us  [swap(): return lax.ppermute(value, axis, [(i, i ^ k) for i in range(n)])]
    pallas_call x3 -> x4, Pallas kernels: 3.73 us -> 4.6 us  [the longest x2 2.74 us: add_slots(): pl.pallas_call(functools.partial(sum_kernel, n, pairs, n_dp), out_shape=j...]
    ppermute x12 -> x11, waiting for transfers between devices: 3.97 us -> 3.61 us  [swap(): return lax.ppermute(value, axis, [(i, i ^ k) for i in range(n)])]
  transfers between devices with their start and end apart: 12 -> 11, of which waited for: 7 -> 6; matrix products, arithmetic and copies ran while one was open for 0% -> 0% of each run, Pallas kernels for 12% -> 21%
where the time goes in v10:
time: 24.7 us; the launch traced here: 24.6 us
  starting transfers between devices  13.4 us (54%)
  Pallas kernels  6.84 us (28%)
  waiting for transfers between devices  3.61 us (15%)
  between operations  0.71 us (3%)
    ppermute x11, starting transfers between devices, swap(): return lax.ppermute(value, axis, [(i, i ^ k) for i in range(n)])  13.4 us
    ppermute x11, waiting for transfers between devices, swap(): return lax.ppermute(value, axis, [(i, i ^ k) for i in range(n)])  3.61 us
    pallas_call x2, Pallas kernels, add_slots(): pl.pallas_call(functools.partial(sum_kernel, n, pairs, n_dp), out_shape=j...  2.74 us
    pallas_call x1, Pallas kernels, on_device(): pl.pallas_call(functools.partial(forward_kernel, count, n_parts, len(toke...  1.84 us
    pallas_call x1, Pallas kernels, on_device(): pl.pallas_call(functools.partial(kernel, count, n_parts, n_tensor), out_s...  1.26 us
    pallas_call x1, Pallas kernels, on_device(): pl.pallas_call(functools.partial(pack_kernel, count, row_count, col_count...  0.98 us
  transfers between devices with their start and end apart: 11, of which 6 were waited for; matrix products, arithmetic and copies ran while one was open for 0% of the time, Pallas kernels for 21%

profile of v10, /device:TPU:0, one launch (start us, length us, event | category | flops | bytes accessed | tf_op | source)
XLA Modules:
  0.0 24.6 jit_solution(5856758962172859721)
XLA Ops:
  0.6 0.0 copy-start
  0.6 3.1 %collective-permute-start.1 = (bf16[8,4096]{1,0:T(8,128)(2,1)}, bf16[8,4096]{1,0:T(8,128)(2,1)S(1)}, u32[]{:S(2)}, u32[]{:S(2)}) collective-permute-start(bf16[8,4096]{1,0:T(8,128)(2,1)} %tokens.1), channel_id=1, source_target_pairs={{0,1},{1,0},{2,3},{3,2},{4,5},{5,4},{6,7},{7,6},{8,9},{9,8},{10,11... | collective-permute-start | bytes 196616 | tf_op jit(solution)/shard_map/ppermute | solution.py:293
  3.7 1.0 %shard_map.59.own = bf16[1,3,64,128]{3,2,1,0:T(8,128)(2,1)S(1)} custom-call(s32[1,5]{1,0:T(1,128)} %slots_hbm.1, bf16[1,5,64,64]{3,2,1,0:T(8,128)(2,1)} %values_hbm.1), custom_call_target="tpu_custom_call" | custom-call | tf_op jit(solution)/shard_map/pallas_call | solution.py:329
  4.7 0.0 copy-start.1
  4.7 1.6 %collective-permute-start = (bf16[1,3,64,128]{3,2,1,0:T(8,128)(2,1)S(1)}, bf16[1,3,64,128]{3,2,1,0:T(8,128)(2,1)S(1)}, u32[]{:S(2)}, u32[]{:S(2)}) collective-permute-start(bf16[1,3,64,128]{3,2,1,0:T(8,128)(2,1)S(1)} %shard_map.59.own), channel_id=1, source_target_pairs={{0,8},{4,12},{8,0},{12,4},{16,24},{20,28},{24,16},{28,20},{1,9},{5... | collective-permute-start | bytes 147464 | tf_op jit(solution)/shard_map/ppermute | solution.py:293
  6.3 1.5 %collective-permute-start.3 = (bf16[1,3,64,128]{3,2,1,0:T(8,128)(2,1)S(1)}, bf16[1,3,64,128]{3,2,1,0:T(8,128)(2,1)S(1)}, u32[]{:S(2)}, u32[]{:S(2)}) collective-permute-start(bf16[1,3,64,128]{3,2,1,0:T(8,128)(2,1)S(1)} %shard_map.59.own), channel_id=1, source_target_pairs={{0,24},{4,28},{8,16},{12,20},{16,8},{20,12},{24,0},{28,4},{1,25},{... | collective-permute-start | bytes 147464 | tf_op jit(solution)/shard_map/ppermute | solution.py:293
  7.8 0.5 %collective-permute-start.2 = (bf16[1,3,64,128]{3,2,1,0:T(8,128)(2,1)S(1)}, bf16[1,3,64,128]{3,2,1,0:T(8,128)(2,1)S(1)}, u32[]{:S(2)}, u32[]{:S(2)}) collective-permute-start(bf16[1,3,64,128]{3,2,1,0:T(8,128)(2,1)S(1)} %shard_map.59.own), channel_id=1, source_target_pairs={{0,16},{4,20},{8,24},{12,28},{16,0},{20,4},{24,8},{28,12},{1,17},{... | collective-permute-start | bytes 147464 | tf_op jit(solution)/shard_map/ppermute | solution.py:293
  8.3 0.6 %collective-permute-done.near = bf16[1,3,64,128]{3,2,1,0:T(8,128)(2,1)S(1)} collective-permute-done((bf16[1,3,64,128]{3,2,1,0:T(8,128)(2,1)S(1)}, bf16[1,3,64,128]{3,2,1,0:T(8,128)(2,1)S(1)}, u32[]{:S(2)}, u32[]{:S(2)}) %collective-permute-start) | collective-permute-done | bytes 49184 | tf_op jit(solution)/shard_map/ppermute | solution.py:293
  8.9 0.0 collective-permute-done.1.near_tokens
  8.9 0.0 copy-done
  8.9 0.1 collective-permute-start.4
  9.0 2.7 %collective-permute-start.7 = (bf16[2,8,4096]{2,1,0:T(8,128)(2,1)S(1)}, bf16[2,8,4096]{2,1,0:T(8,128)(2,1)S(1)}, u32[]{:S(2)}, u32[]{:S(2)}) collective-permute-start(bf16[2,8,4096]{2,1,0:T(8,128)(2,1)S(1)} %get-tuple-element.9.refs_6_), channel_id=1, source_target_pairs={{0,2},{1,3},{2,0},{3,1},{4,6},{5,7},{6,4},{7,5},{8,10},{9,11},{10,... | collective-permute-start | bytes 393224 | tf_op jit(solution)/shard_map/ppermute | solution.py:293
  11.6 0.0 collective-permute-done.3.refs_2_
  11.7 0.2 collective-permute-start.6
  11.8 0.1 collective-permute-done.2.refs_1_
  11.9 0.3 %collective-permute-start.5 = (bf16[1,3,64,128]{3,2,1,0:T(8,128)(2,1)S(1)}, bf16[1,3,64,128]{3,2,1,0:T(8,128)(2,1)S(1)}, u32[]{:S(2)}, u32[]{:S(2)}) collective-permute-start(bf16[1,3,64,128]{3,2,1,0:T(8,128)(2,1)S(1)} %collective-permute-done.2.refs_1_), channel_id=1, source_target_pairs={{0,4},{4,0},{8,12},{12,8},{16,20},{20,16},{24,28},{28,24},{1,5},{5... | collective-permute-start | bytes 147464 | tf_op jit(solution)/shard_map/ppermute | solution.py:293
  12.2 0.7 %collective-permute-done.6.refs_5_ = bf16[1,3,64,128]{3,2,1,0:T(8,128)(2,1)S(1)} collective-permute-done((bf16[1,3,64,128]{3,2,1,0:T(8,128)(2,1)S(1)}, bf16[1,3,64,128]{3,2,1,0:T(8,128)(2,1)S(1)}, u32[]{:S(2)}, u32[]{:S(2)}) %collective-permute-start.6) | collective-permute-done | bytes 49184 | tf_op jit(solution)/shard_map/ppermute | solution.py:293
  12.9 0.2 collective-permute-done.5.refs_4_
  13.1 0.0 collective-permute-done.4.refs_3_
  13.1 0.0 copy-done.1
  13.1 1.3 %shard_map.62 = (bf16[176,128]{1,0:T(8,128)(2,1)S(1)}, bf16[176,128]{1,0:T(8,128)(2,1)S(1)}, bf16[176,128]{1,0:T(8,128)(2,1)S(1)}, bf16[176,128]{1,0:T(8,128)(2,1)S(1)}) custom-call(bf16[2,3,64,128]{3,2,1,0:T(8,128)(2,1)S(1)} %get-tuple-element.8.refs_0_, bf16[1,3,64,128]{3,2,1,0:T(8,128)(2,1)S(1)} %collective-permute-done.2.refs_1_, ...), custom_call_target="tpu_custom_call" | custom-call | tf_op jit(solution)/shard_map/pallas_call | solution.py:355
  14.4 2.7 %collective-permute-start.10 = (bf16[176,128]{1,0:T(8,128)(2,1)S(1)}, bf16[176,128]{1,0:T(8,128)(2,1)S(1)}, u32[]{:S(2)}, u32[]{:S(2)}) collective-permute-start(bf16[176,128]{1,0:T(8,128)(2,1)S(1)} %get-tuple-element.13), channel_id=1, source_target_pairs={{0,2},{1,3},{2,0},{3,1},{4,6},{5,7},{6,4},{7,5},{8,10},{9,11},{10,... | collective-permute-start | bytes 135176 | tf_op jit(solution)/shard_map/ppermute | solution.py:293
  17.0 0.2 collective-permute-start.8
  17.3 0.7 %collective-permute-start.9 = (bf16[176,128]{1,0:T(8,128)(2,1)S(1)}, bf16[176,128]{1,0:T(8,128)(2,1)S(1)}, u32[]{:S(2)}, u32[]{:S(2)}) collective-permute-start(bf16[176,128]{1,0:T(8,128)(2,1)S(1)} %get-tuple-element.11), channel_id=1, source_target_pairs={{0,1},{1,0},{2,3},{3,2},{4,5},{5,4},{6,7},{7,6},{8,9},{9,8},{10,11... | collective-permute-start | bytes 135176 | tf_op jit(solution)/shard_map/ppermute | solution.py:293
  17.9 1.5 %collective-permute-done.7.refs_7_ = bf16[2,8,4096]{2,1,0:T(8,128)(2,1)S(1)} collective-permute-done((bf16[2,8,4096]{2,1,0:T(8,128)(2,1)S(1)}, bf16[2,8,4096]{2,1,0:T(8,128)(2,1)S(1)}, u32[]{:S(2)}, u32[]{:S(2)}) %collective-permute-start.7) | collective-permute-done | bytes 131104 | tf_op jit(solution)/shard_map/ppermute | solution.py:293
  19.4 1.8 %shard_map.61 = bf16[32,896]{1,0:T(8,128)(2,1)} custom-call(bf16[2,3,64,128]{3,2,1,0:T(8,128)(2,1)S(1)} %get-tuple-element.8.refs_0_, bf16[1,3,64,128]{3,2,1,0:T(8,128)(2,1)S(1)} %collective-permute-done.2.refs_1_, bf16[1,3,64,128]{3,2,1,0:T(8,128)(2,1)S(1)} %collective-permute-done.3.refs_2_, bf16[2,3,64,128]{3,2,1,0:T(8,128)(2,1)S(1)} %collective-permute-done.4.refs_3_, ...), custom_call_target="tpu_custom_call" | custom-call | tf_op jit(solution)/shard_map/pallas_call | solution.py:366
  21.3 0.0 collective-permute-done.10.refs_1_
  21.3 1.1 %shard_map.63.refs_2_ = f32[8,4096]{1,0:T(8,128)S(1)} custom-call(bf16[176,128]{1,0:T(8,128)(2,1)S(1)} %get-tuple-element.12.refs_0_, bf16[176,128]{1,0:T(8,128)(2,1)S(1)} %collective-permute-done.10.refs_1_), custom_call_target="tpu_custom_call" | custom-call | tf_op jit(solution)/shard_map/pallas_call | solution.py:191
  22.4 0.5 %collective-permute-done.8.refs_0_ = bf16[176,128]{1,0:T(8,128)(2,1)S(1)} collective-permute-done((bf16[176,128]{1,0:T(8,128)(2,1)S(1)}, bf16[176,128]{1,0:T(8,128)(2,1)S(1)}, u32[]{:S(2)}, u32[]{:S(2)}) %collective-permute-start.8) | collective-permute-done | bytes 45088 | tf_op jit(solution)/shard_map/ppermute | solution.py:293
  22.9 0.0 collective-permute-done.9.refs_1_
  22.9 1.7 %shard_map.64 = bf16[8,4096]{1,0:T(8,128)(2,1)} custom-call(bf16[176,128]{1,0:T(8,128)(2,1)S(1)} %collective-permute-done.8.refs_0_, bf16[176,128]{1,0:T(8,128)(2,1)S(1)} %collective-permute-done.9.refs_1_, f32[8,4096]{1,0:T(8,128)S(1)} %shard_map.63.refs_2_), custom_call_target="tpu_custom_call" | custom-call | tf_op jit(solution)/shard_map/pallas_call | solution.py:191
  (1 shorter events, 0.0 us)
Async XLA Ops:
  0.6 8.3 %copy-start = (bf16[8,4096]{1,0:T(8,128)(2,1)S(1)}, bf16[8,4096]{1,0:T(8,128)(2,1)}, u32[]{:S(2)}) copy-start(bf16[8,4096]{1,0:T(8,128)(2,1)} %tokens.1) | copy-start | bytes 196612
  0.6 8.3 %collective-permute-start.1 = (bf16[8,4096]{1,0:T(8,128)(2,1)}, bf16[8,4096]{1,0:T(8,128)(2,1)S(1)}, u32[]{:S(2)}, u32[]{:S(2)}) collective-permute-start(bf16[8,4096]{1,0:T(8,128)(2,1)} %tokens.1), channel_id=1, source_target_pairs={{0,1},{1,0},{2,3},{3,2},{4,5},{5,4},{6,7},{7,6},{8,9},{9,8},{10,11... | collective-permute-start | bytes 196616 | tf_op jit(solution)/shard_map/ppermute | solution.py:293
  4.7 8.4 %copy-start.1 = (bf16[32,896]{1,0:T(8,128)(2,1)S(1)}, bf16[32,896]{1,0:T(8,128)(2,1)}, u32[]{:S(2)}) copy-start(bf16[32,896]{1,0:T(8,128)(2,1)} %refs_6_.1) | copy-start | bytes 172036
  4.7 4.2 %collective-permute-start = (bf16[1,3,64,128]{3,2,1,0:T(8,128)(2,1)S(1)}, bf16[1,3,64,128]{3,2,1,0:T(8,128)(2,1)S(1)}, u32[]{:S(2)}, u32[]{:S(2)}) collective-permute-start(bf16[1,3,64,128]{3,2,1,0:T(8,128)(2,1)S(1)} %shard_map.59.own), channel_id=1, source_target_pairs={{0,8},{4,12},{8,0},{12,4},{16,24},{20,28},{24,16},{28,20},{1,9},{5... | collective-permute-start | bytes 147464 | tf_op jit(solution)/shard_map/ppermute | solution.py:293
  6.3 5.4 %collective-permute-start.3 = (bf16[1,3,64,128]{3,2,1,0:T(8,128)(2,1)S(1)}, bf16[1,3,64,128]{3,2,1,0:T(8,128)(2,1)S(1)}, u32[]{:S(2)}, u32[]{:S(2)}) collective-permute-start(bf16[1,3,64,128]{3,2,1,0:T(8,128)(2,1)S(1)} %shard_map.59.own), channel_id=1, source_target_pairs={{0,24},{4,28},{8,16},{12,20},{16,8},{20,12},{24,0},{28,4},{1,25},{... | collective-permute-start | bytes 147464 | tf_op jit(solution)/shard_map/ppermute | solution.py:293
  7.8 4.1 %collective-permute-start.2 = (bf16[1,3,64,128]{3,2,1,0:T(8,128)(2,1)S(1)}, bf16[1,3,64,128]{3,2,1,0:T(8,128)(2,1)S(1)}, u32[]{:S(2)}, u32[]{:S(2)}) collective-permute-start(bf16[1,3,64,128]{3,2,1,0:T(8,128)(2,1)S(1)} %shard_map.59.own), channel_id=1, source_target_pairs={{0,16},{4,20},{8,24},{12,28},{16,0},{20,4},{24,8},{28,12},{1,17},{... | collective-permute-start | bytes 147464 | tf_op jit(solution)/shard_map/ppermute | solution.py:293
  8.9 4.2 %collective-permute-start.4 = (bf16[2,3,64,128]{3,2,1,0:T(8,128)(2,1)S(1)}, bf16[2,3,64,128]{3,2,1,0:T(8,128)(2,1)S(1)}, u32[]{:S(2)}, u32[]{:S(2)}) collective-permute-start(bf16[2,3,64,128]{3,2,1,0:T(8,128)(2,1)S(1)} %get-tuple-element.8.refs_0_), channel_id=1, source_target_pairs={{0,4},{4,0},{8,12},{12,8},{16,20},{20,16},{24,28},{28,24},{1,5},{5... | collective-permute-start | bytes 294920 | tf_op jit(solution)/shard_map/ppermute | solution.py:293
  9.0 10.4 %collective-permute-start.7 = (bf16[2,8,4096]{2,1,0:T(8,128)(2,1)S(1)}, bf16[2,8,4096]{2,1,0:T(8,128)(2,1)S(1)}, u32[]{:S(2)}, u32[]{:S(2)}) collective-permute-start(bf16[2,8,4096]{2,1,0:T(8,128)(2,1)S(1)} %get-tuple-element.9.refs_6_), channel_id=1, source_target_pairs={{0,2},{1,3},{2,0},{3,1},{4,6},{5,7},{6,4},{7,5},{8,10},{9,11},{10,... | collective-permute-start | bytes 393224 | tf_op jit(solution)/shard_map/ppermute | solution.py:293
  11.7 1.2 %collective-permute-start.6 = (bf16[1,3,64,128]{3,2,1,0:T(8,128)(2,1)S(1)}, bf16[1,3,64,128]{3,2,1,0:T(8,128)(2,1)S(1)}, u32[]{:S(2)}, u32[]{:S(2)}) collective-permute-start(bf16[1,3,64,128]{3,2,1,0:T(8,128)(2,1)S(1)} %collective-permute-done.3.refs_2_), channel_id=1, source_target_pairs={{0,4},{4,0},{8,12},{12,8},{16,20},{20,16},{24,28},{28,24},{1,5},{5... | collective-permute-start | bytes 147464 | tf_op jit(solution)/shard_map/ppermute | solution.py:293
  11.9 1.2 %collective-permute-start.5 = (bf16[1,3,64,128]{3,2,1,0:T(8,128)(2,1)S(1)}, bf16[1,3,64,128]{3,2,1,0:T(8,128)(2,1)S(1)}, u32[]{:S(2)}, u32[]{:S(2)}) collective-permute-start(bf16[1,3,64,128]{3,2,1,0:T(8,128)(2,1)S(1)} %collective-permute-done.2.refs_1_), channel_id=1, source_target_pairs={{0,4},{4,0},{8,12},{12,8},{16,20},{20,16},{24,28},{28,24},{1,5},{5... | collective-permute-start | bytes 147464 | tf_op jit(solution)/shard_map/ppermute | solution.py:293
  14.4 6.9 %collective-permute-start.10 = (bf16[176,128]{1,0:T(8,128)(2,1)S(1)}, bf16[176,128]{1,0:T(8,128)(2,1)S(1)}, u32[]{:S(2)}, u32[]{:S(2)}) collective-permute-start(bf16[176,128]{1,0:T(8,128)(2,1)S(1)} %get-tuple-element.13), channel_id=1, source_target_pairs={{0,2},{1,3},{2,0},{3,1},{4,6},{5,7},{6,4},{7,5},{8,10},{9,11},{10,... | collective-permute-start | bytes 135176 | tf_op jit(solution)/shard_map/ppermute | solution.py:293
  17.0 5.8 %collective-permute-start.8 = (bf16[176,128]{1,0:T(8,128)(2,1)S(1)}, bf16[176,128]{1,0:T(8,128)(2,1)S(1)}, u32[]{:S(2)}, u32[]{:S(2)}) collective-permute-start(bf16[176,128]{1,0:T(8,128)(2,1)S(1)} %get-tuple-element.10), channel_id=1, source_target_pairs={{0,3},{1,2},{2,1},{3,0},{4,7},{5,6},{6,5},{7,4},{8,11},{9,10},{10,... | collective-permute-start | bytes 135176 | tf_op jit(solution)/shard_map/ppermute | solution.py:293
  17.3 5.6 %collective-permute-start.9 = (bf16[176,128]{1,0:T(8,128)(2,1)S(1)}, bf16[176,128]{1,0:T(8,128)(2,1)S(1)}, u32[]{:S(2)}, u32[]{:S(2)}) collective-permute-start(bf16[176,128]{1,0:T(8,128)(2,1)S(1)} %get-tuple-element.11), channel_id=1, source_target_pairs={{0,1},{1,0},{2,3},{3,2},{4,5},{5,4},{6,7},{7,6},{8,9},{9,8},{10,11... | collective-permute-start | bytes 135176 | tf_op jit(solution)/shard_map/ppermute | solution.py:293

commit v11 on v10

--- a/solution.py
+++ b/solution.py
@@ -40,9 +40,9 @@
         packed[0, k] = jnp.concatenate([left, right], axis=1)
 
 
-def join_kernel(own, near, tokens, near_tokens, joined, joined_tokens):
+def join_kernel(own, near, tokens, far_tokens, joined, joined_tokens):
     joined[0], joined[1] = own[0], near[0]
-    joined_tokens[0], joined_tokens[1] = tokens[...], near_tokens[...]
+    joined_tokens[0], joined_tokens[1] = tokens[...], far_tokens[...]
 
 
 def load_ids(gathered, ids_vmem, ids, sem):
@@ -146,62 +146,6 @@
     return full + [((i, pairs - 1), (i + 1, pairs - 1)) for i in range(0, n, 2)]
 
 
-def sum_kernel(n, pairs, n_dp, *refs):
-    messages, before, out = refs[:n], refs[n:-4 - n], refs[-4 - n]
-    ids_vmem, ids, sem = refs[-3 - n:-n]
-    accs = refs[-n:]
-    share, width = out.shape
-    side = messages[0].shape[1] // 2
-    tiles = slot_tiles(n_dp, pairs)
-    for m, message in enumerate(messages):
-        ids_vmem[m] = message[len(tiles) * share:, :].astype(F32)[:n_dp].astype(I32)
-    copy = pltpu.make_async_copy(ids_vmem, ids, sem)
-    copy.start()
-    for acc in accs:
-        acc[...] = jnp.zeros_like(acc)
-    low = low_half((share, 2 * side))
-    copy.wait()
-    for t in range(0, len(tiles), 2):
-        both = [message[t * share:(t + 2) * share, :].astype(F32) for message in messages]
-        for u in range(2):
-            values = [two[u * share:(u + 1) * share] for two in both]
-            for h, (i, j) in enumerate(tiles[t + u]):
-                rows = [ids[m, i, side + j] for m in range(n)]
-                halves = [jnp.where(low, 0.0, value) if h else jnp.where(low, value, 0.0) for value in values]
-                sums = [acc[row] + half for acc, row, half in zip(accs, rows, halves)]
-                for acc, row, value in zip(accs, rows, sums):
-                    acc[row] = value
-
-    def total(r):
-        value = accs[0][r]
-        for acc in accs[1:]:
-            value = value + acc[r]
-        return fold(value)
-
-    for r in range(0, width // side, 2):
-        here = slice(r * side, (r + 2) * side)
-        value = jnp.where(low, total(r), total(r + 1))
-        for earlier in before:
-            value = value + earlier[:, here]
-        out[:, here] = value.astype(out.dtype)
-
-
-def add_slots(messages, before, shape, dtype, n_dp, pairs, side, params):
-    n, (share, width) = len(messages), shape
-    return pl.pallas_call(
-        functools.partial(sum_kernel, n, pairs, n_dp),
-        out_shape=jax.ShapeDtypeStruct(shape, dtype),
-        in_specs=[VMEM] * (n + len(before)),
-        out_specs=VMEM,
-        scratch_shapes=[
-            pltpu.VMEM((n, n_dp, 2 * side), I32),
-            pltpu.SMEM((n, n_dp, 2 * side), I32),
-            pltpu.SemaphoreType.DMA,
-        ] + [pltpu.VMEM((width // side + 1, share, 2 * side), F32)] * n,
-        compiler_params=params,
-    )(*messages, *before)
-
-
 def rows_kernel(count, n_parts, n_tensor, *refs):
     gathered, cot, outs = refs[:n_parts], refs[n_parts], refs[n_parts + 1:n_parts + 1 + n_tensor]
     ids_vmem, ids, cots, acc, sem = refs[n_parts + 1 + n_tensor:]
@@ -237,24 +181,18 @@
             outs[k][:, r * side:(r + 2) * side] = jnp.where(half, *pair).astype(BF16)
 
 
-def forward_kernel(count, n_parts, n_token_parts, n_tensor, *refs):
-    gathered, token_parts = refs[:n_parts], refs[n_parts:n_parts + n_token_parts]
-    out, ids_vmem, ids, blocks, prod, left_acc, right_acc, stage, sem = refs[n_parts + n_token_parts:]
+def load_tokens(token_parts, blocks):
     tokens = [part.at[i] for part in token_parts for i in range(part.shape[0])]
-    pairs, side = gathered[0].shape[1:3]
-    row_count = blocks.shape[0] - 1
-    col_count = left_acc.shape[0] - 1
-    rows = blocks.shape[1]
-    share = rows // n_tensor
-    copy = load_ids(gathered, ids_vmem, ids, sem)
-    left_acc[...] = jnp.zeros_like(left_acc)
-    right_acc[...] = jnp.zeros_like(right_acc)
+    row_count, width = blocks.shape[0] - 1, blocks.shape[2]
     for r in range(0, row_count, 2):
-        parts = [tokens[k][:, r * side:(r + 2) * side].astype(F32) for k in range(n_tensor)]
+        parts = [value[:, r * width // 2:(r + 2) * width // 2].astype(F32) for value in tokens]
         blocks[r], blocks[r + 1] = twice(jnp.concatenate(parts, axis=0).astype(BF16))
     blocks[row_count] = jnp.zeros_like(blocks[row_count])
-    low = low_half((rows, 2 * side))
-    copy.wait()
+
+
+def multiply_tokens(count, gathered, ids, blocks, prod):
+    pairs, side = gathered[0].shape[1:3]
+    low = low_half(blocks.shape[1:])
 
     def multiply(part, d, i):
         for k in range(pairs):
@@ -266,6 +204,12 @@
                 lhs, tile = lhs[:, :side], part[d, k]
             prod[i * pairs + k] = jnp.dot(lhs, tile, preferred_element_type=F32)
 
+    over(gathered, multiply)
+
+
+def add_tokens(count, gathered, ids, prod, left_acc, right_acc):
+    pairs, side = gathered[0].shape[1:3]
+
     def add(part, d, i):
         for k in range(pairs):
             value, left = prod[i * pairs + k], ids[1, i, side + k]
@@ -276,17 +220,97 @@
                 right_acc[right] = right_sum
             left_acc[left] = left_sum
 
-    over(gathered, multiply)
     over(gathered, add)
+
+
+def place_outputs(n_tensor, left_acc, right_acc, stage):
+    col_count, rows, width = left_acc.shape[0] - 1, left_acc.shape[1], left_acc.shape[2]
+    share = rows // n_tensor
     me = lax.axis_index("tensor")
-    half = low_half((share, 2 * side))
-    for k in range(n_tensor):
+    half = low_half((share, width))
+    for i, k in enumerate(peer_order(n_tensor)):
         start = pl.multiple_of(lax.bitwise_xor(me, k) * share, share)
-        mine = slice(k * share, (k + 1) * share)
+        mine = slice(i * share, (i + 1) * share)
         for c in range(0, col_count, 2):
             sums = [fold(jnp.where(half, left_acc[c + u, mine, :], right_acc[c + u, mine, :])) for u in range(2)]
-            stage[pl.ds(start, share), c * side:(c + 2) * side] = jnp.where(half, *sums)
+            stage[pl.ds(start, share), c * width // 2:(c + 2) * width // 2] = jnp.where(half, *sums)
+
+
+def forward_kernel(count, n_parts, n_token_parts, n_tensor, *refs):
+    gathered, token_parts = refs[:n_parts], refs[n_parts:n_parts + n_token_parts]
+    out, ids_vmem, ids, blocks, prod, left_acc, right_acc, stage, sem = refs[n_parts + n_token_parts:]
+    copy = load_ids(gathered, ids_vmem, ids, sem)
+    left_acc[...] = jnp.zeros_like(left_acc)
+    right_acc[...] = jnp.zeros_like(right_acc)
+    load_tokens(token_parts, blocks)
+    copy.wait()
+    multiply_tokens(count, gathered, ids, blocks, prod)
+    add_tokens(count, gathered, ids, prod, left_acc, right_acc)
+    place_outputs(n_tensor, left_acc, right_acc, stage)
     out[...] = stage[...].astype(BF16)
+
+
+def last_kernel(count, n_parts, n_token_parts, n_tensor, *refs):
+    gathered, refs = refs[:n_parts], refs[n_parts:]
+    token_parts, refs = refs[:n_token_parts], refs[n_token_parts:]
+    messages, refs = refs[:n_tensor], refs[n_tensor:]
+    (out, grad, ids_vmem, ids, blocks, prod, left_acc, right_acc, stage, out_vmem, grad_vmem), refs = refs[:11], refs[11:]
+    accs, (id_sem, out_sem, grad_sems) = refs[:n_tensor], refs[n_tensor:]
+    pairs, side = gathered[0].shape[1:3]
+    n_dp = ids.shape[1]
+    share, width = grad.shape
+    tiles = slot_tiles(n_dp, pairs)
+    for m, message in enumerate(messages):
+        ids_vmem[2 + m] = message[len(tiles) * share:, :].astype(F32)[:n_dp].astype(I32)
+    copy = load_ids(gathered, ids_vmem, ids, id_sem)
+    for acc in (left_acc, right_acc, *accs):
+        acc[...] = jnp.zeros_like(acc)
+    load_tokens(token_parts, blocks)
+    copy.wait()
+    multiply_tokens(count, gathered, ids, blocks, prod)
+    low = low_half((share, 2 * side))
+    for t in range(0, len(tiles), 2):
+        both = [message[t * share:(t + 2) * share, :].astype(F32) for message in messages]
+        for u in range(2):
+            values = [two[u * share:(u + 1) * share] for two in both]
+            for h, (i, j) in enumerate(tiles[t + u]):
+                rows = [ids[2 + m, i, side + j] for m in range(n_tensor)]
+                halves = [jnp.where(low, 0.0, value) if h else jnp.where(low, value, 0.0) for value in values]
+                sums = [acc[row] + half for acc, row, half in zip(accs, rows, halves)]
+                for acc, row, value in zip(accs, rows, sums):
+                    acc[row] = value
+    add_tokens(count, gathered, ids, prod, left_acc, right_acc)
+    place_outputs(n_tensor, left_acc, right_acc, stage)
+    out_vmem[...] = stage[...].astype(BF16)
+    copies = [pltpu.make_async_copy(out_vmem, out, out_sem)]
+    copies[0].start()
+
+    def total(r):
+        value = accs[0][r]
+        for acc in accs[1:]:
+            value = value + acc[r]
+        return fold(value)
+
+    chunk = width // grad_sems.shape[0]
+    for c in range(grad_sems.shape[0]):
+        for r in range(c * chunk // side, (c + 1) * chunk // side, 2):
+            grad_vmem[:, r * side:(r + 2) * side] = jnp.where(low, total(r), total(r + 1)).astype(BF16)
+        here = slice(c * chunk, (c + 1) * chunk)
+        copies.append(pltpu.make_async_copy(grad_vmem.at[:, here], grad.at[:, here], grad_sems.at[c]))
+        copies[-1].start()
+    for copy in copies:
+        copy.wait()
+
+
+def steps(n):
+    return [n >> i for i in range(1, n.bit_length())]
+
+
+def peer_order(n):
+    order = [0]
+    for k in steps(n):
+        order = order + [i ^ k for i in order]
+    return order
 
 
 def swap(value, axis, n, k):
@@ -296,10 +320,10 @@
 def gather_all(packed, inputs, n_dp, n_tensor):
     if (n_dp, n_tensor) != (8, 4):
         tokens = [inputs[None]]
-        while len(tokens) < n_tensor:
-            tokens = tokens + [swap(value, "tensor", n_tensor, len(tokens)) for value in tokens]
+        for k in steps(n_tensor):
+            tokens = tokens + [swap(value, "tensor", n_tensor, k) for value in tokens]
         return [lax.all_gather(packed, "dp", axis=0, tiled=True)], tokens
-    near_tokens = swap(inputs, "tensor", n_tensor, 1)
+    far_tokens = swap(inputs, "tensor", n_tensor, 2)
     near, second, last = [swap(packed, "dp", n_dp, k) for k in (2, 4, 6)]
     joined, tokens = pl.pallas_call(
         join_kernel,
@@ -310,10 +334,10 @@
         in_specs=[VMEM] * 4,
         out_specs=[VMEM] * 2,
         compiler_params=pltpu.CompilerParams(vmem_limit_bytes=4 * MIB),
-    )(packed, near, inputs, near_tokens)
+    )(packed, near, inputs, far_tokens)
     same_core = [joined, second, last]
     parts = same_core + [swap(part, "dp", n_dp, 1) for part in same_core]
-    return parts, [tokens, swap(tokens, "tensor", n_tensor, 2)]
+    return parts, [tokens, swap(tokens, "tensor", n_tensor, 1)]
 
 
 def on_device(n_dp, n_tensor, inputs, block_values, block_slot, grad_out):
@@ -360,33 +384,50 @@
         scratch_shapes=ids + [cots] + scratch + [pltpu.SemaphoreType.DMA],
         compiler_params=params,
     )(*gathered, grad_out)
-    order = sorted(range(1, n_tensor), key=lambda k: (k != 2, -k))
+    order = range(n_tensor - 1, 0, -1)
     received = {k: swap(partial_sums[k], "tensor", n_tensor, k) for k in order}
     arrived = [partial_sums[0]] + [received[k] for k in order]
+    forward = [
+        pltpu.VMEM((row_count + 1, rows, 2 * side), BF16),
+        pltpu.VMEM((n_dp * pairs, rows, 2 * side), F32),
+        pltpu.VMEM((col_count + 1, rows, 2 * side), F32),
+        pltpu.VMEM((col_count + 1, rows, 2 * side), F32),
+        pltpu.VMEM((rows, hidden), F32),
+    ]
+    if per_slot:
+        return pl.pallas_call(
+            functools.partial(last_kernel, count, n_parts, len(tokens), n_tensor),
+            out_shape=[
+                jax.ShapeDtypeStruct((rows, hidden), BF16),
+                jax.ShapeDtypeStruct((share, width), BF16),
+            ],
+            in_specs=[VMEM] * (n_parts + len(tokens) + n_tensor),
+            out_specs=[HBM] * 2,
+            scratch_shapes=[
+                pltpu.VMEM((2 + n_tensor, n_dp, 2 * side), I32),
+                pltpu.SMEM((2 + n_tensor, n_dp, 2 * side), I32),
+            ] + forward + [
+                pltpu.VMEM((rows, hidden), BF16),
+                pltpu.VMEM((share, width), BF16),
+            ] + [pltpu.VMEM((row_count + 1, share, 2 * side), F32)] * n_tensor + [
+                pltpu.SemaphoreType.DMA,
+                pltpu.SemaphoreType.DMA,
+                pltpu.SemaphoreType.DMA((4,)),
+            ],
+            compiler_params=params,
+        )(*gathered, *tokens, *arrived)
     outputs = pl.pallas_call(
         functools.partial(forward_kernel, count, n_parts, len(tokens), n_tensor),
         out_shape=jax.ShapeDtypeStruct((rows, hidden), BF16),
         in_specs=[VMEM] * (n_parts + len(tokens)),
         out_specs=VMEM,
-        scratch_shapes=ids + [
-            pltpu.VMEM((row_count + 1, rows, 2 * side), BF16),
-            pltpu.VMEM((n_dp * pairs, rows, 2 * side), F32),
-            pltpu.VMEM((col_count + 1, rows, 2 * side), F32),
-            pltpu.VMEM((col_count + 1, rows, 2 * side), F32),
-            pltpu.VMEM((rows, hidden), F32),
-            pltpu.SemaphoreType.DMA,
-        ],
+        scratch_shapes=ids + forward + [pltpu.SemaphoreType.DMA],
         compiler_params=params,
     )(*gathered, *tokens)
-    if per_slot:
-        first_sum = add_slots(arrived[:2], [], (share, width), F32, n_dp, pairs, side, params)
-        grad_in = add_slots(arrived[2:], [first_sum], (share, width), BF16, n_dp, pairs, side, params)
-    else:
-        total = arrived[0].astype(F32)
-        for value in arrived[1:]:
-            total = total + value.astype(F32)
-        grad_in = total.astype(BF16)
-    return (outputs, grad_in)
+    total = arrived[0].astype(F32)
+    for value in arrived[1:]:
+        total = total + value.astype(F32)
+    return (outputs, total.astype(BF16))
 
 
 def solution(mesh):

time: 24.7 us -> 25.9 us (1.049)
  waiting for transfers between devices: 3.61 us -> 6.61 us
  Pallas kernels: 6.84 us -> 4.63 us
  starting transfers between devices: 13.4 us -> 13.8 us
    ppermute x11, waiting for transfers between devices: 3.61 us -> 6.61 us  [swap(): return lax.ppermute(value, axis, [(i, i ^ k) for i in range(n)])]
    pallas_call x3 -> x1, Pallas kernels: 4.58 us -> 2.37 us  [on_device(): pl.pallas_call(functools.partial(last_kernel, count, n_parts, len(tokens)...]
    ppermute x11, starting transfers between devices: 13.4 us -> 13.8 us  [swap(): return lax.ppermute(value, axis, [(i, i ^ k) for i in range(n)])]
  transfers between devices with their start and end apart: 11 -> 11, of which waited for: 6 -> 7; matrix products, arithmetic and copies ran while one was open for 0% -> 0% of each run, Pallas kernels for 21% -> 9%
where the time goes in v11:
time: 25.9 us; the launch traced here: 25.8 us
  starting transfers between devices  13.8 us (53%)
  waiting for transfers between devices  6.61 us (26%)
  Pallas kernels  4.63 us (18%)
  between operations  0.69 us (3%)
    ppermute x11, starting transfers between devices, swap(): return lax.ppermute(value, axis, [(i, i ^ k) for i in range(n)])  13.8 us
    ppermute x11, waiting for transfers between devices, swap(): return lax.ppermute(value, axis, [(i, i ^ k) for i in range(n)])  6.61 us
    pallas_call x1, Pallas kernels, on_device(): pl.pallas_call(functools.partial(last_kernel, count, n_parts, len(tokens)...  2.37 us
    pallas_call x1, Pallas kernels, on_device(): pl.pallas_call(functools.partial(kernel, count, n_parts, n_tensor), out_s...  1.26 us
    pallas_call x1, Pallas kernels, on_device(): pl.pallas_call(functools.partial(pack_kernel, count, row_count, col_count...  0.98 us
  transfers between devices with their start and end apart: 11, of which 7 were waited for; matrix products, arithmetic and copies ran while one was open for 0% of the time, Pallas kernels for 9%

profile of v11, /device:TPU:0, one launch (start us, length us, event | category | flops | bytes accessed | tf_op | source)
XLA Modules:
  0.0 25.8 jit_solution(13774953705387757356)
XLA Ops:
  0.6 0.0 copy-start
  0.6 4.1 %collective-permute-start.1 = (bf16[8,4096]{1,0:T(8,128)(2,1)}, bf16[8,4096]{1,0:T(8,128)(2,1)S(1)}, u32[]{:S(2)}, u32[]{:S(2)}) collective-permute-start(bf16[8,4096]{1,0:T(8,128)(2,1)} %tokens.1), channel_id=1, source_target_pairs={{0,2},{1,3},{2,0},{3,1},{4,6},{5,7},{6,4},{7,5},{8,10},{9,11},{10,... | collective-permute-start | bytes 196616 | tf_op jit(solution)/shard_map/ppermute | solution.py:317
  4.7 1.0 %shard_map.59.own = bf16[1,3,64,128]{3,2,1,0:T(8,128)(2,1)S(1)} custom-call(s32[1,5]{1,0:T(1,128)} %slots_hbm.1, bf16[1,5,64,64]{3,2,1,0:T(8,128)(2,1)} %values_hbm.1), custom_call_target="tpu_custom_call" | custom-call | tf_op jit(solution)/shard_map/pallas_call | solution.py:353
  5.7 0.0 copy-start.1
  5.7 1.6 %collective-permute-start = (bf16[1,3,64,128]{3,2,1,0:T(8,128)(2,1)S(1)}, bf16[1,3,64,128]{3,2,1,0:T(8,128)(2,1)S(1)}, u32[]{:S(2)}, u32[]{:S(2)}) collective-permute-start(bf16[1,3,64,128]{3,2,1,0:T(8,128)(2,1)S(1)} %shard_map.59.own), channel_id=1, source_target_pairs={{0,8},{4,12},{8,0},{12,4},{16,24},{20,28},{24,16},{28,20},{1,9},{5... | collective-permute-start | bytes 147464 | tf_op jit(solution)/shard_map/ppermute | solution.py:317
  7.3 1.5 %collective-permute-start.3 = (bf16[1,3,64,128]{3,2,1,0:T(8,128)(2,1)S(1)}, bf16[1,3,64,128]{3,2,1,0:T(8,128)(2,1)S(1)}, u32[]{:S(2)}, u32[]{:S(2)}) collective-permute-start(bf16[1,3,64,128]{3,2,1,0:T(8,128)(2,1)S(1)} %shard_map.59.own), channel_id=1, source_target_pairs={{0,24},{4,28},{8,16},{12,20},{16,8},{20,12},{24,0},{28,4},{1,25},{... | collective-permute-start | bytes 147464 | tf_op jit(solution)/shard_map/ppermute | solution.py:317
  8.8 0.5 %collective-permute-start.2 = (bf16[1,3,64,128]{3,2,1,0:T(8,128)(2,1)S(1)}, bf16[1,3,64,128]{3,2,1,0:T(8,128)(2,1)S(1)}, u32[]{:S(2)}, u32[]{:S(2)}) collective-permute-start(bf16[1,3,64,128]{3,2,1,0:T(8,128)(2,1)S(1)} %shard_map.59.own), channel_id=1, source_target_pairs={{0,16},{4,20},{8,24},{12,28},{16,0},{20,4},{24,8},{28,12},{1,17},{... | collective-permute-start | bytes 147464 | tf_op jit(solution)/shard_map/ppermute | solution.py:317
  9.3 0.6 %collective-permute-done.near = bf16[1,3,64,128]{3,2,1,0:T(8,128)(2,1)S(1)} collective-permute-done((bf16[1,3,64,128]{3,2,1,0:T(8,128)(2,1)S(1)}, bf16[1,3,64,128]{3,2,1,0:T(8,128)(2,1)S(1)}, u32[]{:S(2)}, u32[]{:S(2)}) %collective-permute-start) | collective-permute-done | bytes 49184 | tf_op jit(solution)/shard_map/ppermute | solution.py:317
  9.9 0.0 collective-permute-done.1.far_tokens
  9.9 0.0 copy-done
  9.9 0.1 collective-permute-start.4
  10.0 1.6 %collective-permute-start.7 = (bf16[2,8,4096]{2,1,0:T(8,128)(2,1)S(1)}, bf16[2,8,4096]{2,1,0:T(8,128)(2,1)S(1)}, u32[]{:S(2)}, u32[]{:S(2)}) collective-permute-start(bf16[2,8,4096]{2,1,0:T(8,128)(2,1)S(1)} %get-tuple-element.9.refs_6_), channel_id=1, source_target_pairs={{0,1},{1,0},{2,3},{3,2},{4,5},{5,4},{6,7},{7,6},{8,9},{9,8},{10,11... | collective-permute-start | bytes 393224 | tf_op jit(solution)/shard_map/ppermute | solution.py:317
  11.6 0.6 %collective-permute-done.3.refs_2_ = bf16[1,3,64,128]{3,2,1,0:T(8,128)(2,1)S(1)} collective-permute-done((bf16[1,3,64,128]{3,2,1,0:T(8,128)(2,1)S(1)}, bf16[1,3,64,128]{3,2,1,0:T(8,128)(2,1)S(1)}, u32[]{:S(2)}, u32[]{:S(2)}) %collective-permute-start.3) | collective-permute-done | bytes 49184 | tf_op jit(solution)/shard_map/ppermute | solution.py:317
  12.3 0.0 collective-permute-start.6
  12.3 0.6 %collective-permute-done.2.refs_1_ = bf16[1,3,64,128]{3,2,1,0:T(8,128)(2,1)S(1)} collective-permute-done((bf16[1,3,64,128]{3,2,1,0:T(8,128)(2,1)S(1)}, bf16[1,3,64,128]{3,2,1,0:T(8,128)(2,1)S(1)}, u32[]{:S(2)}, u32[]{:S(2)}) %collective-permute-start.2) | collective-permute-done | bytes 49184 | tf_op jit(solution)/shard_map/ppermute | solution.py:317
  12.9 0.0 collective-permute-start.5
  12.9 0.6 %collective-permute-done.6.refs_5_ = bf16[1,3,64,128]{3,2,1,0:T(8,128)(2,1)S(1)} collective-permute-done((bf16[1,3,64,128]{3,2,1,0:T(8,128)(2,1)S(1)}, bf16[1,3,64,128]{3,2,1,0:T(8,128)(2,1)S(1)}, u32[]{:S(2)}, u32[]{:S(2)}) %collective-permute-start.6) | collective-permute-done | bytes 49184 | tf_op jit(solution)/shard_map/ppermute | solution.py:317
  13.5 0.6 %collective-permute-done.5.refs_4_ = bf16[1,3,64,128]{3,2,1,0:T(8,128)(2,1)S(1)} collective-permute-done((bf16[1,3,64,128]{3,2,1,0:T(8,128)(2,1)S(1)}, bf16[1,3,64,128]{3,2,1,0:T(8,128)(2,1)S(1)}, u32[]{:S(2)}, u32[]{:S(2)}) %collective-permute-start.5) | collective-permute-done | bytes 49184 | tf_op jit(solution)/shard_map/ppermute | solution.py:317
  14.1 0.0 collective-permute-done.4.refs_3_
  14.1 0.0 copy-done.1
  14.1 1.3 %shard_map.61 = (bf16[176,128]{1,0:T(8,128)(2,1)S(1)}, bf16[176,128]{1,0:T(8,128)(2,1)S(1)}, bf16[176,128]{1,0:T(8,128)(2,1)S(1)}, bf16[176,128]{1,0:T(8,128)(2,1)S(1)}) custom-call(bf16[2,3,64,128]{3,2,1,0:T(8,128)(2,1)S(1)} %get-tuple-element.8.refs_0_, bf16[1,3,64,128]{3,2,1,0:T(8,128)(2,1)S(1)} %collective-permute-done.2.refs_1_, ...), custom_call_target="tpu_custom_call" | custom-call | tf_op jit(solution)/shard_map/pallas_call | solution.py:379
  15.4 1.4 %collective-permute-start.8 = (bf16[176,128]{1,0:T(8,128)(2,1)S(1)}, bf16[176,128]{1,0:T(8,128)(2,1)S(1)}, u32[]{:S(2)}, u32[]{:S(2)}) collective-permute-start(bf16[176,128]{1,0:T(8,128)(2,1)S(1)} %get-tuple-element.11), channel_id=1, source_target_pairs={{0,3},{1,2},{2,1},{3,0},{4,7},{5,6},{6,5},{7,4},{8,11},{9,10},{10,... | collective-permute-start | bytes 135176 | tf_op jit(solution)/shard_map/ppermute | solution.py:317
  16.8 1.7 %collective-permute-start.9 = (bf16[176,128]{1,0:T(8,128)(2,1)S(1)}, bf16[176,128]{1,0:T(8,128)(2,1)S(1)}, u32[]{:S(2)}, u32[]{:S(2)}) collective-permute-start(bf16[176,128]{1,0:T(8,128)(2,1)S(1)} %get-tuple-element.12), channel_id=1, source_target_pairs={{0,2},{1,3},{2,0},{3,1},{4,6},{5,7},{6,4},{7,5},{8,10},{9,11},{10,... | collective-permute-start | bytes 135176 | tf_op jit(solution)/shard_map/ppermute | solution.py:317
  18.5 1.3 %collective-permute-start.10 = (bf16[176,128]{1,0:T(8,128)(2,1)S(1)}, bf16[176,128]{1,0:T(8,128)(2,1)S(1)}, u32[]{:S(2)}, u32[]{:S(2)}) collective-permute-start(bf16[176,128]{1,0:T(8,128)(2,1)S(1)} %get-tuple-element.13), channel_id=1, source_target_pairs={{0,1},{1,0},{2,3},{3,2},{4,5},{5,4},{6,7},{7,6},{8,9},{9,8},{10,11... | collective-permute-start | bytes 135176 | tf_op jit(solution)/shard_map/ppermute | solution.py:317
  19.8 0.0 collective-permute-done.7.refs_7_
  19.8 1.8 %collective-permute-done.8.refs_9_ = bf16[176,128]{1,0:T(8,128)(2,1)S(1)} collective-permute-done((bf16[176,128]{1,0:T(8,128)(2,1)S(1)}, bf16[176,128]{1,0:T(8,128)(2,1)S(1)}, u32[]{:S(2)}, u32[]{:S(2)}) %collective-permute-start.8) | collective-permute-done | bytes 45088 | tf_op jit(solution)/shard_map/ppermute | solution.py:317
  21.6 1.8 %collective-permute-done.9.refs_10_ = bf16[176,128]{1,0:T(8,128)(2,1)S(1)} collective-permute-done((bf16[176,128]{1,0:T(8,128)(2,1)S(1)}, bf16[176,128]{1,0:T(8,128)(2,1)S(1)}, u32[]{:S(2)}, u32[]{:S(2)}) %collective-permute-start.9) | collective-permute-done | bytes 45088 | tf_op jit(solution)/shard_map/ppermute | solution.py:317
  23.4 0.0 collective-permute-done.10.refs_11_
  23.4 2.4 %shard_map.62 = (bf16[32,896]{1,0:T(8,128)(2,1)}, bf16[8,4096]{1,0:T(8,128)(2,1)}) custom-call(bf16[2,3,64,128]{3,2,1,0:T(8,128)(2,1)S(1)} %get-tuple-element.8.refs_0_, bf16[1,3,64,128]{3,2,1,0:T(8,128)(2,1)S(1)} %collective-permute-done.2.refs_1_, bf16[1,3,64,128]{3,2,1,0:T(8,128)(2,1)S(1)} %collective-permute-done.3.refs_2_, ...), custom_call_target="tpu_custom_call" | custom-call | tf_op jit(solution)/shard_map/pallas_call | solution.py:398
  (1 shorter events, 0.0 us)
Async XLA Ops:
  0.6 9.3 %copy-start = (bf16[8,4096]{1,0:T(8,128)(2,1)S(1)}, bf16[8,4096]{1,0:T(8,128)(2,1)}, u32[]{:S(2)}) copy-start(bf16[8,4096]{1,0:T(8,128)(2,1)} %tokens.1) | copy-start | bytes 196612
  0.6 9.3 %collective-permute-start.1 = (bf16[8,4096]{1,0:T(8,128)(2,1)}, bf16[8,4096]{1,0:T(8,128)(2,1)S(1)}, u32[]{:S(2)}, u32[]{:S(2)}) collective-permute-start(bf16[8,4096]{1,0:T(8,128)(2,1)} %tokens.1), channel_id=1, source_target_pairs={{0,2},{1,3},{2,0},{3,1},{4,6},{5,7},{6,4},{7,5},{8,10},{9,11},{10,... | collective-permute-start | bytes 196616 | tf_op jit(solution)/shard_map/ppermute | solution.py:317
  5.7 8.4 %copy-start.1 = (bf16[32,896]{1,0:T(8,128)(2,1)S(1)}, bf16[32,896]{1,0:T(8,128)(2,1)}, u32[]{:S(2)}) copy-start(bf16[32,896]{1,0:T(8,128)(2,1)} %refs_6_.1) | copy-start | bytes 172036
  5.7 4.2 %collective-permute-start = (bf16[1,3,64,128]{3,2,1,0:T(8,128)(2,1)S(1)}, bf16[1,3,64,128]{3,2,1,0:T(8,128)(2,1)S(1)}, u32[]{:S(2)}, u32[]{:S(2)}) collective-permute-start(bf16[1,3,64,128]{3,2,1,0:T(8,128)(2,1)S(1)} %shard_map.59.own), channel_id=1, source_target_pairs={{0,8},{4,12},{8,0},{12,4},{16,24},{20,28},{24,16},{28,20},{1,9},{5... | collective-permute-start | bytes 147464 | tf_op jit(solution)/shard_map/ppermute | solution.py:317
  7.3 5.0 %collective-permute-start.3 = (bf16[1,3,64,128]{3,2,1,0:T(8,128)(2,1)S(1)}, bf16[1,3,64,128]{3,2,1,0:T(8,128)(2,1)S(1)}, u32[]{:S(2)}, u32[]{:S(2)}) collective-permute-start(bf16[1,3,64,128]{3,2,1,0:T(8,128)(2,1)S(1)} %shard_map.59.own), channel_id=1, source_target_pairs={{0,24},{4,28},{8,16},{12,20},{16,8},{20,12},{24,0},{28,4},{1,25},{... | collective-permute-start | bytes 147464 | tf_op jit(solution)/shard_map/ppermute | solution.py:317
  8.8 4.1 %collective-permute-start.2 = (bf16[1,3,64,128]{3,2,1,0:T(8,128)(2,1)S(1)}, bf16[1,3,64,128]{3,2,1,0:T(8,128)(2,1)S(1)}, u32[]{:S(2)}, u32[]{:S(2)}) collective-permute-start(bf16[1,3,64,128]{3,2,1,0:T(8,128)(2,1)S(1)} %shard_map.59.own), channel_id=1, source_target_pairs={{0,16},{4,20},{8,24},{12,28},{16,0},{20,4},{24,8},{28,12},{1,17},{... | collective-permute-start | bytes 147464 | tf_op jit(solution)/shard_map/ppermute | solution.py:317
  9.9 4.2 %collective-permute-start.4 = (bf16[2,3,64,128]{3,2,1,0:T(8,128)(2,1)S(1)}, bf16[2,3,64,128]{3,2,1,0:T(8,128)(2,1)S(1)}, u32[]{:S(2)}, u32[]{:S(2)}) collective-permute-start(bf16[2,3,64,128]{3,2,1,0:T(8,128)(2,1)S(1)} %get-tuple-element.8.refs_0_), channel_id=1, source_target_pairs={{0,4},{4,0},{8,12},{12,8},{16,20},{20,16},{24,28},{28,24},{1,5},{5... | collective-permute-start | bytes 294920 | tf_op jit(solution)/shard_map/ppermute | solution.py:317
  10.0 9.8 %collective-permute-start.7 = (bf16[2,8,4096]{2,1,0:T(8,128)(2,1)S(1)}, bf16[2,8,4096]{2,1,0:T(8,128)(2,1)S(1)}, u32[]{:S(2)}, u32[]{:S(2)}) collective-permute-start(bf16[2,8,4096]{2,1,0:T(8,128)(2,1)S(1)} %get-tuple-element.9.refs_6_), channel_id=1, source_target_pairs={{0,1},{1,0},{2,3},{3,2},{4,5},{5,4},{6,7},{7,6},{8,9},{9,8},{10,11... | collective-permute-start | bytes 393224 | tf_op jit(solution)/shard_map/ppermute | solution.py:317
  12.3 1.2 %collective-permute-start.6 = (bf16[1,3,64,128]{3,2,1,0:T(8,128)(2,1)S(1)}, bf16[1,3,64,128]{3,2,1,0:T(8,128)(2,1)S(1)}, u32[]{:S(2)}, u32[]{:S(2)}) collective-permute-start(bf16[1,3,64,128]{3,2,1,0:T(8,128)(2,1)S(1)} %collective-permute-done.3.refs_2_), channel_id=1, source_target_pairs={{0,4},{4,0},{8,12},{12,8},{16,20},{20,16},{24,28},{28,24},{1,5},{5... | collective-permute-start | bytes 147464 | tf_op jit(solution)/shard_map/ppermute | solution.py:317
  12.9 1.2 %collective-permute-start.5 = (bf16[1,3,64,128]{3,2,1,0:T(8,128)(2,1)S(1)}, bf16[1,3,64,128]{3,2,1,0:T(8,128)(2,1)S(1)}, u32[]{:S(2)}, u32[]{:S(2)}) collective-permute-start(bf16[1,3,64,128]{3,2,1,0:T(8,128)(2,1)S(1)} %collective-permute-done.2.refs_1_), channel_id=1, source_target_pairs={{0,4},{4,0},{8,12},{12,8},{16,20},{20,16},{24,28},{28,24},{1,5},{5... | collective-permute-start | bytes 147464 | tf_op jit(solution)/shard_map/ppermute | solution.py:317
  15.4 6.2 %collective-permute-start.8 = (bf16[176,128]{1,0:T(8,128)(2,1)S(1)}, bf16[176,128]{1,0:T(8,128)(2,1)S(1)}, u32[]{:S(2)}, u32[]{:S(2)}) collective-permute-start(bf16[176,128]{1,0:T(8,128)(2,1)S(1)} %get-tuple-element.11), channel_id=1, source_target_pairs={{0,3},{1,2},{2,1},{3,0},{4,7},{5,6},{6,5},{7,4},{8,11},{9,10},{10,... | collective-permute-start | bytes 135176 | tf_op jit(solution)/shard_map/ppermute | solution.py:317
  16.8 6.6 %collective-permute-start.9 = (bf16[176,128]{1,0:T(8,128)(2,1)S(1)}, bf16[176,128]{1,0:T(8,128)(2,1)S(1)}, u32[]{:S(2)}, u32[]{:S(2)}) collective-permute-start(bf16[176,128]{1,0:T(8,128)(2,1)S(1)} %get-tuple-element.12), channel_id=1, source_target_pairs={{0,2},{1,3},{2,0},{3,1},{4,6},{5,7},{6,4},{7,5},{8,10},{9,11},{10,... | collective-permute-start | bytes 135176 | tf_op jit(solution)/shard_map/ppermute | solution.py:317
  18.5 4.9 %collective-permute-start.10 = (bf16[176,128]{1,0:T(8,128)(2,1)S(1)}, bf16[176,128]{1,0:T(8,128)(2,1)S(1)}, u32[]{:S(2)}, u32[]{:S(2)}) collective-permute-start(bf16[176,128]{1,0:T(8,128)(2,1)S(1)} %get-tuple-element.13), channel_id=1, source_target_pairs={{0,1},{1,0},{2,3},{3,2},{4,5},{5,4},{6,7},{7,6},{8,9},{9,8},{10,11... | collective-permute-start | bytes 135176 | tf_op jit(solution)/shard_map/ppermute | solution.py:317

commit v12 on v11

--- a/solution.py
+++ b/solution.py
@@ -22,17 +22,19 @@
         copy.start()
     side = values.shape[2]
     pairs = packed.shape[1]
+    lane = lax.broadcasted_iota(I32, (16, side), 1)
+    line = lax.broadcasted_iota(I32, (16, side), 0)
     copies[0].wait()
-    lane = lax.broadcasted_iota(I32, (side, side), 1)
-    line = lax.broadcasted_iota(I32, (side, side), 0)
-    head = jnp.zeros((side, side), F32)
+    position = jnp.full((16, side), -1, I32)
     for j in range(count):
-        p = slots[0, j]
-        row = jnp.where(p >= 0, p // col_count, row_count)
-        col = jnp.where(p >= 0, p % col_count, col_count)
-        here = jnp.where(line == 0, row, col).astype(F32)
-        head = jnp.where(lane == j, here, head)
-    head = head.astype(BF16)
+        position = jnp.where(lane == j, slots[0, j], position)
+    exact = position.astype(F32)
+    row = jnp.floor((exact + 0.5) * (1.0 / col_count))
+    col = exact - row * col_count
+    row = jnp.where(position >= 0, row, float(row_count))
+    col = jnp.where(position >= 0, col, float(col_count))
+    head = jnp.where(line == 0, row, col).astype(BF16)
+    head = jnp.concatenate([head, jnp.zeros((side - 16, side), BF16)], axis=0)
     copies[1].wait()
     for k in range(pairs):
         left = values[0, k]
@@ -134,7 +136,7 @@
         prod[t] = across(lhs, blocks[t])
     me = lax.axis_index("tensor")
     for k in range(n_tensor):
-        start = pl.multiple_of(lax.bitwise_xor(me, k) * share, share)
+        start = pl.multiple_of(lax.rem(me + k, n_tensor) * share, share)
         for t in range(0, len(tiles), 2):
             two = [prod[t, pl.ds(start, share), :], prod[t + 1, pl.ds(start, share), :]]
             outs[k][t * share:(t + 2) * share, :] = jnp.concatenate(two, axis=0).astype(BF16)
@@ -174,7 +176,7 @@
     me = lax.axis_index("tensor")
     share = rows // n_tensor
     for k in range(n_tensor):
-        start = pl.multiple_of(lax.bitwise_xor(me, k) * share, share)
+        start = pl.multiple_of(lax.rem(me + k, n_tensor) * share, share)
         half = low_half((share, 2 * side))
         for r in range(0, row_count, 2):
             pair = [fold(acc[r + u, pl.ds(start, share), :]) for u in range(2)]
@@ -250,40 +252,31 @@
     out[...] = stage[...].astype(BF16)
 
 
-def last_kernel(count, n_parts, n_token_parts, n_tensor, *refs):
-    gathered, refs = refs[:n_parts], refs[n_parts:]
-    token_parts, refs = refs[:n_token_parts], refs[n_token_parts:]
+def sum_kernel(n_tensor, pairs, *refs):
     messages, refs = refs[:n_tensor], refs[n_tensor:]
-    (out, grad, ids_vmem, ids, blocks, prod, left_acc, right_acc, stage, out_vmem, grad_vmem), refs = refs[:11], refs[11:]
-    accs, (id_sem, out_sem, grad_sems) = refs[:n_tensor], refs[n_tensor:]
-    pairs, side = gathered[0].shape[1:3]
+    (grad, ids_vmem, ids, grad_vmem, id_sem, grad_sems), accs = refs[:6], refs[6:]
     n_dp = ids.shape[1]
     share, width = grad.shape
+    side = messages[0].shape[1] // 2
     tiles = slot_tiles(n_dp, pairs)
     for m, message in enumerate(messages):
-        ids_vmem[2 + m] = message[len(tiles) * share:, :].astype(F32)[:n_dp].astype(I32)
-    copy = load_ids(gathered, ids_vmem, ids, id_sem)
-    for acc in (left_acc, right_acc, *accs):
+        ids_vmem[m] = message[len(tiles) * share:, :].astype(F32)[:n_dp].astype(I32)
+    copy = pltpu.make_async_copy(ids_vmem, ids, id_sem)
+    copy.start()
+    for acc in accs:
         acc[...] = jnp.zeros_like(acc)
-    load_tokens(token_parts, blocks)
+    low = low_half((share, 2 * side))
     copy.wait()
-    multiply_tokens(count, gathered, ids, blocks, prod)
-    low = low_half((share, 2 * side))
     for t in range(0, len(tiles), 2):
         both = [message[t * share:(t + 2) * share, :].astype(F32) for message in messages]
         for u in range(2):
             values = [two[u * share:(u + 1) * share] for two in both]
             for h, (i, j) in enumerate(tiles[t + u]):
-                rows = [ids[2 + m, i, side + j] for m in range(n_tensor)]
+                rows = [ids[m, i, side + j] for m in range(n_tensor)]
                 halves = [jnp.where(low, 0.0, value) if h else jnp.where(low, value, 0.0) for value in values]
                 sums = [acc[row] + half for acc, row, half in zip(accs, rows, halves)]
                 for acc, row, value in zip(accs, rows, sums):
                     acc[row] = value
-    add_tokens(count, gathered, ids, prod, left_acc, right_acc)
-    place_outputs(n_tensor, left_acc, right_acc, stage)
-    out_vmem[...] = stage[...].astype(BF16)
-    copies = [pltpu.make_async_copy(out_vmem, out, out_sem)]
-    copies[0].start()
 
     def total(r):
         value = accs[0][r]
@@ -291,6 +284,7 @@
             value = value + acc[r]
         return fold(value)
 
+    copies = []
     chunk = width // grad_sems.shape[0]
     for c in range(grad_sems.shape[0]):
         for r in range(c * chunk // side, (c + 1) * chunk // side, 2):
@@ -315,6 +309,10 @@
 
 def swap(value, axis, n, k):
     return lax.ppermute(value, axis, [(i, i ^ k) for i in range(n)])
+
+
+def shift(value, axis, n, k):
+    return lax.ppermute(value, axis, [(i, (i + k) % n) for i in range(n)])
 
 
 def gather_all(packed, inputs, n_dp, n_tensor):
@@ -384,46 +382,38 @@
         scratch_shapes=ids + [cots] + scratch + [pltpu.SemaphoreType.DMA],
         compiler_params=params,
     )(*gathered, grad_out)
-    order = range(n_tensor - 1, 0, -1)
-    received = {k: swap(partial_sums[k], "tensor", n_tensor, k) for k in order}
-    arrived = [partial_sums[0]] + [received[k] for k in order]
-    forward = [
-        pltpu.VMEM((row_count + 1, rows, 2 * side), BF16),
-        pltpu.VMEM((n_dp * pairs, rows, 2 * side), F32),
-        pltpu.VMEM((col_count + 1, rows, 2 * side), F32),
-        pltpu.VMEM((col_count + 1, rows, 2 * side), F32),
-        pltpu.VMEM((rows, hidden), F32),
-    ]
-    if per_slot:
-        return pl.pallas_call(
-            functools.partial(last_kernel, count, n_parts, len(tokens), n_tensor),
-            out_shape=[
-                jax.ShapeDtypeStruct((rows, hidden), BF16),
-                jax.ShapeDtypeStruct((share, width), BF16),
-            ],
-            in_specs=[VMEM] * (n_parts + len(tokens) + n_tensor),
-            out_specs=[HBM] * 2,
-            scratch_shapes=[
-                pltpu.VMEM((2 + n_tensor, n_dp, 2 * side), I32),
-                pltpu.SMEM((2 + n_tensor, n_dp, 2 * side), I32),
-            ] + forward + [
-                pltpu.VMEM((rows, hidden), BF16),
-                pltpu.VMEM((share, width), BF16),
-            ] + [pltpu.VMEM((row_count + 1, share, 2 * side), F32)] * n_tensor + [
-                pltpu.SemaphoreType.DMA,
-                pltpu.SemaphoreType.DMA,
-                pltpu.SemaphoreType.DMA((4,)),
-            ],
-            compiler_params=params,
-        )(*gathered, *tokens, *arrived)
+    arrived = [partial_sums[0]] + [shift(partial_sums[k], "tensor", n_tensor, k) for k in range(1, n_tensor)]
     outputs = pl.pallas_call(
         functools.partial(forward_kernel, count, n_parts, len(tokens), n_tensor),
         out_shape=jax.ShapeDtypeStruct((rows, hidden), BF16),
         in_specs=[VMEM] * (n_parts + len(tokens)),
         out_specs=VMEM,
-        scratch_shapes=ids + forward + [pltpu.SemaphoreType.DMA],
+        scratch_shapes=ids + [
+            pltpu.VMEM((row_count + 1, rows, 2 * side), BF16),
+            pltpu.VMEM((n_dp * pairs, rows, 2 * side), F32),
+            pltpu.VMEM((col_count + 1, rows, 2 * side), F32),
+            pltpu.VMEM((col_count + 1, rows, 2 * side), F32),
+            pltpu.VMEM((rows, hidden), F32),
+            pltpu.SemaphoreType.DMA,
+        ],
         compiler_params=params,
     )(*gathered, *tokens)
+    if per_slot:
+        grad_in = pl.pallas_call(
+            functools.partial(sum_kernel, n_tensor, pairs),
+            out_shape=jax.ShapeDtypeStruct((share, width), BF16),
+            in_specs=[VMEM] * n_tensor,
+            out_specs=HBM,
+            scratch_shapes=[
+                pltpu.VMEM((n_tensor, n_dp, 2 * side), I32),
+                pltpu.SMEM((n_tensor, n_dp, 2 * side), I32),
+                pltpu.VMEM((share, width), BF16),
+                pltpu.SemaphoreType.DMA,
+                pltpu.SemaphoreType.DMA((4,)),
+            ] + [pltpu.VMEM((row_count + 1, share, 2 * side), F32)] * n_tensor,
+            compiler_params=params,
+        )(*arrived)
+        return (outputs, grad_in)
     total = arrived[0].astype(F32)
     for value in arrived[1:]:
         total = total + value.astype(F32)

time: 25.9 us -> 25 us (0.965)
  waiting for transfers between devices: 6.61 us -> 4.73 us
  Pallas kernels: 4.63 us -> 5.97 us
  starting transfers between devices: 13.8 us -> 13.4 us
    ppermute x11 -> x8, starting transfers between devices: 13.8 us -> 9.37 us  [swap(): return lax.ppermute(value, axis, [(i, i ^ k) for i in range(n)])]
    ppermute x0 -> x3, starting transfers between devices: none -> 4.07 us  [shift(): return lax.ppermute(value, axis, [(i, (i + k) % n) for i in range(n)])]
    ppermute x11 -> x8, waiting for transfers between devices: 6.61 us -> 3.07 us  [swap(): return lax.ppermute(value, axis, [(i, i ^ k) for i in range(n)])]
    ppermute x0 -> x3, waiting for transfers between devices: none -> 1.67 us  [shift(): return lax.ppermute(value, axis, [(i, (i + k) % n) for i in range(n)])]
    pallas_call x1 -> x2, Pallas kernels: 2.37 us -> 3.74 us  [the longest x1 1.9 us: on_device(): pl.pallas_call(functools.partial(sum_kernel, n_tensor, pairs), out_shape=...]
  transfers between devices with their start and end apart: 11 -> 11, of which waited for: 7 -> 7; matrix products, arithmetic and copies ran while one was open for 0% -> 0% of each run, Pallas kernels for 9% -> 16%
where the time goes in v12:
time: 25 us; the launch traced here: 24.9 us
  starting transfers between devices  13.4 us (54%)
  Pallas kernels  5.97 us (24%)
  waiting for transfers between devices  4.73 us (19%)
  between operations  0.69 us (3%)
    ppermute x8, starting transfers between devices, swap(): return lax.ppermute(value, axis, [(i, i ^ k) for i in range(n)])  9.37 us
    ppermute x3, starting transfers between devices, shift(): return lax.ppermute(value, axis, [(i, (i + k) % n) for i in range(n)])  4.07 us
    ppermute x8, waiting for transfers between devices, swap(): return lax.ppermute(value, axis, [(i, i ^ k) for i in range(n)])  3.07 us
    pallas_call x1, Pallas kernels, on_device(): pl.pallas_call(functools.partial(sum_kernel, n_tensor, pairs), out_shape=...  1.9 us
    pallas_call x1, Pallas kernels, on_device(): pl.pallas_call(functools.partial(forward_kernel, count, n_parts, len(toke...  1.84 us
    ppermute x3, waiting for transfers between devices, shift(): return lax.ppermute(value, axis, [(i, (i + k) % n) for i in range(n)])  1.67 us
    pallas_call x1, Pallas kernels, on_device(): pl.pallas_call(functools.partial(kernel, count, n_parts, n_tensor), out_s...  1.23 us
    pallas_call x1, Pallas kernels, on_device(): pl.pallas_call(functools.partial(pack_kernel, count, row_count, col_count...  0.98 us
  transfers between devices with their start and end apart: 11, of which 7 were waited for; matrix products, arithmetic and copies ran while one was open for 0% of the time, Pallas kernels for 16%

profile of v12, /device:TPU:0, one launch (start us, length us, event | category | flops | bytes accessed | tf_op | source)
XLA Modules:
  0.0 24.9 jit_solution(14189778872918065899)
XLA Ops:
  0.6 0.0 copy-start
  0.6 4.1 %collective-permute-start.1 = (bf16[8,4096]{1,0:T(8,128)(2,1)}, bf16[8,4096]{1,0:T(8,128)(2,1)S(1)}, u32[]{:S(2)}, u32[]{:S(2)}) collective-permute-start(bf16[8,4096]{1,0:T(8,128)(2,1)} %tokens.1), channel_id=1, source_target_pairs={{0,2},{1,3},{2,0},{3,1},{4,6},{5,7},{6,4},{7,5},{8,10},{9,11},{10,... | collective-permute-start | bytes 196616 | tf_op jit(solution)/shard_map/ppermute | solution.py:311
  4.7 1.0 %shard_map.59.own = bf16[1,3,64,128]{3,2,1,0:T(8,128)(2,1)S(1)} custom-call(s32[1,5]{1,0:T(1,128)} %slots_hbm.1, bf16[1,5,64,64]{3,2,1,0:T(8,128)(2,1)} %values_hbm.1), custom_call_target="tpu_custom_call" | custom-call | tf_op jit(solution)/shard_map/pallas_call | solution.py:351
  5.7 0.0 copy-start.1
  5.7 1.6 %collective-permute-start = (bf16[1,3,64,128]{3,2,1,0:T(8,128)(2,1)S(1)}, bf16[1,3,64,128]{3,2,1,0:T(8,128)(2,1)S(1)}, u32[]{:S(2)}, u32[]{:S(2)}) collective-permute-start(bf16[1,3,64,128]{3,2,1,0:T(8,128)(2,1)S(1)} %shard_map.59.own), channel_id=1, source_target_pairs={{0,8},{4,12},{8,0},{12,4},{16,24},{20,28},{24,16},{28,20},{1,9},{5... | collective-permute-start | bytes 147464 | tf_op jit(solution)/shard_map/ppermute | solution.py:311
  7.3 1.5 %collective-permute-start.3 = (bf16[1,3,64,128]{3,2,1,0:T(8,128)(2,1)S(1)}, bf16[1,3,64,128]{3,2,1,0:T(8,128)(2,1)S(1)}, u32[]{:S(2)}, u32[]{:S(2)}) collective-permute-start(bf16[1,3,64,128]{3,2,1,0:T(8,128)(2,1)S(1)} %shard_map.59.own), channel_id=1, source_target_pairs={{0,24},{4,28},{8,16},{12,20},{16,8},{20,12},{24,0},{28,4},{1,25},{... | collective-permute-start | bytes 147464 | tf_op jit(solution)/shard_map/ppermute | solution.py:311
  8.8 0.5 %collective-permute-start.2 = (bf16[1,3,64,128]{3,2,1,0:T(8,128)(2,1)S(1)}, bf16[1,3,64,128]{3,2,1,0:T(8,128)(2,1)S(1)}, u32[]{:S(2)}, u32[]{:S(2)}) collective-permute-start(bf16[1,3,64,128]{3,2,1,0:T(8,128)(2,1)S(1)} %shard_map.59.own), channel_id=1, source_target_pairs={{0,16},{4,20},{8,24},{12,28},{16,0},{20,4},{24,8},{28,12},{1,17},{... | collective-permute-start | bytes 147464 | tf_op jit(solution)/shard_map/ppermute | solution.py:311
  9.3 0.6 %collective-permute-done.near = bf16[1,3,64,128]{3,2,1,0:T(8,128)(2,1)S(1)} collective-permute-done((bf16[1,3,64,128]{3,2,1,0:T(8,128)(2,1)S(1)}, bf16[1,3,64,128]{3,2,1,0:T(8,128)(2,1)S(1)}, u32[]{:S(2)}, u32[]{:S(2)}) %collective-permute-start) | collective-permute-done | bytes 49184 | tf_op jit(solution)/shard_map/ppermute | solution.py:311
  9.9 0.0 collective-permute-done.1.far_tokens
  9.9 0.0 copy-done
  9.9 0.1 collective-permute-start.4
  10.0 1.6 %collective-permute-start.7 = (bf16[2,8,4096]{2,1,0:T(8,128)(2,1)S(1)}, bf16[2,8,4096]{2,1,0:T(8,128)(2,1)S(1)}, u32[]{:S(2)}, u32[]{:S(2)}) collective-permute-start(bf16[2,8,4096]{2,1,0:T(8,128)(2,1)S(1)} %get-tuple-element.9.refs_6_), channel_id=1, source_target_pairs={{0,1},{1,0},{2,3},{3,2},{4,5},{5,4},{6,7},{7,6},{8,9},{9,8},{10,11... | collective-permute-start | bytes 393224 | tf_op jit(solution)/shard_map/ppermute | solution.py:311
  11.6 0.6 %collective-permute-done.3.refs_2_ = bf16[1,3,64,128]{3,2,1,0:T(8,128)(2,1)S(1)} collective-permute-done((bf16[1,3,64,128]{3,2,1,0:T(8,128)(2,1)S(1)}, bf16[1,3,64,128]{3,2,1,0:T(8,128)(2,1)S(1)}, u32[]{:S(2)}, u32[]{:S(2)}) %collective-permute-start.3) | collective-permute-done | bytes 49184 | tf_op jit(solution)/shard_map/ppermute | solution.py:311
  12.3 0.0 collective-permute-start.6
  12.3 0.6 %collective-permute-done.2.refs_1_ = bf16[1,3,64,128]{3,2,1,0:T(8,128)(2,1)S(1)} collective-permute-done((bf16[1,3,64,128]{3,2,1,0:T(8,128)(2,1)S(1)}, bf16[1,3,64,128]{3,2,1,0:T(8,128)(2,1)S(1)}, u32[]{:S(2)}, u32[]{:S(2)}) %collective-permute-start.2) | collective-permute-done | bytes 49184 | tf_op jit(solution)/shard_map/ppermute | solution.py:311
  12.9 0.0 collective-permute-start.5
  12.9 0.6 %collective-permute-done.6.refs_5_ = bf16[1,3,64,128]{3,2,1,0:T(8,128)(2,1)S(1)} collective-permute-done((bf16[1,3,64,128]{3,2,1,0:T(8,128)(2,1)S(1)}, bf16[1,3,64,128]{3,2,1,0:T(8,128)(2,1)S(1)}, u32[]{:S(2)}, u32[]{:S(2)}) %collective-permute-start.6) | collective-permute-done | bytes 49184 | tf_op jit(solution)/shard_map/ppermute | solution.py:311
  13.5 0.6 %collective-permute-done.5.refs_4_ = bf16[1,3,64,128]{3,2,1,0:T(8,128)(2,1)S(1)} collective-permute-done((bf16[1,3,64,128]{3,2,1,0:T(8,128)(2,1)S(1)}, bf16[1,3,64,128]{3,2,1,0:T(8,128)(2,1)S(1)}, u32[]{:S(2)}, u32[]{:S(2)}) %collective-permute-start.5) | collective-permute-done | bytes 49184 | tf_op jit(solution)/shard_map/ppermute | solution.py:311
  14.1 0.0 collective-permute-done.4.refs_3_
  14.1 0.0 copy-done.1
  14.1 1.2 %shard_map.62 = (bf16[176,128]{1,0:T(8,128)(2,1)S(1)}, bf16[176,128]{1,0:T(8,128)(2,1)S(1)}, bf16[176,128]{1,0:T(8,128)(2,1)S(1)}, bf16[176,128]{1,0:T(8,128)(2,1)S(1)}) custom-call(bf16[2,3,64,128]{3,2,1,0:T(8,128)(2,1)S(1)} %get-tuple-element.8.refs_0_, bf16[1,3,64,128]{3,2,1,0:T(8,128)(2,1)S(1)} %collective-permute-done.2.refs_1_, ...), custom_call_target="tpu_custom_call" | custom-call | tf_op jit(solution)/shard_map/pallas_call | solution.py:377
  15.4 1.6 %collective-permute-start.8 = (bf16[176,128]{1,0:T(8,128)(2,1)S(1)}, bf16[176,128]{1,0:T(8,128)(2,1)S(1)}, u32[]{:S(2)}, u32[]{:S(2)}) collective-permute-start(bf16[176,128]{1,0:T(8,128)(2,1)S(1)} %get-tuple-element.11), channel_id=1, source_target_pairs={{0,1},{1,2},{2,3},{3,0},{4,5},{5,6},{6,7},{7,4},{8,9},{9,10},{10,1... | collective-permute-start | bytes 135176 | tf_op jit(solution)/shard_map/ppermute | solution.py:315
  17.0 0.3 %collective-permute-start.9 = (bf16[176,128]{1,0:T(8,128)(2,1)S(1)}, bf16[176,128]{1,0:T(8,128)(2,1)S(1)}, u32[]{:S(2)}, u32[]{:S(2)}) collective-permute-start(bf16[176,128]{1,0:T(8,128)(2,1)S(1)} %get-tuple-element.12), channel_id=1, source_target_pairs={{0,2},{1,3},{2,0},{3,1},{4,6},{5,7},{6,4},{7,5},{8,10},{9,11},{10,... | collective-permute-start | bytes 135176 | tf_op jit(solution)/shard_map/ppermute | solution.py:315
  17.3 2.1 %collective-permute-start.10 = (bf16[176,128]{1,0:T(8,128)(2,1)S(1)}, bf16[176,128]{1,0:T(8,128)(2,1)S(1)}, u32[]{:S(2)}, u32[]{:S(2)}) collective-permute-start(bf16[176,128]{1,0:T(8,128)(2,1)S(1)} %get-tuple-element.13), channel_id=1, source_target_pairs={{0,3},{1,0},{2,1},{3,2},{4,7},{5,4},{6,5},{7,6},{8,11},{9,8},{10,9... | collective-permute-start | bytes 135176 | tf_op jit(solution)/shard_map/ppermute | solution.py:315
  19.4 0.0 collective-permute-done.7.refs_7_
  19.4 1.8 %shard_map.61 = bf16[32,896]{1,0:T(8,128)(2,1)} custom-call(bf16[2,3,64,128]{3,2,1,0:T(8,128)(2,1)S(1)} %get-tuple-element.8.refs_0_, bf16[1,3,64,128]{3,2,1,0:T(8,128)(2,1)S(1)} %collective-permute-done.2.refs_1_, bf16[1,3,64,128]{3,2,1,0:T(8,128)(2,1)S(1)} %collective-permute-done.3.refs_2_, bf16[2,3,64,128]{3,2,1,0:T(8,128)(2,1)S(1)} %collective-permute-done.4.refs_3_, ...), custom_call_target="tpu_custom_call" | custom-call | tf_op jit(solution)/shard_map/pallas_call | solution.py:386
  21.3 0.2 collective-permute-done.8.refs_1_
  21.5 1.4 %collective-permute-done.9.refs_2_ = bf16[176,128]{1,0:T(8,128)(2,1)S(1)} collective-permute-done((bf16[176,128]{1,0:T(8,128)(2,1)S(1)}, bf16[176,128]{1,0:T(8,128)(2,1)S(1)}, u32[]{:S(2)}, u32[]{:S(2)}) %collective-permute-start.9) | collective-permute-done | bytes 45088 | tf_op jit(solution)/shard_map/ppermute | solution.py:315
  23.0 0.0 collective-permute-done.10.refs_3_
  23.0 1.9 %shard_map.63 = bf16[8,4096]{1,0:T(8,128)(2,1)} custom-call(bf16[176,128]{1,0:T(8,128)(2,1)S(1)} %get-tuple-element.10.refs_0_, bf16[176,128]{1,0:T(8,128)(2,1)S(1)} %collective-permute-done.8.refs_1_, bf16[176,128]{1,0:T(8,128)(2,1)S(1)} %collective-permute-done.9.refs_2_, bf16[176,128]{1,0:T(8,128)(2,1)S(1)} %collective-permute-done.10.refs_3_), custom_call_target="tpu_custom_call" | custom-call | tf_op jit(solution)/shard_map/pallas_call | solution.py:402
  (1 shorter events, 0.0 us)
Async XLA Ops:
  0.6 9.3 %copy-start = (bf16[8,4096]{1,0:T(8,128)(2,1)S(1)}, bf16[8,4096]{1,0:T(8,128)(2,1)}, u32[]{:S(2)}) copy-start(bf16[8,4096]{1,0:T(8,128)(2,1)} %tokens.1) | copy-start | bytes 196612
  0.6 9.3 %collective-permute-start.1 = (bf16[8,4096]{1,0:T(8,128)(2,1)}, bf16[8,4096]{1,0:T(8,128)(2,1)S(1)}, u32[]{:S(2)}, u32[]{:S(2)}) collective-permute-start(bf16[8,4096]{1,0:T(8,128)(2,1)} %tokens.1), channel_id=1, source_target_pairs={{0,2},{1,3},{2,0},{3,1},{4,6},{5,7},{6,4},{7,5},{8,10},{9,11},{10,... | collective-permute-start | bytes 196616 | tf_op jit(solution)/shard_map/ppermute | solution.py:311
  5.7 8.4 %copy-start.1 = (bf16[32,896]{1,0:T(8,128)(2,1)S(1)}, bf16[32,896]{1,0:T(8,128)(2,1)}, u32[]{:S(2)}) copy-start(bf16[32,896]{1,0:T(8,128)(2,1)} %refs_6_.1) | copy-start | bytes 172036
  5.7 4.2 %collective-permute-start = (bf16[1,3,64,128]{3,2,1,0:T(8,128)(2,1)S(1)}, bf16[1,3,64,128]{3,2,1,0:T(8,128)(2,1)S(1)}, u32[]{:S(2)}, u32[]{:S(2)}) collective-permute-start(bf16[1,3,64,128]{3,2,1,0:T(8,128)(2,1)S(1)} %shard_map.59.own), channel_id=1, source_target_pairs={{0,8},{4,12},{8,0},{12,4},{16,24},{20,28},{24,16},{28,20},{1,9},{5... | collective-permute-start | bytes 147464 | tf_op jit(solution)/shard_map/ppermute | solution.py:311
  7.3 5.0 %collective-permute-start.3 = (bf16[1,3,64,128]{3,2,1,0:T(8,128)(2,1)S(1)}, bf16[1,3,64,128]{3,2,1,0:T(8,128)(2,1)S(1)}, u32[]{:S(2)}, u32[]{:S(2)}) collective-permute-start(bf16[1,3,64,128]{3,2,1,0:T(8,128)(2,1)S(1)} %shard_map.59.own), channel_id=1, source_target_pairs={{0,24},{4,28},{8,16},{12,20},{16,8},{20,12},{24,0},{28,4},{1,25},{... | collective-permute-start | bytes 147464 | tf_op jit(solution)/shard_map/ppermute | solution.py:311
  8.8 4.1 %collective-permute-start.2 = (bf16[1,3,64,128]{3,2,1,0:T(8,128)(2,1)S(1)}, bf16[1,3,64,128]{3,2,1,0:T(8,128)(2,1)S(1)}, u32[]{:S(2)}, u32[]{:S(2)}) collective-permute-start(bf16[1,3,64,128]{3,2,1,0:T(8,128)(2,1)S(1)} %shard_map.59.own), channel_id=1, source_target_pairs={{0,16},{4,20},{8,24},{12,28},{16,0},{20,4},{24,8},{28,12},{1,17},{... | collective-permute-start | bytes 147464 | tf_op jit(solution)/shard_map/ppermute | solution.py:311
  9.9 4.2 %collective-permute-start.4 = (bf16[2,3,64,128]{3,2,1,0:T(8,128)(2,1)S(1)}, bf16[2,3,64,128]{3,2,1,0:T(8,128)(2,1)S(1)}, u32[]{:S(2)}, u32[]{:S(2)}) collective-permute-start(bf16[2,3,64,128]{3,2,1,0:T(8,128)(2,1)S(1)} %get-tuple-element.8.refs_0_), channel_id=1, source_target_pairs={{0,4},{4,0},{8,12},{12,8},{16,20},{20,16},{24,28},{28,24},{1,5},{5... | collective-permute-start | bytes 294920 | tf_op jit(solution)/shard_map/ppermute | solution.py:311
  10.0 9.4 %collective-permute-start.7 = (bf16[2,8,4096]{2,1,0:T(8,128)(2,1)S(1)}, bf16[2,8,4096]{2,1,0:T(8,128)(2,1)S(1)}, u32[]{:S(2)}, u32[]{:S(2)}) collective-permute-start(bf16[2,8,4096]{2,1,0:T(8,128)(2,1)S(1)} %get-tuple-element.9.refs_6_), channel_id=1, source_target_pairs={{0,1},{1,0},{2,3},{3,2},{4,5},{5,4},{6,7},{7,6},{8,9},{9,8},{10,11... | collective-permute-start | bytes 393224 | tf_op jit(solution)/shard_map/ppermute | solution.py:311
  12.3 1.2 %collective-permute-start.6 = (bf16[1,3,64,128]{3,2,1,0:T(8,128)(2,1)S(1)}, bf16[1,3,64,128]{3,2,1,0:T(8,128)(2,1)S(1)}, u32[]{:S(2)}, u32[]{:S(2)}) collective-permute-start(bf16[1,3,64,128]{3,2,1,0:T(8,128)(2,1)S(1)} %collective-permute-done.3.refs_2_), channel_id=1, source_target_pairs={{0,4},{4,0},{8,12},{12,8},{16,20},{20,16},{24,28},{28,24},{1,5},{5... | collective-permute-start | bytes 147464 | tf_op jit(solution)/shard_map/ppermute | solution.py:311
  12.9 1.2 %collective-permute-start.5 = (bf16[1,3,64,128]{3,2,1,0:T(8,128)(2,1)S(1)}, bf16[1,3,64,128]{3,2,1,0:T(8,128)(2,1)S(1)}, u32[]{:S(2)}, u32[]{:S(2)}) collective-permute-start(bf16[1,3,64,128]{3,2,1,0:T(8,128)(2,1)S(1)} %collective-permute-done.2.refs_1_), channel_id=1, source_target_pairs={{0,4},{4,0},{8,12},{12,8},{16,20},{20,16},{24,28},{28,24},{1,5},{5... | collective-permute-start | bytes 147464 | tf_op jit(solution)/shard_map/ppermute | solution.py:311
  15.4 6.2 %collective-permute-start.8 = (bf16[176,128]{1,0:T(8,128)(2,1)S(1)}, bf16[176,128]{1,0:T(8,128)(2,1)S(1)}, u32[]{:S(2)}, u32[]{:S(2)}) collective-permute-start(bf16[176,128]{1,0:T(8,128)(2,1)S(1)} %get-tuple-element.11), channel_id=1, source_target_pairs={{0,1},{1,2},{2,3},{3,0},{4,5},{5,6},{6,7},{7,4},{8,9},{9,10},{10,1... | collective-permute-start | bytes 135176 | tf_op jit(solution)/shard_map/ppermute | solution.py:315
  17.0 6.0 %collective-permute-start.9 = (bf16[176,128]{1,0:T(8,128)(2,1)S(1)}, bf16[176,128]{1,0:T(8,128)(2,1)S(1)}, u32[]{:S(2)}, u32[]{:S(2)}) collective-permute-start(bf16[176,128]{1,0:T(8,128)(2,1)S(1)} %get-tuple-element.12), channel_id=1, source_target_pairs={{0,2},{1,3},{2,0},{3,1},{4,6},{5,7},{6,4},{7,5},{8,10},{9,11},{10,... | collective-permute-start | bytes 135176 | tf_op jit(solution)/shard_map/ppermute | solution.py:315
  17.3 5.6 %collective-permute-start.10 = (bf16[176,128]{1,0:T(8,128)(2,1)S(1)}, bf16[176,128]{1,0:T(8,128)(2,1)S(1)}, u32[]{:S(2)}, u32[]{:S(2)}) collective-permute-start(bf16[176,128]{1,0:T(8,128)(2,1)S(1)} %get-tuple-element.13), channel_id=1, source_target_pairs={{0,3},{1,0},{2,1},{3,2},{4,7},{5,4},{6,5},{7,6},{8,11},{9,8},{10,9... | collective-permute-start | bytes 135176 | tf_op jit(solution)/shard_map/ppermute | solution.py:315

commit v13 on v12

--- a/solution.py
+++ b/solution.py
@@ -114,18 +114,23 @@
     cots[col_count] = jnp.zeros_like(cots[col_count])
 
 
-def slots_kernel(count, n_parts, n_tensor, *refs):
-    gathered, cot, outs = refs[:n_parts], refs[n_parts], refs[n_parts + 1:n_parts + 1 + n_tensor]
-    ids_vmem, ids, cots, prod, blocks, sem = refs[n_parts + 1 + n_tensor:]
+def slots_kernel(first, n_parts, n_tensor, *refs):
+    gathered, refs = refs[:n_parts], refs[n_parts:]
+    if first:
+        cot, (*outs, cots), (ids_vmem, ids, prod, blocks, sem) = refs[0], refs[1:n_tensor + 2], refs[n_tensor + 2:]
+        before = []
+    else:
+        cots, before, outs = refs[0], refs[1:n_tensor + 1], refs[n_tensor + 1:2 * n_tensor + 1]
+        ids_vmem, ids, prod, blocks, sem = refs[2 * n_tensor + 1:]
     pairs, side = gathered[0].shape[1:3]
-    rows = cot.shape[0]
+    rows = cots.shape[1]
     share = rows // n_tensor
     copy = load_ids(gathered, ids_vmem, ids, sem)
-    load_cotangent(cot, cots)
+    if first:
+        load_cotangent(cot, cots)
     low = low_half((rows, 2 * side))
-    heads = jnp.concatenate([ids_vmem[0].astype(F32)] * 2, axis=0).astype(BF16)
     where = [(part, d) for part in gathered for d in range(part.shape[0])]
-    tiles = slot_tiles(len(where), pairs)
+    tiles = slot_tiles(len(where), pairs)[-prod.shape[0]:]
     for t, ((i, j), (m, l)) in enumerate(tiles):
         part, d = where[i]
         other, e = where[m]
@@ -135,17 +140,27 @@
         lhs = jnp.where(low, cots[ids[1, i, side + j]], cots[ids[1, m, side + l]])
         prod[t] = across(lhs, blocks[t])
     me = lax.axis_index("tensor")
+    begin = 0
+    if not first:
+        begin = before[0].shape[0]
+        heads = jnp.concatenate([ids_vmem[0].astype(F32)] * 2, axis=0).astype(BF16)
+        for k in range(n_tensor):
+            outs[k][:begin, :] = before[k][...]
+            outs[k][begin + len(tiles) * share:, :] = heads
     for k in range(n_tensor):
         start = pl.multiple_of(lax.rem(me + k, n_tensor) * share, share)
         for t in range(0, len(tiles), 2):
             two = [prod[t, pl.ds(start, share), :], prod[t + 1, pl.ds(start, share), :]]
-            outs[k][t * share:(t + 2) * share, :] = jnp.concatenate(two, axis=0).astype(BF16)
-        outs[k][len(tiles) * share:, :] = heads
+            here = slice(begin + t * share, begin + (t + 2) * share)
+            outs[k][here, :] = jnp.concatenate(two, axis=0).astype(BF16)
 
 
 def slot_tiles(n, pairs):
-    full = [((i, j), (i, j + pairs)) for i in range(n) for j in range(pairs - 1)]
-    return full + [((i, pairs - 1), (i + 1, pairs - 1)) for i in range(0, n, 2)]
+    tiles = []
+    for i in range(0, n, 4):
+        tiles += [((m, j), (m, j + pairs)) for m in range(i, i + 4) for j in range(pairs - 1)]
+        tiles += [((m, pairs - 1), (m + 1, pairs - 1)) for m in range(i, i + 4, 2)]
+    return tiles
 
 
 def rows_kernel(count, n_parts, n_tensor, *refs):
@@ -252,15 +267,25 @@
     out[...] = stage[...].astype(BF16)
 
 
-def sum_kernel(n_tensor, pairs, *refs):
-    messages, refs = refs[:n_tensor], refs[n_tensor:]
+def sum_kernel(sizes, pairs, *refs):
+    groups = []
+    for size in sizes:
+        groups, refs = groups + [refs[:size]], refs[size:]
+    n_tensor = len(groups)
     (grad, ids_vmem, ids, grad_vmem, id_sem, grad_sems), accs = refs[:6], refs[6:]
     n_dp = ids.shape[1]
     share, width = grad.shape
-    side = messages[0].shape[1] // 2
+    side = groups[0][0].shape[1] // 2
     tiles = slot_tiles(n_dp, pairs)
-    for m, message in enumerate(messages):
-        ids_vmem[m] = message[len(tiles) * share:, :].astype(F32)[:n_dp].astype(I32)
+
+    def load(group, start, stop):
+        value = group[0][start:stop, :].astype(F32)
+        for message in group[1:]:
+            value = value + message[start:stop, :].astype(F32)
+        return value
+
+    for m, group in enumerate(groups):
+        ids_vmem[m] = load(group, len(tiles) * share, groups[0][0].shape[0])[:n_dp].astype(I32)
     copy = pltpu.make_async_copy(ids_vmem, ids, id_sem)
     copy.start()
     for acc in accs:
@@ -268,7 +293,7 @@
     low = low_half((share, 2 * side))
     copy.wait()
     for t in range(0, len(tiles), 2):
-        both = [message[t * share:(t + 2) * share, :].astype(F32) for message in messages]
+        both = [load(group, t * share, (t + 2) * share) for group in groups]
         for u in range(2):
             values = [two[u * share:(u + 1) * share] for two in both]
             for h, (i, j) in enumerate(tiles[t + u]):
@@ -366,23 +391,48 @@
     gathered, tokens = gather_all(packed, inputs, n_dp, n_tensor)
     n_parts = len(gathered)
     ids = [pltpu.VMEM((2, n_dp, 2 * side), I32), pltpu.SMEM((2, n_dp, 2 * side), I32)]
-    cots = pltpu.VMEM((col_count + 1, rows, 2 * side), BF16)
-    tiles = len(slot_tiles(n_dp, pairs))
+    cots = (col_count + 1, rows, 2 * side)
     if per_slot:
-        kernel, shape = slots_kernel, (tiles * share + 2 * n_dp, 2 * side)
-        scratch = [pltpu.VMEM((tiles, rows, 2 * side), F32), pltpu.VMEM((tiles, 2 * side, 2 * side), BF16)]
+        half, tiles = n_parts // 2, len(slot_tiles(n_dp, pairs)) // 2
+        scratch = [
+            pltpu.VMEM((tiles, rows, 2 * side), F32),
+            pltpu.VMEM((tiles, 2 * side, 2 * side), BF16),
+            pltpu.SemaphoreType.DMA,
+        ]
+        *first_slots, cotangent = pl.pallas_call(
+            functools.partial(slots_kernel, True, half, n_tensor),
+            out_shape=[pltpu.VMEM((tiles * share, 2 * side), BF16)] * n_tensor + [pltpu.VMEM(cots, BF16)],
+            in_specs=[VMEM] * (half + 1),
+            out_specs=[VMEM] * (n_tensor + 1),
+            scratch_shapes=[
+                pltpu.VMEM((2, n_dp // 2, 2 * side), I32),
+                pltpu.SMEM((2, n_dp // 2, 2 * side), I32),
+            ] + scratch,
+            compiler_params=params,
+        )(*gathered[:half], grad_out)
+        partial_sums = pl.pallas_call(
+            functools.partial(slots_kernel, False, n_parts, n_tensor),
+            out_shape=[pltpu.VMEM((2 * tiles * share + 2 * n_dp, 2 * side), BF16)] * n_tensor,
+            in_specs=[VMEM] * (n_parts + 1 + n_tensor),
+            out_specs=[VMEM] * n_tensor,
+            scratch_shapes=ids + scratch,
+            compiler_params=params,
+        )(*gathered, cotangent, *first_slots)
+        groups = [[partial_sums[0]]] + [[shift(partial_sums[k], "tensor", n_tensor, k)] for k in (2, 1, 3)]
     else:
-        kernel, shape = rows_kernel, (share, width)
-        scratch = [pltpu.VMEM((row_count + 1, rows, 2 * side), F32)]
-    partial_sums = pl.pallas_call(
-        functools.partial(kernel, count, n_parts, n_tensor),
-        out_shape=[jax.ShapeDtypeStruct(shape, BF16)] * n_tensor,
-        in_specs=[VMEM] * (n_parts + 1),
-        out_specs=[VMEM] * n_tensor,
-        scratch_shapes=ids + [cots] + scratch + [pltpu.SemaphoreType.DMA],
-        compiler_params=params,
-    )(*gathered, grad_out)
-    arrived = [partial_sums[0]] + [shift(partial_sums[k], "tensor", n_tensor, k) for k in range(1, n_tensor)]
+        partial_sums = pl.pallas_call(
+            functools.partial(rows_kernel, count, n_parts, n_tensor),
+            out_shape=[jax.ShapeDtypeStruct((share, width), BF16)] * n_tensor,
+            in_specs=[VMEM] * (n_parts + 1),
+            out_specs=[VMEM] * n_tensor,
+            scratch_shapes=ids + [
+                pltpu.VMEM(cots, BF16),
+                pltpu.VMEM((row_count + 1, rows, 2 * side), F32),
+                pltpu.SemaphoreType.DMA,
+            ],
+            compiler_params=params,
+        )(*gathered, grad_out)
+        arrived = [partial_sums[0]] + [shift(partial_sums[k], "tensor", n_tensor, k) for k in range(1, n_tensor)]
     outputs = pl.pallas_call(
         functools.partial(forward_kernel, count, n_parts, len(tokens), n_tensor),
         out_shape=jax.ShapeDtypeStruct((rows, hidden), BF16),
@@ -400,9 +450,9 @@
     )(*gathered, *tokens)
     if per_slot:
         grad_in = pl.pallas_call(
-            functools.partial(sum_kernel, n_tensor, pairs),
+            functools.partial(sum_kernel, tuple(map(len, groups)), pairs),
             out_shape=jax.ShapeDtypeStruct((share, width), BF16),
-            in_specs=[VMEM] * n_tensor,
+            in_specs=[VMEM] * sum(map(len, groups)),
             out_specs=HBM,
             scratch_shapes=[
                 pltpu.VMEM((n_tensor, n_dp, 2 * side), I32),
@@ -412,7 +462,7 @@
                 pltpu.SemaphoreType.DMA((4,)),
             ] + [pltpu.VMEM((row_count + 1, share, 2 * side), F32)] * n_tensor,
             compiler_params=params,
-        )(*arrived)
+        )(*(message for group in groups for message in group))
         return (outputs, grad_in)
     total = arrived[0].astype(F32)
     for value in arrived[1:]:

time: 25 us -> 24.5 us (0.980)
  waiting for transfers between devices: 4.73 us -> 3.34 us
  Pallas kernels: 5.97 us -> 6.7 us
    ppermute x8, waiting for transfers between devices: 3.07 us -> 2.09 us  [swap(): return lax.ppermute(value, axis, [(i, i ^ k) for i in range(n)])]
    pallas_call x2 -> x3, Pallas kernels: 3.13 us -> 3.87 us  [the longest x1 1.9 us: on_device(): pl.pallas_call(functools.partial(sum_kernel, tuple(map(len, groups)), pai...]
    ppermute x3, waiting for transfers between devices: 1.67 us -> 1.24 us  [shift(): return lax.ppermute(value, axis, [(i, (i + k) % n) for i in range(n)])]
  transfers between devices with their start and end apart: 11 -> 11, of which waited for: 7 -> 6; matrix products, arithmetic and copies ran while one was open for 0% -> 0% of each run, Pallas kernels for 16% -> 20%
where the time goes in v13:
time: 24.5 us; the launch traced here: 24.4 us
  starting transfers between devices  13.6 us (56%)
  Pallas kernels  6.7 us (27%)
  waiting for transfers between devices  3.34 us (14%)
  between operations  0.71 us (3%)
    ppermute x8, starting transfers between devices, swap(): return lax.ppermute(value, axis, [(i, i ^ k) for i in range(n)])  9.37 us
    ppermute x3, starting transfers between devices, shift(): return lax.ppermute(value, axis, [(i, (i + k) % n) for i in range(n)])  4.22 us
    ppermute x8, waiting for transfers between devices, swap(): return lax.ppermute(value, axis, [(i, i ^ k) for i in range(n)])  2.09 us
    pallas_call x1, Pallas kernels, on_device(): pl.pallas_call(functools.partial(sum_kernel, tuple(map(len, groups)), pai...  1.9 us
    pallas_call x1, Pallas kernels, on_device(): pl.pallas_call(functools.partial(forward_kernel, count, n_parts, len(toke...  1.83 us
    ppermute x3, waiting for transfers between devices, shift(): return lax.ppermute(value, axis, [(i, (i + k) % n) for i in range(n)])  1.24 us
    pallas_call x1, Pallas kernels, on_device(): pl.pallas_call(functools.partial(slots_kernel, False, n_parts, n_tensor),...  1.02 us
    pallas_call x1, Pallas kernels, on_device(): pl.pallas_call(functools.partial(pack_kernel, count, row_count, col_count...  0.98 us
  transfers between devices with their start and end apart: 11, of which 6 were waited for; matrix products, arithmetic and copies ran while one was open for 0% of the time, Pallas kernels for 20%

profile of v13, /device:TPU:0, one launch (start us, length us, event | category | flops | bytes accessed | tf_op | source)
XLA Modules:
  0.0 24.4 jit_solution(8544993629773876855)
XLA Ops:
  0.6 0.0 copy-start
  0.6 4.1 %collective-permute-start.1 = (bf16[8,4096]{1,0:T(8,128)(2,1)}, bf16[8,4096]{1,0:T(8,128)(2,1)S(1)}, u32[]{:S(2)}, u32[]{:S(2)}) collective-permute-start(bf16[8,4096]{1,0:T(8,128)(2,1)} %tokens.1), channel_id=1, source_target_pairs={{0,2},{1,3},{2,0},{3,1},{4,6},{5,7},{6,4},{7,5},{8,10},{9,11},{10,... | collective-permute-start | bytes 196616 | tf_op jit(solution)/shard_map/ppermute | solution.py:336
  4.7 1.0 %shard_map.59.own = bf16[1,3,64,128]{3,2,1,0:T(8,128)(2,1)S(1)} custom-call(s32[1,5]{1,0:T(1,128)} %slots_hbm.1, bf16[1,5,64,64]{3,2,1,0:T(8,128)(2,1)} %values_hbm.1), custom_call_target="tpu_custom_call" | custom-call | tf_op jit(solution)/shard_map/pallas_call | solution.py:376
  5.7 0.0 copy-start.1
  5.7 1.6 %collective-permute-start = (bf16[1,3,64,128]{3,2,1,0:T(8,128)(2,1)S(1)}, bf16[1,3,64,128]{3,2,1,0:T(8,128)(2,1)S(1)}, u32[]{:S(2)}, u32[]{:S(2)}) collective-permute-start(bf16[1,3,64,128]{3,2,1,0:T(8,128)(2,1)S(1)} %shard_map.59.own), channel_id=1, source_target_pairs={{0,8},{4,12},{8,0},{12,4},{16,24},{20,28},{24,16},{28,20},{1,9},{5... | collective-permute-start | bytes 147464 | tf_op jit(solution)/shard_map/ppermute | solution.py:336
  7.3 1.5 %collective-permute-start.3 = (bf16[1,3,64,128]{3,2,1,0:T(8,128)(2,1)S(1)}, bf16[1,3,64,128]{3,2,1,0:T(8,128)(2,1)S(1)}, u32[]{:S(2)}, u32[]{:S(2)}) collective-permute-start(bf16[1,3,64,128]{3,2,1,0:T(8,128)(2,1)S(1)} %shard_map.59.own), channel_id=1, source_target_pairs={{0,24},{4,28},{8,16},{12,20},{16,8},{20,12},{24,0},{28,4},{1,25},{... | collective-permute-start | bytes 147464 | tf_op jit(solution)/shard_map/ppermute | solution.py:336
  8.8 0.5 %collective-permute-start.2 = (bf16[1,3,64,128]{3,2,1,0:T(8,128)(2,1)S(1)}, bf16[1,3,64,128]{3,2,1,0:T(8,128)(2,1)S(1)}, u32[]{:S(2)}, u32[]{:S(2)}) collective-permute-start(bf16[1,3,64,128]{3,2,1,0:T(8,128)(2,1)S(1)} %shard_map.59.own), channel_id=1, source_target_pairs={{0,16},{4,20},{8,24},{12,28},{16,0},{20,4},{24,8},{28,12},{1,17},{... | collective-permute-start | bytes 147464 | tf_op jit(solution)/shard_map/ppermute | solution.py:336
  9.3 0.6 %collective-permute-done.near = bf16[1,3,64,128]{3,2,1,0:T(8,128)(2,1)S(1)} collective-permute-done((bf16[1,3,64,128]{3,2,1,0:T(8,128)(2,1)S(1)}, bf16[1,3,64,128]{3,2,1,0:T(8,128)(2,1)S(1)}, u32[]{:S(2)}, u32[]{:S(2)}) %collective-permute-start) | collective-permute-done | bytes 49184 | tf_op jit(solution)/shard_map/ppermute | solution.py:336
  9.9 0.0 collective-permute-done.1.far_tokens
  9.9 0.0 copy-done
  9.9 0.1 collective-permute-start.4
  10.0 1.6 %collective-permute-start.7 = (bf16[2,8,4096]{2,1,0:T(8,128)(2,1)S(1)}, bf16[2,8,4096]{2,1,0:T(8,128)(2,1)S(1)}, u32[]{:S(2)}, u32[]{:S(2)}) collective-permute-start(bf16[2,8,4096]{2,1,0:T(8,128)(2,1)S(1)} %get-tuple-element.14.refs_6_), channel_id=1, source_target_pairs={{0,1},{1,0},{2,3},{3,2},{4,5},{5,4},{6,7},{7,6},{8,9},{9,8},{10,11... | collective-permute-start | bytes 393224 | tf_op jit(solution)/shard_map/ppermute | solution.py:336
  11.6 0.6 %collective-permute-done.3.refs_2_ = bf16[1,3,64,128]{3,2,1,0:T(8,128)(2,1)S(1)} collective-permute-done((bf16[1,3,64,128]{3,2,1,0:T(8,128)(2,1)S(1)}, bf16[1,3,64,128]{3,2,1,0:T(8,128)(2,1)S(1)}, u32[]{:S(2)}, u32[]{:S(2)}) %collective-permute-start.3) | collective-permute-done | bytes 49184 | tf_op jit(solution)/shard_map/ppermute | solution.py:336
  12.3 0.0 collective-permute-start.6
  12.3 0.6 %collective-permute-done.2.refs_1_ = bf16[1,3,64,128]{3,2,1,0:T(8,128)(2,1)S(1)} collective-permute-done((bf16[1,3,64,128]{3,2,1,0:T(8,128)(2,1)S(1)}, bf16[1,3,64,128]{3,2,1,0:T(8,128)(2,1)S(1)}, u32[]{:S(2)}, u32[]{:S(2)}) %collective-permute-start.2) | collective-permute-done | bytes 49184 | tf_op jit(solution)/shard_map/ppermute | solution.py:336
  12.9 0.0 collective-permute-start.5
  12.9 0.0 copy-done.1
  12.9 1.0 %shard_map.62 = (bf16[80,128]{1,0:T(8,128)(2,1)S(1)}, bf16[80,128]{1,0:T(8,128)(2,1)S(1)}, bf16[80,128]{1,0:T(8,128)(2,1)S(1)}, bf16[80,128]{1,0:T(8,128)(2,1)S(1)}, bf16[15,32,128]{2,1,0:T(8,128)(2,1)S(1)}) custom-call(bf16[2,3,64,128]{3,2,1,0:T(8,128)(2,1)S(1)} %get-tuple-element.13.refs_0_, bf16[1,3,64,128]{3,2,1,0:T(8,128)(2,1)S(1)} %collective-permute-done.2.refs_1_, ...), custom_call_target="tpu_custom_call" | custom-call | tf_op jit(solution)/shard_map/pallas_call | solution.py:402
  13.9 0.0 collective-permute-done.6.refs_5_
  13.9 0.3 %collective-permute-done.5.refs_4_ = bf16[1,3,64,128]{3,2,1,0:T(8,128)(2,1)S(1)} collective-permute-done((bf16[1,3,64,128]{3,2,1,0:T(8,128)(2,1)S(1)}, bf16[1,3,64,128]{3,2,1,0:T(8,128)(2,1)S(1)}, u32[]{:S(2)}, u32[]{:S(2)}) %collective-permute-start.5) | collective-permute-done | bytes 49184 | tf_op jit(solution)/shard_map/ppermute | solution.py:336
  14.1 0.0 collective-permute-done.4.refs_3_
  14.1 1.0 %shard_map.63 = (bf16[176,128]{1,0:T(8,128)(2,1)S(1)}, bf16[176,128]{1,0:T(8,128)(2,1)S(1)}, bf16[176,128]{1,0:T(8,128)(2,1)S(1)}, bf16[176,128]{1,0:T(8,128)(2,1)S(1)}) custom-call(bf16[2,3,64,128]{3,2,1,0:T(8,128)(2,1)S(1)} %get-tuple-element.13.refs_0_, bf16[1,3,64,128]{3,2,1,0:T(8,128)(2,1)S(1)} %collective-permute-done.2.refs_1_, ...), custom_call_target="tpu_custom_call" | custom-call | tf_op jit(solution)/shard_map/pallas_call | solution.py:413
  15.1 0.4 %collective-permute-start.8 = (bf16[176,128]{1,0:T(8,128)(2,1)S(1)}, bf16[176,128]{1,0:T(8,128)(2,1)S(1)}, u32[]{:S(2)}, u32[]{:S(2)}) collective-permute-start(bf16[176,128]{1,0:T(8,128)(2,1)S(1)} %get-tuple-element.21), channel_id=1, source_target_pairs={{0,2},{1,3},{2,0},{3,1},{4,6},{5,7},{6,4},{7,5},{8,10},{9,11},{10,... | collective-permute-start | bytes 135176 | tf_op jit(solution)/shard_map/ppermute | solution.py:340
  15.5 1.6 %collective-permute-start.9 = (bf16[176,128]{1,0:T(8,128)(2,1)S(1)}, bf16[176,128]{1,0:T(8,128)(2,1)S(1)}, u32[]{:S(2)}, u32[]{:S(2)}) collective-permute-start(bf16[176,128]{1,0:T(8,128)(2,1)S(1)} %get-tuple-element.22), channel_id=1, source_target_pairs={{0,1},{1,2},{2,3},{3,0},{4,5},{5,6},{6,7},{7,4},{8,9},{9,10},{10,1... | collective-permute-start | bytes 135176 | tf_op jit(solution)/shard_map/ppermute | solution.py:340
  17.1 2.2 %collective-permute-start.10 = (bf16[176,128]{1,0:T(8,128)(2,1)S(1)}, bf16[176,128]{1,0:T(8,128)(2,1)S(1)}, u32[]{:S(2)}, u32[]{:S(2)}) collective-permute-start(bf16[176,128]{1,0:T(8,128)(2,1)S(1)} %get-tuple-element.23), channel_id=1, source_target_pairs={{0,3},{1,0},{2,1},{3,2},{4,7},{5,4},{6,5},{7,6},{8,11},{9,8},{10,9... | collective-permute-start | bytes 135176 | tf_op jit(solution)/shard_map/ppermute | solution.py:340
  19.4 0.0 collective-permute-done.7.refs_7_
  19.4 1.8 %shard_map.61 = bf16[32,896]{1,0:T(8,128)(2,1)} custom-call(bf16[2,3,64,128]{3,2,1,0:T(8,128)(2,1)S(1)} %get-tuple-element.13.refs_0_, bf16[1,3,64,128]{3,2,1,0:T(8,128)(2,1)S(1)} %collective-permute-done.2.refs_1_, bf16[1,3,64,128]{3,2,1,0:T(8,128)(2,1)S(1)} %collective-permute-done.3.refs_2_, bf16[2,3,64,128]{3,2,1,0:T(8,128)(2,1)S(1)} %collective-permute-done.4.refs_3_, ...), custom_call_target="tpu_custom_call" | custom-call | tf_op jit(solution)/shard_map/pallas_call | solution.py:436
  21.2 0.6 %collective-permute-done.8.refs_1_ = bf16[176,128]{1,0:T(8,128)(2,1)S(1)} collective-permute-done((bf16[176,128]{1,0:T(8,128)(2,1)S(1)}, bf16[176,128]{1,0:T(8,128)(2,1)S(1)}, u32[]{:S(2)}, u32[]{:S(2)}) %collective-permute-start.8) | collective-permute-done | bytes 45088 | tf_op jit(solution)/shard_map/ppermute | solution.py:340
  21.9 0.6 %collective-permute-done.9.refs_2_ = bf16[176,128]{1,0:T(8,128)(2,1)S(1)} collective-permute-done((bf16[176,128]{1,0:T(8,128)(2,1)S(1)}, bf16[176,128]{1,0:T(8,128)(2,1)S(1)}, u32[]{:S(2)}, u32[]{:S(2)}) %collective-permute-start.9) | collective-permute-done | bytes 45088 | tf_op jit(solution)/shard_map/ppermute | solution.py:340
  22.5 0.0 collective-permute-done.10.refs_3_
  22.5 1.9 %shard_map.64 = bf16[8,4096]{1,0:T(8,128)(2,1)} custom-call(bf16[176,128]{1,0:T(8,128)(2,1)S(1)} %get-tuple-element.20.refs_0_, bf16[176,128]{1,0:T(8,128)(2,1)S(1)} %collective-permute-done.8.refs_1_, bf16[176,128]{1,0:T(8,128)(2,1)S(1)} %collective-permute-done.9.refs_2_, bf16[176,128]{1,0:T(8,128)(2,1)S(1)} %collective-permute-done.10.refs_3_), custom_call_target="tpu_custom_call" | custom-call | tf_op jit(solution)/shard_map/pallas_call | solution.py:452
  (1 shorter events, 0.0 us)
Async XLA Ops:
  0.6 9.3 %copy-start = (bf16[8,4096]{1,0:T(8,128)(2,1)S(1)}, bf16[8,4096]{1,0:T(8,128)(2,1)}, u32[]{:S(2)}) copy-start(bf16[8,4096]{1,0:T(8,128)(2,1)} %tokens.1) | copy-start | bytes 196612
  0.6 9.3 %collective-permute-start.1 = (bf16[8,4096]{1,0:T(8,128)(2,1)}, bf16[8,4096]{1,0:T(8,128)(2,1)S(1)}, u32[]{:S(2)}, u32[]{:S(2)}) collective-permute-start(bf16[8,4096]{1,0:T(8,128)(2,1)} %tokens.1), channel_id=1, source_target_pairs={{0,2},{1,3},{2,0},{3,1},{4,6},{5,7},{6,4},{7,5},{8,10},{9,11},{10,... | collective-permute-start | bytes 196616 | tf_op jit(solution)/shard_map/ppermute | solution.py:336
  5.7 7.2 %copy-start.1 = (bf16[32,896]{1,0:T(8,128)(2,1)S(1)}, bf16[32,896]{1,0:T(8,128)(2,1)}, u32[]{:S(2)}) copy-start(bf16[32,896]{1,0:T(8,128)(2,1)} %refs_3_.1) | copy-start | bytes 172036
  5.7 4.2 %collective-permute-start = (bf16[1,3,64,128]{3,2,1,0:T(8,128)(2,1)S(1)}, bf16[1,3,64,128]{3,2,1,0:T(8,128)(2,1)S(1)}, u32[]{:S(2)}, u32[]{:S(2)}) collective-permute-start(bf16[1,3,64,128]{3,2,1,0:T(8,128)(2,1)S(1)} %shard_map.59.own), channel_id=1, source_target_pairs={{0,8},{4,12},{8,0},{12,4},{16,24},{20,28},{24,16},{28,20},{1,9},{5... | collective-permute-start | bytes 147464 | tf_op jit(solution)/shard_map/ppermute | solution.py:336
  7.3 5.0 %collective-permute-start.3 = (bf16[1,3,64,128]{3,2,1,0:T(8,128)(2,1)S(1)}, bf16[1,3,64,128]{3,2,1,0:T(8,128)(2,1)S(1)}, u32[]{:S(2)}, u32[]{:S(2)}) collective-permute-start(bf16[1,3,64,128]{3,2,1,0:T(8,128)(2,1)S(1)} %shard_map.59.own), channel_id=1, source_target_pairs={{0,24},{4,28},{8,16},{12,20},{16,8},{20,12},{24,0},{28,4},{1,25},{... | collective-permute-start | bytes 147464 | tf_op jit(solution)/shard_map/ppermute | solution.py:336
  8.8 4.1 %collective-permute-start.2 = (bf16[1,3,64,128]{3,2,1,0:T(8,128)(2,1)S(1)}, bf16[1,3,64,128]{3,2,1,0:T(8,128)(2,1)S(1)}, u32[]{:S(2)}, u32[]{:S(2)}) collective-permute-start(bf16[1,3,64,128]{3,2,1,0:T(8,128)(2,1)S(1)} %shard_map.59.own), channel_id=1, source_target_pairs={{0,16},{4,20},{8,24},{12,28},{16,0},{20,4},{24,8},{28,12},{1,17},{... | collective-permute-start | bytes 147464 | tf_op jit(solution)/shard_map/ppermute | solution.py:336
  9.9 4.2 %collective-permute-start.4 = (bf16[2,3,64,128]{3,2,1,0:T(8,128)(2,1)S(1)}, bf16[2,3,64,128]{3,2,1,0:T(8,128)(2,1)S(1)}, u32[]{:S(2)}, u32[]{:S(2)}) collective-permute-start(bf16[2,3,64,128]{3,2,1,0:T(8,128)(2,1)S(1)} %get-tuple-element.13.refs_0_), channel_id=1, source_target_pairs={{0,4},{4,0},{8,12},{12,8},{16,20},{20,16},{24,28},{28,24},{1,5},{5... | collective-permute-start | bytes 294920 | tf_op jit(solution)/shard_map/ppermute | solution.py:336
  10.0 9.4 %collective-permute-start.7 = (bf16[2,8,4096]{2,1,0:T(8,128)(2,1)S(1)}, bf16[2,8,4096]{2,1,0:T(8,128)(2,1)S(1)}, u32[]{:S(2)}, u32[]{:S(2)}) collective-permute-start(bf16[2,8,4096]{2,1,0:T(8,128)(2,1)S(1)} %get-tuple-element.14.refs_6_), channel_id=1, source_target_pairs={{0,1},{1,0},{2,3},{3,2},{4,5},{5,4},{6,7},{7,6},{8,9},{9,8},{10,11... | collective-permute-start | bytes 393224 | tf_op jit(solution)/shard_map/ppermute | solution.py:336
  12.3 1.6 %collective-permute-start.6 = (bf16[1,3,64,128]{3,2,1,0:T(8,128)(2,1)S(1)}, bf16[1,3,64,128]{3,2,1,0:T(8,128)(2,1)S(1)}, u32[]{:S(2)}, u32[]{:S(2)}) collective-permute-start(bf16[1,3,64,128]{3,2,1,0:T(8,128)(2,1)S(1)} %collective-permute-done.3.refs_2_), channel_id=1, source_target_pairs={{0,4},{4,0},{8,12},{12,8},{16,20},{20,16},{24,28},{28,24},{1,5},{5... | collective-permute-start | bytes 147464 | tf_op jit(solution)/shard_map/ppermute | solution.py:336
  12.9 1.2 %collective-permute-start.5 = (bf16[1,3,64,128]{3,2,1,0:T(8,128)(2,1)S(1)}, bf16[1,3,64,128]{3,2,1,0:T(8,128)(2,1)S(1)}, u32[]{:S(2)}, u32[]{:S(2)}) collective-permute-start(bf16[1,3,64,128]{3,2,1,0:T(8,128)(2,1)S(1)} %collective-permute-done.2.refs_1_), channel_id=1, source_target_pairs={{0,4},{4,0},{8,12},{12,8},{16,20},{20,16},{24,28},{28,24},{1,5},{5... | collective-permute-start | bytes 147464 | tf_op jit(solution)/shard_map/ppermute | solution.py:336
  15.1 6.7 %collective-permute-start.8 = (bf16[176,128]{1,0:T(8,128)(2,1)S(1)}, bf16[176,128]{1,0:T(8,128)(2,1)S(1)}, u32[]{:S(2)}, u32[]{:S(2)}) collective-permute-start(bf16[176,128]{1,0:T(8,128)(2,1)S(1)} %get-tuple-element.21), channel_id=1, source_target_pairs={{0,2},{1,3},{2,0},{3,1},{4,6},{5,7},{6,4},{7,5},{8,10},{9,11},{10,... | collective-permute-start | bytes 135176 | tf_op jit(solution)/shard_map/ppermute | solution.py:340
  15.5 6.9 %collective-permute-start.9 = (bf16[176,128]{1,0:T(8,128)(2,1)S(1)}, bf16[176,128]{1,0:T(8,128)(2,1)S(1)}, u32[]{:S(2)}, u32[]{:S(2)}) collective-permute-start(bf16[176,128]{1,0:T(8,128)(2,1)S(1)} %get-tuple-element.22), channel_id=1, source_target_pairs={{0,1},{1,2},{2,3},{3,0},{4,5},{5,6},{6,7},{7,4},{8,9},{9,10},{10,1... | collective-permute-start | bytes 135176 | tf_op jit(solution)/shard_map/ppermute | solution.py:340
  17.1 5.3 %collective-permute-start.10 = (bf16[176,128]{1,0:T(8,128)(2,1)S(1)}, bf16[176,128]{1,0:T(8,128)(2,1)S(1)}, u32[]{:S(2)}, u32[]{:S(2)}) collective-permute-start(bf16[176,128]{1,0:T(8,128)(2,1)S(1)} %get-tuple-element.23), channel_id=1, source_target_pairs={{0,3},{1,0},{2,1},{3,2},{4,7},{5,4},{6,5},{7,6},{8,11},{9,8},{10,9... | collective-permute-start | bytes 135176 | tf_op jit(solution)/shard_map/ppermute | solution.py:340

commit v14 on v13

--- a/solution.py
+++ b/solution.py
@@ -22,19 +22,14 @@
         copy.start()
     side = values.shape[2]
     pairs = packed.shape[1]
-    lane = lax.broadcasted_iota(I32, (16, side), 1)
-    line = lax.broadcasted_iota(I32, (16, side), 0)
     copies[0].wait()
-    position = jnp.full((16, side), -1, I32)
-    for j in range(count):
-        position = jnp.where(lane == j, slots[0, j], position)
+    position = jnp.concatenate([slots[...], jnp.full((1, side - count), -1, I32)], axis=1)
     exact = position.astype(F32)
     row = jnp.floor((exact + 0.5) * (1.0 / col_count))
     col = exact - row * col_count
     row = jnp.where(position >= 0, row, float(row_count))
     col = jnp.where(position >= 0, col, float(col_count))
-    head = jnp.where(line == 0, row, col).astype(BF16)
-    head = jnp.concatenate([head, jnp.zeros((side - 16, side), BF16)], axis=0)
+    head = jnp.concatenate([row, col, jnp.zeros((side - 2, side), F32)], axis=0).astype(BF16)
     copies[1].wait()
     for k in range(pairs):
         left = values[0, k]
@@ -117,36 +112,36 @@
 def slots_kernel(first, n_parts, n_tensor, *refs):
     gathered, refs = refs[:n_parts], refs[n_parts:]
     if first:
-        cot, (*outs, cots), (ids_vmem, ids, prod, blocks, sem) = refs[0], refs[1:n_tensor + 2], refs[n_tensor + 2:]
+        cot, (*outs, cots), (prod, blocks) = refs[0], refs[1:n_tensor + 2], refs[n_tensor + 2:]
         before = []
     else:
         cots, before, outs = refs[0], refs[1:n_tensor + 1], refs[n_tensor + 1:2 * n_tensor + 1]
-        ids_vmem, ids, prod, blocks, sem = refs[2 * n_tensor + 1:]
+        prod, blocks = refs[2 * n_tensor + 1:]
     pairs, side = gathered[0].shape[1:3]
     rows = cots.shape[1]
     share = rows // n_tensor
-    copy = load_ids(gathered, ids_vmem, ids, sem)
     if first:
         load_cotangent(cot, cots)
     low = low_half((rows, 2 * side))
     where = [(part, d) for part in gathered for d in range(part.shape[0])]
+    heads = [part[d, pairs - 1, 0:16, :].astype(F32) for part, d in where]
+    columns = [head.astype(I32) for head in heads]
     tiles = slot_tiles(len(where), pairs)[-prod.shape[0]:]
     for t, ((i, j), (m, l)) in enumerate(tiles):
         part, d = where[i]
         other, e = where[m]
         blocks[t] = diagonal(part[d, j]) if i == m else diagonal(part[d, j], other[e, l])
-    copy.wait()
     for t, ((i, j), (m, l)) in enumerate(tiles):
-        lhs = jnp.where(low, cots[ids[1, i, side + j]], cots[ids[1, m, side + l]])
+        lhs = jnp.where(low, cots[columns[i][1, side + j]], cots[columns[m][1, side + l]])
         prod[t] = across(lhs, blocks[t])
     me = lax.axis_index("tensor")
     begin = 0
     if not first:
         begin = before[0].shape[0]
-        heads = jnp.concatenate([ids_vmem[0].astype(F32)] * 2, axis=0).astype(BF16)
+        rows_of_slots = jnp.concatenate([head[0:1] for head in heads] * 2, axis=0).astype(BF16)
         for k in range(n_tensor):
             outs[k][:begin, :] = before[k][...]
-            outs[k][begin + len(tiles) * share:, :] = heads
+            outs[k][begin + len(tiles) * share:, :] = rows_of_slots
     for k in range(n_tensor):
         start = pl.multiple_of(lax.rem(me + k, n_tensor) * share, share)
         for t in range(0, len(tiles), 2):
@@ -267,16 +262,16 @@
     out[...] = stage[...].astype(BF16)
 
 
-def sum_kernel(sizes, pairs, *refs):
+def sum_kernel(sizes, pairs, n_dp, *refs):
     groups = []
     for size in sizes:
         groups, refs = groups + [refs[:size]], refs[size:]
     n_tensor = len(groups)
-    (grad, ids_vmem, ids, grad_vmem, id_sem, grad_sems), accs = refs[:6], refs[6:]
-    n_dp = ids.shape[1]
+    (grad, grad_vmem, grad_sems), accs = refs[:3], refs[3:]
     share, width = grad.shape
     side = groups[0][0].shape[1] // 2
     tiles = slot_tiles(n_dp, pairs)
+    end = len(tiles) * share
 
     def load(group, start, stop):
         value = group[0][start:stop, :].astype(F32)
@@ -284,20 +279,16 @@
             value = value + message[start:stop, :].astype(F32)
         return value
 
-    for m, group in enumerate(groups):
-        ids_vmem[m] = load(group, len(tiles) * share, groups[0][0].shape[0])[:n_dp].astype(I32)
-    copy = pltpu.make_async_copy(ids_vmem, ids, id_sem)
-    copy.start()
+    places = [load(group, end, end + 2 * n_dp)[:n_dp].astype(I32) for group in groups]
     for acc in accs:
         acc[...] = jnp.zeros_like(acc)
     low = low_half((share, 2 * side))
-    copy.wait()
     for t in range(0, len(tiles), 2):
         both = [load(group, t * share, (t + 2) * share) for group in groups]
         for u in range(2):
             values = [two[u * share:(u + 1) * share] for two in both]
             for h, (i, j) in enumerate(tiles[t + u]):
-                rows = [ids[m, i, side + j] for m in range(n_tensor)]
+                rows = [place[i, side + j] for place in places]
                 halves = [jnp.where(low, 0.0, value) if h else jnp.where(low, value, 0.0) for value in values]
                 sums = [acc[row] + half for acc, row, half in zip(accs, rows, halves)]
                 for acc, row, value in zip(accs, rows, sums):
@@ -379,7 +370,7 @@
         in_specs=[HBM, HBM],
         out_specs=VMEM,
         scratch_shapes=[
-            pltpu.SMEM(block_slot.shape, I32),
+            pltpu.VMEM(block_slot.shape, I32),
             pltpu.VMEM(block_values.shape, BF16),
             pltpu.SemaphoreType.DMA((2,)),
         ],
@@ -397,17 +388,13 @@
         scratch = [
             pltpu.VMEM((tiles, rows, 2 * side), F32),
             pltpu.VMEM((tiles, 2 * side, 2 * side), BF16),
-            pltpu.SemaphoreType.DMA,
         ]
         *first_slots, cotangent = pl.pallas_call(
             functools.partial(slots_kernel, True, half, n_tensor),
             out_shape=[pltpu.VMEM((tiles * share, 2 * side), BF16)] * n_tensor + [pltpu.VMEM(cots, BF16)],
             in_specs=[VMEM] * (half + 1),
             out_specs=[VMEM] * (n_tensor + 1),
-            scratch_shapes=[
-                pltpu.VMEM((2, n_dp // 2, 2 * side), I32),
-                pltpu.SMEM((2, n_dp // 2, 2 * side), I32),
-            ] + scratch,
+            scratch_shapes=scratch,
             compiler_params=params,
         )(*gathered[:half], grad_out)
         partial_sums = pl.pallas_call(
@@ -415,7 +402,7 @@
             out_shape=[pltpu.VMEM((2 * tiles * share + 2 * n_dp, 2 * side), BF16)] * n_tensor,
             in_specs=[VMEM] * (n_parts + 1 + n_tensor),
             out_specs=[VMEM] * n_tensor,
-            scratch_shapes=ids + scratch,
+            scratch_shapes=scratch,
             compiler_params=params,
         )(*gathered, cotangent, *first_slots)
         groups = [[partial_sums[0]]] + [[shift(partial_sums[k], "tensor", n_tensor, k)] for k in (2, 1, 3)]
@@ -450,15 +437,12 @@
     )(*gathered, *tokens)
     if per_slot:
         grad_in = pl.pallas_call(
-            functools.partial(sum_kernel, tuple(map(len, groups)), pairs),
+            functools.partial(sum_kernel, tuple(map(len, groups)), pairs, n_dp),
             out_shape=jax.ShapeDtypeStruct((share, width), BF16),
             in_specs=[VMEM] * sum(map(len, groups)),
             out_specs=HBM,
             scratch_shapes=[
-                pltpu.VMEM((n_tensor, n_dp, 2 * side), I32),
-                pltpu.SMEM((n_tensor, n_dp, 2 * side), I32),
                 pltpu.VMEM((share, width), BF16),
-                pltpu.SemaphoreType.DMA,
                 pltpu.SemaphoreType.DMA((4,)),
             ] + [pltpu.VMEM((row_count + 1, share, 2 * side), F32)] * n_tensor,
             compiler_params=params,

time: 24.5 us -> 23 us (0.939)
  Pallas kernels: 6.7 us -> 4.75 us
  waiting for transfers between devices: 3.34 us -> 3.8 us
    pallas_call x1, Pallas kernels: 1.9 us -> 1.15 us  [on_device(): pl.pallas_call(functools.partial(sum_kernel, tuple(map(len, groups)), pai...]
    pallas_call x1, Pallas kernels: 1.02 us -> 0.38 us  [on_device(): pl.pallas_call(functools.partial(slots_kernel, False, n_parts, n_tensor),...]
    ppermute x8, waiting for transfers between devices: 2.09 us -> 2.68 us  [swap(): return lax.ppermute(value, axis, [(i, i ^ k) for i in range(n)])]
    pallas_call x1, Pallas kernels: 0.95 us -> 0.38 us  [on_device(): pl.pallas_call(functools.partial(slots_kernel, True, half, n_tensor), out...]
  transfers between devices with their start and end apart: 11 -> 11, of which waited for: 6 -> 7; matrix products, arithmetic and copies ran while one was open for 0% -> 0% of each run, Pallas kernels for 20% -> 16%
where the time goes in v14:
time: 23 us; the launch traced here: 22.9 us
  starting transfers between devices  13.6 us (59%)
  Pallas kernels  4.75 us (21%)
  waiting for transfers between devices  3.8 us (17%)
  between operations  0.7 us (3%)
    ppermute x8, starting transfers between devices, swap(): return lax.ppermute(value, axis, [(i, i ^ k) for i in range(n)])  9.37 us
    ppermute x3, starting transfers between devices, shift(): return lax.ppermute(value, axis, [(i, (i + k) % n) for i in range(n)])  4.22 us
    ppermute x8, waiting for transfers between devices, swap(): return lax.ppermute(value, axis, [(i, i ^ k) for i in range(n)])  2.68 us
    pallas_call x1, Pallas kernels, on_device(): pl.pallas_call(functools.partial(forward_kernel, count, n_parts, len(toke...  1.83 us
    pallas_call x1, Pallas kernels, on_device(): pl.pallas_call(functools.partial(sum_kernel, tuple(map(len, groups)), pai...  1.15 us
    ppermute x3, waiting for transfers between devices, shift(): return lax.ppermute(value, axis, [(i, (i + k) % n) for i in range(n)])  1.12 us
    pallas_call x1, Pallas kernels, on_device(): pl.pallas_call(functools.partial(pack_kernel, count, row_count, col_count...  1 us
  transfers between devices with their start and end apart: 11, of which 7 were waited for; matrix products, arithmetic and copies ran while one was open for 0% of the time, Pallas kernels for 16%

profile of v14, /device:TPU:0, one launch (start us, length us, event | category | flops | bytes accessed | tf_op | source)
XLA Modules:
  0.0 22.9 jit_solution(7030124921546103363)
XLA Ops:
  0.6 0.0 copy-start
  0.6 4.1 %collective-permute-start.1 = (bf16[8,4096]{1,0:T(8,128)(2,1)}, bf16[8,4096]{1,0:T(8,128)(2,1)S(1)}, u32[]{:S(2)}, u32[]{:S(2)}) collective-permute-start(bf16[8,4096]{1,0:T(8,128)(2,1)} %tokens.1), channel_id=1, source_target_pairs={{0,2},{1,3},{2,0},{3,1},{4,6},{5,7},{6,4},{7,5},{8,10},{9,11},{10,... | collective-permute-start | bytes 196616 | tf_op jit(solution)/shard_map/ppermute | solution.py:327
  4.7 1.0 %shard_map.59.own = bf16[1,3,64,128]{3,2,1,0:T(8,128)(2,1)S(1)} custom-call(s32[1,5]{1,0:T(1,128)} %slots_hbm.1, bf16[1,5,64,64]{3,2,1,0:T(8,128)(2,1)} %values_hbm.1), custom_call_target="tpu_custom_call" | custom-call | tf_op jit(solution)/shard_map/pallas_call | solution.py:367
  5.7 0.0 copy-start.1
  5.8 1.6 %collective-permute-start = (bf16[1,3,64,128]{3,2,1,0:T(8,128)(2,1)S(1)}, bf16[1,3,64,128]{3,2,1,0:T(8,128)(2,1)S(1)}, u32[]{:S(2)}, u32[]{:S(2)}) collective-permute-start(bf16[1,3,64,128]{3,2,1,0:T(8,128)(2,1)S(1)} %shard_map.59.own), channel_id=1, source_target_pairs={{0,8},{4,12},{8,0},{12,4},{16,24},{20,28},{24,16},{28,20},{1,9},{5... | collective-permute-start | bytes 147464 | tf_op jit(solution)/shard_map/ppermute | solution.py:327
  7.3 1.5 %collective-permute-start.3 = (bf16[1,3,64,128]{3,2,1,0:T(8,128)(2,1)S(1)}, bf16[1,3,64,128]{3,2,1,0:T(8,128)(2,1)S(1)}, u32[]{:S(2)}, u32[]{:S(2)}) collective-permute-start(bf16[1,3,64,128]{3,2,1,0:T(8,128)(2,1)S(1)} %shard_map.59.own), channel_id=1, source_target_pairs={{0,24},{4,28},{8,16},{12,20},{16,8},{20,12},{24,0},{28,4},{1,25},{... | collective-permute-start | bytes 147464 | tf_op jit(solution)/shard_map/ppermute | solution.py:327
  8.8 0.5 %collective-permute-start.2 = (bf16[1,3,64,128]{3,2,1,0:T(8,128)(2,1)S(1)}, bf16[1,3,64,128]{3,2,1,0:T(8,128)(2,1)S(1)}, u32[]{:S(2)}, u32[]{:S(2)}) collective-permute-start(bf16[1,3,64,128]{3,2,1,0:T(8,128)(2,1)S(1)} %shard_map.59.own), channel_id=1, source_target_pairs={{0,16},{4,20},{8,24},{12,28},{16,0},{20,4},{24,8},{28,12},{1,17},{... | collective-permute-start | bytes 147464 | tf_op jit(solution)/shard_map/ppermute | solution.py:327
  9.3 0.6 %collective-permute-done.near = bf16[1,3,64,128]{3,2,1,0:T(8,128)(2,1)S(1)} collective-permute-done((bf16[1,3,64,128]{3,2,1,0:T(8,128)(2,1)S(1)}, bf16[1,3,64,128]{3,2,1,0:T(8,128)(2,1)S(1)}, u32[]{:S(2)}, u32[]{:S(2)}) %collective-permute-start) | collective-permute-done | bytes 49184 | tf_op jit(solution)/shard_map/ppermute | solution.py:327
  9.9 0.0 collective-permute-done.1.far_tokens
  9.9 0.0 copy-done
  9.9 0.1 collective-permute-start.4
  10.0 1.6 %collective-permute-start.7 = (bf16[2,8,4096]{2,1,0:T(8,128)(2,1)S(1)}, bf16[2,8,4096]{2,1,0:T(8,128)(2,1)S(1)}, u32[]{:S(2)}, u32[]{:S(2)}) collective-permute-start(bf16[2,8,4096]{2,1,0:T(8,128)(2,1)S(1)} %get-tuple-element.14.refs_6_), channel_id=1, source_target_pairs={{0,1},{1,0},{2,3},{3,2},{4,5},{5,4},{6,7},{7,6},{8,9},{9,8},{10,11... | collective-permute-start | bytes 393224 | tf_op jit(solution)/shard_map/ppermute | solution.py:327
  11.7 0.6 %collective-permute-done.3.refs_2_ = bf16[1,3,64,128]{3,2,1,0:T(8,128)(2,1)S(1)} collective-permute-done((bf16[1,3,64,128]{3,2,1,0:T(8,128)(2,1)S(1)}, bf16[1,3,64,128]{3,2,1,0:T(8,128)(2,1)S(1)}, u32[]{:S(2)}, u32[]{:S(2)}) %collective-permute-start.3) | collective-permute-done | bytes 49184 | tf_op jit(solution)/shard_map/ppermute | solution.py:327
  12.3 0.0 collective-permute-start.6
  12.3 0.6 %collective-permute-done.2.refs_1_ = bf16[1,3,64,128]{3,2,1,0:T(8,128)(2,1)S(1)} collective-permute-done((bf16[1,3,64,128]{3,2,1,0:T(8,128)(2,1)S(1)}, bf16[1,3,64,128]{3,2,1,0:T(8,128)(2,1)S(1)}, u32[]{:S(2)}, u32[]{:S(2)}) %collective-permute-start.2) | collective-permute-done | bytes 49184 | tf_op jit(solution)/shard_map/ppermute | solution.py:327
  12.9 0.0 collective-permute-start.5
  12.9 0.0 copy-done.1
  12.9 0.4 %shard_map.62 = (bf16[80,128]{1,0:T(8,128)(2,1)S(1)}, bf16[80,128]{1,0:T(8,128)(2,1)S(1)}, bf16[80,128]{1,0:T(8,128)(2,1)S(1)}, bf16[80,128]{1,0:T(8,128)(2,1)S(1)}, bf16[15,32,128]{2,1,0:T(8,128)(2,1)S(1)}) custom-call(bf16[2,3,64,128]{3,2,1,0:T(8,128)(2,1)S(1)} %get-tuple-element.13.refs_0_, bf16[1,3,64,128]{3,2,1,0:T(8,128)(2,1)S(1)} %collective-permute-done.2.refs_1_, ...), custom_call_target="tpu_custom_call" | custom-call | tf_op jit(solution)/shard_map/pallas_call | solution.py:392
  13.3 0.2 %collective-permute-done.6.refs_5_ = bf16[1,3,64,128]{3,2,1,0:T(8,128)(2,1)S(1)} collective-permute-done((bf16[1,3,64,128]{3,2,1,0:T(8,128)(2,1)S(1)}, bf16[1,3,64,128]{3,2,1,0:T(8,128)(2,1)S(1)}, u32[]{:S(2)}, u32[]{:S(2)}) %collective-permute-start.6) | collective-permute-done | bytes 49184 | tf_op jit(solution)/shard_map/ppermute | solution.py:327
  13.5 0.6 %collective-permute-done.5.refs_4_ = bf16[1,3,64,128]{3,2,1,0:T(8,128)(2,1)S(1)} collective-permute-done((bf16[1,3,64,128]{3,2,1,0:T(8,128)(2,1)S(1)}, bf16[1,3,64,128]{3,2,1,0:T(8,128)(2,1)S(1)}, u32[]{:S(2)}, u32[]{:S(2)}) %collective-permute-start.5) | collective-permute-done | bytes 49184 | tf_op jit(solution)/shard_map/ppermute | solution.py:327
  14.1 0.0 collective-permute-done.4.refs_3_
  14.1 0.4 %shard_map.63 = (bf16[176,128]{1,0:T(8,128)(2,1)S(1)}, bf16[176,128]{1,0:T(8,128)(2,1)S(1)}, bf16[176,128]{1,0:T(8,128)(2,1)S(1)}, bf16[176,128]{1,0:T(8,128)(2,1)S(1)}) custom-call(bf16[2,3,64,128]{3,2,1,0:T(8,128)(2,1)S(1)} %get-tuple-element.13.refs_0_, bf16[1,3,64,128]{3,2,1,0:T(8,128)(2,1)S(1)} %collective-permute-done.2.refs_1_, ...), custom_call_target="tpu_custom_call" | custom-call | tf_op jit(solution)/shard_map/pallas_call | solution.py:400
  14.5 0.4 %collective-permute-start.8 = (bf16[176,128]{1,0:T(8,128)(2,1)S(1)}, bf16[176,128]{1,0:T(8,128)(2,1)S(1)}, u32[]{:S(2)}, u32[]{:S(2)}) collective-permute-start(bf16[176,128]{1,0:T(8,128)(2,1)S(1)} %get-tuple-element.21), channel_id=1, source_target_pairs={{0,2},{1,3},{2,0},{3,1},{4,6},{5,7},{6,4},{7,5},{8,10},{9,11},{10,... | collective-permute-start | bytes 135176 | tf_op jit(solution)/shard_map/ppermute | solution.py:331
  14.9 1.6 %collective-permute-start.9 = (bf16[176,128]{1,0:T(8,128)(2,1)S(1)}, bf16[176,128]{1,0:T(8,128)(2,1)S(1)}, u32[]{:S(2)}, u32[]{:S(2)}) collective-permute-start(bf16[176,128]{1,0:T(8,128)(2,1)S(1)} %get-tuple-element.22), channel_id=1, source_target_pairs={{0,1},{1,2},{2,3},{3,0},{4,5},{5,6},{6,7},{7,4},{8,9},{9,10},{10,1... | collective-permute-start | bytes 135176 | tf_op jit(solution)/shard_map/ppermute | solution.py:331
  16.5 2.2 %collective-permute-start.10 = (bf16[176,128]{1,0:T(8,128)(2,1)S(1)}, bf16[176,128]{1,0:T(8,128)(2,1)S(1)}, u32[]{:S(2)}, u32[]{:S(2)}) collective-permute-start(bf16[176,128]{1,0:T(8,128)(2,1)S(1)} %get-tuple-element.23), channel_id=1, source_target_pairs={{0,3},{1,0},{2,1},{3,2},{4,7},{5,4},{6,5},{7,6},{8,11},{9,8},{10,9... | collective-permute-start | bytes 135176 | tf_op jit(solution)/shard_map/ppermute | solution.py:331
  18.7 0.0 collective-permute-done.7.refs_7_
  18.7 1.8 %shard_map.61 = bf16[32,896]{1,0:T(8,128)(2,1)} custom-call(bf16[2,3,64,128]{3,2,1,0:T(8,128)(2,1)S(1)} %get-tuple-element.13.refs_0_, bf16[1,3,64,128]{3,2,1,0:T(8,128)(2,1)S(1)} %collective-permute-done.2.refs_1_, bf16[1,3,64,128]{3,2,1,0:T(8,128)(2,1)S(1)} %collective-permute-done.3.refs_2_, bf16[2,3,64,128]{3,2,1,0:T(8,128)(2,1)S(1)} %collective-permute-done.4.refs_3_, ...), custom_call_target="tpu_custom_call" | custom-call | tf_op jit(solution)/shard_map/pallas_call | solution.py:423
  20.6 0.9 %collective-permute-done.8.refs_1_ = bf16[176,128]{1,0:T(8,128)(2,1)S(1)} collective-permute-done((bf16[176,128]{1,0:T(8,128)(2,1)S(1)}, bf16[176,128]{1,0:T(8,128)(2,1)S(1)}, u32[]{:S(2)}, u32[]{:S(2)}) %collective-permute-start.8) | collective-permute-done | bytes 45088 | tf_op jit(solution)/shard_map/ppermute | solution.py:331
  21.5 0.2 collective-permute-done.9.refs_2_
  21.7 0.0 collective-permute-done.10.refs_3_
  21.7 1.1 %shard_map.64 = bf16[8,4096]{1,0:T(8,128)(2,1)} custom-call(bf16[176,128]{1,0:T(8,128)(2,1)S(1)} %get-tuple-element.20.refs_0_, bf16[176,128]{1,0:T(8,128)(2,1)S(1)} %collective-permute-done.8.refs_1_, bf16[176,128]{1,0:T(8,128)(2,1)S(1)} %collective-permute-done.9.refs_2_, bf16[176,128]{1,0:T(8,128)(2,1)S(1)} %collective-permute-done.10.refs_3_), custom_call_target="tpu_custom_call" | custom-call | tf_op jit(solution)/shard_map/pallas_call | solution.py:439
  (1 shorter events, 0.0 us)
Async XLA Ops:
  0.6 9.3 %copy-start = (bf16[8,4096]{1,0:T(8,128)(2,1)S(1)}, bf16[8,4096]{1,0:T(8,128)(2,1)}, u32[]{:S(2)}) copy-start(bf16[8,4096]{1,0:T(8,128)(2,1)} %tokens.1) | copy-start | bytes 196612
  0.6 9.3 %collective-permute-start.1 = (bf16[8,4096]{1,0:T(8,128)(2,1)}, bf16[8,4096]{1,0:T(8,128)(2,1)S(1)}, u32[]{:S(2)}, u32[]{:S(2)}) collective-permute-start(bf16[8,4096]{1,0:T(8,128)(2,1)} %tokens.1), channel_id=1, source_target_pairs={{0,2},{1,3},{2,0},{3,1},{4,6},{5,7},{6,4},{7,5},{8,10},{9,11},{10,... | collective-permute-start | bytes 196616 | tf_op jit(solution)/shard_map/ppermute | solution.py:327
  5.7 7.2 %copy-start.1 = (bf16[32,896]{1,0:T(8,128)(2,1)S(1)}, bf16[32,896]{1,0:T(8,128)(2,1)}, u32[]{:S(2)}) copy-start(bf16[32,896]{1,0:T(8,128)(2,1)} %refs_3_.1) | copy-start | bytes 172036
  5.8 4.2 %collective-permute-start = (bf16[1,3,64,128]{3,2,1,0:T(8,128)(2,1)S(1)}, bf16[1,3,64,128]{3,2,1,0:T(8,128)(2,1)S(1)}, u32[]{:S(2)}, u32[]{:S(2)}) collective-permute-start(bf16[1,3,64,128]{3,2,1,0:T(8,128)(2,1)S(1)} %shard_map.59.own), channel_id=1, source_target_pairs={{0,8},{4,12},{8,0},{12,4},{16,24},{20,28},{24,16},{28,20},{1,9},{5... | collective-permute-start | bytes 147464 | tf_op jit(solution)/shard_map/ppermute | solution.py:327
  7.3 5.0 %collective-permute-start.3 = (bf16[1,3,64,128]{3,2,1,0:T(8,128)(2,1)S(1)}, bf16[1,3,64,128]{3,2,1,0:T(8,128)(2,1)S(1)}, u32[]{:S(2)}, u32[]{:S(2)}) collective-permute-start(bf16[1,3,64,128]{3,2,1,0:T(8,128)(2,1)S(1)} %shard_map.59.own), channel_id=1, source_target_pairs={{0,24},{4,28},{8,16},{12,20},{16,8},{20,12},{24,0},{28,4},{1,25},{... | collective-permute-start | bytes 147464 | tf_op jit(solution)/shard_map/ppermute | solution.py:327
  8.8 4.1 %collective-permute-start.2 = (bf16[1,3,64,128]{3,2,1,0:T(8,128)(2,1)S(1)}, bf16[1,3,64,128]{3,2,1,0:T(8,128)(2,1)S(1)}, u32[]{:S(2)}, u32[]{:S(2)}) collective-permute-start(bf16[1,3,64,128]{3,2,1,0:T(8,128)(2,1)S(1)} %shard_map.59.own), channel_id=1, source_target_pairs={{0,16},{4,20},{8,24},{12,28},{16,0},{20,4},{24,8},{28,12},{1,17},{... | collective-permute-start | bytes 147464 | tf_op jit(solution)/shard_map/ppermute | solution.py:327
  9.9 4.2 %collective-permute-start.4 = (bf16[2,3,64,128]{3,2,1,0:T(8,128)(2,1)S(1)}, bf16[2,3,64,128]{3,2,1,0:T(8,128)(2,1)S(1)}, u32[]{:S(2)}, u32[]{:S(2)}) collective-permute-start(bf16[2,3,64,128]{3,2,1,0:T(8,128)(2,1)S(1)} %get-tuple-element.13.refs_0_), channel_id=1, source_target_pairs={{0,4},{4,0},{8,12},{12,8},{16,20},{20,16},{24,28},{28,24},{1,5},{5... | collective-permute-start | bytes 294920 | tf_op jit(solution)/shard_map/ppermute | solution.py:327
  10.0 8.7 %collective-permute-start.7 = (bf16[2,8,4096]{2,1,0:T(8,128)(2,1)S(1)}, bf16[2,8,4096]{2,1,0:T(8,128)(2,1)S(1)}, u32[]{:S(2)}, u32[]{:S(2)}) collective-permute-start(bf16[2,8,4096]{2,1,0:T(8,128)(2,1)S(1)} %get-tuple-element.14.refs_6_), channel_id=1, source_target_pairs={{0,1},{1,0},{2,3},{3,2},{4,5},{5,4},{6,7},{7,6},{8,9},{9,8},{10,11... | collective-permute-start | bytes 393224 | tf_op jit(solution)/shard_map/ppermute | solution.py:327
  12.3 1.2 %collective-permute-start.6 = (bf16[1,3,64,128]{3,2,1,0:T(8,128)(2,1)S(1)}, bf16[1,3,64,128]{3,2,1,0:T(8,128)(2,1)S(1)}, u32[]{:S(2)}, u32[]{:S(2)}) collective-permute-start(bf16[1,3,64,128]{3,2,1,0:T(8,128)(2,1)S(1)} %collective-permute-done.3.refs_2_), channel_id=1, source_target_pairs={{0,4},{4,0},{8,12},{12,8},{16,20},{20,16},{24,28},{28,24},{1,5},{5... | collective-permute-start | bytes 147464 | tf_op jit(solution)/shard_map/ppermute | solution.py:327
  12.9 1.2 %collective-permute-start.5 = (bf16[1,3,64,128]{3,2,1,0:T(8,128)(2,1)S(1)}, bf16[1,3,64,128]{3,2,1,0:T(8,128)(2,1)S(1)}, u32[]{:S(2)}, u32[]{:S(2)}) collective-permute-start(bf16[1,3,64,128]{3,2,1,0:T(8,128)(2,1)S(1)} %collective-permute-done.2.refs_1_), channel_id=1, source_target_pairs={{0,4},{4,0},{8,12},{12,8},{16,20},{20,16},{24,28},{28,24},{1,5},{5... | collective-permute-start | bytes 147464 | tf_op jit(solution)/shard_map/ppermute | solution.py:327
  14.5 7.0 %collective-permute-start.8 = (bf16[176,128]{1,0:T(8,128)(2,1)S(1)}, bf16[176,128]{1,0:T(8,128)(2,1)S(1)}, u32[]{:S(2)}, u32[]{:S(2)}) collective-permute-start(bf16[176,128]{1,0:T(8,128)(2,1)S(1)} %get-tuple-element.21), channel_id=1, source_target_pairs={{0,2},{1,3},{2,0},{3,1},{4,6},{5,7},{6,4},{7,5},{8,10},{9,11},{10,... | collective-permute-start | bytes 135176 | tf_op jit(solution)/shard_map/ppermute | solution.py:331
  14.9 6.8 %collective-permute-start.9 = (bf16[176,128]{1,0:T(8,128)(2,1)S(1)}, bf16[176,128]{1,0:T(8,128)(2,1)S(1)}, u32[]{:S(2)}, u32[]{:S(2)}) collective-permute-start(bf16[176,128]{1,0:T(8,128)(2,1)S(1)} %get-tuple-element.22), channel_id=1, source_target_pairs={{0,1},{1,2},{2,3},{3,0},{4,5},{5,6},{6,7},{7,4},{8,9},{9,10},{10,1... | collective-permute-start | bytes 135176 | tf_op jit(solution)/shard_map/ppermute | solution.py:331
  16.5 5.2 %collective-permute-start.10 = (bf16[176,128]{1,0:T(8,128)(2,1)S(1)}, bf16[176,128]{1,0:T(8,128)(2,1)S(1)}, u32[]{:S(2)}, u32[]{:S(2)}) collective-permute-start(bf16[176,128]{1,0:T(8,128)(2,1)S(1)} %get-tuple-element.23), channel_id=1, source_target_pairs={{0,3},{1,0},{2,1},{3,2},{4,7},{5,4},{6,5},{7,6},{8,11},{9,8},{10,9... | collective-permute-start | bytes 135176 | tf_op jit(solution)/shard_map/ppermute | solution.py:331

commit v15 on v14

--- a/solution.py
+++ b/solution.py
@@ -14,10 +14,8 @@
 
 
 def pack_kernel(count, row_count, col_count, slots_hbm, values_hbm, packed, slots, values, sems):
-    copies = [
-        pltpu.make_async_copy(slots_hbm, slots, sems.at[0]),
-        pltpu.make_async_copy(values_hbm, values, sems.at[1]),
-    ]
+    copies = [pltpu.make_async_copy(slots_hbm, slots, sems.at[count])]
+    copies += [pltpu.make_async_copy(values_hbm.at[0, j], values.at[0, j], sems.at[j]) for j in range(count)]
     for copy in copies:
         copy.start()
     side = values.shape[2]
@@ -30,7 +28,8 @@
     row = jnp.where(position >= 0, row, float(row_count))
     col = jnp.where(position >= 0, col, float(col_count))
     head = jnp.concatenate([row, col, jnp.zeros((side - 2, side), F32)], axis=0).astype(BF16)
-    copies[1].wait()
+    for copy in copies[1:]:
+        copy.wait()
     for k in range(pairs):
         left = values[0, k]
         right = values[0, k + pairs] if k + pairs < count else head
@@ -208,9 +207,9 @@
 
     def multiply(part, d, i):
         for k in range(pairs):
-            lhs = blocks[ids[0, i, side + k]]
+            lhs = blocks[ids(0, i, side + k)]
             if k + pairs < count:
-                lhs = jnp.where(low, lhs, blocks[ids[0, i, side + k + pairs]])
+                lhs = jnp.where(low, lhs, blocks[ids(0, i, side + k + pairs)])
                 tile = diagonal(part[d, k])
             else:
                 lhs, tile = lhs[:, :side], part[d, k]
@@ -224,10 +223,10 @@
 
     def add(part, d, i):
         for k in range(pairs):
-            value, left = prod[i * pairs + k], ids[1, i, side + k]
+            value, left = prod[i * pairs + k], ids(1, i, side + k)
             left_sum = left_acc[left] + value
             if k + pairs < count:
-                right = ids[1, i, side + k + pairs]
+                right = ids(1, i, side + k + pairs)
                 right_sum = right_acc[right] + value
                 right_acc[right] = right_sum
             left_acc[left] = left_sum
@@ -248,14 +247,22 @@
             stage[pl.ds(start, share), c * width // 2:(c + 2) * width // 2] = jnp.where(half, *sums)
 
 
-def forward_kernel(count, n_parts, n_token_parts, n_tensor, *refs):
+def forward_kernel(count, few, n_parts, n_token_parts, n_tensor, *refs):
     gathered, token_parts = refs[:n_parts], refs[n_parts:n_parts + n_token_parts]
-    out, ids_vmem, ids, blocks, prod, left_acc, right_acc, stage, sem = refs[n_parts + n_token_parts:]
-    copy = load_ids(gathered, ids_vmem, ids, sem)
+    out, blocks, prod, left_acc, right_acc, stage = refs[n_parts + n_token_parts:][:6]
+    if few:
+        heads = [part[d, part.shape[1] - 1, 0:16, :].astype(F32) for part in gathered for d in range(part.shape[0])]
+        heads = [head.astype(I32) for head in heads]
+        ids = lambda line, i, lane: heads[i][line, lane]
+    else:
+        ids_vmem, scalars, sem = refs[-3:]
+        copy = load_ids(gathered, ids_vmem, scalars, sem)
+        ids = lambda line, i, lane: scalars[line, i, lane]
     left_acc[...] = jnp.zeros_like(left_acc)
     right_acc[...] = jnp.zeros_like(right_acc)
     load_tokens(token_parts, blocks)
-    copy.wait()
+    if not few:
+        copy.wait()
     multiply_tokens(count, gathered, ids, blocks, prod)
     add_tokens(count, gathered, ids, prod, left_acc, right_acc)
     place_outputs(n_tensor, left_acc, right_acc, stage)
@@ -338,7 +345,7 @@
             tokens = tokens + [swap(value, "tensor", n_tensor, k) for value in tokens]
         return [lax.all_gather(packed, "dp", axis=0, tiled=True)], tokens
     far_tokens = swap(inputs, "tensor", n_tensor, 2)
-    near, second, last = [swap(packed, "dp", n_dp, k) for k in (2, 4, 6)]
+    near, second, last = [swap(packed, "dp", n_dp, k) for k in (6, 2, 4)]
     joined, tokens = pl.pallas_call(
         join_kernel,
         out_shape=[
@@ -372,7 +379,7 @@
         scratch_shapes=[
             pltpu.VMEM(block_slot.shape, I32),
             pltpu.VMEM(block_values.shape, BF16),
-            pltpu.SemaphoreType.DMA((2,)),
+            pltpu.SemaphoreType.DMA((count + 1,)),
         ],
         compiler_params=pltpu.CompilerParams(vmem_limit_bytes=4 * MIB),
     )(
@@ -421,18 +428,17 @@
         )(*gathered, grad_out)
         arrived = [partial_sums[0]] + [shift(partial_sums[k], "tensor", n_tensor, k) for k in range(1, n_tensor)]
     outputs = pl.pallas_call(
-        functools.partial(forward_kernel, count, n_parts, len(tokens), n_tensor),
+        functools.partial(forward_kernel, count, per_slot, n_parts, len(tokens), n_tensor),
         out_shape=jax.ShapeDtypeStruct((rows, hidden), BF16),
         in_specs=[VMEM] * (n_parts + len(tokens)),
         out_specs=VMEM,
-        scratch_shapes=ids + [
+        scratch_shapes=[
             pltpu.VMEM((row_count + 1, rows, 2 * side), BF16),
             pltpu.VMEM((n_dp * pairs, rows, 2 * side), F32),
             pltpu.VMEM((col_count + 1, rows, 2 * side), F32),
             pltpu.VMEM((col_count + 1, rows, 2 * side), F32),
             pltpu.VMEM((rows, hidden), F32),
-            pltpu.SemaphoreType.DMA,
-        ],
+        ] + ([] if per_slot else ids + [pltpu.SemaphoreType.DMA]),
         compiler_params=params,
     )(*gathered, *tokens)
     if per_slot:

time: 23 us -> 23 us (level)
  Pallas kernels: 4.75 us -> 4.07 us
  starting transfers between devices: 13.6 us -> 14.1 us
    ppermute x3, waiting for transfers between devices: 1.12 us -> 1.73 us  [shift(): return lax.ppermute(value, axis, [(i, (i + k) % n) for i in range(n)])]
    pallas_call x1, Pallas kernels: 1.83 us -> 1.23 us  [on_device(): pl.pallas_call(functools.partial(forward_kernel, count, per_slot, n_parts...]
    ppermute x8, waiting for transfers between devices: 2.68 us -> 2.17 us  [swap(): return lax.ppermute(value, axis, [(i, i ^ k) for i in range(n)])]
    ppermute x8, starting transfers between devices: 9.37 us -> 9.85 us  [swap(): return lax.ppermute(value, axis, [(i, i ^ k) for i in range(n)])]
  transfers between devices with their start and end apart: 11 -> 11, of which waited for: 7 -> 5; matrix products, arithmetic and copies ran while one was open for 0% -> 0% of each run, Pallas kernels for 16% -> 13%
where the time goes in v15:
time: 23 us; the launch traced here: 22.8 us
  starting transfers between devices  14.1 us (61%)
  Pallas kernels  4.07 us (18%)
  waiting for transfers between devices  3.91 us (17%)
  between operations  0.69 us (3%)
    ppermute x8, starting transfers between devices, swap(): return lax.ppermute(value, axis, [(i, i ^ k) for i in range(n)])  9.85 us
    ppermute x3, starting transfers between devices, shift(): return lax.ppermute(value, axis, [(i, (i + k) % n) for i in range(n)])  4.22 us
    ppermute x8, waiting for transfers between devices, swap(): return lax.ppermute(value, axis, [(i, i ^ k) for i in range(n)])  2.17 us
    ppermute x3, waiting for transfers between devices, shift(): return lax.ppermute(value, axis, [(i, (i + k) % n) for i in range(n)])  1.73 us
    pallas_call x1, Pallas kernels, on_device(): pl.pallas_call(functools.partial(forward_kernel, count, per_slot, n_parts...  1.23 us
    pallas_call x1, Pallas kernels, on_device(): pl.pallas_call(functools.partial(sum_kernel, tuple(map(len, groups)), pai...  1.14 us
    pallas_call x1, Pallas kernels, on_device(): pl.pallas_call(functools.partial(pack_kernel, count, row_count, col_count...  0.93 us
  transfers between devices with their start and end apart: 11, of which 5 were waited for; matrix products, arithmetic and copies ran while one was open for 0% of the time, Pallas kernels for 13%

profile of v15, /device:TPU:0, one launch (start us, length us, event | category | flops | bytes accessed | tf_op | source)
XLA Modules:
  0.0 22.8 jit_solution(10676511159068018723)
XLA Ops:
  0.6 0.0 copy-start
  0.6 4.1 %collective-permute-start.1 = (bf16[8,4096]{1,0:T(8,128)(2,1)}, bf16[8,4096]{1,0:T(8,128)(2,1)S(1)}, u32[]{:S(2)}, u32[]{:S(2)}) collective-permute-start(bf16[8,4096]{1,0:T(8,128)(2,1)} %tokens.1), channel_id=1, source_target_pairs={{0,2},{1,3},{2,0},{3,1},{4,6},{5,7},{6,4},{7,5},{8,10},{9,11},{10,... | collective-permute-start | bytes 196616 | tf_op jit(solution)/shard_map/ppermute | solution.py:334
  4.7 0.9 %shard_map.59.own = bf16[1,3,64,128]{3,2,1,0:T(8,128)(2,1)S(1)} custom-call(s32[1,5]{1,0:T(1,128)} %slots_hbm.1, bf16[1,5,64,64]{3,2,1,0:T(8,128)(2,1)} %values_hbm.1), custom_call_target="tpu_custom_call" | custom-call | tf_op jit(solution)/shard_map/pallas_call | solution.py:374
  5.7 0.0 copy-start.1
  5.7 2.5 %collective-permute-start = (bf16[1,3,64,128]{3,2,1,0:T(8,128)(2,1)S(1)}, bf16[1,3,64,128]{3,2,1,0:T(8,128)(2,1)S(1)}, u32[]{:S(2)}, u32[]{:S(2)}) collective-permute-start(bf16[1,3,64,128]{3,2,1,0:T(8,128)(2,1)S(1)} %shard_map.59.own), channel_id=1, source_target_pairs={{0,24},{4,28},{8,16},{12,20},{16,8},{20,12},{24,0},{28,4},{1,25},{... | collective-permute-start | bytes 147464 | tf_op jit(solution)/shard_map/ppermute | solution.py:334
  8.2 0.5 %collective-permute-start.3 = (bf16[1,3,64,128]{3,2,1,0:T(8,128)(2,1)S(1)}, bf16[1,3,64,128]{3,2,1,0:T(8,128)(2,1)S(1)}, u32[]{:S(2)}, u32[]{:S(2)}) collective-permute-start(bf16[1,3,64,128]{3,2,1,0:T(8,128)(2,1)S(1)} %shard_map.59.own), channel_id=1, source_target_pairs={{0,16},{4,20},{8,24},{12,28},{16,0},{20,4},{24,8},{28,12},{1,17},{... | collective-permute-start | bytes 147464 | tf_op jit(solution)/shard_map/ppermute | solution.py:334
  8.7 0.5 %collective-permute-start.2 = (bf16[1,3,64,128]{3,2,1,0:T(8,128)(2,1)S(1)}, bf16[1,3,64,128]{3,2,1,0:T(8,128)(2,1)S(1)}, u32[]{:S(2)}, u32[]{:S(2)}) collective-permute-start(bf16[1,3,64,128]{3,2,1,0:T(8,128)(2,1)S(1)} %shard_map.59.own), channel_id=1, source_target_pairs={{0,8},{4,12},{8,0},{12,4},{16,24},{20,28},{24,16},{28,20},{1,9},{5... | collective-permute-start | bytes 147464 | tf_op jit(solution)/shard_map/ppermute | solution.py:334
  9.2 1.6 %collective-permute-done.near = bf16[1,3,64,128]{3,2,1,0:T(8,128)(2,1)S(1)} collective-permute-done((bf16[1,3,64,128]{3,2,1,0:T(8,128)(2,1)S(1)}, bf16[1,3,64,128]{3,2,1,0:T(8,128)(2,1)S(1)}, u32[]{:S(2)}, u32[]{:S(2)}) %collective-permute-start) | collective-permute-done | bytes 49184 | tf_op jit(solution)/shard_map/ppermute | solution.py:334
  10.9 0.0 collective-permute-done.1.far_tokens
  10.9 0.0 copy-done
  10.9 0.1 collective-permute-start.4
  11.0 1.6 %collective-permute-start.7 = (bf16[2,8,4096]{2,1,0:T(8,128)(2,1)S(1)}, bf16[2,8,4096]{2,1,0:T(8,128)(2,1)S(1)}, u32[]{:S(2)}, u32[]{:S(2)}) collective-permute-start(bf16[2,8,4096]{2,1,0:T(8,128)(2,1)S(1)} %get-tuple-element.14.refs_6_), channel_id=1, source_target_pairs={{0,1},{1,0},{2,3},{3,2},{4,5},{5,4},{6,7},{7,6},{8,9},{9,8},{10,11... | collective-permute-start | bytes 393224 | tf_op jit(solution)/shard_map/ppermute | solution.py:334
  12.6 0.0 collective-permute-done.3.refs_2_
  12.6 0.2 collective-permute-start.6
  12.8 0.0 collective-permute-done.2.refs_1_
  12.8 0.3 %collective-permute-start.5 = (bf16[1,3,64,128]{3,2,1,0:T(8,128)(2,1)S(1)}, bf16[1,3,64,128]{3,2,1,0:T(8,128)(2,1)S(1)}, u32[]{:S(2)}, u32[]{:S(2)}) collective-permute-start(bf16[1,3,64,128]{3,2,1,0:T(8,128)(2,1)S(1)} %collective-permute-done.2.refs_1_), channel_id=1, source_target_pairs={{0,4},{4,0},{8,12},{12,8},{16,20},{20,16},{24,28},{28,24},{1,5},{5... | collective-permute-start | bytes 147464 | tf_op jit(solution)/shard_map/ppermute | solution.py:334
  13.1 0.0 copy-done.1
  13.1 0.4 %shard_map.62 = (bf16[80,128]{1,0:T(8,128)(2,1)S(1)}, bf16[80,128]{1,0:T(8,128)(2,1)S(1)}, bf16[80,128]{1,0:T(8,128)(2,1)S(1)}, bf16[80,128]{1,0:T(8,128)(2,1)S(1)}, bf16[15,32,128]{2,1,0:T(8,128)(2,1)S(1)}) custom-call(bf16[2,3,64,128]{3,2,1,0:T(8,128)(2,1)S(1)} %get-tuple-element.13.refs_0_, bf16[1,3,64,128]{3,2,1,0:T(8,128)(2,1)S(1)} %collective-permute-done.2.refs_1_, ...), custom_call_target="tpu_custom_call" | custom-call | tf_op jit(solution)/shard_map/pallas_call | solution.py:399
  13.5 0.3 %collective-permute-done.6.refs_5_ = bf16[1,3,64,128]{3,2,1,0:T(8,128)(2,1)S(1)} collective-permute-done((bf16[1,3,64,128]{3,2,1,0:T(8,128)(2,1)S(1)}, bf16[1,3,64,128]{3,2,1,0:T(8,128)(2,1)S(1)}, u32[]{:S(2)}, u32[]{:S(2)}) %collective-permute-start.6) | collective-permute-done | bytes 49184 | tf_op jit(solution)/shard_map/ppermute | solution.py:334
  13.8 0.2 collective-permute-done.5.refs_4_
  14.0 0.0 collective-permute-done.4.refs_3_
  14.0 0.4 %shard_map.63 = (bf16[176,128]{1,0:T(8,128)(2,1)S(1)}, bf16[176,128]{1,0:T(8,128)(2,1)S(1)}, bf16[176,128]{1,0:T(8,128)(2,1)S(1)}, bf16[176,128]{1,0:T(8,128)(2,1)S(1)}) custom-call(bf16[2,3,64,128]{3,2,1,0:T(8,128)(2,1)S(1)} %get-tuple-element.13.refs_0_, bf16[1,3,64,128]{3,2,1,0:T(8,128)(2,1)S(1)} %collective-permute-done.2.refs_1_, ...), custom_call_target="tpu_custom_call" | custom-call | tf_op jit(solution)/shard_map/pallas_call | solution.py:407
  14.4 0.4 %collective-permute-start.8 = (bf16[176,128]{1,0:T(8,128)(2,1)S(1)}, bf16[176,128]{1,0:T(8,128)(2,1)S(1)}, u32[]{:S(2)}, u32[]{:S(2)}) collective-permute-start(bf16[176,128]{1,0:T(8,128)(2,1)S(1)} %get-tuple-element.21), channel_id=1, source_target_pairs={{0,2},{1,3},{2,0},{3,1},{4,6},{5,7},{6,4},{7,5},{8,10},{9,11},{10,... | collective-permute-start | bytes 135176 | tf_op jit(solution)/shard_map/ppermute | solution.py:338
  14.8 1.6 %collective-permute-start.9 = (bf16[176,128]{1,0:T(8,128)(2,1)S(1)}, bf16[176,128]{1,0:T(8,128)(2,1)S(1)}, u32[]{:S(2)}, u32[]{:S(2)}) collective-permute-start(bf16[176,128]{1,0:T(8,128)(2,1)S(1)} %get-tuple-element.22), channel_id=1, source_target_pairs={{0,1},{1,2},{2,3},{3,0},{4,5},{5,6},{6,7},{7,4},{8,9},{9,10},{10,1... | collective-permute-start | bytes 135176 | tf_op jit(solution)/shard_map/ppermute | solution.py:338
  16.4 2.2 %collective-permute-start.10 = (bf16[176,128]{1,0:T(8,128)(2,1)S(1)}, bf16[176,128]{1,0:T(8,128)(2,1)S(1)}, u32[]{:S(2)}, u32[]{:S(2)}) collective-permute-start(bf16[176,128]{1,0:T(8,128)(2,1)S(1)} %get-tuple-element.23), channel_id=1, source_target_pairs={{0,3},{1,0},{2,1},{3,2},{4,7},{5,4},{6,5},{7,6},{8,11},{9,8},{10,9... | collective-permute-start | bytes 135176 | tf_op jit(solution)/shard_map/ppermute | solution.py:338
  18.6 0.0 collective-permute-done.7.refs_7_
  18.6 1.2 %shard_map.61 = bf16[32,896]{1,0:T(8,128)(2,1)} custom-call(bf16[2,3,64,128]{3,2,1,0:T(8,128)(2,1)S(1)} %get-tuple-element.13.refs_0_, bf16[1,3,64,128]{3,2,1,0:T(8,128)(2,1)S(1)} %collective-permute-done.2.refs_1_, bf16[1,3,64,128]{3,2,1,0:T(8,128)(2,1)S(1)} %collective-permute-done.3.refs_2_, bf16[2,3,64,128]{3,2,1,0:T(8,128)(2,1)S(1)} %collective-permute-done.4.refs_3_, ...), custom_call_target="tpu_custom_call" | custom-call | tf_op jit(solution)/shard_map/pallas_call | solution.py:430
  19.9 1.5 %collective-permute-done.8.refs_1_ = bf16[176,128]{1,0:T(8,128)(2,1)S(1)} collective-permute-done((bf16[176,128]{1,0:T(8,128)(2,1)S(1)}, bf16[176,128]{1,0:T(8,128)(2,1)S(1)}, u32[]{:S(2)}, u32[]{:S(2)}) %collective-permute-start.8) | collective-permute-done | bytes 45088 | tf_op jit(solution)/shard_map/ppermute | solution.py:338
  21.4 0.2 collective-permute-done.9.refs_2_
  21.6 0.0 collective-permute-done.10.refs_3_
  21.6 1.1 %shard_map.64 = bf16[8,4096]{1,0:T(8,128)(2,1)} custom-call(bf16[176,128]{1,0:T(8,128)(2,1)S(1)} %get-tuple-element.20.refs_0_, bf16[176,128]{1,0:T(8,128)(2,1)S(1)} %collective-permute-done.8.refs_1_, bf16[176,128]{1,0:T(8,128)(2,1)S(1)} %collective-permute-done.9.refs_2_, bf16[176,128]{1,0:T(8,128)(2,1)S(1)} %collective-permute-done.10.refs_3_), custom_call_target="tpu_custom_call" | custom-call | tf_op jit(solution)/shard_map/pallas_call | solution.py:445
  (1 shorter events, 0.0 us)
Async XLA Ops:
  0.6 10.2 %copy-start = (bf16[8,4096]{1,0:T(8,128)(2,1)S(1)}, bf16[8,4096]{1,0:T(8,128)(2,1)}, u32[]{:S(2)}) copy-start(bf16[8,4096]{1,0:T(8,128)(2,1)} %tokens.1) | copy-start | bytes 196612
  0.6 10.2 %collective-permute-start.1 = (bf16[8,4096]{1,0:T(8,128)(2,1)}, bf16[8,4096]{1,0:T(8,128)(2,1)S(1)}, u32[]{:S(2)}, u32[]{:S(2)}) collective-permute-start(bf16[8,4096]{1,0:T(8,128)(2,1)} %tokens.1), channel_id=1, source_target_pairs={{0,2},{1,3},{2,0},{3,1},{4,6},{5,7},{6,4},{7,5},{8,10},{9,11},{10,... | collective-permute-start | bytes 196616 | tf_op jit(solution)/shard_map/ppermute | solution.py:334
  5.7 7.4 %copy-start.1 = (bf16[32,896]{1,0:T(8,128)(2,1)S(1)}, bf16[32,896]{1,0:T(8,128)(2,1)}, u32[]{:S(2)}) copy-start(bf16[32,896]{1,0:T(8,128)(2,1)} %refs_3_.1) | copy-start | bytes 172036
  5.7 5.2 %collective-permute-start = (bf16[1,3,64,128]{3,2,1,0:T(8,128)(2,1)S(1)}, bf16[1,3,64,128]{3,2,1,0:T(8,128)(2,1)S(1)}, u32[]{:S(2)}, u32[]{:S(2)}) collective-permute-start(bf16[1,3,64,128]{3,2,1,0:T(8,128)(2,1)S(1)} %shard_map.59.own), channel_id=1, source_target_pairs={{0,24},{4,28},{8,16},{12,20},{16,8},{20,12},{24,0},{28,4},{1,25},{... | collective-permute-start | bytes 147464 | tf_op jit(solution)/shard_map/ppermute | solution.py:334
  8.2 4.4 %collective-permute-start.3 = (bf16[1,3,64,128]{3,2,1,0:T(8,128)(2,1)S(1)}, bf16[1,3,64,128]{3,2,1,0:T(8,128)(2,1)S(1)}, u32[]{:S(2)}, u32[]{:S(2)}) collective-permute-start(bf16[1,3,64,128]{3,2,1,0:T(8,128)(2,1)S(1)} %shard_map.59.own), channel_id=1, source_target_pairs={{0,16},{4,20},{8,24},{12,28},{16,0},{20,4},{24,8},{28,12},{1,17},{... | collective-permute-start | bytes 147464 | tf_op jit(solution)/shard_map/ppermute | solution.py:334
  8.7 4.1 %collective-permute-start.2 = (bf16[1,3,64,128]{3,2,1,0:T(8,128)(2,1)S(1)}, bf16[1,3,64,128]{3,2,1,0:T(8,128)(2,1)S(1)}, u32[]{:S(2)}, u32[]{:S(2)}) collective-permute-start(bf16[1,3,64,128]{3,2,1,0:T(8,128)(2,1)S(1)} %shard_map.59.own), channel_id=1, source_target_pairs={{0,8},{4,12},{8,0},{12,4},{16,24},{20,28},{24,16},{28,20},{1,9},{5... | collective-permute-start | bytes 147464 | tf_op jit(solution)/shard_map/ppermute | solution.py:334
  10.9 3.2 %collective-permute-start.4 = (bf16[2,3,64,128]{3,2,1,0:T(8,128)(2,1)S(1)}, bf16[2,3,64,128]{3,2,1,0:T(8,128)(2,1)S(1)}, u32[]{:S(2)}, u32[]{:S(2)}) collective-permute-start(bf16[2,3,64,128]{3,2,1,0:T(8,128)(2,1)S(1)} %get-tuple-element.13.refs_0_), channel_id=1, source_target_pairs={{0,4},{4,0},{8,12},{12,8},{16,20},{20,16},{24,28},{28,24},{1,5},{5... | collective-permute-start | bytes 294920 | tf_op jit(solution)/shard_map/ppermute | solution.py:334
  11.0 7.7 %collective-permute-start.7 = (bf16[2,8,4096]{2,1,0:T(8,128)(2,1)S(1)}, bf16[2,8,4096]{2,1,0:T(8,128)(2,1)S(1)}, u32[]{:S(2)}, u32[]{:S(2)}) collective-permute-start(bf16[2,8,4096]{2,1,0:T(8,128)(2,1)S(1)} %get-tuple-element.14.refs_6_), channel_id=1, source_target_pairs={{0,1},{1,0},{2,3},{3,2},{4,5},{5,4},{6,7},{7,6},{8,9},{9,8},{10,11... | collective-permute-start | bytes 393224 | tf_op jit(solution)/shard_map/ppermute | solution.py:334
  12.6 1.2 %collective-permute-start.6 = (bf16[1,3,64,128]{3,2,1,0:T(8,128)(2,1)S(1)}, bf16[1,3,64,128]{3,2,1,0:T(8,128)(2,1)S(1)}, u32[]{:S(2)}, u32[]{:S(2)}) collective-permute-start(bf16[1,3,64,128]{3,2,1,0:T(8,128)(2,1)S(1)} %collective-permute-done.3.refs_2_), channel_id=1, source_target_pairs={{0,4},{4,0},{8,12},{12,8},{16,20},{20,16},{24,28},{28,24},{1,5},{5... | collective-permute-start | bytes 147464 | tf_op jit(solution)/shard_map/ppermute | solution.py:334
  12.8 1.2 %collective-permute-start.5 = (bf16[1,3,64,128]{3,2,1,0:T(8,128)(2,1)S(1)}, bf16[1,3,64,128]{3,2,1,0:T(8,128)(2,1)S(1)}, u32[]{:S(2)}, u32[]{:S(2)}) collective-permute-start(bf16[1,3,64,128]{3,2,1,0:T(8,128)(2,1)S(1)} %collective-permute-done.2.refs_1_), channel_id=1, source_target_pairs={{0,4},{4,0},{8,12},{12,8},{16,20},{20,16},{24,28},{28,24},{1,5},{5... | collective-permute-start | bytes 147464 | tf_op jit(solution)/shard_map/ppermute | solution.py:334
  14.4 7.0 %collective-permute-start.8 = (bf16[176,128]{1,0:T(8,128)(2,1)S(1)}, bf16[176,128]{1,0:T(8,128)(2,1)S(1)}, u32[]{:S(2)}, u32[]{:S(2)}) collective-permute-start(bf16[176,128]{1,0:T(8,128)(2,1)S(1)} %get-tuple-element.21), channel_id=1, source_target_pairs={{0,2},{1,3},{2,0},{3,1},{4,6},{5,7},{6,4},{7,5},{8,10},{9,11},{10,... | collective-permute-start | bytes 135176 | tf_op jit(solution)/shard_map/ppermute | solution.py:338
  14.8 6.8 %collective-permute-start.9 = (bf16[176,128]{1,0:T(8,128)(2,1)S(1)}, bf16[176,128]{1,0:T(8,128)(2,1)S(1)}, u32[]{:S(2)}, u32[]{:S(2)}) collective-permute-start(bf16[176,128]{1,0:T(8,128)(2,1)S(1)} %get-tuple-element.22), channel_id=1, source_target_pairs={{0,1},{1,2},{2,3},{3,0},{4,5},{5,6},{6,7},{7,4},{8,9},{9,10},{10,1... | collective-permute-start | bytes 135176 | tf_op jit(solution)/shard_map/ppermute | solution.py:338
  16.4 5.2 %collective-permute-start.10 = (bf16[176,128]{1,0:T(8,128)(2,1)S(1)}, bf16[176,128]{1,0:T(8,128)(2,1)S(1)}, u32[]{:S(2)}, u32[]{:S(2)}) collective-permute-start(bf16[176,128]{1,0:T(8,128)(2,1)S(1)} %get-tuple-element.23), channel_id=1, source_target_pairs={{0,3},{1,0},{2,1},{3,2},{4,7},{5,4},{6,5},{7,6},{8,11},{9,8},{10,9... | collective-permute-start | bytes 135176 | tf_op jit(solution)/shard_map/ppermute | solution.py:338

commit v16 on v15

--- a/solution.py
+++ b/solution.py
@@ -137,7 +137,7 @@
     begin = 0
     if not first:
         begin = before[0].shape[0]
-        rows_of_slots = jnp.concatenate([head[0:1] for head in heads] * 2, axis=0).astype(BF16)
+        rows_of_slots = jnp.concatenate([head[0:1] for head in heads], axis=0).astype(BF16)
         for k in range(n_tensor):
             outs[k][:begin, :] = before[k][...]
             outs[k][begin + len(tiles) * share:, :] = rows_of_slots
@@ -286,7 +286,7 @@
             value = value + message[start:stop, :].astype(F32)
         return value
 
-    places = [load(group, end, end + 2 * n_dp)[:n_dp].astype(I32) for group in groups]
+    places = [load(group, end, end + n_dp).astype(I32) for group in groups]
     for acc in accs:
         acc[...] = jnp.zeros_like(acc)
     low = low_half((share, 2 * side))
@@ -345,7 +345,7 @@
             tokens = tokens + [swap(value, "tensor", n_tensor, k) for value in tokens]
         return [lax.all_gather(packed, "dp", axis=0, tiled=True)], tokens
     far_tokens = swap(inputs, "tensor", n_tensor, 2)
-    near, second, last = [swap(packed, "dp", n_dp, k) for k in (6, 2, 4)]
+    near, second, last = [swap(packed, "dp", n_dp, k) for k in (2, 4, 6)]
     joined, tokens = pl.pallas_call(
         join_kernel,
         out_shape=[
@@ -406,7 +406,7 @@
         )(*gathered[:half], grad_out)
         partial_sums = pl.pallas_call(
             functools.partial(slots_kernel, False, n_parts, n_tensor),
-            out_shape=[pltpu.VMEM((2 * tiles * share + 2 * n_dp, 2 * side), BF16)] * n_tensor,
+            out_shape=[pltpu.VMEM((2 * tiles * share + n_dp, 2 * side), BF16)] * n_tensor,
             in_specs=[VMEM] * (n_parts + 1 + n_tensor),
             out_specs=[VMEM] * n_tensor,
             scratch_shapes=scratch,

time: 23 us -> 22.9 us (level)
  starting transfers between devices: 14.1 us -> 13.6 us
  waiting for transfers between devices: 3.91 us -> 4.3 us
    ppermute x8, waiting for transfers between devices: 2.17 us -> 2.68 us  [swap(): return lax.ppermute(value, axis, [(i, i ^ k) for i in range(n)])]
    ppermute x8, starting transfers between devices: 9.85 us -> 9.37 us  [swap(): return lax.ppermute(value, axis, [(i, i ^ k) for i in range(n)])]
  transfers between devices with their start and end apart: 11 -> 11, of which waited for: 5 -> 7; matrix products, arithmetic and copies ran while one was open for 0% -> 0% of each run, Pallas kernels for 13% -> 13%
where the time goes in v16:
time: 22.9 us; the launch traced here: 22.7 us
  starting transfers between devices  13.6 us (59%)
  waiting for transfers between devices  4.3 us (19%)
  Pallas kernels  4.09 us (18%)
  between operations  0.69 us (3%)
    ppermute x8, starting transfers between devices, swap(): return lax.ppermute(value, axis, [(i, i ^ k) for i in range(n)])  9.37 us
    ppermute x3, starting transfers between devices, shift(): return lax.ppermute(value, axis, [(i, (i + k) % n) for i in range(n)])  4.23 us
    ppermute x8, waiting for transfers between devices, swap(): return lax.ppermute(value, axis, [(i, i ^ k) for i in range(n)])  2.68 us
    ppermute x3, waiting for transfers between devices, shift(): return lax.ppermute(value, axis, [(i, (i + k) % n) for i in range(n)])  1.62 us
    pallas_call x1, Pallas kernels, on_device(): pl.pallas_call(functools.partial(forward_kernel, count, per_slot, n_parts...  1.24 us
    pallas_call x1, Pallas kernels, on_device(): pl.pallas_call(functools.partial(sum_kernel, tuple(map(len, groups)), pai...  1.15 us
    pallas_call x1, Pallas kernels, on_device(): pl.pallas_call(functools.partial(pack_kernel, count, row_count, col_count...  0.93 us
  transfers between devices with their start and end apart: 11, of which 7 were waited for; matrix products, arithmetic and copies ran while one was open for 0% of the time, Pallas kernels for 13%

profile of v16, /device:TPU:0, one launch (start us, length us, event | category | flops | bytes accessed | tf_op | source)
XLA Modules:
  0.0 22.7 jit_solution(9369794898972304105)
XLA Ops:
  0.6 0.0 copy-start
  0.6 4.1 %collective-permute-start.1 = (bf16[8,4096]{1,0:T(8,128)(2,1)}, bf16[8,4096]{1,0:T(8,128)(2,1)S(1)}, u32[]{:S(2)}, u32[]{:S(2)}) collective-permute-start(bf16[8,4096]{1,0:T(8,128)(2,1)} %tokens.1), channel_id=1, source_target_pairs={{0,2},{1,3},{2,0},{3,1},{4,6},{5,7},{6,4},{7,5},{8,10},{9,11},{10,... | collective-permute-start | bytes 196616 | tf_op jit(solution)/shard_map/ppermute | solution.py:334
  4.7 0.9 %shard_map.59.own = bf16[1,3,64,128]{3,2,1,0:T(8,128)(2,1)S(1)} custom-call(s32[1,5]{1,0:T(1,128)} %slots_hbm.1, bf16[1,5,64,64]{3,2,1,0:T(8,128)(2,1)} %values_hbm.1), custom_call_target="tpu_custom_call" | custom-call | tf_op jit(solution)/shard_map/pallas_call | solution.py:374
  5.7 0.0 copy-start.1
  5.7 1.6 %collective-permute-start = (bf16[1,3,64,128]{3,2,1,0:T(8,128)(2,1)S(1)}, bf16[1,3,64,128]{3,2,1,0:T(8,128)(2,1)S(1)}, u32[]{:S(2)}, u32[]{:S(2)}) collective-permute-start(bf16[1,3,64,128]{3,2,1,0:T(8,128)(2,1)S(1)} %shard_map.59.own), channel_id=1, source_target_pairs={{0,8},{4,12},{8,0},{12,4},{16,24},{20,28},{24,16},{28,20},{1,9},{5... | collective-permute-start | bytes 147464 | tf_op jit(solution)/shard_map/ppermute | solution.py:334
  7.2 1.5 %collective-permute-start.3 = (bf16[1,3,64,128]{3,2,1,0:T(8,128)(2,1)S(1)}, bf16[1,3,64,128]{3,2,1,0:T(8,128)(2,1)S(1)}, u32[]{:S(2)}, u32[]{:S(2)}) collective-permute-start(bf16[1,3,64,128]{3,2,1,0:T(8,128)(2,1)S(1)} %shard_map.59.own), channel_id=1, source_target_pairs={{0,24},{4,28},{8,16},{12,20},{16,8},{20,12},{24,0},{28,4},{1,25},{... | collective-permute-start | bytes 147464 | tf_op jit(solution)/shard_map/ppermute | solution.py:334
  8.7 0.5 %collective-permute-start.2 = (bf16[1,3,64,128]{3,2,1,0:T(8,128)(2,1)S(1)}, bf16[1,3,64,128]{3,2,1,0:T(8,128)(2,1)S(1)}, u32[]{:S(2)}, u32[]{:S(2)}) collective-permute-start(bf16[1,3,64,128]{3,2,1,0:T(8,128)(2,1)S(1)} %shard_map.59.own), channel_id=1, source_target_pairs={{0,16},{4,20},{8,24},{12,28},{16,0},{20,4},{24,8},{28,12},{1,17},{... | collective-permute-start | bytes 147464 | tf_op jit(solution)/shard_map/ppermute | solution.py:334
  9.2 0.6 %collective-permute-done.near = bf16[1,3,64,128]{3,2,1,0:T(8,128)(2,1)S(1)} collective-permute-done((bf16[1,3,64,128]{3,2,1,0:T(8,128)(2,1)S(1)}, bf16[1,3,64,128]{3,2,1,0:T(8,128)(2,1)S(1)}, u32[]{:S(2)}, u32[]{:S(2)}) %collective-permute-start) | collective-permute-done | bytes 49184 | tf_op jit(solution)/shard_map/ppermute | solution.py:334
  9.8 0.0 collective-permute-done.1.far_tokens
  9.9 0.0 copy-done
  9.9 0.1 collective-permute-start.4
  10.0 1.6 %collective-permute-start.7 = (bf16[2,8,4096]{2,1,0:T(8,128)(2,1)S(1)}, bf16[2,8,4096]{2,1,0:T(8,128)(2,1)S(1)}, u32[]{:S(2)}, u32[]{:S(2)}) collective-permute-start(bf16[2,8,4096]{2,1,0:T(8,128)(2,1)S(1)} %get-tuple-element.14.refs_6_), channel_id=1, source_target_pairs={{0,1},{1,0},{2,3},{3,2},{4,5},{5,4},{6,7},{7,6},{8,9},{9,8},{10,11... | collective-permute-start | bytes 393224 | tf_op jit(solution)/shard_map/ppermute | solution.py:334
  11.6 0.6 %collective-permute-done.3.refs_2_ = bf16[1,3,64,128]{3,2,1,0:T(8,128)(2,1)S(1)} collective-permute-done((bf16[1,3,64,128]{3,2,1,0:T(8,128)(2,1)S(1)}, bf16[1,3,64,128]{3,2,1,0:T(8,128)(2,1)S(1)}, u32[]{:S(2)}, u32[]{:S(2)}) %collective-permute-start.3) | collective-permute-done | bytes 49184 | tf_op jit(solution)/shard_map/ppermute | solution.py:334
  12.2 0.0 collective-permute-start.6
  12.2 0.6 %collective-permute-done.2.refs_1_ = bf16[1,3,64,128]{3,2,1,0:T(8,128)(2,1)S(1)} collective-permute-done((bf16[1,3,64,128]{3,2,1,0:T(8,128)(2,1)S(1)}, bf16[1,3,64,128]{3,2,1,0:T(8,128)(2,1)S(1)}, u32[]{:S(2)}, u32[]{:S(2)}) %collective-permute-start.2) | collective-permute-done | bytes 49184 | tf_op jit(solution)/shard_map/ppermute | solution.py:334
  12.8 0.0 collective-permute-start.5
  12.8 0.0 copy-done.1
  12.8 0.4 %shard_map.62 = (bf16[80,128]{1,0:T(8,128)(2,1)S(1)}, bf16[80,128]{1,0:T(8,128)(2,1)S(1)}, bf16[80,128]{1,0:T(8,128)(2,1)S(1)}, bf16[80,128]{1,0:T(8,128)(2,1)S(1)}, bf16[15,32,128]{2,1,0:T(8,128)(2,1)S(1)}) custom-call(bf16[2,3,64,128]{3,2,1,0:T(8,128)(2,1)S(1)} %get-tuple-element.13.refs_0_, bf16[1,3,64,128]{3,2,1,0:T(8,128)(2,1)S(1)} %collective-permute-done.2.refs_1_, ...), custom_call_target="tpu_custom_call" | custom-call | tf_op jit(solution)/shard_map/pallas_call | solution.py:399
  13.2 0.2 %collective-permute-done.6.refs_5_ = bf16[1,3,64,128]{3,2,1,0:T(8,128)(2,1)S(1)} collective-permute-done((bf16[1,3,64,128]{3,2,1,0:T(8,128)(2,1)S(1)}, bf16[1,3,64,128]{3,2,1,0:T(8,128)(2,1)S(1)}, u32[]{:S(2)}, u32[]{:S(2)}) %collective-permute-start.6) | collective-permute-done | bytes 49184 | tf_op jit(solution)/shard_map/ppermute | solution.py:334
  13.5 0.6 %collective-permute-done.5.refs_4_ = bf16[1,3,64,128]{3,2,1,0:T(8,128)(2,1)S(1)} collective-permute-done((bf16[1,3,64,128]{3,2,1,0:T(8,128)(2,1)S(1)}, bf16[1,3,64,128]{3,2,1,0:T(8,128)(2,1)S(1)}, u32[]{:S(2)}, u32[]{:S(2)}) %collective-permute-start.5) | collective-permute-done | bytes 49184 | tf_op jit(solution)/shard_map/ppermute | solution.py:334
  14.1 0.0 collective-permute-done.4.refs_3_
  14.1 0.4 %shard_map.63 = (bf16[168,128]{1,0:T(8,128)(2,1)S(1)}, bf16[168,128]{1,0:T(8,128)(2,1)S(1)}, bf16[168,128]{1,0:T(8,128)(2,1)S(1)}, bf16[168,128]{1,0:T(8,128)(2,1)S(1)}) custom-call(bf16[2,3,64,128]{3,2,1,0:T(8,128)(2,1)S(1)} %get-tuple-element.13.refs_0_, bf16[1,3,64,128]{3,2,1,0:T(8,128)(2,1)S(1)} %collective-permute-done.2.refs_1_, ...), custom_call_target="tpu_custom_call" | custom-call | tf_op jit(solution)/shard_map/pallas_call | solution.py:407
  14.4 0.4 %collective-permute-start.8 = (bf16[168,128]{1,0:T(8,128)(2,1)S(1)}, bf16[168,128]{1,0:T(8,128)(2,1)S(1)}, u32[]{:S(2)}, u32[]{:S(2)}) collective-permute-start(bf16[168,128]{1,0:T(8,128)(2,1)S(1)} %get-tuple-element.21), channel_id=1, source_target_pairs={{0,2},{1,3},{2,0},{3,1},{4,6},{5,7},{6,4},{7,5},{8,10},{9,11},{10,... | collective-permute-start | bytes 129032 | tf_op jit(solution)/shard_map/ppermute | solution.py:338
  14.8 1.6 %collective-permute-start.9 = (bf16[168,128]{1,0:T(8,128)(2,1)S(1)}, bf16[168,128]{1,0:T(8,128)(2,1)S(1)}, u32[]{:S(2)}, u32[]{:S(2)}) collective-permute-start(bf16[168,128]{1,0:T(8,128)(2,1)S(1)} %get-tuple-element.22), channel_id=1, source_target_pairs={{0,1},{1,2},{2,3},{3,0},{4,5},{5,6},{6,7},{7,4},{8,9},{9,10},{10,1... | collective-permute-start | bytes 129032 | tf_op jit(solution)/shard_map/ppermute | solution.py:338
  16.4 2.2 %collective-permute-start.10 = (bf16[168,128]{1,0:T(8,128)(2,1)S(1)}, bf16[168,128]{1,0:T(8,128)(2,1)S(1)}, u32[]{:S(2)}, u32[]{:S(2)}) collective-permute-start(bf16[168,128]{1,0:T(8,128)(2,1)S(1)} %get-tuple-element.23), channel_id=1, source_target_pairs={{0,3},{1,0},{2,1},{3,2},{4,7},{5,4},{6,5},{7,6},{8,11},{9,8},{10,9... | collective-permute-start | bytes 129032 | tf_op jit(solution)/shard_map/ppermute | solution.py:338
  18.7 0.0 collective-permute-done.7.refs_7_
  18.7 1.2 %shard_map.61 = bf16[32,896]{1,0:T(8,128)(2,1)} custom-call(bf16[2,3,64,128]{3,2,1,0:T(8,128)(2,1)S(1)} %get-tuple-element.13.refs_0_, bf16[1,3,64,128]{3,2,1,0:T(8,128)(2,1)S(1)} %collective-permute-done.2.refs_1_, bf16[1,3,64,128]{3,2,1,0:T(8,128)(2,1)S(1)} %collective-permute-done.3.refs_2_, bf16[2,3,64,128]{3,2,1,0:T(8,128)(2,1)S(1)} %collective-permute-done.4.refs_3_, ...), custom_call_target="tpu_custom_call" | custom-call | tf_op jit(solution)/shard_map/pallas_call | solution.py:430
  19.9 1.4 %collective-permute-done.8.refs_1_ = bf16[168,128]{1,0:T(8,128)(2,1)S(1)} collective-permute-done((bf16[168,128]{1,0:T(8,128)(2,1)S(1)}, bf16[168,128]{1,0:T(8,128)(2,1)S(1)}, u32[]{:S(2)}, u32[]{:S(2)}) %collective-permute-start.8) | collective-permute-done | bytes 43040 | tf_op jit(solution)/shard_map/ppermute | solution.py:338
  21.3 0.2 collective-permute-done.9.refs_2_
  21.5 0.0 collective-permute-done.10.refs_3_
  21.5 1.1 %shard_map.64 = bf16[8,4096]{1,0:T(8,128)(2,1)} custom-call(bf16[168,128]{1,0:T(8,128)(2,1)S(1)} %get-tuple-element.20.refs_0_, bf16[168,128]{1,0:T(8,128)(2,1)S(1)} %collective-permute-done.8.refs_1_, bf16[168,128]{1,0:T(8,128)(2,1)S(1)} %collective-permute-done.9.refs_2_, bf16[168,128]{1,0:T(8,128)(2,1)S(1)} %collective-permute-done.10.refs_3_), custom_call_target="tpu_custom_call" | custom-call | tf_op jit(solution)/shard_map/pallas_call | solution.py:445
  (1 shorter events, 0.0 us)
Async XLA Ops:
  0.6 9.2 %copy-start = (bf16[8,4096]{1,0:T(8,128)(2,1)S(1)}, bf16[8,4096]{1,0:T(8,128)(2,1)}, u32[]{:S(2)}) copy-start(bf16[8,4096]{1,0:T(8,128)(2,1)} %tokens.1) | copy-start | bytes 196612
  0.6 9.2 %collective-permute-start.1 = (bf16[8,4096]{1,0:T(8,128)(2,1)}, bf16[8,4096]{1,0:T(8,128)(2,1)S(1)}, u32[]{:S(2)}, u32[]{:S(2)}) collective-permute-start(bf16[8,4096]{1,0:T(8,128)(2,1)} %tokens.1), channel_id=1, source_target_pairs={{0,2},{1,3},{2,0},{3,1},{4,6},{5,7},{6,4},{7,5},{8,10},{9,11},{10,... | collective-permute-start | bytes 196616 | tf_op jit(solution)/shard_map/ppermute | solution.py:334
  5.7 7.2 %copy-start.1 = (bf16[32,896]{1,0:T(8,128)(2,1)S(1)}, bf16[32,896]{1,0:T(8,128)(2,1)}, u32[]{:S(2)}) copy-start(bf16[32,896]{1,0:T(8,128)(2,1)} %refs_3_.1) | copy-start | bytes 172036
  5.7 4.2 %collective-permute-start = (bf16[1,3,64,128]{3,2,1,0:T(8,128)(2,1)S(1)}, bf16[1,3,64,128]{3,2,1,0:T(8,128)(2,1)S(1)}, u32[]{:S(2)}, u32[]{:S(2)}) collective-permute-start(bf16[1,3,64,128]{3,2,1,0:T(8,128)(2,1)S(1)} %shard_map.59.own), channel_id=1, source_target_pairs={{0,8},{4,12},{8,0},{12,4},{16,24},{20,28},{24,16},{28,20},{1,9},{5... | collective-permute-start | bytes 147464 | tf_op jit(solution)/shard_map/ppermute | solution.py:334
  7.2 5.0 %collective-permute-start.3 = (bf16[1,3,64,128]{3,2,1,0:T(8,128)(2,1)S(1)}, bf16[1,3,64,128]{3,2,1,0:T(8,128)(2,1)S(1)}, u32[]{:S(2)}, u32[]{:S(2)}) collective-permute-start(bf16[1,3,64,128]{3,2,1,0:T(8,128)(2,1)S(1)} %shard_map.59.own), channel_id=1, source_target_pairs={{0,24},{4,28},{8,16},{12,20},{16,8},{20,12},{24,0},{28,4},{1,25},{... | collective-permute-start | bytes 147464 | tf_op jit(solution)/shard_map/ppermute | solution.py:334
  8.7 4.1 %collective-permute-start.2 = (bf16[1,3,64,128]{3,2,1,0:T(8,128)(2,1)S(1)}, bf16[1,3,64,128]{3,2,1,0:T(8,128)(2,1)S(1)}, u32[]{:S(2)}, u32[]{:S(2)}) collective-permute-start(bf16[1,3,64,128]{3,2,1,0:T(8,128)(2,1)S(1)} %shard_map.59.own), channel_id=1, source_target_pairs={{0,16},{4,20},{8,24},{12,28},{16,0},{20,4},{24,8},{28,12},{1,17},{... | collective-permute-start | bytes 147464 | tf_op jit(solution)/shard_map/ppermute | solution.py:334
  9.9 4.2 %collective-permute-start.4 = (bf16[2,3,64,128]{3,2,1,0:T(8,128)(2,1)S(1)}, bf16[2,3,64,128]{3,2,1,0:T(8,128)(2,1)S(1)}, u32[]{:S(2)}, u32[]{:S(2)}) collective-permute-start(bf16[2,3,64,128]{3,2,1,0:T(8,128)(2,1)S(1)} %get-tuple-element.13.refs_0_), channel_id=1, source_target_pairs={{0,4},{4,0},{8,12},{12,8},{16,20},{20,16},{24,28},{28,24},{1,5},{5... | collective-permute-start | bytes 294920 | tf_op jit(solution)/shard_map/ppermute | solution.py:334
  10.0 8.7 %collective-permute-start.7 = (bf16[2,8,4096]{2,1,0:T(8,128)(2,1)S(1)}, bf16[2,8,4096]{2,1,0:T(8,128)(2,1)S(1)}, u32[]{:S(2)}, u32[]{:S(2)}) collective-permute-start(bf16[2,8,4096]{2,1,0:T(8,128)(2,1)S(1)} %get-tuple-element.14.refs_6_), channel_id=1, source_target_pairs={{0,1},{1,0},{2,3},{3,2},{4,5},{5,4},{6,7},{7,6},{8,9},{9,8},{10,11... | collective-permute-start | bytes 393224 | tf_op jit(solution)/shard_map/ppermute | solution.py:334
  12.2 1.2 %collective-permute-start.6 = (bf16[1,3,64,128]{3,2,1,0:T(8,128)(2,1)S(1)}, bf16[1,3,64,128]{3,2,1,0:T(8,128)(2,1)S(1)}, u32[]{:S(2)}, u32[]{:S(2)}) collective-permute-start(bf16[1,3,64,128]{3,2,1,0:T(8,128)(2,1)S(1)} %collective-permute-done.3.refs_2_), channel_id=1, source_target_pairs={{0,4},{4,0},{8,12},{12,8},{16,20},{20,16},{24,28},{28,24},{1,5},{5... | collective-permute-start | bytes 147464 | tf_op jit(solution)/shard_map/ppermute | solution.py:334
  12.8 1.2 %collective-permute-start.5 = (bf16[1,3,64,128]{3,2,1,0:T(8,128)(2,1)S(1)}, bf16[1,3,64,128]{3,2,1,0:T(8,128)(2,1)S(1)}, u32[]{:S(2)}, u32[]{:S(2)}) collective-permute-start(bf16[1,3,64,128]{3,2,1,0:T(8,128)(2,1)S(1)} %collective-permute-done.2.refs_1_), channel_id=1, source_target_pairs={{0,4},{4,0},{8,12},{12,8},{16,20},{20,16},{24,28},{28,24},{1,5},{5... | collective-permute-start | bytes 147464 | tf_op jit(solution)/shard_map/ppermute | solution.py:334
  14.4 6.9 %collective-permute-start.8 = (bf16[168,128]{1,0:T(8,128)(2,1)S(1)}, bf16[168,128]{1,0:T(8,128)(2,1)S(1)}, u32[]{:S(2)}, u32[]{:S(2)}) collective-permute-start(bf16[168,128]{1,0:T(8,128)(2,1)S(1)} %get-tuple-element.21), channel_id=1, source_target_pairs={{0,2},{1,3},{2,0},{3,1},{4,6},{5,7},{6,4},{7,5},{8,10},{9,11},{10,... | collective-permute-start | bytes 129032 | tf_op jit(solution)/shard_map/ppermute | solution.py:338
  14.8 6.7 %collective-permute-start.9 = (bf16[168,128]{1,0:T(8,128)(2,1)S(1)}, bf16[168,128]{1,0:T(8,128)(2,1)S(1)}, u32[]{:S(2)}, u32[]{:S(2)}) collective-permute-start(bf16[168,128]{1,0:T(8,128)(2,1)S(1)} %get-tuple-element.22), channel_id=1, source_target_pairs={{0,1},{1,2},{2,3},{3,0},{4,5},{5,6},{6,7},{7,4},{8,9},{9,10},{10,1... | collective-permute-start | bytes 129032 | tf_op jit(solution)/shard_map/ppermute | solution.py:338
  16.4 5.1 %collective-permute-start.10 = (bf16[168,128]{1,0:T(8,128)(2,1)S(1)}, bf16[168,128]{1,0:T(8,128)(2,1)S(1)}, u32[]{:S(2)}, u32[]{:S(2)}) collective-permute-start(bf16[168,128]{1,0:T(8,128)(2,1)S(1)} %get-tuple-element.23), channel_id=1, source_target_pairs={{0,3},{1,0},{2,1},{3,2},{4,7},{5,4},{6,5},{7,6},{8,11},{9,8},{10,9... | collective-permute-start | bytes 129032 | tf_op jit(solution)/shard_map/ppermute | solution.py:338

commit v17 on v16

--- a/solution.py
+++ b/solution.py
@@ -345,7 +345,7 @@
             tokens = tokens + [swap(value, "tensor", n_tensor, k) for value in tokens]
         return [lax.all_gather(packed, "dp", axis=0, tiled=True)], tokens
     far_tokens = swap(inputs, "tensor", n_tensor, 2)
-    near, second, last = [swap(packed, "dp", n_dp, k) for k in (2, 4, 6)]
+    near, second, last = [swap(packed, "dp", n_dp, k) for k in (6, 2, 4)]
     joined, tokens = pl.pallas_call(
         join_kernel,
         out_shape=[

time: 22.9 us -> 22.9 us (level)
  waiting for transfers between devices: 4.3 us -> 3.79 us
  starting transfers between devices: 13.6 us -> 14.1 us
    ppermute x8, waiting for transfers between devices: 2.68 us -> 2.17 us  [swap(): return lax.ppermute(value, axis, [(i, i ^ k) for i in range(n)])]
    ppermute x8, starting transfers between devices: 9.37 us -> 9.85 us  [swap(): return lax.ppermute(value, axis, [(i, i ^ k) for i in range(n)])]
  transfers between devices with their start and end apart: 11 -> 11, of which waited for: 7 -> 5; matrix products, arithmetic and copies ran while one was open for 0% -> 0% of each run, Pallas kernels for 13% -> 13%
where the time goes in v17:
time: 22.9 us; the launch traced here: 22.6 us
  starting transfers between devices  14.1 us (62%)
  Pallas kernels  4.08 us (18%)
  waiting for transfers between devices  3.79 us (17%)
  between operations  0.69 us (3%)
    ppermute x8, starting transfers between devices, swap(): return lax.ppermute(value, axis, [(i, i ^ k) for i in range(n)])  9.85 us
    ppermute x3, starting transfers between devices, shift(): return lax.ppermute(value, axis, [(i, (i + k) % n) for i in range(n)])  4.23 us
    ppermute x8, waiting for transfers between devices, swap(): return lax.ppermute(value, axis, [(i, i ^ k) for i in range(n)])  2.17 us
    ppermute x3, waiting for transfers between devices, shift(): return lax.ppermute(value, axis, [(i, (i + k) % n) for i in range(n)])  1.62 us
    pallas_call x1, Pallas kernels, on_device(): pl.pallas_call(functools.partial(forward_kernel, count, per_slot, n_parts...  1.23 us
    pallas_call x1, Pallas kernels, on_device(): pl.pallas_call(functools.partial(sum_kernel, tuple(map(len, groups)), pai...  1.14 us
    pallas_call x1, Pallas kernels, on_device(): pl.pallas_call(functools.partial(pack_kernel, count, row_count, col_count...  0.93 us
  transfers between devices with their start and end apart: 11, of which 5 were waited for; matrix products, arithmetic and copies ran while one was open for 0% of the time, Pallas kernels for 13%

profile of v17, /device:TPU:0, one launch (start us, length us, event | category | flops | bytes accessed | tf_op | source)
XLA Modules:
  0.0 22.6 jit_solution(626736514059053328)
XLA Ops:
  0.6 0.0 copy-start
  0.6 4.1 %collective-permute-start.1 = (bf16[8,4096]{1,0:T(8,128)(2,1)}, bf16[8,4096]{1,0:T(8,128)(2,1)S(1)}, u32[]{:S(2)}, u32[]{:S(2)}) collective-permute-start(bf16[8,4096]{1,0:T(8,128)(2,1)} %tokens.1), channel_id=1, source_target_pairs={{0,2},{1,3},{2,0},{3,1},{4,6},{5,7},{6,4},{7,5},{8,10},{9,11},{10,... | collective-permute-start | bytes 196616 | tf_op jit(solution)/shard_map/ppermute | solution.py:334
  4.7 0.9 %shard_map.59.own = bf16[1,3,64,128]{3,2,1,0:T(8,128)(2,1)S(1)} custom-call(s32[1,5]{1,0:T(1,128)} %slots_hbm.1, bf16[1,5,64,64]{3,2,1,0:T(8,128)(2,1)} %values_hbm.1), custom_call_target="tpu_custom_call" | custom-call | tf_op jit(solution)/shard_map/pallas_call | solution.py:374
  5.7 0.0 copy-start.1
  5.7 2.5 %collective-permute-start = (bf16[1,3,64,128]{3,2,1,0:T(8,128)(2,1)S(1)}, bf16[1,3,64,128]{3,2,1,0:T(8,128)(2,1)S(1)}, u32[]{:S(2)}, u32[]{:S(2)}) collective-permute-start(bf16[1,3,64,128]{3,2,1,0:T(8,128)(2,1)S(1)} %shard_map.59.own), channel_id=1, source_target_pairs={{0,24},{4,28},{8,16},{12,20},{16,8},{20,12},{24,0},{28,4},{1,25},{... | collective-permute-start | bytes 147464 | tf_op jit(solution)/shard_map/ppermute | solution.py:334
  8.2 0.5 %collective-permute-start.3 = (bf16[1,3,64,128]{3,2,1,0:T(8,128)(2,1)S(1)}, bf16[1,3,64,128]{3,2,1,0:T(8,128)(2,1)S(1)}, u32[]{:S(2)}, u32[]{:S(2)}) collective-permute-start(bf16[1,3,64,128]{3,2,1,0:T(8,128)(2,1)S(1)} %shard_map.59.own), channel_id=1, source_target_pairs={{0,16},{4,20},{8,24},{12,28},{16,0},{20,4},{24,8},{28,12},{1,17},{... | collective-permute-start | bytes 147464 | tf_op jit(solution)/shard_map/ppermute | solution.py:334
  8.7 0.5 %collective-permute-start.2 = (bf16[1,3,64,128]{3,2,1,0:T(8,128)(2,1)S(1)}, bf16[1,3,64,128]{3,2,1,0:T(8,128)(2,1)S(1)}, u32[]{:S(2)}, u32[]{:S(2)}) collective-permute-start(bf16[1,3,64,128]{3,2,1,0:T(8,128)(2,1)S(1)} %shard_map.59.own), channel_id=1, source_target_pairs={{0,8},{4,12},{8,0},{12,4},{16,24},{20,28},{24,16},{28,20},{1,9},{5... | collective-permute-start | bytes 147464 | tf_op jit(solution)/shard_map/ppermute | solution.py:334
  9.2 1.6 %collective-permute-done.near = bf16[1,3,64,128]{3,2,1,0:T(8,128)(2,1)S(1)} collective-permute-done((bf16[1,3,64,128]{3,2,1,0:T(8,128)(2,1)S(1)}, bf16[1,3,64,128]{3,2,1,0:T(8,128)(2,1)S(1)}, u32[]{:S(2)}, u32[]{:S(2)}) %collective-permute-start) | collective-permute-done | bytes 49184 | tf_op jit(solution)/shard_map/ppermute | solution.py:334
  10.9 0.0 collective-permute-done.1.far_tokens
  10.9 0.0 copy-done
  10.9 0.1 collective-permute-start.4
  11.0 1.6 %collective-permute-start.7 = (bf16[2,8,4096]{2,1,0:T(8,128)(2,1)S(1)}, bf16[2,8,4096]{2,1,0:T(8,128)(2,1)S(1)}, u32[]{:S(2)}, u32[]{:S(2)}) collective-permute-start(bf16[2,8,4096]{2,1,0:T(8,128)(2,1)S(1)} %get-tuple-element.14.refs_6_), channel_id=1, source_target_pairs={{0,1},{1,0},{2,3},{3,2},{4,5},{5,4},{6,7},{7,6},{8,9},{9,8},{10,11... | collective-permute-start | bytes 393224 | tf_op jit(solution)/shard_map/ppermute | solution.py:334
  12.6 0.0 collective-permute-done.3.refs_2_
  12.6 0.2 collective-permute-start.6
  12.8 0.0 collective-permute-done.2.refs_1_
  12.8 0.3 %collective-permute-start.5 = (bf16[1,3,64,128]{3,2,1,0:T(8,128)(2,1)S(1)}, bf16[1,3,64,128]{3,2,1,0:T(8,128)(2,1)S(1)}, u32[]{:S(2)}, u32[]{:S(2)}) collective-permute-start(bf16[1,3,64,128]{3,2,1,0:T(8,128)(2,1)S(1)} %collective-permute-done.2.refs_1_), channel_id=1, source_target_pairs={{0,4},{4,0},{8,12},{12,8},{16,20},{20,16},{24,28},{28,24},{1,5},{5... | collective-permute-start | bytes 147464 | tf_op jit(solution)/shard_map/ppermute | solution.py:334
  13.1 0.0 copy-done.1
  13.1 0.4 %shard_map.62 = (bf16[80,128]{1,0:T(8,128)(2,1)S(1)}, bf16[80,128]{1,0:T(8,128)(2,1)S(1)}, bf16[80,128]{1,0:T(8,128)(2,1)S(1)}, bf16[80,128]{1,0:T(8,128)(2,1)S(1)}, bf16[15,32,128]{2,1,0:T(8,128)(2,1)S(1)}) custom-call(bf16[2,3,64,128]{3,2,1,0:T(8,128)(2,1)S(1)} %get-tuple-element.13.refs_0_, bf16[1,3,64,128]{3,2,1,0:T(8,128)(2,1)S(1)} %collective-permute-done.2.refs_1_, ...), custom_call_target="tpu_custom_call" | custom-call | tf_op jit(solution)/shard_map/pallas_call | solution.py:399
  13.5 0.3 %collective-permute-done.6.refs_5_ = bf16[1,3,64,128]{3,2,1,0:T(8,128)(2,1)S(1)} collective-permute-done((bf16[1,3,64,128]{3,2,1,0:T(8,128)(2,1)S(1)}, bf16[1,3,64,128]{3,2,1,0:T(8,128)(2,1)S(1)}, u32[]{:S(2)}, u32[]{:S(2)}) %collective-permute-start.6) | collective-permute-done | bytes 49184 | tf_op jit(solution)/shard_map/ppermute | solution.py:334
  13.8 0.2 collective-permute-done.5.refs_4_
  14.0 0.0 collective-permute-done.4.refs_3_
  14.0 0.4 %shard_map.63 = (bf16[168,128]{1,0:T(8,128)(2,1)S(1)}, bf16[168,128]{1,0:T(8,128)(2,1)S(1)}, bf16[168,128]{1,0:T(8,128)(2,1)S(1)}, bf16[168,128]{1,0:T(8,128)(2,1)S(1)}) custom-call(bf16[2,3,64,128]{3,2,1,0:T(8,128)(2,1)S(1)} %get-tuple-element.13.refs_0_, bf16[1,3,64,128]{3,2,1,0:T(8,128)(2,1)S(1)} %collective-permute-done.2.refs_1_, ...), custom_call_target="tpu_custom_call" | custom-call | tf_op jit(solution)/shard_map/pallas_call | solution.py:407
  14.4 0.4 %collective-permute-start.8 = (bf16[168,128]{1,0:T(8,128)(2,1)S(1)}, bf16[168,128]{1,0:T(8,128)(2,1)S(1)}, u32[]{:S(2)}, u32[]{:S(2)}) collective-permute-start(bf16[168,128]{1,0:T(8,128)(2,1)S(1)} %get-tuple-element.21), channel_id=1, source_target_pairs={{0,2},{1,3},{2,0},{3,1},{4,6},{5,7},{6,4},{7,5},{8,10},{9,11},{10,... | collective-permute-start | bytes 129032 | tf_op jit(solution)/shard_map/ppermute | solution.py:338
  14.8 1.6 %collective-permute-start.9 = (bf16[168,128]{1,0:T(8,128)(2,1)S(1)}, bf16[168,128]{1,0:T(8,128)(2,1)S(1)}, u32[]{:S(2)}, u32[]{:S(2)}) collective-permute-start(bf16[168,128]{1,0:T(8,128)(2,1)S(1)} %get-tuple-element.22), channel_id=1, source_target_pairs={{0,1},{1,2},{2,3},{3,0},{4,5},{5,6},{6,7},{7,4},{8,9},{9,10},{10,1... | collective-permute-start | bytes 129032 | tf_op jit(solution)/shard_map/ppermute | solution.py:338
  16.4 2.2 %collective-permute-start.10 = (bf16[168,128]{1,0:T(8,128)(2,1)S(1)}, bf16[168,128]{1,0:T(8,128)(2,1)S(1)}, u32[]{:S(2)}, u32[]{:S(2)}) collective-permute-start(bf16[168,128]{1,0:T(8,128)(2,1)S(1)} %get-tuple-element.23), channel_id=1, source_target_pairs={{0,3},{1,0},{2,1},{3,2},{4,7},{5,4},{6,5},{7,6},{8,11},{9,8},{10,9... | collective-permute-start | bytes 129032 | tf_op jit(solution)/shard_map/ppermute | solution.py:338
  18.6 0.0 collective-permute-done.7.refs_7_
  18.6 1.2 %shard_map.61 = bf16[32,896]{1,0:T(8,128)(2,1)} custom-call(bf16[2,3,64,128]{3,2,1,0:T(8,128)(2,1)S(1)} %get-tuple-element.13.refs_0_, bf16[1,3,64,128]{3,2,1,0:T(8,128)(2,1)S(1)} %collective-permute-done.2.refs_1_, bf16[1,3,64,128]{3,2,1,0:T(8,128)(2,1)S(1)} %collective-permute-done.3.refs_2_, bf16[2,3,64,128]{3,2,1,0:T(8,128)(2,1)S(1)} %collective-permute-done.4.refs_3_, ...), custom_call_target="tpu_custom_call" | custom-call | tf_op jit(solution)/shard_map/pallas_call | solution.py:430
  19.9 1.4 %collective-permute-done.8.refs_1_ = bf16[168,128]{1,0:T(8,128)(2,1)S(1)} collective-permute-done((bf16[168,128]{1,0:T(8,128)(2,1)S(1)}, bf16[168,128]{1,0:T(8,128)(2,1)S(1)}, u32[]{:S(2)}, u32[]{:S(2)}) %collective-permute-start.8) | collective-permute-done | bytes 43040 | tf_op jit(solution)/shard_map/ppermute | solution.py:338
  21.3 0.2 collective-permute-done.9.refs_2_
  21.5 0.0 collective-permute-done.10.refs_3_
  21.5 1.1 %shard_map.64 = bf16[8,4096]{1,0:T(8,128)(2,1)} custom-call(bf16[168,128]{1,0:T(8,128)(2,1)S(1)} %get-tuple-element.20.refs_0_, bf16[168,128]{1,0:T(8,128)(2,1)S(1)} %collective-permute-done.8.refs_1_, bf16[168,128]{1,0:T(8,128)(2,1)S(1)} %collective-permute-done.9.refs_2_, bf16[168,128]{1,0:T(8,128)(2,1)S(1)} %collective-permute-done.10.refs_3_), custom_call_target="tpu_custom_call" | custom-call | tf_op jit(solution)/shard_map/pallas_call | solution.py:445
  (1 shorter events, 0.0 us)
Async XLA Ops:
  0.6 10.2 %copy-start = (bf16[8,4096]{1,0:T(8,128)(2,1)S(1)}, bf16[8,4096]{1,0:T(8,128)(2,1)}, u32[]{:S(2)}) copy-start(bf16[8,4096]{1,0:T(8,128)(2,1)} %tokens.1) | copy-start | bytes 196612
  0.6 10.2 %collective-permute-start.1 = (bf16[8,4096]{1,0:T(8,128)(2,1)}, bf16[8,4096]{1,0:T(8,128)(2,1)S(1)}, u32[]{:S(2)}, u32[]{:S(2)}) collective-permute-start(bf16[8,4096]{1,0:T(8,128)(2,1)} %tokens.1), channel_id=1, source_target_pairs={{0,2},{1,3},{2,0},{3,1},{4,6},{5,7},{6,4},{7,5},{8,10},{9,11},{10,... | collective-permute-start | bytes 196616 | tf_op jit(solution)/shard_map/ppermute | solution.py:334
  5.7 7.4 %copy-start.1 = (bf16[32,896]{1,0:T(8,128)(2,1)S(1)}, bf16[32,896]{1,0:T(8,128)(2,1)}, u32[]{:S(2)}) copy-start(bf16[32,896]{1,0:T(8,128)(2,1)} %refs_3_.1) | copy-start | bytes 172036
  5.7 5.2 %collective-permute-start = (bf16[1,3,64,128]{3,2,1,0:T(8,128)(2,1)S(1)}, bf16[1,3,64,128]{3,2,1,0:T(8,128)(2,1)S(1)}, u32[]{:S(2)}, u32[]{:S(2)}) collective-permute-start(bf16[1,3,64,128]{3,2,1,0:T(8,128)(2,1)S(1)} %shard_map.59.own), channel_id=1, source_target_pairs={{0,24},{4,28},{8,16},{12,20},{16,8},{20,12},{24,0},{28,4},{1,25},{... | collective-permute-start | bytes 147464 | tf_op jit(solution)/shard_map/ppermute | solution.py:334
  8.2 4.4 %collective-permute-start.3 = (bf16[1,3,64,128]{3,2,1,0:T(8,128)(2,1)S(1)}, bf16[1,3,64,128]{3,2,1,0:T(8,128)(2,1)S(1)}, u32[]{:S(2)}, u32[]{:S(2)}) collective-permute-start(bf16[1,3,64,128]{3,2,1,0:T(8,128)(2,1)S(1)} %shard_map.59.own), channel_id=1, source_target_pairs={{0,16},{4,20},{8,24},{12,28},{16,0},{20,4},{24,8},{28,12},{1,17},{... | collective-permute-start | bytes 147464 | tf_op jit(solution)/shard_map/ppermute | solution.py:334
  8.7 4.1 %collective-permute-start.2 = (bf16[1,3,64,128]{3,2,1,0:T(8,128)(2,1)S(1)}, bf16[1,3,64,128]{3,2,1,0:T(8,128)(2,1)S(1)}, u32[]{:S(2)}, u32[]{:S(2)}) collective-permute-start(bf16[1,3,64,128]{3,2,1,0:T(8,128)(2,1)S(1)} %shard_map.59.own), channel_id=1, source_target_pairs={{0,8},{4,12},{8,0},{12,4},{16,24},{20,28},{24,16},{28,20},{1,9},{5... | collective-permute-start | bytes 147464 | tf_op jit(solution)/shard_map/ppermute | solution.py:334
  10.9 3.2 %collective-permute-start.4 = (bf16[2,3,64,128]{3,2,1,0:T(8,128)(2,1)S(1)}, bf16[2,3,64,128]{3,2,1,0:T(8,128)(2,1)S(1)}, u32[]{:S(2)}, u32[]{:S(2)}) collective-permute-start(bf16[2,3,64,128]{3,2,1,0:T(8,128)(2,1)S(1)} %get-tuple-element.13.refs_0_), channel_id=1, source_target_pairs={{0,4},{4,0},{8,12},{12,8},{16,20},{20,16},{24,28},{28,24},{1,5},{5... | collective-permute-start | bytes 294920 | tf_op jit(solution)/shard_map/ppermute | solution.py:334
  11.0 7.7 %collective-permute-start.7 = (bf16[2,8,4096]{2,1,0:T(8,128)(2,1)S(1)}, bf16[2,8,4096]{2,1,0:T(8,128)(2,1)S(1)}, u32[]{:S(2)}, u32[]{:S(2)}) collective-permute-start(bf16[2,8,4096]{2,1,0:T(8,128)(2,1)S(1)} %get-tuple-element.14.refs_6_), channel_id=1, source_target_pairs={{0,1},{1,0},{2,3},{3,2},{4,5},{5,4},{6,7},{7,6},{8,9},{9,8},{10,11... | collective-permute-start | bytes 393224 | tf_op jit(solution)/shard_map/ppermute | solution.py:334
  12.6 1.2 %collective-permute-start.6 = (bf16[1,3,64,128]{3,2,1,0:T(8,128)(2,1)S(1)}, bf16[1,3,64,128]{3,2,1,0:T(8,128)(2,1)S(1)}, u32[]{:S(2)}, u32[]{:S(2)}) collective-permute-start(bf16[1,3,64,128]{3,2,1,0:T(8,128)(2,1)S(1)} %collective-permute-done.3.refs_2_), channel_id=1, source_target_pairs={{0,4},{4,0},{8,12},{12,8},{16,20},{20,16},{24,28},{28,24},{1,5},{5... | collective-permute-start | bytes 147464 | tf_op jit(solution)/shard_map/ppermute | solution.py:334
  12.8 1.2 %collective-permute-start.5 = (bf16[1,3,64,128]{3,2,1,0:T(8,128)(2,1)S(1)}, bf16[1,3,64,128]{3,2,1,0:T(8,128)(2,1)S(1)}, u32[]{:S(2)}, u32[]{:S(2)}) collective-permute-start(bf16[1,3,64,128]{3,2,1,0:T(8,128)(2,1)S(1)} %collective-permute-done.2.refs_1_), channel_id=1, source_target_pairs={{0,4},{4,0},{8,12},{12,8},{16,20},{20,16},{24,28},{28,24},{1,5},{5... | collective-permute-start | bytes 147464 | tf_op jit(solution)/shard_map/ppermute | solution.py:334
  14.4 6.9 %collective-permute-start.8 = (bf16[168,128]{1,0:T(8,128)(2,1)S(1)}, bf16[168,128]{1,0:T(8,128)(2,1)S(1)}, u32[]{:S(2)}, u32[]{:S(2)}) collective-permute-start(bf16[168,128]{1,0:T(8,128)(2,1)S(1)} %get-tuple-element.21), channel_id=1, source_target_pairs={{0,2},{1,3},{2,0},{3,1},{4,6},{5,7},{6,4},{7,5},{8,10},{9,11},{10,... | collective-permute-start | bytes 129032 | tf_op jit(solution)/shard_map/ppermute | solution.py:338
  14.8 6.7 %collective-permute-start.9 = (bf16[168,128]{1,0:T(8,128)(2,1)S(1)}, bf16[168,128]{1,0:T(8,128)(2,1)S(1)}, u32[]{:S(2)}, u32[]{:S(2)}) collective-permute-start(bf16[168,128]{1,0:T(8,128)(2,1)S(1)} %get-tuple-element.22), channel_id=1, source_target_pairs={{0,1},{1,2},{2,3},{3,0},{4,5},{5,6},{6,7},{7,4},{8,9},{9,10},{10,1... | collective-permute-start | bytes 129032 | tf_op jit(solution)/shard_map/ppermute | solution.py:338
  16.4 5.1 %collective-permute-start.10 = (bf16[168,128]{1,0:T(8,128)(2,1)S(1)}, bf16[168,128]{1,0:T(8,128)(2,1)S(1)}, u32[]{:S(2)}, u32[]{:S(2)}) collective-permute-start(bf16[168,128]{1,0:T(8,128)(2,1)S(1)} %get-tuple-element.23), channel_id=1, source_target_pairs={{0,3},{1,0},{2,1},{3,2},{4,7},{5,4},{6,5},{7,6},{8,11},{9,8},{10,9... | collective-permute-start | bytes 129032 | tf_op jit(solution)/shard_map/ppermute | solution.py:338

commit v18 on v15

--- a/solution.py
+++ b/solution.py
@@ -274,7 +274,7 @@
     for size in sizes:
         groups, refs = groups + [refs[:size]], refs[size:]
     n_tensor = len(groups)
-    (grad, grad_vmem, grad_sems), accs = refs[:3], refs[3:]
+    grad, accs = refs[0], refs[1:]
     share, width = grad.shape
     side = groups[0][0].shape[1] // 2
     tiles = slot_tiles(n_dp, pairs)
@@ -307,16 +307,8 @@
             value = value + acc[r]
         return fold(value)
 
-    copies = []
-    chunk = width // grad_sems.shape[0]
-    for c in range(grad_sems.shape[0]):
-        for r in range(c * chunk // side, (c + 1) * chunk // side, 2):
-            grad_vmem[:, r * side:(r + 2) * side] = jnp.where(low, total(r), total(r + 1)).astype(BF16)
-        here = slice(c * chunk, (c + 1) * chunk)
-        copies.append(pltpu.make_async_copy(grad_vmem.at[:, here], grad.at[:, here], grad_sems.at[c]))
-        copies[-1].start()
-    for copy in copies:
-        copy.wait()
+    for r in range(0, width // side, 2):
+        grad[:, r * side:(r + 2) * side] = jnp.where(low, total(r), total(r + 1)).astype(BF16)
 
 
 def steps(n):
@@ -446,11 +438,8 @@
             functools.partial(sum_kernel, tuple(map(len, groups)), pairs, n_dp),
             out_shape=jax.ShapeDtypeStruct((share, width), BF16),
             in_specs=[VMEM] * sum(map(len, groups)),
-            out_specs=HBM,
-            scratch_shapes=[
-                pltpu.VMEM((share, width), BF16),
-                pltpu.SemaphoreType.DMA((4,)),
-            ] + [pltpu.VMEM((row_count + 1, share, 2 * side), F32)] * n_tensor,
+            out_specs=VMEM,
+            scratch_shapes=[pltpu.VMEM((row_count + 1, share, 2 * side), F32)] * n_tensor,
             compiler_params=params,
         )(*(message for group in groups for message in group))
         return (outputs, grad_in)

time: 23 us -> 23 us (level)
  no operation moved by 1% of the time
where the time goes in v18:
time: 23 us; the launch traced here: 22.8 us
  starting transfers between devices  14.1 us (61%)
  Pallas kernels  4.07 us (18%)
  waiting for transfers between devices  3.91 us (17%)
  between operations  0.69 us (3%)
    ppermute x8, starting transfers between devices, swap(): return lax.ppermute(value, axis, [(i, i ^ k) for i in range(n)])  9.85 us
    ppermute x3, starting transfers between devices, shift(): return lax.ppermute(value, axis, [(i, (i + k) % n) for i in range(n)])  4.23 us
    ppermute x8, waiting for transfers between devices, swap(): return lax.ppermute(value, axis, [(i, i ^ k) for i in range(n)])  2.17 us
    ppermute x3, waiting for transfers between devices, shift(): return lax.ppermute(value, axis, [(i, (i + k) % n) for i in range(n)])  1.74 us
    pallas_call x1, Pallas kernels, on_device(): pl.pallas_call(functools.partial(forward_kernel, count, per_slot, n_parts...  1.23 us
    pallas_call x1, Pallas kernels, on_device(): pl.pallas_call(functools.partial(sum_kernel, tuple(map(len, groups)), pai...  1.13 us
    pallas_call x1, Pallas kernels, on_device(): pl.pallas_call(functools.partial(pack_kernel, count, row_count, col_count...  0.93 us
  transfers between devices with their start and end apart: 11, of which 5 were waited for; matrix products, arithmetic and copies ran while one was open for 0% of the time, Pallas kernels for 13%

profile of v18, /device:TPU:0, one launch (start us, length us, event | category | flops | bytes accessed | tf_op | source)
XLA Modules:
  0.0 22.8 jit_solution(5225840006084217013)
XLA Ops:
  0.6 0.0 copy-start
  0.6 4.1 %collective-permute-start.1 = (bf16[8,4096]{1,0:T(8,128)(2,1)}, bf16[8,4096]{1,0:T(8,128)(2,1)S(1)}, u32[]{:S(2)}, u32[]{:S(2)}) collective-permute-start(bf16[8,4096]{1,0:T(8,128)(2,1)} %tokens.1), channel_id=1, source_target_pairs={{0,2},{1,3},{2,0},{3,1},{4,6},{5,7},{6,4},{7,5},{8,10},{9,11},{10,... | collective-permute-start | bytes 196616 | tf_op jit(solution)/shard_map/ppermute | solution.py:326
  4.7 0.9 %shard_map.59.own = bf16[1,3,64,128]{3,2,1,0:T(8,128)(2,1)S(1)} custom-call(s32[1,5]{1,0:T(1,128)} %slots_hbm.1, bf16[1,5,64,64]{3,2,1,0:T(8,128)(2,1)} %values_hbm.1), custom_call_target="tpu_custom_call" | custom-call | tf_op jit(solution)/shard_map/pallas_call | solution.py:366
  5.7 0.0 copy-start.1
  5.7 2.5 %collective-permute-start = (bf16[1,3,64,128]{3,2,1,0:T(8,128)(2,1)S(1)}, bf16[1,3,64,128]{3,2,1,0:T(8,128)(2,1)S(1)}, u32[]{:S(2)}, u32[]{:S(2)}) collective-permute-start(bf16[1,3,64,128]{3,2,1,0:T(8,128)(2,1)S(1)} %shard_map.59.own), channel_id=1, source_target_pairs={{0,24},{4,28},{8,16},{12,20},{16,8},{20,12},{24,0},{28,4},{1,25},{... | collective-permute-start | bytes 147464 | tf_op jit(solution)/shard_map/ppermute | solution.py:326
  8.2 0.5 %collective-permute-start.3 = (bf16[1,3,64,128]{3,2,1,0:T(8,128)(2,1)S(1)}, bf16[1,3,64,128]{3,2,1,0:T(8,128)(2,1)S(1)}, u32[]{:S(2)}, u32[]{:S(2)}) collective-permute-start(bf16[1,3,64,128]{3,2,1,0:T(8,128)(2,1)S(1)} %shard_map.59.own), channel_id=1, source_target_pairs={{0,16},{4,20},{8,24},{12,28},{16,0},{20,4},{24,8},{28,12},{1,17},{... | collective-permute-start | bytes 147464 | tf_op jit(solution)/shard_map/ppermute | solution.py:326
  8.7 0.5 %collective-permute-start.2 = (bf16[1,3,64,128]{3,2,1,0:T(8,128)(2,1)S(1)}, bf16[1,3,64,128]{3,2,1,0:T(8,128)(2,1)S(1)}, u32[]{:S(2)}, u32[]{:S(2)}) collective-permute-start(bf16[1,3,64,128]{3,2,1,0:T(8,128)(2,1)S(1)} %shard_map.59.own), channel_id=1, source_target_pairs={{0,8},{4,12},{8,0},{12,4},{16,24},{20,28},{24,16},{28,20},{1,9},{5... | collective-permute-start | bytes 147464 | tf_op jit(solution)/shard_map/ppermute | solution.py:326
  9.2 1.6 %collective-permute-done.near = bf16[1,3,64,128]{3,2,1,0:T(8,128)(2,1)S(1)} collective-permute-done((bf16[1,3,64,128]{3,2,1,0:T(8,128)(2,1)S(1)}, bf16[1,3,64,128]{3,2,1,0:T(8,128)(2,1)S(1)}, u32[]{:S(2)}, u32[]{:S(2)}) %collective-permute-start) | collective-permute-done | bytes 49184 | tf_op jit(solution)/shard_map/ppermute | solution.py:326
  10.9 0.0 collective-permute-done.1.far_tokens
  10.9 0.0 copy-done
  10.9 0.1 collective-permute-start.4
  11.0 1.6 %collective-permute-start.7 = (bf16[2,8,4096]{2,1,0:T(8,128)(2,1)S(1)}, bf16[2,8,4096]{2,1,0:T(8,128)(2,1)S(1)}, u32[]{:S(2)}, u32[]{:S(2)}) collective-permute-start(bf16[2,8,4096]{2,1,0:T(8,128)(2,1)S(1)} %get-tuple-element.14.refs_6_), channel_id=1, source_target_pairs={{0,1},{1,0},{2,3},{3,2},{4,5},{5,4},{6,7},{7,6},{8,9},{9,8},{10,11... | collective-permute-start | bytes 393224 | tf_op jit(solution)/shard_map/ppermute | solution.py:326
  12.6 0.0 collective-permute-done.3.refs_2_
  12.6 0.2 collective-permute-start.6
  12.8 0.0 collective-permute-done.2.refs_1_
  12.8 0.3 %collective-permute-start.5 = (bf16[1,3,64,128]{3,2,1,0:T(8,128)(2,1)S(1)}, bf16[1,3,64,128]{3,2,1,0:T(8,128)(2,1)S(1)}, u32[]{:S(2)}, u32[]{:S(2)}) collective-permute-start(bf16[1,3,64,128]{3,2,1,0:T(8,128)(2,1)S(1)} %collective-permute-done.2.refs_1_), channel_id=1, source_target_pairs={{0,4},{4,0},{8,12},{12,8},{16,20},{20,16},{24,28},{28,24},{1,5},{5... | collective-permute-start | bytes 147464 | tf_op jit(solution)/shard_map/ppermute | solution.py:326
  13.1 0.0 copy-done.1
  13.1 0.4 %shard_map.62 = (bf16[80,128]{1,0:T(8,128)(2,1)S(1)}, bf16[80,128]{1,0:T(8,128)(2,1)S(1)}, bf16[80,128]{1,0:T(8,128)(2,1)S(1)}, bf16[80,128]{1,0:T(8,128)(2,1)S(1)}, bf16[15,32,128]{2,1,0:T(8,128)(2,1)S(1)}) custom-call(bf16[2,3,64,128]{3,2,1,0:T(8,128)(2,1)S(1)} %get-tuple-element.13.refs_0_, bf16[1,3,64,128]{3,2,1,0:T(8,128)(2,1)S(1)} %collective-permute-done.2.refs_1_, ...), custom_call_target="tpu_custom_call" | custom-call | tf_op jit(solution)/shard_map/pallas_call | solution.py:391
  13.5 0.3 %collective-permute-done.6.refs_5_ = bf16[1,3,64,128]{3,2,1,0:T(8,128)(2,1)S(1)} collective-permute-done((bf16[1,3,64,128]{3,2,1,0:T(8,128)(2,1)S(1)}, bf16[1,3,64,128]{3,2,1,0:T(8,128)(2,1)S(1)}, u32[]{:S(2)}, u32[]{:S(2)}) %collective-permute-start.6) | collective-permute-done | bytes 49184 | tf_op jit(solution)/shard_map/ppermute | solution.py:326
  13.8 0.2 collective-permute-done.5.refs_4_
  14.0 0.0 collective-permute-done.4.refs_3_
  14.0 0.4 %shard_map.63 = (bf16[176,128]{1,0:T(8,128)(2,1)S(1)}, bf16[176,128]{1,0:T(8,128)(2,1)S(1)}, bf16[176,128]{1,0:T(8,128)(2,1)S(1)}, bf16[176,128]{1,0:T(8,128)(2,1)S(1)}) custom-call(bf16[2,3,64,128]{3,2,1,0:T(8,128)(2,1)S(1)} %get-tuple-element.13.refs_0_, bf16[1,3,64,128]{3,2,1,0:T(8,128)(2,1)S(1)} %collective-permute-done.2.refs_1_, ...), custom_call_target="tpu_custom_call" | custom-call | tf_op jit(solution)/shard_map/pallas_call | solution.py:399
  14.4 0.4 %collective-permute-start.8 = (bf16[176,128]{1,0:T(8,128)(2,1)S(1)}, bf16[176,128]{1,0:T(8,128)(2,1)S(1)}, u32[]{:S(2)}, u32[]{:S(2)}) collective-permute-start(bf16[176,128]{1,0:T(8,128)(2,1)S(1)} %get-tuple-element.21), channel_id=1, source_target_pairs={{0,2},{1,3},{2,0},{3,1},{4,6},{5,7},{6,4},{7,5},{8,10},{9,11},{10,... | collective-permute-start | bytes 135176 | tf_op jit(solution)/shard_map/ppermute | solution.py:330
  14.8 1.6 %collective-permute-start.9 = (bf16[176,128]{1,0:T(8,128)(2,1)S(1)}, bf16[176,128]{1,0:T(8,128)(2,1)S(1)}, u32[]{:S(2)}, u32[]{:S(2)}) collective-permute-start(bf16[176,128]{1,0:T(8,128)(2,1)S(1)} %get-tuple-element.22), channel_id=1, source_target_pairs={{0,1},{1,2},{2,3},{3,0},{4,5},{5,6},{6,7},{7,4},{8,9},{9,10},{10,1... | collective-permute-start | bytes 135176 | tf_op jit(solution)/shard_map/ppermute | solution.py:330
  16.4 2.2 %collective-permute-start.10 = (bf16[176,128]{1,0:T(8,128)(2,1)S(1)}, bf16[176,128]{1,0:T(8,128)(2,1)S(1)}, u32[]{:S(2)}, u32[]{:S(2)}) collective-permute-start(bf16[176,128]{1,0:T(8,128)(2,1)S(1)} %get-tuple-element.23), channel_id=1, source_target_pairs={{0,3},{1,0},{2,1},{3,2},{4,7},{5,4},{6,5},{7,6},{8,11},{9,8},{10,9... | collective-permute-start | bytes 135176 | tf_op jit(solution)/shard_map/ppermute | solution.py:330
  18.6 0.0 collective-permute-done.7.refs_7_
  18.6 1.2 %shard_map.61 = bf16[32,896]{1,0:T(8,128)(2,1)} custom-call(bf16[2,3,64,128]{3,2,1,0:T(8,128)(2,1)S(1)} %get-tuple-element.13.refs_0_, bf16[1,3,64,128]{3,2,1,0:T(8,128)(2,1)S(1)} %collective-permute-done.2.refs_1_, bf16[1,3,64,128]{3,2,1,0:T(8,128)(2,1)S(1)} %collective-permute-done.3.refs_2_, bf16[2,3,64,128]{3,2,1,0:T(8,128)(2,1)S(1)} %collective-permute-done.4.refs_3_, ...), custom_call_target="tpu_custom_call" | custom-call | tf_op jit(solution)/shard_map/pallas_call | solution.py:422
  19.9 1.5 %collective-permute-done.8.refs_1_ = bf16[176,128]{1,0:T(8,128)(2,1)S(1)} collective-permute-done((bf16[176,128]{1,0:T(8,128)(2,1)S(1)}, bf16[176,128]{1,0:T(8,128)(2,1)S(1)}, u32[]{:S(2)}, u32[]{:S(2)}) %collective-permute-start.8) | collective-permute-done | bytes 45088 | tf_op jit(solution)/shard_map/ppermute | solution.py:330
  21.4 0.2 %collective-permute-done.9.refs_2_ = bf16[176,128]{1,0:T(8,128)(2,1)S(1)} collective-permute-done((bf16[176,128]{1,0:T(8,128)(2,1)S(1)}, bf16[176,128]{1,0:T(8,128)(2,1)S(1)}, u32[]{:S(2)}, u32[]{:S(2)}) %collective-permute-start.9) | collective-permute-done | bytes 45088 | tf_op jit(solution)/shard_map/ppermute | solution.py:330
  21.6 0.0 collective-permute-done.10.refs_3_
  21.6 1.1 %shard_map.64 = bf16[8,4096]{1,0:T(8,128)(2,1)} custom-call(bf16[176,128]{1,0:T(8,128)(2,1)S(1)} %get-tuple-element.20.refs_0_, bf16[176,128]{1,0:T(8,128)(2,1)S(1)} %collective-permute-done.8.refs_1_, bf16[176,128]{1,0:T(8,128)(2,1)S(1)} %collective-permute-done.9.refs_2_, bf16[176,128]{1,0:T(8,128)(2,1)S(1)} %collective-permute-done.10.refs_3_), custom_call_target="tpu_custom_call" | custom-call | tf_op jit(solution)/shard_map/pallas_call | solution.py:437
  (1 shorter events, 0.0 us)
Async XLA Ops:
  0.6 10.2 %copy-start = (bf16[8,4096]{1,0:T(8,128)(2,1)S(1)}, bf16[8,4096]{1,0:T(8,128)(2,1)}, u32[]{:S(2)}) copy-start(bf16[8,4096]{1,0:T(8,128)(2,1)} %tokens.1) | copy-start | bytes 196612
  0.6 10.2 %collective-permute-start.1 = (bf16[8,4096]{1,0:T(8,128)(2,1)}, bf16[8,4096]{1,0:T(8,128)(2,1)S(1)}, u32[]{:S(2)}, u32[]{:S(2)}) collective-permute-start(bf16[8,4096]{1,0:T(8,128)(2,1)} %tokens.1), channel_id=1, source_target_pairs={{0,2},{1,3},{2,0},{3,1},{4,6},{5,7},{6,4},{7,5},{8,10},{9,11},{10,... | collective-permute-start | bytes 196616 | tf_op jit(solution)/shard_map/ppermute | solution.py:326
  5.7 7.4 %copy-start.1 = (bf16[32,896]{1,0:T(8,128)(2,1)S(1)}, bf16[32,896]{1,0:T(8,128)(2,1)}, u32[]{:S(2)}) copy-start(bf16[32,896]{1,0:T(8,128)(2,1)} %refs_3_.1) | copy-start | bytes 172036
  5.7 5.2 %collective-permute-start = (bf16[1,3,64,128]{3,2,1,0:T(8,128)(2,1)S(1)}, bf16[1,3,64,128]{3,2,1,0:T(8,128)(2,1)S(1)}, u32[]{:S(2)}, u32[]{:S(2)}) collective-permute-start(bf16[1,3,64,128]{3,2,1,0:T(8,128)(2,1)S(1)} %shard_map.59.own), channel_id=1, source_target_pairs={{0,24},{4,28},{8,16},{12,20},{16,8},{20,12},{24,0},{28,4},{1,25},{... | collective-permute-start | bytes 147464 | tf_op jit(solution)/shard_map/ppermute | solution.py:326
  8.2 4.4 %collective-permute-start.3 = (bf16[1,3,64,128]{3,2,1,0:T(8,128)(2,1)S(1)}, bf16[1,3,64,128]{3,2,1,0:T(8,128)(2,1)S(1)}, u32[]{:S(2)}, u32[]{:S(2)}) collective-permute-start(bf16[1,3,64,128]{3,2,1,0:T(8,128)(2,1)S(1)} %shard_map.59.own), channel_id=1, source_target_pairs={{0,16},{4,20},{8,24},{12,28},{16,0},{20,4},{24,8},{28,12},{1,17},{... | collective-permute-start | bytes 147464 | tf_op jit(solution)/shard_map/ppermute | solution.py:326
  8.7 4.1 %collective-permute-start.2 = (bf16[1,3,64,128]{3,2,1,0:T(8,128)(2,1)S(1)}, bf16[1,3,64,128]{3,2,1,0:T(8,128)(2,1)S(1)}, u32[]{:S(2)}, u32[]{:S(2)}) collective-permute-start(bf16[1,3,64,128]{3,2,1,0:T(8,128)(2,1)S(1)} %shard_map.59.own), channel_id=1, source_target_pairs={{0,8},{4,12},{8,0},{12,4},{16,24},{20,28},{24,16},{28,20},{1,9},{5... | collective-permute-start | bytes 147464 | tf_op jit(solution)/shard_map/ppermute | solution.py:326
  10.9 3.2 %collective-permute-start.4 = (bf16[2,3,64,128]{3,2,1,0:T(8,128)(2,1)S(1)}, bf16[2,3,64,128]{3,2,1,0:T(8,128)(2,1)S(1)}, u32[]{:S(2)}, u32[]{:S(2)}) collective-permute-start(bf16[2,3,64,128]{3,2,1,0:T(8,128)(2,1)S(1)} %get-tuple-element.13.refs_0_), channel_id=1, source_target_pairs={{0,4},{4,0},{8,12},{12,8},{16,20},{20,16},{24,28},{28,24},{1,5},{5... | collective-permute-start | bytes 294920 | tf_op jit(solution)/shard_map/ppermute | solution.py:326
  11.0 7.7 %collective-permute-start.7 = (bf16[2,8,4096]{2,1,0:T(8,128)(2,1)S(1)}, bf16[2,8,4096]{2,1,0:T(8,128)(2,1)S(1)}, u32[]{:S(2)}, u32[]{:S(2)}) collective-permute-start(bf16[2,8,4096]{2,1,0:T(8,128)(2,1)S(1)} %get-tuple-element.14.refs_6_), channel_id=1, source_target_pairs={{0,1},{1,0},{2,3},{3,2},{4,5},{5,4},{6,7},{7,6},{8,9},{9,8},{10,11... | collective-permute-start | bytes 393224 | tf_op jit(solution)/shard_map/ppermute | solution.py:326
  12.6 1.2 %collective-permute-start.6 = (bf16[1,3,64,128]{3,2,1,0:T(8,128)(2,1)S(1)}, bf16[1,3,64,128]{3,2,1,0:T(8,128)(2,1)S(1)}, u32[]{:S(2)}, u32[]{:S(2)}) collective-permute-start(bf16[1,3,64,128]{3,2,1,0:T(8,128)(2,1)S(1)} %collective-permute-done.3.refs_2_), channel_id=1, source_target_pairs={{0,4},{4,0},{8,12},{12,8},{16,20},{20,16},{24,28},{28,24},{1,5},{5... | collective-permute-start | bytes 147464 | tf_op jit(solution)/shard_map/ppermute | solution.py:326
  12.8 1.2 %collective-permute-start.5 = (bf16[1,3,64,128]{3,2,1,0:T(8,128)(2,1)S(1)}, bf16[1,3,64,128]{3,2,1,0:T(8,128)(2,1)S(1)}, u32[]{:S(2)}, u32[]{:S(2)}) collective-permute-start(bf16[1,3,64,128]{3,2,1,0:T(8,128)(2,1)S(1)} %collective-permute-done.2.refs_1_), channel_id=1, source_target_pairs={{0,4},{4,0},{8,12},{12,8},{16,20},{20,16},{24,28},{28,24},{1,5},{5... | collective-permute-start | bytes 147464 | tf_op jit(solution)/shard_map/ppermute | solution.py:326
  14.4 7.0 %collective-permute-start.8 = (bf16[176,128]{1,0:T(8,128)(2,1)S(1)}, bf16[176,128]{1,0:T(8,128)(2,1)S(1)}, u32[]{:S(2)}, u32[]{:S(2)}) collective-permute-start(bf16[176,128]{1,0:T(8,128)(2,1)S(1)} %get-tuple-element.21), channel_id=1, source_target_pairs={{0,2},{1,3},{2,0},{3,1},{4,6},{5,7},{6,4},{7,5},{8,10},{9,11},{10,... | collective-permute-start | bytes 135176 | tf_op jit(solution)/shard_map/ppermute | solution.py:330
  14.8 6.8 %collective-permute-start.9 = (bf16[176,128]{1,0:T(8,128)(2,1)S(1)}, bf16[176,128]{1,0:T(8,128)(2,1)S(1)}, u32[]{:S(2)}, u32[]{:S(2)}) collective-permute-start(bf16[176,128]{1,0:T(8,128)(2,1)S(1)} %get-tuple-element.22), channel_id=1, source_target_pairs={{0,1},{1,2},{2,3},{3,0},{4,5},{5,6},{6,7},{7,4},{8,9},{9,10},{10,1... | collective-permute-start | bytes 135176 | tf_op jit(solution)/shard_map/ppermute | solution.py:330
  16.4 5.2 %collective-permute-start.10 = (bf16[176,128]{1,0:T(8,128)(2,1)S(1)}, bf16[176,128]{1,0:T(8,128)(2,1)S(1)}, u32[]{:S(2)}, u32[]{:S(2)}) collective-permute-start(bf16[176,128]{1,0:T(8,128)(2,1)S(1)} %get-tuple-element.23), channel_id=1, source_target_pairs={{0,3},{1,0},{2,1},{3,2},{4,7},{5,4},{6,5},{7,6},{8,11},{9,8},{10,9... | collective-permute-start | bytes 135176 | tf_op jit(solution)/shard_map/ppermute | solution.py:330

commit v19 on v18

--- a/solution.py
+++ b/solution.py
@@ -274,7 +274,7 @@
     for size in sizes:
         groups, refs = groups + [refs[:size]], refs[size:]
     n_tensor = len(groups)
-    grad, accs = refs[0], refs[1:]
+    before, grad, accs = refs[:-1 - n_tensor], refs[-1 - n_tensor], refs[-n_tensor:]
     share, width = grad.shape
     side = groups[0][0].shape[1] // 2
     tiles = slot_tiles(n_dp, pairs)
@@ -308,7 +308,10 @@
         return fold(value)
 
     for r in range(0, width // side, 2):
-        grad[:, r * side:(r + 2) * side] = jnp.where(low, total(r), total(r + 1)).astype(BF16)
+        value = jnp.where(low, total(r), total(r + 1))
+        for earlier in before:
+            value = value + earlier[:, r * side:(r + 2) * side]
+        grad[:, r * side:(r + 2) * side] = value.astype(grad.dtype)
 
 
 def steps(n):
@@ -434,14 +437,17 @@
         compiler_params=params,
     )(*gathered, *tokens)
     if per_slot:
-        grad_in = pl.pallas_call(
-            functools.partial(sum_kernel, tuple(map(len, groups)), pairs, n_dp),
-            out_shape=jax.ShapeDtypeStruct((share, width), BF16),
-            in_specs=[VMEM] * sum(map(len, groups)),
-            out_specs=VMEM,
-            scratch_shapes=[pltpu.VMEM((row_count + 1, share, 2 * side), F32)] * n_tensor,
-            compiler_params=params,
-        )(*(message for group in groups for message in group))
+        def add(groups, before, dtype):
+            return pl.pallas_call(
+                functools.partial(sum_kernel, tuple(map(len, groups)), pairs, n_dp),
+                out_shape=jax.ShapeDtypeStruct((share, width), dtype),
+                in_specs=[VMEM] * (sum(map(len, groups)) + len(before)),
+                out_specs=VMEM,
+                scratch_shapes=[pltpu.VMEM((row_count + 1, share, 2 * side), F32)] * len(groups),
+                compiler_params=params,
+            )(*(message for group in groups for message in group), *before)
+
+        grad_in = add(groups[1:], [add(groups[:1], [], F32)], BF16)
         return (outputs, grad_in)
     total = arrived[0].astype(F32)
     for value in arrived[1:]:

time: 23 us -> 23 us (level)
  waiting for transfers between devices: 3.91 us -> 3.45 us
  Pallas kernels: 4.07 us -> 4.5 us
    ppermute x3, waiting for transfers between devices: 1.74 us -> 1.27 us  [shift(): return lax.ppermute(value, axis, [(i, (i + k) % n) for i in range(n)])]
    pallas_call x1 -> x2, Pallas kernels: 1.13 us -> 1.56 us  [add(): pl.pallas_call(functools.partial(sum_kernel, tuple(map(len, groups)), pai...]
  transfers between devices with their start and end apart: 11 -> 11, of which waited for: 5 -> 5; matrix products, arithmetic and copies ran while one was open for 0% -> 0% of each run, Pallas kernels for 13% -> 15%
where the time goes in v19:
time: 23 us; the launch traced here: 22.7 us
  starting transfers between devices  14.1 us (61%)
  Pallas kernels  4.5 us (20%)
  waiting for transfers between devices  3.45 us (15%)
  between operations  0.7 us (3%)
    ppermute x8, starting transfers between devices, swap(): return lax.ppermute(value, axis, [(i, i ^ k) for i in range(n)])  9.85 us
    ppermute x3, starting transfers between devices, shift(): return lax.ppermute(value, axis, [(i, (i + k) % n) for i in range(n)])  4.23 us
    ppermute x8, waiting for transfers between devices, swap(): return lax.ppermute(value, axis, [(i, i ^ k) for i in range(n)])  2.17 us
    pallas_call x2, Pallas kernels, add(): pl.pallas_call(functools.partial(sum_kernel, tuple(map(len, groups)), pai...  1.56 us
    ppermute x3, waiting for transfers between devices, shift(): return lax.ppermute(value, axis, [(i, (i + k) % n) for i in range(n)])  1.27 us
    pallas_call x1, Pallas kernels, on_device(): pl.pallas_call(functools.partial(forward_kernel, count, per_slot, n_parts...  1.24 us
    pallas_call x1, Pallas kernels, on_device(): pl.pallas_call(functools.partial(pack_kernel, count, row_count, col_count...  0.93 us
  transfers between devices with their start and end apart: 11, of which 5 were waited for; matrix products, arithmetic and copies ran while one was open for 0% of the time, Pallas kernels for 15%

profile of v19, /device:TPU:0, one launch (start us, length us, event | category | flops | bytes accessed | tf_op | source)
XLA Modules:
  0.0 22.7 jit_solution(2223599814354870501)
XLA Ops:
  0.6 0.0 copy-start
  0.6 4.1 %collective-permute-start.1 = (bf16[8,4096]{1,0:T(8,128)(2,1)}, bf16[8,4096]{1,0:T(8,128)(2,1)S(1)}, u32[]{:S(2)}, u32[]{:S(2)}) collective-permute-start(bf16[8,4096]{1,0:T(8,128)(2,1)} %tokens.1), channel_id=1, source_target_pairs={{0,2},{1,3},{2,0},{3,1},{4,6},{5,7},{6,4},{7,5},{8,10},{9,11},{10,... | collective-permute-start | bytes 196616 | tf_op jit(solution)/shard_map/ppermute | solution.py:329
  4.7 0.9 %shard_map.59.own = bf16[1,3,64,128]{3,2,1,0:T(8,128)(2,1)S(1)} custom-call(s32[1,5]{1,0:T(1,128)} %slots_hbm.1, bf16[1,5,64,64]{3,2,1,0:T(8,128)(2,1)} %values_hbm.1), custom_call_target="tpu_custom_call" | custom-call | tf_op jit(solution)/shard_map/pallas_call | solution.py:369
  5.7 0.0 copy-start.1
  5.7 2.5 %collective-permute-start = (bf16[1,3,64,128]{3,2,1,0:T(8,128)(2,1)S(1)}, bf16[1,3,64,128]{3,2,1,0:T(8,128)(2,1)S(1)}, u32[]{:S(2)}, u32[]{:S(2)}) collective-permute-start(bf16[1,3,64,128]{3,2,1,0:T(8,128)(2,1)S(1)} %shard_map.59.own), channel_id=1, source_target_pairs={{0,24},{4,28},{8,16},{12,20},{16,8},{20,12},{24,0},{28,4},{1,25},{... | collective-permute-start | bytes 147464 | tf_op jit(solution)/shard_map/ppermute | solution.py:329
  8.2 0.5 %collective-permute-start.3 = (bf16[1,3,64,128]{3,2,1,0:T(8,128)(2,1)S(1)}, bf16[1,3,64,128]{3,2,1,0:T(8,128)(2,1)S(1)}, u32[]{:S(2)}, u32[]{:S(2)}) collective-permute-start(bf16[1,3,64,128]{3,2,1,0:T(8,128)(2,1)S(1)} %shard_map.59.own), channel_id=1, source_target_pairs={{0,16},{4,20},{8,24},{12,28},{16,0},{20,4},{24,8},{28,12},{1,17},{... | collective-permute-start | bytes 147464 | tf_op jit(solution)/shard_map/ppermute | solution.py:329
  8.7 0.5 %collective-permute-start.2 = (bf16[1,3,64,128]{3,2,1,0:T(8,128)(2,1)S(1)}, bf16[1,3,64,128]{3,2,1,0:T(8,128)(2,1)S(1)}, u32[]{:S(2)}, u32[]{:S(2)}) collective-permute-start(bf16[1,3,64,128]{3,2,1,0:T(8,128)(2,1)S(1)} %shard_map.59.own), channel_id=1, source_target_pairs={{0,8},{4,12},{8,0},{12,4},{16,24},{20,28},{24,16},{28,20},{1,9},{5... | collective-permute-start | bytes 147464 | tf_op jit(solution)/shard_map/ppermute | solution.py:329
  9.2 1.6 %collective-permute-done.near = bf16[1,3,64,128]{3,2,1,0:T(8,128)(2,1)S(1)} collective-permute-done((bf16[1,3,64,128]{3,2,1,0:T(8,128)(2,1)S(1)}, bf16[1,3,64,128]{3,2,1,0:T(8,128)(2,1)S(1)}, u32[]{:S(2)}, u32[]{:S(2)}) %collective-permute-start) | collective-permute-done | bytes 49184 | tf_op jit(solution)/shard_map/ppermute | solution.py:329
  10.9 0.0 collective-permute-done.1.far_tokens
  10.9 0.0 copy-done
  10.9 0.1 collective-permute-start.4
  11.0 1.6 %collective-permute-start.7 = (bf16[2,8,4096]{2,1,0:T(8,128)(2,1)S(1)}, bf16[2,8,4096]{2,1,0:T(8,128)(2,1)S(1)}, u32[]{:S(2)}, u32[]{:S(2)}) collective-permute-start(bf16[2,8,4096]{2,1,0:T(8,128)(2,1)S(1)} %get-tuple-element.14.refs_6_), channel_id=1, source_target_pairs={{0,1},{1,0},{2,3},{3,2},{4,5},{5,4},{6,7},{7,6},{8,9},{9,8},{10,11... | collective-permute-start | bytes 393224 | tf_op jit(solution)/shard_map/ppermute | solution.py:329
  12.6 0.0 collective-permute-done.3.refs_2_
  12.6 0.2 collective-permute-start.6
  12.8 0.0 collective-permute-done.2.refs_1_
  12.8 0.3 %collective-permute-start.5 = (bf16[1,3,64,128]{3,2,1,0:T(8,128)(2,1)S(1)}, bf16[1,3,64,128]{3,2,1,0:T(8,128)(2,1)S(1)}, u32[]{:S(2)}, u32[]{:S(2)}) collective-permute-start(bf16[1,3,64,128]{3,2,1,0:T(8,128)(2,1)S(1)} %collective-permute-done.2.refs_1_), channel_id=1, source_target_pairs={{0,4},{4,0},{8,12},{12,8},{16,20},{20,16},{24,28},{28,24},{1,5},{5... | collective-permute-start | bytes 147464 | tf_op jit(solution)/shard_map/ppermute | solution.py:329
  13.1 0.0 copy-done.1
  13.1 0.4 %shard_map.62 = (bf16[80,128]{1,0:T(8,128)(2,1)S(1)}, bf16[80,128]{1,0:T(8,128)(2,1)S(1)}, bf16[80,128]{1,0:T(8,128)(2,1)S(1)}, bf16[80,128]{1,0:T(8,128)(2,1)S(1)}, bf16[15,32,128]{2,1,0:T(8,128)(2,1)S(1)}) custom-call(bf16[2,3,64,128]{3,2,1,0:T(8,128)(2,1)S(1)} %get-tuple-element.13.refs_0_, bf16[1,3,64,128]{3,2,1,0:T(8,128)(2,1)S(1)} %collective-permute-done.2.refs_1_, ...), custom_call_target="tpu_custom_call" | custom-call | tf_op jit(solution)/shard_map/pallas_call | solution.py:394
  13.5 0.3 %collective-permute-done.6.refs_5_ = bf16[1,3,64,128]{3,2,1,0:T(8,128)(2,1)S(1)} collective-permute-done((bf16[1,3,64,128]{3,2,1,0:T(8,128)(2,1)S(1)}, bf16[1,3,64,128]{3,2,1,0:T(8,128)(2,1)S(1)}, u32[]{:S(2)}, u32[]{:S(2)}) %collective-permute-start.6) | collective-permute-done | bytes 49184 | tf_op jit(solution)/shard_map/ppermute | solution.py:329
  13.8 0.2 collective-permute-done.5.refs_4_
  14.0 0.0 collective-permute-done.4.refs_3_
  14.0 0.4 %shard_map.63 = (bf16[176,128]{1,0:T(8,128)(2,1)S(1)}, bf16[176,128]{1,0:T(8,128)(2,1)S(1)}, bf16[176,128]{1,0:T(8,128)(2,1)S(1)}, bf16[176,128]{1,0:T(8,128)(2,1)S(1)}) custom-call(bf16[2,3,64,128]{3,2,1,0:T(8,128)(2,1)S(1)} %get-tuple-element.13.refs_0_, bf16[1,3,64,128]{3,2,1,0:T(8,128)(2,1)S(1)} %collective-permute-done.2.refs_1_, ...), custom_call_target="tpu_custom_call" | custom-call | tf_op jit(solution)/shard_map/pallas_call | solution.py:402
  14.4 0.4 %collective-permute-start.8 = (bf16[176,128]{1,0:T(8,128)(2,1)S(1)}, bf16[176,128]{1,0:T(8,128)(2,1)S(1)}, u32[]{:S(2)}, u32[]{:S(2)}) collective-permute-start(bf16[176,128]{1,0:T(8,128)(2,1)S(1)} %get-tuple-element.20), channel_id=1, source_target_pairs={{0,2},{1,3},{2,0},{3,1},{4,6},{5,7},{6,4},{7,5},{8,10},{9,11},{10,... | collective-permute-start | bytes 135176 | tf_op jit(solution)/shard_map/ppermute | solution.py:333
  14.8 1.6 %collective-permute-start.9 = (bf16[176,128]{1,0:T(8,128)(2,1)S(1)}, bf16[176,128]{1,0:T(8,128)(2,1)S(1)}, u32[]{:S(2)}, u32[]{:S(2)}) collective-permute-start(bf16[176,128]{1,0:T(8,128)(2,1)S(1)} %get-tuple-element.21), channel_id=1, source_target_pairs={{0,1},{1,2},{2,3},{3,0},{4,5},{5,6},{6,7},{7,4},{8,9},{9,10},{10,1... | collective-permute-start | bytes 135176 | tf_op jit(solution)/shard_map/ppermute | solution.py:333
  16.4 2.2 %collective-permute-start.10 = (bf16[176,128]{1,0:T(8,128)(2,1)S(1)}, bf16[176,128]{1,0:T(8,128)(2,1)S(1)}, u32[]{:S(2)}, u32[]{:S(2)}) collective-permute-start(bf16[176,128]{1,0:T(8,128)(2,1)S(1)} %get-tuple-element.22), channel_id=1, source_target_pairs={{0,3},{1,0},{2,1},{3,2},{4,7},{5,4},{6,5},{7,6},{8,11},{9,8},{10,9... | collective-permute-start | bytes 135176 | tf_op jit(solution)/shard_map/ppermute | solution.py:333
  18.6 0.4 %shard_map.64.refs_3_ = f32[8,4096]{1,0:T(8,128)S(1)} custom-call(bf16[176,128]{1,0:T(8,128)(2,1)S(1)} %get-tuple-element.23.refs_0_), custom_call_target="tpu_custom_call" | custom-call | tf_op jit(solution)/shard_map/pallas_call | solution.py:441
  19.1 0.0 collective-permute-done.7.refs_7_
  19.1 1.2 %shard_map.61 = bf16[32,896]{1,0:T(8,128)(2,1)} custom-call(bf16[2,3,64,128]{3,2,1,0:T(8,128)(2,1)S(1)} %get-tuple-element.13.refs_0_, bf16[1,3,64,128]{3,2,1,0:T(8,128)(2,1)S(1)} %collective-permute-done.2.refs_1_, bf16[1,3,64,128]{3,2,1,0:T(8,128)(2,1)S(1)} %collective-permute-done.3.refs_2_, bf16[2,3,64,128]{3,2,1,0:T(8,128)(2,1)S(1)} %collective-permute-done.4.refs_3_, ...), custom_call_target="tpu_custom_call" | custom-call | tf_op jit(solution)/shard_map/pallas_call | solution.py:425
  20.3 1.0 %collective-permute-done.8.refs_0_ = bf16[176,128]{1,0:T(8,128)(2,1)S(1)} collective-permute-done((bf16[176,128]{1,0:T(8,128)(2,1)S(1)}, bf16[176,128]{1,0:T(8,128)(2,1)S(1)}, u32[]{:S(2)}, u32[]{:S(2)}) %collective-permute-start.8) | collective-permute-done | bytes 45088 | tf_op jit(solution)/shard_map/ppermute | solution.py:333
  21.4 0.2 %collective-permute-done.9.refs_1_ = bf16[176,128]{1,0:T(8,128)(2,1)S(1)} collective-permute-done((bf16[176,128]{1,0:T(8,128)(2,1)S(1)}, bf16[176,128]{1,0:T(8,128)(2,1)S(1)}, u32[]{:S(2)}, u32[]{:S(2)}) %collective-permute-start.9) | collective-permute-done | bytes 45088 | tf_op jit(solution)/shard_map/ppermute | solution.py:333
  21.6 0.0 collective-permute-done.10.refs_2_
  21.6 1.1 %shard_map.65 = bf16[8,4096]{1,0:T(8,128)(2,1)} custom-call(bf16[176,128]{1,0:T(8,128)(2,1)S(1)} %collective-permute-done.8.refs_0_, bf16[176,128]{1,0:T(8,128)(2,1)S(1)} %collective-permute-done.9.refs_1_, bf16[176,128]{1,0:T(8,128)(2,1)S(1)} %collective-permute-done.10.refs_2_, f32[8,4096]{1,0:T(8,128)S(1)} %shard_map.64.refs_3_), custom_call_target="tpu_custom_call" | custom-call | tf_op jit(solution)/shard_map/pallas_call | solution.py:441
  (1 shorter events, 0.0 us)
Async XLA Ops:
  0.6 10.2 %copy-start = (bf16[8,4096]{1,0:T(8,128)(2,1)S(1)}, bf16[8,4096]{1,0:T(8,128)(2,1)}, u32[]{:S(2)}) copy-start(bf16[8,4096]{1,0:T(8,128)(2,1)} %tokens.1) | copy-start | bytes 196612
  0.6 10.2 %collective-permute-start.1 = (bf16[8,4096]{1,0:T(8,128)(2,1)}, bf16[8,4096]{1,0:T(8,128)(2,1)S(1)}, u32[]{:S(2)}, u32[]{:S(2)}) collective-permute-start(bf16[8,4096]{1,0:T(8,128)(2,1)} %tokens.1), channel_id=1, source_target_pairs={{0,2},{1,3},{2,0},{3,1},{4,6},{5,7},{6,4},{7,5},{8,10},{9,11},{10,... | collective-permute-start | bytes 196616 | tf_op jit(solution)/shard_map/ppermute | solution.py:329
  5.7 7.4 %copy-start.1 = (bf16[32,896]{1,0:T(8,128)(2,1)S(1)}, bf16[32,896]{1,0:T(8,128)(2,1)}, u32[]{:S(2)}) copy-start(bf16[32,896]{1,0:T(8,128)(2,1)} %refs_3_.1) | copy-start | bytes 172036
  5.7 5.2 %collective-permute-start = (bf16[1,3,64,128]{3,2,1,0:T(8,128)(2,1)S(1)}, bf16[1,3,64,128]{3,2,1,0:T(8,128)(2,1)S(1)}, u32[]{:S(2)}, u32[]{:S(2)}) collective-permute-start(bf16[1,3,64,128]{3,2,1,0:T(8,128)(2,1)S(1)} %shard_map.59.own), channel_id=1, source_target_pairs={{0,24},{4,28},{8,16},{12,20},{16,8},{20,12},{24,0},{28,4},{1,25},{... | collective-permute-start | bytes 147464 | tf_op jit(solution)/shard_map/ppermute | solution.py:329
  8.2 4.4 %collective-permute-start.3 = (bf16[1,3,64,128]{3,2,1,0:T(8,128)(2,1)S(1)}, bf16[1,3,64,128]{3,2,1,0:T(8,128)(2,1)S(1)}, u32[]{:S(2)}, u32[]{:S(2)}) collective-permute-start(bf16[1,3,64,128]{3,2,1,0:T(8,128)(2,1)S(1)} %shard_map.59.own), channel_id=1, source_target_pairs={{0,16},{4,20},{8,24},{12,28},{16,0},{20,4},{24,8},{28,12},{1,17},{... | collective-permute-start | bytes 147464 | tf_op jit(solution)/shard_map/ppermute | solution.py:329
  8.7 4.1 %collective-permute-start.2 = (bf16[1,3,64,128]{3,2,1,0:T(8,128)(2,1)S(1)}, bf16[1,3,64,128]{3,2,1,0:T(8,128)(2,1)S(1)}, u32[]{:S(2)}, u32[]{:S(2)}) collective-permute-start(bf16[1,3,64,128]{3,2,1,0:T(8,128)(2,1)S(1)} %shard_map.59.own), channel_id=1, source_target_pairs={{0,8},{4,12},{8,0},{12,4},{16,24},{20,28},{24,16},{28,20},{1,9},{5... | collective-permute-start | bytes 147464 | tf_op jit(solution)/shard_map/ppermute | solution.py:329
  10.9 3.2 %collective-permute-start.4 = (bf16[2,3,64,128]{3,2,1,0:T(8,128)(2,1)S(1)}, bf16[2,3,64,128]{3,2,1,0:T(8,128)(2,1)S(1)}, u32[]{:S(2)}, u32[]{:S(2)}) collective-permute-start(bf16[2,3,64,128]{3,2,1,0:T(8,128)(2,1)S(1)} %get-tuple-element.13.refs_0_), channel_id=1, source_target_pairs={{0,4},{4,0},{8,12},{12,8},{16,20},{20,16},{24,28},{28,24},{1,5},{5... | collective-permute-start | bytes 294920 | tf_op jit(solution)/shard_map/ppermute | solution.py:329
  11.0 8.1 %collective-permute-start.7 = (bf16[2,8,4096]{2,1,0:T(8,128)(2,1)S(1)}, bf16[2,8,4096]{2,1,0:T(8,128)(2,1)S(1)}, u32[]{:S(2)}, u32[]{:S(2)}) collective-permute-start(bf16[2,8,4096]{2,1,0:T(8,128)(2,1)S(1)} %get-tuple-element.14.refs_6_), channel_id=1, source_target_pairs={{0,1},{1,0},{2,3},{3,2},{4,5},{5,4},{6,7},{7,6},{8,9},{9,8},{10,11... | collective-permute-start | bytes 393224 | tf_op jit(solution)/shard_map/ppermute | solution.py:329
  12.6 1.2 %collective-permute-start.6 = (bf16[1,3,64,128]{3,2,1,0:T(8,128)(2,1)S(1)}, bf16[1,3,64,128]{3,2,1,0:T(8,128)(2,1)S(1)}, u32[]{:S(2)}, u32[]{:S(2)}) collective-permute-start(bf16[1,3,64,128]{3,2,1,0:T(8,128)(2,1)S(1)} %collective-permute-done.3.refs_2_), channel_id=1, source_target_pairs={{0,4},{4,0},{8,12},{12,8},{16,20},{20,16},{24,28},{28,24},{1,5},{5... | collective-permute-start | bytes 147464 | tf_op jit(solution)/shard_map/ppermute | solution.py:329
  12.8 1.2 %collective-permute-start.5 = (bf16[1,3,64,128]{3,2,1,0:T(8,128)(2,1)S(1)}, bf16[1,3,64,128]{3,2,1,0:T(8,128)(2,1)S(1)}, u32[]{:S(2)}, u32[]{:S(2)}) collective-permute-start(bf16[1,3,64,128]{3,2,1,0:T(8,128)(2,1)S(1)} %collective-permute-done.2.refs_1_), channel_id=1, source_target_pairs={{0,4},{4,0},{8,12},{12,8},{16,20},{20,16},{24,28},{28,24},{1,5},{5... | collective-permute-start | bytes 147464 | tf_op jit(solution)/shard_map/ppermute | solution.py:329
  14.4 7.0 %collective-permute-start.8 = (bf16[176,128]{1,0:T(8,128)(2,1)S(1)}, bf16[176,128]{1,0:T(8,128)(2,1)S(1)}, u32[]{:S(2)}, u32[]{:S(2)}) collective-permute-start(bf16[176,128]{1,0:T(8,128)(2,1)S(1)} %get-tuple-element.20), channel_id=1, source_target_pairs={{0,2},{1,3},{2,0},{3,1},{4,6},{5,7},{6,4},{7,5},{8,10},{9,11},{10,... | collective-permute-start | bytes 135176 | tf_op jit(solution)/shard_map/ppermute | solution.py:333
  14.8 6.8 %collective-permute-start.9 = (bf16[176,128]{1,0:T(8,128)(2,1)S(1)}, bf16[176,128]{1,0:T(8,128)(2,1)S(1)}, u32[]{:S(2)}, u32[]{:S(2)}) collective-permute-start(bf16[176,128]{1,0:T(8,128)(2,1)S(1)} %get-tuple-element.21), channel_id=1, source_target_pairs={{0,1},{1,2},{2,3},{3,0},{4,5},{5,6},{6,7},{7,4},{8,9},{9,10},{10,1... | collective-permute-start | bytes 135176 | tf_op jit(solution)/shard_map/ppermute | solution.py:333
  16.4 5.2 %collective-permute-start.10 = (bf16[176,128]{1,0:T(8,128)(2,1)S(1)}, bf16[176,128]{1,0:T(8,128)(2,1)S(1)}, u32[]{:S(2)}, u32[]{:S(2)}) collective-permute-start(bf16[176,128]{1,0:T(8,128)(2,1)S(1)} %get-tuple-element.22), channel_id=1, source_target_pairs={{0,3},{1,0},{2,1},{3,2},{4,7},{5,4},{6,5},{7,6},{8,11},{9,8},{10,9... | collective-permute-start | bytes 135176 | tf_op jit(solution)/shard_map/ppermute | solution.py:333

commit v20 on v18

--- a/solution.py
+++ b/solution.py
@@ -337,7 +337,7 @@
             tokens = tokens + [swap(value, "tensor", n_tensor, k) for value in tokens]
         return [lax.all_gather(packed, "dp", axis=0, tiled=True)], tokens
     far_tokens = swap(inputs, "tensor", n_tensor, 2)
-    near, second, last = [swap(packed, "dp", n_dp, k) for k in (6, 2, 4)]
+    near, second, last = [swap(packed, "dp", n_dp, k) for k in (4, 2, 6)]
     joined, tokens = pl.pallas_call(
         join_kernel,
         out_shape=[

time: 23 us -> 23 us (level)
  starting transfers between devices: 14.1 us -> 13.6 us
  waiting for transfers between devices: 3.91 us -> 4.36 us
    ppermute x8, starting transfers between devices: 9.85 us -> 9.39 us  [swap(): return lax.ppermute(value, axis, [(i, i ^ k) for i in range(n)])]
    ppermute x8, waiting for transfers between devices: 2.17 us -> 2.63 us  [swap(): return lax.ppermute(value, axis, [(i, i ^ k) for i in range(n)])]
  transfers between devices with their start and end apart: 11 -> 11, of which waited for: 5 -> 7; matrix products, arithmetic and copies ran while one was open for 0% -> 0% of each run, Pallas kernels for 13% -> 13%
where the time goes in v20:
time: 23 us; the launch traced here: 22.8 us
  starting transfers between devices  13.6 us (59%)
  waiting for transfers between devices  4.36 us (19%)
  Pallas kernels  4.07 us (18%)
  between operations  0.69 us (3%)
    ppermute x8, starting transfers between devices, swap(): return lax.ppermute(value, axis, [(i, i ^ k) for i in range(n)])  9.39 us
    ppermute x3, starting transfers between devices, shift(): return lax.ppermute(value, axis, [(i, (i + k) % n) for i in range(n)])  4.22 us
    ppermute x8, waiting for transfers between devices, swap(): return lax.ppermute(value, axis, [(i, i ^ k) for i in range(n)])  2.63 us
    ppermute x3, waiting for transfers between devices, shift(): return lax.ppermute(value, axis, [(i, (i + k) % n) for i in range(n)])  1.73 us
    pallas_call x1, Pallas kernels, on_device(): pl.pallas_call(functools.partial(forward_kernel, count, per_slot, n_parts...  1.24 us
    pallas_call x1, Pallas kernels, on_device(): pl.pallas_call(functools.partial(sum_kernel, tuple(map(len, groups)), pai...  1.13 us
    pallas_call x1, Pallas kernels, on_device(): pl.pallas_call(functools.partial(pack_kernel, count, row_count, col_count...  0.93 us
  transfers between devices with their start and end apart: 11, of which 7 were waited for; matrix products, arithmetic and copies ran while one was open for 0% of the time, Pallas kernels for 13%

profile of v20, /device:TPU:0, one launch (start us, length us, event | category | flops | bytes accessed | tf_op | source)
XLA Modules:
  0.0 22.8 jit_solution(15155499241613745535)
XLA Ops:
  0.6 0.0 copy-start
  0.6 4.1 %collective-permute-start.1 = (bf16[8,4096]{1,0:T(8,128)(2,1)}, bf16[8,4096]{1,0:T(8,128)(2,1)S(1)}, u32[]{:S(2)}, u32[]{:S(2)}) collective-permute-start(bf16[8,4096]{1,0:T(8,128)(2,1)} %tokens.1), channel_id=1, source_target_pairs={{0,2},{1,3},{2,0},{3,1},{4,6},{5,7},{6,4},{7,5},{8,10},{9,11},{10,... | collective-permute-start | bytes 196616 | tf_op jit(solution)/shard_map/ppermute | solution.py:326
  4.7 0.9 %shard_map.59.own = bf16[1,3,64,128]{3,2,1,0:T(8,128)(2,1)S(1)} custom-call(s32[1,5]{1,0:T(1,128)} %slots_hbm.1, bf16[1,5,64,64]{3,2,1,0:T(8,128)(2,1)} %values_hbm.1), custom_call_target="tpu_custom_call" | custom-call | tf_op jit(solution)/shard_map/pallas_call | solution.py:366
  5.7 0.0 copy-start.1
  5.7 1.6 %collective-permute-start = (bf16[1,3,64,128]{3,2,1,0:T(8,128)(2,1)S(1)}, bf16[1,3,64,128]{3,2,1,0:T(8,128)(2,1)S(1)}, u32[]{:S(2)}, u32[]{:S(2)}) collective-permute-start(bf16[1,3,64,128]{3,2,1,0:T(8,128)(2,1)S(1)} %shard_map.59.own), channel_id=1, source_target_pairs={{0,16},{4,20},{8,24},{12,28},{16,0},{20,4},{24,8},{28,12},{1,17},{... | collective-permute-start | bytes 147464 | tf_op jit(solution)/shard_map/ppermute | solution.py:326
  7.3 1.4 %collective-permute-start.3 = (bf16[1,3,64,128]{3,2,1,0:T(8,128)(2,1)S(1)}, bf16[1,3,64,128]{3,2,1,0:T(8,128)(2,1)S(1)}, u32[]{:S(2)}, u32[]{:S(2)}) collective-permute-start(bf16[1,3,64,128]{3,2,1,0:T(8,128)(2,1)S(1)} %shard_map.59.own), channel_id=1, source_target_pairs={{0,24},{4,28},{8,16},{12,20},{16,8},{20,12},{24,0},{28,4},{1,25},{... | collective-permute-start | bytes 147464 | tf_op jit(solution)/shard_map/ppermute | solution.py:326
  8.7 0.5 %collective-permute-start.2 = (bf16[1,3,64,128]{3,2,1,0:T(8,128)(2,1)S(1)}, bf16[1,3,64,128]{3,2,1,0:T(8,128)(2,1)S(1)}, u32[]{:S(2)}, u32[]{:S(2)}) collective-permute-start(bf16[1,3,64,128]{3,2,1,0:T(8,128)(2,1)S(1)} %shard_map.59.own), channel_id=1, source_target_pairs={{0,8},{4,12},{8,0},{12,4},{16,24},{20,28},{24,16},{28,20},{1,9},{5... | collective-permute-start | bytes 147464 | tf_op jit(solution)/shard_map/ppermute | solution.py:326
  9.2 0.6 %collective-permute-done.near = bf16[1,3,64,128]{3,2,1,0:T(8,128)(2,1)S(1)} collective-permute-done((bf16[1,3,64,128]{3,2,1,0:T(8,128)(2,1)S(1)}, bf16[1,3,64,128]{3,2,1,0:T(8,128)(2,1)S(1)}, u32[]{:S(2)}, u32[]{:S(2)}) %collective-permute-start) | collective-permute-done | bytes 49184 | tf_op jit(solution)/shard_map/ppermute | solution.py:326
  9.8 0.0 collective-permute-done.1.far_tokens
  9.9 0.0 copy-done
  9.9 0.1 collective-permute-start.4
  10.0 1.6 %collective-permute-start.7 = (bf16[2,8,4096]{2,1,0:T(8,128)(2,1)S(1)}, bf16[2,8,4096]{2,1,0:T(8,128)(2,1)S(1)}, u32[]{:S(2)}, u32[]{:S(2)}) collective-permute-start(bf16[2,8,4096]{2,1,0:T(8,128)(2,1)S(1)} %get-tuple-element.14.refs_6_), channel_id=1, source_target_pairs={{0,1},{1,0},{2,3},{3,2},{4,5},{5,4},{6,7},{7,6},{8,9},{9,8},{10,11... | collective-permute-start | bytes 393224 | tf_op jit(solution)/shard_map/ppermute | solution.py:326
  11.6 0.7 %collective-permute-done.3.refs_2_ = bf16[1,3,64,128]{3,2,1,0:T(8,128)(2,1)S(1)} collective-permute-done((bf16[1,3,64,128]{3,2,1,0:T(8,128)(2,1)S(1)}, bf16[1,3,64,128]{3,2,1,0:T(8,128)(2,1)S(1)}, u32[]{:S(2)}, u32[]{:S(2)}) %collective-permute-start.3) | collective-permute-done | bytes 49184 | tf_op jit(solution)/shard_map/ppermute | solution.py:326
  12.3 0.0 collective-permute-start.6
  12.3 0.5 %collective-permute-done.2.refs_1_ = bf16[1,3,64,128]{3,2,1,0:T(8,128)(2,1)S(1)} collective-permute-done((bf16[1,3,64,128]{3,2,1,0:T(8,128)(2,1)S(1)}, bf16[1,3,64,128]{3,2,1,0:T(8,128)(2,1)S(1)}, u32[]{:S(2)}, u32[]{:S(2)}) %collective-permute-start.2) | collective-permute-done | bytes 49184 | tf_op jit(solution)/shard_map/ppermute | solution.py:326
  12.8 0.0 collective-permute-start.5
  12.8 0.0 copy-done.1
  12.8 0.4 %shard_map.62 = (bf16[80,128]{1,0:T(8,128)(2,1)S(1)}, bf16[80,128]{1,0:T(8,128)(2,1)S(1)}, bf16[80,128]{1,0:T(8,128)(2,1)S(1)}, bf16[80,128]{1,0:T(8,128)(2,1)S(1)}, bf16[15,32,128]{2,1,0:T(8,128)(2,1)S(1)}) custom-call(bf16[2,3,64,128]{3,2,1,0:T(8,128)(2,1)S(1)} %get-tuple-element.13.refs_0_, bf16[1,3,64,128]{3,2,1,0:T(8,128)(2,1)S(1)} %collective-permute-done.2.refs_1_, ...), custom_call_target="tpu_custom_call" | custom-call | tf_op jit(solution)/shard_map/pallas_call | solution.py:391
  13.2 0.3 %collective-permute-done.6.refs_5_ = bf16[1,3,64,128]{3,2,1,0:T(8,128)(2,1)S(1)} collective-permute-done((bf16[1,3,64,128]{3,2,1,0:T(8,128)(2,1)S(1)}, bf16[1,3,64,128]{3,2,1,0:T(8,128)(2,1)S(1)}, u32[]{:S(2)}, u32[]{:S(2)}) %collective-permute-start.6) | collective-permute-done | bytes 49184 | tf_op jit(solution)/shard_map/ppermute | solution.py:326
  13.5 0.5 %collective-permute-done.5.refs_4_ = bf16[1,3,64,128]{3,2,1,0:T(8,128)(2,1)S(1)} collective-permute-done((bf16[1,3,64,128]{3,2,1,0:T(8,128)(2,1)S(1)}, bf16[1,3,64,128]{3,2,1,0:T(8,128)(2,1)S(1)}, u32[]{:S(2)}, u32[]{:S(2)}) %collective-permute-start.5) | collective-permute-done | bytes 49184 | tf_op jit(solution)/shard_map/ppermute | solution.py:326
  14.0 0.0 collective-permute-done.4.refs_3_
  14.0 0.4 %shard_map.63 = (bf16[176,128]{1,0:T(8,128)(2,1)S(1)}, bf16[176,128]{1,0:T(8,128)(2,1)S(1)}, bf16[176,128]{1,0:T(8,128)(2,1)S(1)}, bf16[176,128]{1,0:T(8,128)(2,1)S(1)}) custom-call(bf16[2,3,64,128]{3,2,1,0:T(8,128)(2,1)S(1)} %get-tuple-element.13.refs_0_, bf16[1,3,64,128]{3,2,1,0:T(8,128)(2,1)S(1)} %collective-permute-done.2.refs_1_, ...), custom_call_target="tpu_custom_call" | custom-call | tf_op jit(solution)/shard_map/pallas_call | solution.py:399
  14.4 0.4 %collective-permute-start.8 = (bf16[176,128]{1,0:T(8,128)(2,1)S(1)}, bf16[176,128]{1,0:T(8,128)(2,1)S(1)}, u32[]{:S(2)}, u32[]{:S(2)}) collective-permute-start(bf16[176,128]{1,0:T(8,128)(2,1)S(1)} %get-tuple-element.21), channel_id=1, source_target_pairs={{0,2},{1,3},{2,0},{3,1},{4,6},{5,7},{6,4},{7,5},{8,10},{9,11},{10,... | collective-permute-start | bytes 135176 | tf_op jit(solution)/shard_map/ppermute | solution.py:330
  14.8 1.6 %collective-permute-start.9 = (bf16[176,128]{1,0:T(8,128)(2,1)S(1)}, bf16[176,128]{1,0:T(8,128)(2,1)S(1)}, u32[]{:S(2)}, u32[]{:S(2)}) collective-permute-start(bf16[176,128]{1,0:T(8,128)(2,1)S(1)} %get-tuple-element.22), channel_id=1, source_target_pairs={{0,1},{1,2},{2,3},{3,0},{4,5},{5,6},{6,7},{7,4},{8,9},{9,10},{10,1... | collective-permute-start | bytes 135176 | tf_op jit(solution)/shard_map/ppermute | solution.py:330
  16.4 2.2 %collective-permute-start.10 = (bf16[176,128]{1,0:T(8,128)(2,1)S(1)}, bf16[176,128]{1,0:T(8,128)(2,1)S(1)}, u32[]{:S(2)}, u32[]{:S(2)}) collective-permute-start(bf16[176,128]{1,0:T(8,128)(2,1)S(1)} %get-tuple-element.23), channel_id=1, source_target_pairs={{0,3},{1,0},{2,1},{3,2},{4,7},{5,4},{6,5},{7,6},{8,11},{9,8},{10,9... | collective-permute-start | bytes 135176 | tf_op jit(solution)/shard_map/ppermute | solution.py:330
  18.6 0.0 collective-permute-done.7.refs_7_
  18.6 1.2 %shard_map.61 = bf16[32,896]{1,0:T(8,128)(2,1)} custom-call(bf16[2,3,64,128]{3,2,1,0:T(8,128)(2,1)S(1)} %get-tuple-element.13.refs_0_, bf16[1,3,64,128]{3,2,1,0:T(8,128)(2,1)S(1)} %collective-permute-done.2.refs_1_, bf16[1,3,64,128]{3,2,1,0:T(8,128)(2,1)S(1)} %collective-permute-done.3.refs_2_, bf16[2,3,64,128]{3,2,1,0:T(8,128)(2,1)S(1)} %collective-permute-done.4.refs_3_, ...), custom_call_target="tpu_custom_call" | custom-call | tf_op jit(solution)/shard_map/pallas_call | solution.py:422
  19.9 1.5 %collective-permute-done.8.refs_1_ = bf16[176,128]{1,0:T(8,128)(2,1)S(1)} collective-permute-done((bf16[176,128]{1,0:T(8,128)(2,1)S(1)}, bf16[176,128]{1,0:T(8,128)(2,1)S(1)}, u32[]{:S(2)}, u32[]{:S(2)}) %collective-permute-start.8) | collective-permute-done | bytes 45088 | tf_op jit(solution)/shard_map/ppermute | solution.py:330
  21.4 0.2 %collective-permute-done.9.refs_2_ = bf16[176,128]{1,0:T(8,128)(2,1)S(1)} collective-permute-done((bf16[176,128]{1,0:T(8,128)(2,1)S(1)}, bf16[176,128]{1,0:T(8,128)(2,1)S(1)}, u32[]{:S(2)}, u32[]{:S(2)}) %collective-permute-start.9) | collective-permute-done | bytes 45088 | tf_op jit(solution)/shard_map/ppermute | solution.py:330
  21.6 0.0 collective-permute-done.10.refs_3_
  21.6 1.1 %shard_map.64 = bf16[8,4096]{1,0:T(8,128)(2,1)} custom-call(bf16[176,128]{1,0:T(8,128)(2,1)S(1)} %get-tuple-element.20.refs_0_, bf16[176,128]{1,0:T(8,128)(2,1)S(1)} %collective-permute-done.8.refs_1_, bf16[176,128]{1,0:T(8,128)(2,1)S(1)} %collective-permute-done.9.refs_2_, bf16[176,128]{1,0:T(8,128)(2,1)S(1)} %collective-permute-done.10.refs_3_), custom_call_target="tpu_custom_call" | custom-call | tf_op jit(solution)/shard_map/pallas_call | solution.py:437
  (1 shorter events, 0.0 us)
Async XLA Ops:
  0.6 9.2 %copy-start = (bf16[8,4096]{1,0:T(8,128)(2,1)S(1)}, bf16[8,4096]{1,0:T(8,128)(2,1)}, u32[]{:S(2)}) copy-start(bf16[8,4096]{1,0:T(8,128)(2,1)} %tokens.1) | copy-start | bytes 196612
  0.6 9.2 %collective-permute-start.1 = (bf16[8,4096]{1,0:T(8,128)(2,1)}, bf16[8,4096]{1,0:T(8,128)(2,1)S(1)}, u32[]{:S(2)}, u32[]{:S(2)}) collective-permute-start(bf16[8,4096]{1,0:T(8,128)(2,1)} %tokens.1), channel_id=1, source_target_pairs={{0,2},{1,3},{2,0},{3,1},{4,6},{5,7},{6,4},{7,5},{8,10},{9,11},{10,... | collective-permute-start | bytes 196616 | tf_op jit(solution)/shard_map/ppermute | solution.py:326
  5.7 7.1 %copy-start.1 = (bf16[32,896]{1,0:T(8,128)(2,1)S(1)}, bf16[32,896]{1,0:T(8,128)(2,1)}, u32[]{:S(2)}) copy-start(bf16[32,896]{1,0:T(8,128)(2,1)} %refs_3_.1) | copy-start | bytes 172036
  5.7 4.2 %collective-permute-start = (bf16[1,3,64,128]{3,2,1,0:T(8,128)(2,1)S(1)}, bf16[1,3,64,128]{3,2,1,0:T(8,128)(2,1)S(1)}, u32[]{:S(2)}, u32[]{:S(2)}) collective-permute-start(bf16[1,3,64,128]{3,2,1,0:T(8,128)(2,1)S(1)} %shard_map.59.own), channel_id=1, source_target_pairs={{0,16},{4,20},{8,24},{12,28},{16,0},{20,4},{24,8},{28,12},{1,17},{... | collective-permute-start | bytes 147464 | tf_op jit(solution)/shard_map/ppermute | solution.py:326
  7.3 5.0 %collective-permute-start.3 = (bf16[1,3,64,128]{3,2,1,0:T(8,128)(2,1)S(1)}, bf16[1,3,64,128]{3,2,1,0:T(8,128)(2,1)S(1)}, u32[]{:S(2)}, u32[]{:S(2)}) collective-permute-start(bf16[1,3,64,128]{3,2,1,0:T(8,128)(2,1)S(1)} %shard_map.59.own), channel_id=1, source_target_pairs={{0,24},{4,28},{8,16},{12,20},{16,8},{20,12},{24,0},{28,4},{1,25},{... | collective-permute-start | bytes 147464 | tf_op jit(solution)/shard_map/ppermute | solution.py:326
  8.7 4.1 %collective-permute-start.2 = (bf16[1,3,64,128]{3,2,1,0:T(8,128)(2,1)S(1)}, bf16[1,3,64,128]{3,2,1,0:T(8,128)(2,1)S(1)}, u32[]{:S(2)}, u32[]{:S(2)}) collective-permute-start(bf16[1,3,64,128]{3,2,1,0:T(8,128)(2,1)S(1)} %shard_map.59.own), channel_id=1, source_target_pairs={{0,8},{4,12},{8,0},{12,4},{16,24},{20,28},{24,16},{28,20},{1,9},{5... | collective-permute-start | bytes 147464 | tf_op jit(solution)/shard_map/ppermute | solution.py:326
  9.9 4.2 %collective-permute-start.4 = (bf16[2,3,64,128]{3,2,1,0:T(8,128)(2,1)S(1)}, bf16[2,3,64,128]{3,2,1,0:T(8,128)(2,1)S(1)}, u32[]{:S(2)}, u32[]{:S(2)}) collective-permute-start(bf16[2,3,64,128]{3,2,1,0:T(8,128)(2,1)S(1)} %get-tuple-element.13.refs_0_), channel_id=1, source_target_pairs={{0,4},{4,0},{8,12},{12,8},{16,20},{20,16},{24,28},{28,24},{1,5},{5... | collective-permute-start | bytes 294920 | tf_op jit(solution)/shard_map/ppermute | solution.py:326
  10.0 8.7 %collective-permute-start.7 = (bf16[2,8,4096]{2,1,0:T(8,128)(2,1)S(1)}, bf16[2,8,4096]{2,1,0:T(8,128)(2,1)S(1)}, u32[]{:S(2)}, u32[]{:S(2)}) collective-permute-start(bf16[2,8,4096]{2,1,0:T(8,128)(2,1)S(1)} %get-tuple-element.14.refs_6_), channel_id=1, source_target_pairs={{0,1},{1,0},{2,3},{3,2},{4,5},{5,4},{6,7},{7,6},{8,9},{9,8},{10,11... | collective-permute-start | bytes 393224 | tf_op jit(solution)/shard_map/ppermute | solution.py:326
  12.3 1.2 %collective-permute-start.6 = (bf16[1,3,64,128]{3,2,1,0:T(8,128)(2,1)S(1)}, bf16[1,3,64,128]{3,2,1,0:T(8,128)(2,1)S(1)}, u32[]{:S(2)}, u32[]{:S(2)}) collective-permute-start(bf16[1,3,64,128]{3,2,1,0:T(8,128)(2,1)S(1)} %collective-permute-done.3.refs_2_), channel_id=1, source_target_pairs={{0,4},{4,0},{8,12},{12,8},{16,20},{20,16},{24,28},{28,24},{1,5},{5... | collective-permute-start | bytes 147464 | tf_op jit(solution)/shard_map/ppermute | solution.py:326
  12.8 1.2 %collective-permute-start.5 = (bf16[1,3,64,128]{3,2,1,0:T(8,128)(2,1)S(1)}, bf16[1,3,64,128]{3,2,1,0:T(8,128)(2,1)S(1)}, u32[]{:S(2)}, u32[]{:S(2)}) collective-permute-start(bf16[1,3,64,128]{3,2,1,0:T(8,128)(2,1)S(1)} %collective-permute-done.2.refs_1_), channel_id=1, source_target_pairs={{0,4},{4,0},{8,12},{12,8},{16,20},{20,16},{24,28},{28,24},{1,5},{5... | collective-permute-start | bytes 147464 | tf_op jit(solution)/shard_map/ppermute | solution.py:326
  14.4 7.0 %collective-permute-start.8 = (bf16[176,128]{1,0:T(8,128)(2,1)S(1)}, bf16[176,128]{1,0:T(8,128)(2,1)S(1)}, u32[]{:S(2)}, u32[]{:S(2)}) collective-permute-start(bf16[176,128]{1,0:T(8,128)(2,1)S(1)} %get-tuple-element.21), channel_id=1, source_target_pairs={{0,2},{1,3},{2,0},{3,1},{4,6},{5,7},{6,4},{7,5},{8,10},{9,11},{10,... | collective-permute-start | bytes 135176 | tf_op jit(solution)/shard_map/ppermute | solution.py:330
  14.8 6.8 %collective-permute-start.9 = (bf16[176,128]{1,0:T(8,128)(2,1)S(1)}, bf16[176,128]{1,0:T(8,128)(2,1)S(1)}, u32[]{:S(2)}, u32[]{:S(2)}) collective-permute-start(bf16[176,128]{1,0:T(8,128)(2,1)S(1)} %get-tuple-element.22), channel_id=1, source_target_pairs={{0,1},{1,2},{2,3},{3,0},{4,5},{5,6},{6,7},{7,4},{8,9},{9,10},{10,1... | collective-permute-start | bytes 135176 | tf_op jit(solution)/shard_map/ppermute | solution.py:330
  16.4 5.2 %collective-permute-start.10 = (bf16[176,128]{1,0:T(8,128)(2,1)S(1)}, bf16[176,128]{1,0:T(8,128)(2,1)S(1)}, u32[]{:S(2)}, u32[]{:S(2)}) collective-permute-start(bf16[176,128]{1,0:T(8,128)(2,1)S(1)} %get-tuple-element.23), channel_id=1, source_target_pairs={{0,3},{1,0},{2,1},{3,2},{4,7},{5,4},{6,5},{7,6},{8,11},{9,8},{10,9... | collective-permute-start | bytes 135176 | tf_op jit(solution)/shard_map/ppermute | solution.py:330
